TPU v7x, 32 devices: a whole 2x2x4 slice. The times are simulated.
32 devices in a mesh: groups: 2 (over x), elec: 16 (over z, y, core).
Axes of the slice: x: 2, y: 2, z: 4, core: 2. Of those that a mesh axis runs over, the one named last changes fastest.
Arguments:
- features: bfloat16 [131072, 256], P(('groups', 'elec')), parts along dimension 0, may hold values from -6 to 6
- assignment: int32 [131072], P(('groups', 'elec')), parts along dimension 0, may hold values from 0 to 65535, as said below
- pairs: int32 [2048, 3], P(('groups', 'elec')), parts along dimension 0, may hold values from 0 to 1023, as said below
- w_query: bfloat16 [256, 256], replicated
- w_key: bfloat16 [256, 256], replicated
- w_value: bfloat16 [256, 256], replicated, may hold values from -0.375 to 0.375
- w_out: bfloat16 [256, 256], replicated, may hold values from -0.375 to 0.375
- w_mix: bfloat16 [256, 256], replicated, may hold values from -0.375 to 0.375
Outputs:
- mixed: bfloat16 [131072, 256], P(('groups', 'elec')), parts along dimension 0
There are 2 independent parts, one for each index of `groups`. A program takes and returns all parts, laid end to end along the dimension named above; an argument that names none is the same for every part. Nothing has to cross between parts.
Inputs may be any that keep to these rules, and one draw needn't show every extreme that they name: assignment is a permutation of the rows; each group of 512 rows of one walker on one device is filled from electrons of that same group. pairs[b, :] name blocks of block b's own walker (its blocks lie on the 8 devices whose index has the same remainder modulo 1024 // 512 as block b's device, 8 on each). Over the 64 reader blocks of one device, at most 25 of the listed key blocks lie on any one device (blocks d * 64 to (d + 1) * 64 - 1 lie on device d), and exactly 25 on some device.
All inputs are finite; a program needn't handle non-finite values.
Results may differ from a plain program's by a relative error of at most 0.0078.
Values may be sent and summed in bfloat16 or wider, within the bound.
No kernel may reach another device: no remote copies, remote signals or barrier semaphores. Data moves between devices by JAX's collectives and lax.ppermute only.
A program may use at most 128 MiB of HBM per device.

v0:
```python
import jax
import jax.numpy as jnp
from jax import lax
from jax.sharding import PartitionSpec as P

HEADS = 16
SPAN = 8


def shifted(x, axis, by):
    peers = lax.axis_size(axis)
    return lax.ppermute(x, axis, [(i, (i + by) % peers) for i in range(peers)])


def layer_norm(rows):
    mean = jnp.mean(rows, axis=-1, keepdims=True)
    centred = rows - mean
    variance = jnp.mean(centred * centred, axis=-1, keepdims=True)
    return centred * lax.rsqrt(variance + 1e-05)


def slot_table(listed, block_count, capacity, position, stride):
    flattened = listed.reshape(-1)
    owner_device = flattened // block_count
    within = flattened % block_count
    entries = flattened.shape[0]
    offset = (position - owner_device // stride) % SPAN
    alike = offset[:, None] == offset[None, :]
    earlier = jnp.arange(entries)[None, :] < jnp.arange(entries)[:, None]
    ranking = jnp.sum(jnp.where(alike & earlier, 1, 0), axis=1).astype(jnp.int32)
    slots = offset * capacity + ranking
    matches = slots[None, :] == jnp.arange(SPAN * capacity, dtype=jnp.int32)[:, None]
    tables = jnp.sum(jnp.where(matches, within[None, :], 0), axis=1)
    return (slots, tables.reshape(SPAN, capacity))


def body(features, assignment, pairs, w_query, w_key, w_value, w_out, w_mix):
    rows_dev, width = features.shape
    block_count, pair_count = pairs.shape
    cluster = rows_dev // block_count
    heads = HEADS
    head_width = width // heads
    capacity = (block_count * pair_count + SPAN - 1) // SPAN + 1
    stride = lax.axis_size("elec") // SPAN
    device_index = lax.axis_index("elec")
    position = device_index // stride
    local_rows = assignment - device_index * rows_dev
    placed = jnp.take(features, local_rows, axis=0)
    normed = layer_norm(placed.astype(jnp.float32)).astype(jnp.bfloat16)
    query = jnp.dot(normed, w_query, preferred_element_type=jnp.float32).astype(jnp.bfloat16)
    w_both = jnp.concatenate([w_key, w_value], axis=1)
    own_pairs = jnp.dot(normed, w_both, preferred_element_type=jnp.float32).astype(jnp.bfloat16)
    own_blocks = own_pairs.reshape(block_count, cluster, 2 * width)
    slots, tables = slot_table(pairs, block_count, capacity, position, stride)
    wanted_rows = [tables[0]]
    for offset_step in range(1, SPAN):
        incoming = shifted(tables[offset_step], "elec", -offset_step * stride)
        wanted_rows.append(incoming)
    demanded = jnp.stack(wanted_rows)
    outgoing = [jnp.take(own_blocks, demanded[step], axis=0) for step in range(SPAN)]
    pieces = [outgoing[0]]
    for offset_step in range(1, SPAN):
        pieces.append(shifted(outgoing[offset_step], "elec", offset_step * stride))
    arrived = jnp.stack(pieces).reshape(SPAN * capacity, cluster, 2 * width)
    remote = jnp.take(arrived, slots, axis=0).reshape(block_count, pair_count, cluster, 2 * width)
    query_blocks = query.reshape(block_count, cluster, width)
    scale = 1.0 / head_width**0.5

    def attend(args):
        block_query, own_block, listed = args
        gathered = jnp.concatenate([own_block[None], listed], axis=0).reshape(-1, 2 * width)
        set_keys = gathered[:, :width].reshape(-1, heads, head_width)
        set_values = gathered[:, width:].reshape(-1, heads, head_width)
        heads_query = block_query.reshape(cluster, heads, head_width)
        scores = (
            jnp.einsum("qhd,khd->hqk", heads_query, set_keys, preferred_element_type=jnp.float32)
            * scale
        )
        weights = jax.nn.softmax(scores, axis=-1).astype(jnp.bfloat16)
        result = jnp.einsum("hqk,khd->qhd", weights, set_values, preferred_element_type=jnp.float32)
        return result.astype(jnp.bfloat16).reshape(cluster, width)

    attended = lax.map(attend, (query_blocks, own_blocks, remote), batch_size=8)
    attended = attended.reshape(rows_dev, width)
    middle = (
        placed.astype(jnp.float32) + jnp.dot(attended, w_out, preferred_element_type=jnp.float32)
    ).astype(jnp.bfloat16)
    second = layer_norm(middle.astype(jnp.float32)).astype(jnp.bfloat16)
    mixed = middle.astype(jnp.float32) + jnp.tanh(
        jnp.dot(second, w_mix, preferred_element_type=jnp.float32)
    )
    return mixed.astype(jnp.bfloat16)


def solution(mesh):
    placed = (
        P(("groups", "elec"), None),
        P(("groups", "elec")),
        P(("groups", "elec"), None),
        P(),
        P(),
        P(),
        P(),
        P(),
    )
    return jax.shard_map(
        body, mesh=mesh, in_specs=placed, out_specs=P(("groups", "elec"), None), check_vma=False
    )
```

profile of v0, /device:TPU:8, one launch (start us, length us, event | category | flops | bytes accessed | tf_op | source)
XLA Modules:
  0.0 500.9 jit_solution(3416347615789687061)
XLA Ops:
  2.9 3.6 collective-permute-start.2
  12.4 17.0 %gather_fusion = bf16[4096,256]{1,0:T(8,128)(2,1)} fusion(bf16[4096,256]{1,0:T(8,128)(2,1)S(1)} %copy-done, s32[4096]{0:T(1024)S(1)} %fusion.40), kind=kCustom, calls=%fused_computation.8 | custom fusion | bytes 4210688 | tf_op jit(solution)/shard_map/jit(_take)/gather | solution.py:48
  36.1 3.3 convolution_convert_fusion
  50.4 4.1 gather_fusion.4
  57.3 4.1 gather_fusion.5
  61.4 4.1 gather_fusion.6
  65.5 4.1 gather_fusion.7
  82.6 4.1 gather_fusion.8
  96.4 29.6 %collective-permute-start.13 = (bf16[25,64,512]{2,1,0:T(8,128)(2,1)S(1)}, bf16[25,64,512]{2,1,0:T(8,128)(2,1)S(1)}, u32[]{:S(2)}, u32[]{:S(2)}) collective-permute-start(bf16[25,64,512]{2,1,0:T(8,128)(2,1)S(1)} %broadcast_select_fusion.2), channel_id=1, source_target_pairs={{0,14},{1,15},{2,0},{3,1},{4,2},{5,3},{6,4},{7,5},{8,6},{9,7},{10,... | collective-permute-start | bytes 4915208 | tf_op jit(solution)/shard_map/ppermute | solution.py:12
  131.6 137.9 %collective-permute-done.5 = bf16[25,64,512]{2,1,0:T(8,128)(2,1)} collective-permute-done((bf16[25,64,512]{2,1,0:T(8,128)(2,1)}, bf16[25,64,512]{2,1,0:T(8,128)(2,1)}, u32[]{:S(2)}, u32[]{:S(2)}) %collective-permute-start.5) | collective-permute-done | bytes 1638432 | tf_op jit(solution)/shard_map/ppermute | solution.py:12
  272.2 32.4 %collective-permute-done.7 = bf16[25,64,512]{2,1,0:T(8,128)(2,1)} collective-permute-done((bf16[25,64,512]{2,1,0:T(8,128)(2,1)}, bf16[25,64,512]{2,1,0:T(8,128)(2,1)}, u32[]{:S(2)}, u32[]{:S(2)}) %collective-permute-start.7) | collective-permute-done | bytes 1638432 | tf_op jit(solution)/shard_map/ppermute | solution.py:12
  307.3 29.2 %collective-permute-done.9 = bf16[25,64,512]{2,1,0:T(8,128)(2,1)} collective-permute-done((bf16[25,64,512]{2,1,0:T(8,128)(2,1)}, bf16[25,64,512]{2,1,0:T(8,128)(2,1)}, u32[]{:S(2)}, u32[]{:S(2)}) %collective-permute-start.9) | collective-permute-done | bytes 1638432 | tf_op jit(solution)/shard_map/ppermute | solution.py:12
  342.0 12.9 %gather_fusion.1 = bf16[192,64,512]{2,1,0:T(8,128)(2,1)} fusion(bf16[200,64,512]{2,1,0:T(8,128)(2,1)} %bitcast.100, s32[1024]{0:T(1024)S(1)} %pad_clamp_fusion), kind=kCustom, calls=%fused_computation.9 | custom fusion | bytes 25166592 | tf_op jit(solution)/shard_map/jit(_take)/gather | solution.py:65
  354.9 10.7 %broadcast_select_fusion = bf16[8,8,3,64,512]{4,3,2,1,0:T(8,128)(2,1)} fusion(bf16[8,8,3,64,512]{4,3,2,1,0:T(8,128)(2,1)} %bitcast.98, pred[8,8,3]{2,1,0:T(8,128)(4,1)S(1)} %compare_and_fusion), kind=kLoop, calls=%fused_computation.25 | loop fusion | flops 6291456 | bytes 25166016 | tf_op jit(solution)/shard_map/jit(_take)/select_n | solution.py:65
  365.6 124.7 %while.10 = (s32[]{:T(128)}, bf16[8,8,64,256]{3,2,1,0:T(8,128)(2,1)}, bf16[8,8,64,512]{3,2,1,0:T(8,128)(2,1)}, bf16[8,8,3,64,512]{4,3,2,1,0:T(8,128)(2,1)}, bf16[8,8,64,256]{3,2,1,0:T(8,128)(2,1)}, /*index=5*/s32[]{:T(128)}) while((s32[]{:T(128)}, bf16[8,8,64,256]{3,2,1,0:T(8,128)(2,1)}, bf16[8,8,64,512]{3,2,1,0:T(8,128)(2,1)}, ...), condition=%wide.region_7.9_spmd, body=%wide.region_4.8_spmd.sunk | while | flops 145883392 | bytes 38339152 | solution.py:83
  370.5 5.1 %fusion.70 = (f32[8,16,64]{2,1,0:T(8,128)S(1)}, f32[8,16,64,256]{3,2,1,0:T(8,128)}) fusion(bf16[8,64,16,16]{1,3,2,0:T(8,128)(2,1)S(1)} %bitcast.97, bf16[8,256,16,16]{1,3,2,0:T(8,128)(2,1)S(1)} %bitcast.87), kind=kOutput, calls=%fused_computation.165.clone.1 | convolution fusion | flops 73400576 | bytes 9732096 | tf_op jit(solution)/shard_map/while/body/eval_jaxpr/vmap()/sub | solution.py:79
  376.1 4.2 fusion.71
  386.1 5.1 %fusion.70 = (f32[8,16,64]{2,1,0:T(8,128)S(1)}, f32[8,16,64,256]{3,2,1,0:T(8,128)}) fusion(bf16[8,64,16,16]{1,3,2,0:T(8,128)(2,1)S(1)} %bitcast.97, bf16[8,256,16,16]{1,3,2,0:T(8,128)(2,1)S(1)} %bitcast.87), kind=kOutput, calls=%fused_computation.165.clone.1 | convolution fusion | flops 73400576 | bytes 9732096 | tf_op jit(solution)/shard_map/while/body/eval_jaxpr/vmap()/sub | solution.py:79
  391.6 4.2 fusion.71
  401.6 5.1 %fusion.70 = (f32[8,16,64]{2,1,0:T(8,128)S(1)}, f32[8,16,64,256]{3,2,1,0:T(8,128)}) fusion(bf16[8,64,16,16]{1,3,2,0:T(8,128)(2,1)S(1)} %bitcast.97, bf16[8,256,16,16]{1,3,2,0:T(8,128)(2,1)S(1)} %bitcast.87), kind=kOutput, calls=%fused_computation.165.clone.1 | convolution fusion | flops 73400576 | bytes 9732096 | tf_op jit(solution)/shard_map/while/body/eval_jaxpr/vmap()/sub | solution.py:79
  407.2 4.2 fusion.71
  417.2 5.1 %fusion.70 = (f32[8,16,64]{2,1,0:T(8,128)S(1)}, f32[8,16,64,256]{3,2,1,0:T(8,128)}) fusion(bf16[8,64,16,16]{1,3,2,0:T(8,128)(2,1)S(1)} %bitcast.97, bf16[8,256,16,16]{1,3,2,0:T(8,128)(2,1)S(1)} %bitcast.87), kind=kOutput, calls=%fused_computation.165.clone.1 | convolution fusion | flops 73400576 | bytes 9732096 | tf_op jit(solution)/shard_map/while/body/eval_jaxpr/vmap()/sub | solution.py:79
  422.8 4.2 fusion.71
  432.8 5.1 %fusion.70 = (f32[8,16,64]{2,1,0:T(8,128)S(1)}, f32[8,16,64,256]{3,2,1,0:T(8,128)}) fusion(bf16[8,64,16,16]{1,3,2,0:T(8,128)(2,1)S(1)} %bitcast.97, bf16[8,256,16,16]{1,3,2,0:T(8,128)(2,1)S(1)} %bitcast.87), kind=kOutput, calls=%fused_computation.165.clone.1 | convolution fusion | flops 73400576 | bytes 9732096 | tf_op jit(solution)/shard_map/while/body/eval_jaxpr/vmap()/sub | solution.py:79
  438.4 4.2 fusion.71
  448.4 5.1 %fusion.70 = (f32[8,16,64]{2,1,0:T(8,128)S(1)}, f32[8,16,64,256]{3,2,1,0:T(8,128)}) fusion(bf16[8,64,16,16]{1,3,2,0:T(8,128)(2,1)S(1)} %bitcast.97, bf16[8,256,16,16]{1,3,2,0:T(8,128)(2,1)S(1)} %bitcast.87), kind=kOutput, calls=%fused_computation.165.clone.1 | convolution fusion | flops 73400576 | bytes 9732096 | tf_op jit(solution)/shard_map/while/body/eval_jaxpr/vmap()/sub | solution.py:79
  454.0 4.2 fusion.71
  464.0 5.1 %fusion.70 = (f32[8,16,64]{2,1,0:T(8,128)S(1)}, f32[8,16,64,256]{3,2,1,0:T(8,128)}) fusion(bf16[8,64,16,16]{1,3,2,0:T(8,128)(2,1)S(1)} %bitcast.97, bf16[8,256,16,16]{1,3,2,0:T(8,128)(2,1)S(1)} %bitcast.87), kind=kOutput, calls=%fused_computation.165.clone.1 | convolution fusion | flops 73400576 | bytes 9732096 | tf_op jit(solution)/shard_map/while/body/eval_jaxpr/vmap()/sub | solution.py:79
  469.6 4.2 fusion.71
  479.6 5.1 %fusion.70 = (f32[8,16,64]{2,1,0:T(8,128)S(1)}, f32[8,16,64,256]{3,2,1,0:T(8,128)}) fusion(bf16[8,64,16,16]{1,3,2,0:T(8,128)(2,1)S(1)} %bitcast.97, bf16[8,256,16,16]{1,3,2,0:T(8,128)(2,1)S(1)} %bitcast.87), kind=kOutput, calls=%fused_computation.165.clone.1 | convolution fusion | flops 73400576 | bytes 9732096 | tf_op jit(solution)/shard_map/while/body/eval_jaxpr/vmap()/sub | solution.py:79
  485.2 4.2 fusion.71
  496.9 4.1 copy.39
  (188 shorter events, 124.8 us)
Async XLA Ops:
  0.0 12.4 %copy-start = (bf16[4096,256]{1,0:T(8,128)(2,1)S(1)}, bf16[4096,256]{1,0:T(8,128)(2,1)}, u32[]{:S(2)}) copy-start(bf16[4096,256]{1,0:T(8,128)(2,1)} %param.12) | copy-start | bytes 6291460
  1.5 37.9 %collective-permute-start = (s32[25]{0:T(128)S(1)}, s32[25]{0:T(128)S(1)}, u32[]{:S(2)}, u32[]{:S(2)}) collective-permute-start(s32[25]{0:T(128)S(1)} %get-tuple-element.71), channel_id=1, source_target_pairs={{0,14},{1,15},{2,0},{3,1},{4,2},{5,3},{6,4},{7,5},{8,6},{9,7},{10,... | collective-permute-start | bytes 308 | tf_op jit(solution)/shard_map/ppermute | solution.py:12
  2.9 41.1 %collective-permute-start.2 = (s32[25]{0:T(128)S(1)}, s32[25]{0:T(128)S(1)}, u32[]{:S(2)}, u32[]{:S(2)}) collective-permute-start(s32[25]{0:T(128)S(1)} %get-tuple-element.70), channel_id=1, source_target_pairs={{0,12},{1,13},{2,14},{3,15},{4,0},{5,1},{6,2},{7,3},{8,4},{9,5},{1... | collective-permute-start | bytes 308 | tf_op jit(solution)/shard_map/ppermute | solution.py:12
  6.5 42.3 %collective-permute-start.4 = (s32[25]{0:T(128)S(1)}, s32[25]{0:T(128)S(1)}, u32[]{:S(2)}, u32[]{:S(2)}) collective-permute-start(s32[25]{0:T(128)S(1)} %get-tuple-element.69), channel_id=1, source_target_pairs={{0,10},{1,11},{2,12},{3,13},{4,14},{5,15},{6,0},{7,1},{8,2},{9,3},... | collective-permute-start | bytes 308 | tf_op jit(solution)/shard_map/ppermute | solution.py:12
  6.5 50.8 %collective-permute-start.8 = (s32[25]{0:T(128)S(1)}, s32[25]{0:T(128)S(1)}, u32[]{:S(2)}, u32[]{:S(2)}) collective-permute-start(s32[25]{0:T(128)S(1)} %get-tuple-element.67), channel_id=1, source_target_pairs={{0,6},{1,7},{2,8},{3,9},{4,10},{5,11},{6,12},{7,13},{8,14},{9,15},... | collective-permute-start | bytes 308 | tf_op jit(solution)/shard_map/ppermute | solution.py:12
  9.5 52.0 %collective-permute-start.6 = (s32[25]{0:T(128)S(1)}, s32[25]{0:T(128)S(1)}, u32[]{:S(2)}, u32[]{:S(2)}) collective-permute-start(s32[25]{0:T(128)S(1)} %get-tuple-element.68), channel_id=1, source_target_pairs={{0,8},{1,9},{2,10},{3,11},{4,12},{5,13},{6,14},{7,15},{8,0},{9,1},... | collective-permute-start | bytes 308 | tf_op jit(solution)/shard_map/ppermute | solution.py:12
  32.4 3.7 copy-start.2
  32.4 1.3 copy-start.6
  33.7 2.4 copy-start.7
  33.7 2.3 copy-start.8
  39.5 38.9 %collective-permute-start.12 = (s32[25]{0:T(128)S(1)}, s32[25]{0:T(128)S(1)}, u32[]{:S(2)}, u32[]{:S(2)}) collective-permute-start(s32[25]{0:T(128)S(1)} %get-tuple-element.65), channel_id=1, source_target_pairs={{0,2},{1,3},{2,4},{3,5},{4,6},{5,7},{6,8},{7,9},{8,10},{9,11},{10,... | collective-permute-start | bytes 308 | tf_op jit(solution)/shard_map/ppermute | solution.py:12
  44.0 35.9 %collective-permute-start.10 = (s32[25]{0:T(128)S(1)}, s32[25]{0:T(128)S(1)}, u32[]{:S(2)}, u32[]{:S(2)}) collective-permute-start(s32[25]{0:T(128)S(1)} %get-tuple-element.66), channel_id=1, source_target_pairs={{0,4},{1,5},{2,6},{3,7},{4,8},{5,9},{6,10},{7,11},{8,12},{9,13},{1... | collective-permute-start | bytes 308 | tf_op jit(solution)/shard_map/ppermute | solution.py:12
  48.8 43.9 %collective-permute-start.1 = (bf16[25,64,512]{2,1,0:T(8,128)(2,1)}, bf16[25,64,512]{2,1,0:T(8,128)(2,1)}, u32[]{:S(2)}, u32[]{:S(2)}) collective-permute-start(bf16[25,64,512]{2,1,0:T(8,128)(2,1)} %broadcast_select_fusion.8), channel_id=1, source_target_pairs={{0,2},{1,3},{2,4},{3,5},{4,6},{5,7},{6,8},{7,9},{8,10},{9,11},{10,... | collective-permute-start | bytes 4915208 | tf_op jit(solution)/shard_map/ppermute | solution.py:12
  57.3 39.1 %collective-permute-start.3 = (bf16[25,64,512]{2,1,0:T(8,128)(2,1)}, bf16[25,64,512]{2,1,0:T(8,128)(2,1)}, u32[]{:S(2)}, u32[]{:S(2)}) collective-permute-start(bf16[25,64,512]{2,1,0:T(8,128)(2,1)} %broadcast_select_fusion.7), channel_id=1, source_target_pairs={{0,4},{1,5},{2,6},{3,7},{4,8},{5,9},{6,10},{7,11},{8,12},{9,13},{1... | collective-permute-start | bytes 4915208 | tf_op jit(solution)/shard_map/ppermute | solution.py:12
  69.6 3.0 copy-start.4
  72.6 2.0 copy-start.3
  76.0 193.5 %collective-permute-start.5 = (bf16[25,64,512]{2,1,0:T(8,128)(2,1)}, bf16[25,64,512]{2,1,0:T(8,128)(2,1)}, u32[]{:S(2)}, u32[]{:S(2)}) collective-permute-start(bf16[25,64,512]{2,1,0:T(8,128)(2,1)} %broadcast_select_fusion.6), channel_id=1, source_target_pairs={{0,6},{1,7},{2,8},{3,9},{4,10},{5,11},{6,12},{7,13},{8,14},{9,15},... | collective-permute-start | bytes 4915208 | tf_op jit(solution)/shard_map/ppermute | solution.py:12
  78.4 226.2 %collective-permute-start.7 = (bf16[25,64,512]{2,1,0:T(8,128)(2,1)}, bf16[25,64,512]{2,1,0:T(8,128)(2,1)}, u32[]{:S(2)}, u32[]{:S(2)}) collective-permute-start(bf16[25,64,512]{2,1,0:T(8,128)(2,1)} %broadcast_select_fusion.5), channel_id=1, source_target_pairs={{0,8},{1,9},{2,10},{3,11},{4,12},{5,13},{6,14},{7,15},{8,0},{9,1},... | collective-permute-start | bytes 4915208 | tf_op jit(solution)/shard_map/ppermute | solution.py:12
  79.9 256.7 %collective-permute-start.9 = (bf16[25,64,512]{2,1,0:T(8,128)(2,1)}, bf16[25,64,512]{2,1,0:T(8,128)(2,1)}, u32[]{:S(2)}, u32[]{:S(2)}) collective-permute-start(bf16[25,64,512]{2,1,0:T(8,128)(2,1)} %broadcast_select_fusion.4), channel_id=1, source_target_pairs={{0,10},{1,11},{2,12},{3,13},{4,14},{5,15},{6,0},{7,1},{8,2},{9,3},... | collective-permute-start | bytes 4915208 | tf_op jit(solution)/shard_map/ppermute | solution.py:12
  86.7 1.7 copy-start.5
  92.7 246.6 %collective-permute-start.11 = (bf16[25,64,512]{2,1,0:T(8,128)(2,1)}, bf16[25,64,512]{2,1,0:T(8,128)(2,1)S(1)}, u32[]{:S(2)}, u32[]{:S(2)}) collective-permute-start(bf16[25,64,512]{2,1,0:T(8,128)(2,1)} %broadcast_select_fusion.3), channel_id=1, source_target_pairs={{0,12},{1,13},{2,14},{3,15},{4,0},{5,1},{6,2},{7,3},{8,4},{9,5},{1... | collective-permute-start | bytes 4915208 | tf_op jit(solution)/shard_map/ppermute | solution.py:12
  96.4 244.3 %collective-permute-start.13 = (bf16[25,64,512]{2,1,0:T(8,128)(2,1)S(1)}, bf16[25,64,512]{2,1,0:T(8,128)(2,1)S(1)}, u32[]{:S(2)}, u32[]{:S(2)}) collective-permute-start(bf16[25,64,512]{2,1,0:T(8,128)(2,1)S(1)} %broadcast_select_fusion.2), channel_id=1, source_target_pairs={{0,14},{1,15},{2,0},{3,1},{4,2},{5,3},{6,4},{7,5},{8,6},{9,7},{10,... | collective-permute-start | bytes 4915208 | tf_op jit(solution)/shard_map/ppermute | solution.py:12
  365.6 124.8 %copy-start.9 = (bf16[256,256]{1,0:T(8,128)(2,1)S(1)}, bf16[256,256]{1,0:T(8,128)(2,1)}, u32[]{:S(2)}) copy-start(bf16[256,256]{1,0:T(8,128)(2,1)} %param.18) | copy-start | bytes 393220
  493.4 0.9 copy-start.10
  494.3 6.6 %copy-start.1 = (bf16[4096,256]{1,0:T(8,128)(2,1)S(1)}, bf16[4096,256]{1,0:T(8,128)(2,1)}, u32[]{:S(2)}) copy-start(bf16[4096,256]{1,0:T(8,128)(2,1)} %param.12) | copy-start | bytes 6291460
where the time goes:
time: 503 us; the launch traced here: 501 us
  waiting for transfers between devices  202 us (40%)
  local copies, waits for them, and re-layouts  133 us (26%)
  matrix products  85.5 us (17%)
  starting transfers between devices  50.6 us (10%)
  other arithmetic  29.2 us (6%)
    ppermute x14, waiting for transfers between devices, shifted(): return lax.ppermute(x, axis, [(i, (i + by) % peers) for i in range(peers)])  202 us
    ppermute x14, starting transfers between devices, shifted(): return lax.ppermute(x, axis, [(i, (i + by) % peers) for i in range(peers)])  50.6 us
    sub x8, matrix products, attend(): weights = jax.nn.softmax(scores, axis=-1).astype(jnp.bfloat16)  40.5 us
    dot_general x8, matrix products, attend(): jnp.einsum('hqk,khd->qhd', weights, set_values, preferred_element_type=jn...  33.7 us
    gather x8, local copies, waits for them, and re-layouts, body(): jnp.take(own_blocks, demanded[step], axis=0)  28.9 us
    gather x2, local copies, waits for them, and re-layouts, body(): placed = jnp.take(features, local_rows, axis=0)  20 us
    unnamed x29, local copies, waits for them, and re-layouts  17.1 us
    gather x1, local copies, waits for them, and re-layouts, body(): jnp.take(arrived, slots, axis=0)  12.9 us
  transfers between devices with their start and end apart: 14, of which 4 were waited for; matrix products, arithmetic and copies ran while one was open for 17% of the time, Pallas kernels for 0%

commit v1 on v0

v1 whole, which is shorter than its diff:
```python
import functools

import jax
import jax.numpy as jnp
from jax import lax
from jax.experimental import pallas as pl
from jax.experimental.pallas import tpu as pltpu
from jax.sharding import PartitionSpec as P

HEADS = 16
SPAN = 8
SUB = 8
CHUNKS = 4
VMEM_BYTES = 48 * 1024 * 1024

NT = (((1,), (1,)), ((), ()))


def layer_norm(rows):
    mean = jnp.mean(rows, axis=-1, keepdims=True)
    centred = rows - mean
    variance = jnp.mean(centred * centred, axis=-1, keepdims=True)
    return centred * lax.rsqrt(variance + 1e-05)


def place_kernel(features_ref, assignment_ref, placed_ref, normed_ref):
    rows = features_ref.shape[0]
    lane = 128
    features = features_ref[...]
    columns = lax.broadcasted_iota(jnp.int32, (lane, rows), 1)
    for part in range(rows // lane):
        chosen = assignment_ref[0, :, part * lane : (part + 1) * lane] & (rows - 1)
        chosen = jnp.broadcast_to(chosen, (lane, lane)).T
        chosen = jnp.concatenate([chosen] * (rows // lane), axis=1)
        one_hot = jnp.where(chosen == columns, 1.0, 0.0).astype(jnp.bfloat16)
        placed = jnp.dot(one_hot, features, preferred_element_type=jnp.float32)
        placed_ref[pl.ds(part * lane, lane), :] = placed.astype(jnp.bfloat16)
        normed_ref[pl.ds(part * lane, lane), :] = layer_norm(placed).astype(jnp.bfloat16)


def place(features, assignment, first, count, rows):
    width = features.shape[1]
    out = jax.ShapeDtypeStruct((count * rows, width), jnp.bfloat16)
    return pl.pallas_call(
        place_kernel,
        grid=(count,),
        in_specs=[
            pl.BlockSpec((rows, width), lambda i: (first + i, 0)),
            pl.BlockSpec((1, 1, rows), lambda i: (first + i, 0, 0)),
        ],
        out_specs=[pl.BlockSpec((rows, width), lambda i: (i, 0))] * 2,
        out_shape=[out, out],
        cost_estimate=pl.CostEstimate(
            flops=2 * count * rows * rows * width,
            bytes_accessed=6 * count * rows * width,
            transcendentals=0,
        ),
        compiler_params=pltpu.CompilerParams(vmem_limit_bytes=VMEM_BYTES),
        name="place_rows",
    )(features, assignment)


def attend_kernel(
    table_ref,
    source_ref,
    normed_ref,
    placed_ref,
    query_ref,
    key_ref,
    value_ref,
    out_w_ref,
    mix_ref,
    *rest,
    pair_count,
):
    mixed_ref, attended_ref = rest[-2:]
    walker = pl.program_id(0)
    rows, width = normed_ref.shape
    cluster = rows // SUB
    head_width = width // HEADS
    group = 4
    span = group * head_width
    tile = group * cluster
    row_head = lax.broadcasted_iota(jnp.int32, (width, tile), 0) // head_width % group
    lane_head = lax.broadcasted_iota(jnp.int32, (width, tile), 1) // cluster
    diagonal = row_head == lane_head
    fold_row = lax.broadcasted_iota(jnp.int32, (cluster, tile), 0)
    fold_lane = lax.broadcasted_iota(jnp.int32, (cluster, tile), 1) % cluster
    fold = jnp.where(fold_row == fold_lane, 1.0, 0.0).astype(jnp.bfloat16)

    def one_block(block, carry):
        own = normed_ref[pl.ds(pl.multiple_of(block * cluster, cluster), cluster), :]
        base = (walker * SUB + block) * pair_count
        listed = [source_ref[table_ref[base + j]] for j in range(pair_count)]
        members = jnp.concatenate([own] + listed, axis=0)
        keys = jnp.dot(members, key_ref[...], preferred_element_type=jnp.float32)
        keys = keys.astype(jnp.bfloat16)
        values = lax.dot_general(value_ref[...], members, NT, preferred_element_type=jnp.float32)
        values = values.astype(jnp.bfloat16)
        own_tiled = jnp.concatenate([own] * group, axis=0)
        query = lax.dot_general(query_ref[...], own_tiled, NT, preferred_element_type=jnp.float32)
        query = query.astype(jnp.bfloat16) * jnp.bfloat16(1.0 / head_width**0.5)
        query = jnp.where(diagonal, query, jnp.bfloat16(0.0))
        pieces = []
        for t in range(HEADS // group):
            lo = t * span // 128 * 128
            zeros = jnp.zeros((span, tile), jnp.bfloat16)
            picked = query[t * span : (t + 1) * span]
            ahead, behind = t * span - lo, lo + 128 - (t + 1) * span
            stack = [zeros] * (ahead // span) + [picked] + [zeros] * (behind // span)
            scores = jnp.dot(
                keys[:, lo : lo + 128],
                jnp.concatenate(stack, axis=0),
                preferred_element_type=jnp.float32,
            )
            top = jnp.max(scores, axis=0, keepdims=True)
            weights = jnp.exp(scores - top)
            total = jnp.sum(weights, axis=0, keepdims=True)
            result = jnp.dot(
                values[t * span : (t + 1) * span],
                weights.astype(jnp.bfloat16),
                preferred_element_type=jnp.float32,
            )
            result = result * (1.0 / total)
            pieces.append(jnp.where(diagonal[:span], result, 0.0).astype(jnp.bfloat16))
        stacked = jnp.concatenate(pieces, axis=0)
        attended = lax.dot_general(fold, stacked, NT, preferred_element_type=jnp.float32)
        attended_ref[pl.ds(pl.multiple_of(block * cluster, cluster), cluster), :] = attended.astype(
            jnp.bfloat16
        )
        return carry

    lax.fori_loop(0, SUB, one_block, 0)
    middle = placed_ref[...].astype(jnp.float32) + jnp.dot(
        attended_ref[...], out_w_ref[...], preferred_element_type=jnp.float32
    )
    middle = middle.astype(jnp.bfloat16).astype(jnp.float32)
    second = layer_norm(middle).astype(jnp.bfloat16)
    mixed = middle + jnp.tanh(jnp.dot(second, mix_ref[...], preferred_element_type=jnp.float32))
    mixed_ref[...] = mixed.astype(jnp.bfloat16)


def attend(table, source, normed, placed, weights, so_far, first, total_rows, pair_count):
    rows_here, width = normed.shape
    cluster = source.shape[-2]
    rows = SUB * cluster
    count = rows_here // rows
    whole = pl.BlockSpec((width, width), lambda i, t: (0, 0))
    local = pl.BlockSpec((rows, width), lambda i, t: (i, 0))
    in_specs = [
        pl.BlockSpec(source.shape, lambda i, t: (0, 0, 0)),
        local,
        local,
    ] + [whole] * 5
    operands = [source, normed, placed, *weights]
    aliases = {}
    if so_far is not None:
        in_specs.append(pl.BlockSpec(memory_space=pl.ANY))
        operands.append(so_far)
        aliases = {len(operands): 0}
    return pl.pallas_call(
        functools.partial(attend_kernel, pair_count=pair_count),
        grid_spec=pltpu.PrefetchScalarGridSpec(
            num_scalar_prefetch=1,
            grid=(count,),
            in_specs=in_specs,
            out_specs=pl.BlockSpec((rows, width), lambda i, t: (first + i, 0)),
            scratch_shapes=[pltpu.VMEM((rows, width), jnp.bfloat16)],
        ),
        out_shape=jax.ShapeDtypeStruct((total_rows, width), jnp.bfloat16),
        input_output_aliases=aliases,
        cost_estimate=pl.CostEstimate(
            flops=count * SUB * 4 * 1024 * 1024 * 1024 // 4,
            bytes_accessed=source.size * 2 + 6 * rows_here * width,
            transcendentals=rows_here * HEADS * (pair_count + 1) * cluster,
        ),
        compiler_params=pltpu.CompilerParams(vmem_limit_bytes=VMEM_BYTES),
        name="attend_walkers",
    )(table, *operands)


def body(features, assignment, pairs, w_query, w_key, w_value, w_out, w_mix):
    rows_dev, width = features.shape
    block_count, pair_count = pairs.shape
    cluster = rows_dev // block_count
    walkers = block_count // SUB
    rows = SUB * cluster
    stride = lax.axis_size("elec") // SPAN
    groups = [[rest + place_ * stride for place_ in range(SPAN)] for rest in range(stride)]
    assignment = assignment.reshape(walkers, 1, rows)
    weights = (w_query.T, w_key, w_value.T, w_out, w_mix)
    each = walkers // CHUNKS
    owner = pairs // block_count // stride
    within = pairs % block_count % (each * SUB)
    table = (owner * (each * SUB) + within).reshape(CHUNKS, -1)
    mixed = None
    local = [place(features, assignment, c * each, each, rows) for c in range(CHUNKS)]
    gathered = [
        lax.all_gather(normed, "elec", axis_index_groups=groups, axis=0, tiled=True)
        for _, normed in local
    ]
    for c in range(CHUNKS):
        placed, normed = local[c]
        source = gathered[c].reshape(SPAN * each * SUB, cluster, width)
        mixed = attend(
            table[c], source, normed, placed, weights, mixed, c * each, rows_dev, pair_count
        )
    return mixed


def solution(mesh):
    placed = (
        P(("groups", "elec"), None),
        P(("groups", "elec")),
        P(("groups", "elec"), None),
        P(),
        P(),
        P(),
        P(),
        P(),
    )
    return jax.shard_map(
        body, mesh=mesh, in_specs=placed, out_specs=P(("groups", "elec"), None), check_vma=False
    )
```

time: 503 us -> 346 us (0.69)
  Pallas kernels: 0 us -> 122 us
  local copies, waits for them, and re-layouts: 133 us -> 15.5 us
  matrix products: 85.5 us -> 0 us
  starting transfers between devices: 50.6 us -> 0.13 us
  other arithmetic: 29.2 us -> 0.7 us
  between operations: 0.29 us -> 13.2 us
  waiting for transfers between devices: 202 us -> 192 us
    ppermute x14 -> x0, waiting for transfers between devices: 202 us -> none  [shifted(): return lax.ppermute(x, axis, [(i, (i + by) % peers) for i in range(peers)])]
    all_gather x0 -> x4, waiting for transfers between devices: none -> 192 us  [body(): lax.all_gather(normed, 'elec', axis_index_groups=groups, axis=0, tiled=True)]
    pallas_call x0 -> x8, Pallas kernels: none -> 122 us  [the longest x4 115 us: attend(): pl.pallas_call(functools.partial(attend_kernel, pair_count=pair_count), g...]
    gather x11 -> x0, local copies, waits for them, and re-layouts: 61.8 us -> none  [the longest x8 28.9 us: body(): jnp.take(own_blocks, demanded[step], axis=0)]
    ppermute x14 -> x0, starting transfers between devices: 50.6 us -> none  [shifted(): return lax.ppermute(x, axis, [(i, (i + by) % peers) for i in range(peers)])]
    dot_general x12 -> x0, matrix products: 45 us -> none  [the longest x8 33.7 us: attend(): jnp.einsum('hqk,khd->qhd', weights, set_values, preferred_element_type=jn...]
    sub x8 -> x0, matrix products: 40.5 us -> none  [attend(): weights = jax.nn.softmax(scores, axis=-1).astype(jnp.bfloat16)]
    select_n x17 -> x0, other arithmetic: 22.4 us -> none  [the longest x14 11.6 us: body(): jnp.take(own_blocks, demanded[step], axis=0)]
  transfers between devices with their start and end apart: 14 -> 4, of which waited for: 4 -> 4; matrix products, arithmetic and copies ran while one was open for 17% -> 1% of each run, Pallas kernels for 0% -> 27%
where the time goes in v1:
time: 346 us; the launch traced here: 344 us
  waiting for transfers between devices  192 us (55%)
  Pallas kernels  122 us (35%)
  local copies, waits for them, and re-layouts  15.5 us (4%)
  between operations  13.2 us (4%)
    all_gather x4, waiting for transfers between devices, body(): lax.all_gather(normed, 'elec', axis_index_groups=groups, axis=0, tiled=True)  192 us
    pallas_call x4, Pallas kernels, attend(): pl.pallas_call(functools.partial(attend_kernel, pair_count=pair_count), g...  115 us
    unnamed x32, local copies, waits for them, and re-layouts  14.7 us
    pallas_call x4, Pallas kernels, place(): pl.pallas_call(place_kernel, grid=(count,), in_specs=[pl.BlockSpec((rows,...  7.28 us
  transfers between devices with their start and end apart: 4, of which 4 were waited for; matrix products, arithmetic and copies ran while one was open for 1% of the time, Pallas kernels for 27%

profile of v1, /device:TPU:8, one launch (start us, length us, event | category | flops | bytes accessed | tf_op | source)
XLA Modules:
  0.0 343.7 jit_solution(15084358652102768223)
XLA Ops:
  6.5 1.6 copy-done
  8.1 0.7 copy-done.2
  8.9 1.8 place_rows.7
  10.7 1.8 place_rows.6
  12.6 1.8 place_rows.5
  14.5 0.8 copy-done.8
  15.3 1.8 place_rows.4
  17.2 0.8 copy-done.10
  18.0 0.7 fusion.2
  18.7 0.1 fusion.6
  18.8 0.1 copy.23
  18.9 0.1 squeeze.15.table_ref
  19.0 0.1 copy.22
  19.0 0.1 squeeze.14.table_ref
  19.1 0.1 copy.21
  19.2 0.1 squeeze.13.table_ref
  19.3 0.1 copy.18
  19.4 0.1 squeeze.12.table_ref
  19.5 1.0 copy.19
  20.5 1.0 copy.20
  21.5 63.2 %all-gather.11.cloned.1.call-done = bf16[8192,256]{1,0:T(8,128)(2,1)} async-done(((bf16[1024,256]{1,0:T(8,128)(2,1)}), bf16[8192,256]{1,0:T(8,128)(2,1)}) %all-gather.11.cloned.1.call-update) | async-done | bytes 4194320 | tf_op jit(solution)/shard_map/all_gather | solution.py:199
  84.7 2.2 copy-done.4
  86.9 28.7 %attend_walkers.4.rest_0_ = bf16[4096,256]{1,0:T(8,128)(2,1)} custom-call(s32[48]{0:T(128)S(1)} %squeeze.15.table_ref, bf16[128,64,256]{2,1,0:T(8,128)(2,1)S(1)} %bitcast.19, bf16[1024,256]{1,0:T(8,128)(2,1)} %get-tuple-element.19.normed_ref, bf16[1024,256]{1,0:T(8,128)(2,1)S(1)} %get-tuple-element.20.placed_ref, bf16[256,256]{1,0:T(8,128)(2,1)S(1)} %bitcast.11, ...), custom_call_target="tpu_custom_call" | custom-call | flops 17179869184 | bytes 5767168 | tf_op jit(solution)/shard_map/attend_walkers/pallas_call | solution.py:161
  115.7 43.0 %all-gather.9.cloned.1.call-done = bf16[8192,256]{1,0:T(8,128)(2,1)} async-done(((bf16[1024,256]{1,0:T(8,128)(2,1)}), bf16[8192,256]{1,0:T(8,128)(2,1)}) %all-gather.9.cloned.1.call-update) | async-done | bytes 4194320 | tf_op jit(solution)/shard_map/all_gather | solution.py:199
  158.6 2.2 copy-done.5
  160.8 28.8 %attend_walkers.5.rest_0_ = bf16[4096,256]{1,0:T(8,128)(2,1)} custom-call(s32[48]{0:T(128)S(1)} %squeeze.14.table_ref, bf16[128,64,256]{2,1,0:T(8,128)(2,1)S(1)} %bitcast.20, bf16[1024,256]{1,0:T(8,128)(2,1)} %get-tuple-element.17.normed_ref, bf16[1024,256]{1,0:T(8,128)(2,1)S(1)} %get-tuple-element.18.placed_ref, ...), custom_call_target="tpu_custom_call", output_to_operand_aliasing={{}: (9, {})} | custom-call | flops 17179869184 | bytes 5767168 | tf_op jit(solution)/shard_map/attend_walkers/pallas_call | solution.py:161
  189.6 43.0 %all-gather.7.cloned.1.call-done = bf16[8192,256]{1,0:T(8,128)(2,1)} async-done(((bf16[1024,256]{1,0:T(8,128)(2,1)}), bf16[8192,256]{1,0:T(8,128)(2,1)}) %all-gather.7.cloned.1.call-update) | async-done | bytes 4194320 | tf_op jit(solution)/shard_map/all_gather | solution.py:199
  232.6 2.2 copy-done.6
  234.7 28.7 %attend_walkers.6.rest_0_ = bf16[4096,256]{1,0:T(8,128)(2,1)} custom-call(s32[48]{0:T(128)S(1)} %squeeze.13.table_ref, bf16[128,64,256]{2,1,0:T(8,128)(2,1)S(1)} %bitcast.21, bf16[1024,256]{1,0:T(8,128)(2,1)} %get-tuple-element.15.normed_ref, bf16[1024,256]{1,0:T(8,128)(2,1)S(1)} %copy-done.9, ...), custom_call_target="tpu_custom_call", output_to_operand_aliasing={{}: (9, {})} | custom-call | flops 17179869184 | bytes 5767168 | tf_op jit(solution)/shard_map/attend_walkers/pallas_call | solution.py:161
  263.5 42.7 %all-gather.5.cloned.1.call-done = bf16[8192,256]{1,0:T(8,128)(2,1)} async-done(((bf16[1024,256]{1,0:T(8,128)(2,1)}), bf16[8192,256]{1,0:T(8,128)(2,1)}) %all-gather.5.cloned.1.call-update) | async-done | bytes 4194320 | tf_op jit(solution)/shard_map/all_gather | solution.py:199
  306.2 2.2 copy-done.7
  308.4 28.7 %attend_walkers.7 = bf16[4096,256]{1,0:T(8,128)(2,1)} custom-call(s32[48]{0:T(128)S(1)} %squeeze.12.table_ref, bf16[128,64,256]{2,1,0:T(8,128)(2,1)S(1)} %bitcast.22, bf16[1024,256]{1,0:T(8,128)(2,1)} %get-tuple-element.13.normed_ref, bf16[1024,256]{1,0:T(8,128)(2,1)S(1)} %copy-done.11, ...), custom_call_target="tpu_custom_call", output_to_operand_aliasing={{}: (9, {})} | custom-call | flops 17179869184 | bytes 5767168 | tf_op jit(solution)/shard_map/attend_walkers/pallas_call | solution.py:161
  (30 shorter events, 0.2 us)
Async XLA Ops:
  6.5 78.2 %all-gather.11.cloned.1.call-start = ((), (), s32[]{:S(2)}) async-start(), calls=%async_computation.3 | async-start | bytes 4718592 | tf_op jit(solution)/shard_map/all_gather | solution.py:199
  6.5 1.6 copy-start
  8.1 0.7 copy-start.2
  8.8 1.9 copy-start.1
  8.8 1.9 copy-start.3
  10.7 147.9 %all-gather.9.cloned.1.call-start = ((), (), s32[]{:S(2)}) async-start(), calls=%async_computation.2 | async-start | bytes 4718592 | tf_op jit(solution)/shard_map/all_gather | solution.py:199
  12.6 220.0 %all-gather.7.cloned.1.call-start = ((), (), s32[]{:S(2)}) async-start(), calls=%async_computation.1 | async-start | bytes 4718592 | tf_op jit(solution)/shard_map/all_gather | solution.py:199
  14.5 0.8 copy-start.8
  15.3 69.5 %copy-start.12 = (bf16[256,256]{1,0:T(8,128)(2,1)S(1)}, bf16[256,256]{1,0:T(8,128)(2,1)}, u32[]{:S(2)}) copy-start(bf16[256,256]{1,0:T(8,128)(2,1)} %key_ref.7) | copy-start | bytes 393220
  15.3 69.5 %copy-start.13 = (bf16[256,256]{1,0:T(8,128)(2,1)S(1)}, bf16[256,256]{1,0:T(8,128)(2,1)}, u32[]{:S(2)}) copy-start(bf16[256,256]{1,0:T(8,128)(2,1)} %out_w_ref.7) | copy-start | bytes 393220
  15.3 69.5 %copy-start.14 = (bf16[256,256]{1,0:T(8,128)(2,1)S(1)}, bf16[256,256]{1,0:T(8,128)(2,1)}, u32[]{:S(2)}) copy-start(bf16[256,256]{1,0:T(8,128)(2,1)} %mix_ref.7) | copy-start | bytes 393220
  15.3 290.9 %all-gather.5.cloned.1.call-start = ((), (), s32[]{:S(2)}) async-start(), calls=%async_computation | async-start | bytes 4718592 | tf_op jit(solution)/shard_map/all_gather | solution.py:199
  17.2 0.8 copy-start.10
  84.7 2.2 copy-start.4
  158.6 2.2 copy-start.5
  160.8 71.8 %copy-start.9 = (bf16[1024,256]{1,0:T(8,128)(2,1)S(1)}, bf16[1024,256]{1,0:T(8,128)(2,1)}, u32[]{:S(2)}) copy-start(bf16[1024,256]{1,0:T(8,128)(2,1)} %copy-done.8) | copy-start | bytes 1572868
  232.6 2.2 copy-start.6
  234.7 71.5 %copy-start.11 = (bf16[1024,256]{1,0:T(8,128)(2,1)S(1)}, bf16[1024,256]{1,0:T(8,128)(2,1)}, u32[]{:S(2)}) copy-start(bf16[1024,256]{1,0:T(8,128)(2,1)} %copy-done.10) | copy-start | bytes 1572868
  306.2 2.2 copy-start.7
Sparse Core Ops, SparseCore 0:
  10.8 73.8 all-gather.10
  86.9 71.7 all-gather.8
  160.7 71.7 all-gather.6
  234.5 71.6 all-gather.4

commit v2 on v1

v2 whole, which is shorter than its diff:
```python
import functools

import jax
import jax.numpy as jnp
from jax import lax
from jax.experimental import pallas as pl
from jax.experimental.pallas import tpu as pltpu
from jax.sharding import PartitionSpec as P

HEADS = 16
SPAN = 8
SUB = 8
GROUP = 4
STEP = 4
VMEM_BYTES = 48 * 1024 * 1024

NT = (((1,), (1,)), ((), ()))


def kernel_params():
    return pltpu.CompilerParams(vmem_limit_bytes=VMEM_BYTES)


def layer_norm(rows):
    mean = jnp.mean(rows, axis=-1, keepdims=True)
    centred = rows - mean
    variance = jnp.mean(centred * centred, axis=-1, keepdims=True)
    return centred * lax.rsqrt(variance + 1e-05)


def head_mask(shape, head_width, cluster):
    row_head = lax.broadcasted_iota(jnp.int32, shape, 0) // head_width % GROUP
    lane_head = lax.broadcasted_iota(jnp.int32, shape, 1) // cluster
    return row_head == lane_head


def place_kernel(features_ref, assignment_ref, placed_ref, normed_ref):
    rows = features_ref.shape[0]
    lane = 128
    features = features_ref[...]
    columns = lax.broadcasted_iota(jnp.int32, (lane, rows), 1)
    for part in range(rows // lane):
        chosen = assignment_ref[0, :, part * lane : (part + 1) * lane] & (rows - 1)
        chosen = jnp.broadcast_to(chosen, (lane, lane)).T
        chosen = jnp.concatenate([chosen] * (rows // lane), axis=1)
        one_hot = jnp.where(chosen == columns, 1.0, 0.0).astype(jnp.bfloat16)
        placed = jnp.dot(one_hot, features, preferred_element_type=jnp.float32)
        placed_ref[pl.ds(part * lane, lane), :] = placed.astype(jnp.bfloat16)
        normed_ref[pl.ds(part * lane, lane), :] = layer_norm(placed).astype(jnp.bfloat16)


def place(features, assignment):
    width = features.shape[1]
    walkers, _, rows = assignment.shape
    local = pl.BlockSpec((rows, width), lambda i: (i, 0))
    out = jax.ShapeDtypeStruct(features.shape, jnp.bfloat16)
    return pl.pallas_call(
        place_kernel,
        grid=(walkers,),
        in_specs=[local, pl.BlockSpec((1, 1, rows), lambda i: (i, 0, 0))],
        out_specs=[local] * 2,
        out_shape=[out, out],
        cost_estimate=pl.CostEstimate(
            flops=2 * walkers * rows * rows * width,
            bytes_accessed=6 * walkers * rows * width,
            transcendentals=0,
        ),
        compiler_params=kernel_params(),
        name="place_rows",
    )(features, assignment)


def pick_kernel(position_ref, demanded_ref, blocks_ref, *out_refs):
    for step, out_ref in enumerate(out_refs):
        reader = (position_ref[0] + step + 1) % SPAN

        def one_slot(slot, carry, reader=reader, out_ref=out_ref):
            out_ref[slot] = blocks_ref[demanded_ref[reader, slot]]
            return carry

        lax.fori_loop(0, out_ref.shape[0], one_slot, 0)


def pick(position, demanded, blocks):
    capacity = demanded.shape[1]
    piece = jax.ShapeDtypeStruct((capacity,) + blocks.shape[1:], blocks.dtype)
    smem = pl.BlockSpec(memory_space=pltpu.SMEM)
    vmem = pl.BlockSpec(memory_space=pltpu.VMEM)
    return pl.pallas_call(
        pick_kernel,
        in_specs=[smem, smem, vmem],
        out_specs=[vmem] * (SPAN - 1),
        out_shape=[piece] * (SPAN - 1),
        cost_estimate=pl.CostEstimate(
            flops=0, bytes_accessed=4 * (SPAN - 1) * piece.size, transcendentals=0
        ),
        compiler_params=kernel_params(),
        name="pick_blocks",
    )(position, demanded, blocks)


def query_kernel(normed_ref, query_w_ref, query_ref, *, cluster, head_width):
    width = normed_ref.shape[1]
    mask = head_mask((width, GROUP * cluster), head_width, cluster)
    for block in range(query_ref.shape[0]):
        own = normed_ref[pl.ds(block * cluster, cluster), :]
        own = jnp.concatenate([own] * GROUP, axis=0)
        query = lax.dot_general(query_w_ref[...], own, NT, preferred_element_type=jnp.float32)
        query = query.astype(jnp.bfloat16) * jnp.bfloat16(1.0 / head_width**0.5)
        query_ref[block] = jnp.where(mask, query, jnp.bfloat16(0.0))


def project_queries(normed, w_query, cluster):
    rows, width = normed.shape
    blocks = rows // cluster
    return pl.pallas_call(
        functools.partial(query_kernel, cluster=cluster, head_width=width // HEADS),
        grid=(blocks // SUB,),
        in_specs=[
            pl.BlockSpec((SUB * cluster, width), lambda i: (i, 0)),
            pl.BlockSpec((width, width), lambda i: (0, 0)),
        ],
        out_specs=pl.BlockSpec((SUB, width, GROUP * cluster), lambda i: (i, 0, 0)),
        out_shape=jax.ShapeDtypeStruct((blocks, width, GROUP * cluster), jnp.bfloat16),
        cost_estimate=pl.CostEstimate(
            flops=2 * rows * GROUP * width * width,
            bytes_accessed=2 * rows * width * (GROUP + 1),
            transcendentals=0,
        ),
        compiler_params=kernel_params(),
        name="queries",
    )(normed, w_query.T)


def key_value_kernel(rows_ref, w_ref, *rest):
    out_ref = rest[-1]
    blocks, cluster, width = rows_ref.shape
    rows = rows_ref[...].reshape(blocks * cluster, width)
    both = jnp.dot(rows, w_ref[...], preferred_element_type=jnp.float32)
    out_ref[...] = both.astype(jnp.bfloat16).reshape(out_ref.shape)


def project_pairs(piece, w_both, so_far, at, total):
    blocks, cluster, width = piece.shape
    per = 5 if blocks % 5 == 0 else 8
    in_specs = [
        pl.BlockSpec((per, cluster, width), lambda i: (i, 0, 0)),
        pl.BlockSpec((width, 2 * width), lambda i: (0, 0)),
    ]
    operands = [piece, w_both]
    aliases = {}
    if so_far is not None:
        in_specs.append(pl.BlockSpec(memory_space=pl.ANY))
        operands.append(so_far)
        aliases = {2: 0}
    return pl.pallas_call(
        key_value_kernel,
        grid=(blocks // per,),
        in_specs=in_specs,
        out_specs=pl.BlockSpec((per, cluster, 2 * width), lambda i: (at // per + i, 0, 0)),
        out_shape=jax.ShapeDtypeStruct((total, cluster, 2 * width), jnp.bfloat16),
        input_output_aliases=aliases,
        cost_estimate=pl.CostEstimate(
            flops=4 * piece.size * width, bytes_accessed=6 * piece.size, transcendentals=0
        ),
        compiler_params=kernel_params(),
        name="keys_values",
    )(*operands)


def attend_kernel(table_ref, query_ref, own_ref, *rest, pair_count, head_width):
    listed_refs = rest[: STEP * pair_count]
    placed_ref, out_w_ref, mix_ref, mixed_ref = rest[STEP * pair_count :]
    cluster = own_ref.shape[1]
    width = placed_ref.shape[1]
    span = GROUP * head_width
    tile = GROUP * cluster
    diagonal = head_mask((span, tile), head_width, cluster)
    fold_row = lax.broadcasted_iota(jnp.int32, (cluster, tile), 0)
    fold_lane = lax.broadcasted_iota(jnp.int32, (cluster, tile), 1) % cluster
    fold = jnp.where(fold_row == fold_lane, 1.0, 0.0).astype(jnp.bfloat16)
    zeros = jnp.zeros((span, tile), jnp.bfloat16)
    attended = []
    for block in range(STEP):
        members = [own_ref[block]]
        members += [listed_refs[block * pair_count + j][0] for j in range(pair_count)]
        keys = jnp.concatenate([m[:, :width] for m in members], axis=0)
        values = jnp.concatenate([m[:, width:] for m in members], axis=0).T
        pieces = []
        for t in range(HEADS // GROUP):
            lo = t * span // 128 * 128
            picked = query_ref[block, t * span : (t + 1) * span, :]
            ahead, behind = t * span - lo, lo + 128 - (t + 1) * span
            stack = [zeros] * (ahead // span) + [picked] + [zeros] * (behind // span)
            scores = jnp.dot(
                keys[:, lo : lo + 128],
                jnp.concatenate(stack, axis=0),
                preferred_element_type=jnp.float32,
            )
            top = jnp.max(scores, axis=0, keepdims=True)
            weights = jnp.exp(scores - top)
            total = jnp.sum(weights, axis=0, keepdims=True)
            result = jnp.dot(
                values[t * span : (t + 1) * span],
                weights.astype(jnp.bfloat16),
                preferred_element_type=jnp.float32,
            )
            result = result * (1.0 / total)
            pieces.append(jnp.where(diagonal, result, 0.0).astype(jnp.bfloat16))
        stacked = jnp.concatenate(pieces, axis=0)
        folded = lax.dot_general(fold, stacked, NT, preferred_element_type=jnp.float32)
        attended.append(folded.astype(jnp.bfloat16))
    middle = placed_ref[...].astype(jnp.float32) + jnp.dot(
        jnp.concatenate(attended, axis=0), out_w_ref[...], preferred_element_type=jnp.float32
    )
    middle = middle.astype(jnp.bfloat16).astype(jnp.float32)
    second = layer_norm(middle).astype(jnp.bfloat16)
    mixed = middle + jnp.tanh(jnp.dot(second, mix_ref[...], preferred_element_type=jnp.float32))
    mixed_ref[...] = mixed.astype(jnp.bfloat16)


def attend(table, queries, pairs_buffer, own_at, placed, w_out, w_mix, pair_count):
    rows, width = placed.shape
    blocks, _, tile = queries.shape
    cluster = rows // blocks
    whole = pl.BlockSpec((width, width), lambda i, t: (0, 0))
    local = pl.BlockSpec((STEP * cluster, width), lambda i, t: (i, 0))

    def listed(j):
        return pl.BlockSpec(
            (1, cluster, 2 * width), lambda i, t: (t[i * STEP * pair_count + j], 0, 0)
        )

    return pl.pallas_call(
        functools.partial(attend_kernel, pair_count=pair_count, head_width=width // HEADS),
        grid_spec=pltpu.PrefetchScalarGridSpec(
            num_scalar_prefetch=1,
            grid=(blocks // STEP,),
            in_specs=[
                pl.BlockSpec((STEP, width, tile), lambda i, t: (i, 0, 0)),
                pl.BlockSpec((STEP, cluster, 2 * width), lambda i, t: (own_at // STEP + i, 0, 0)),
            ]
            + [listed(j) for j in range(STEP * pair_count)]
            + [local, whole, whole],
            out_specs=local,
        ),
        out_shape=jax.ShapeDtypeStruct((rows, width), jnp.bfloat16),
        cost_estimate=pl.CostEstimate(
            flops=4 * rows * HEADS * width * (pair_count + 1) * cluster,
            bytes_accessed=24 * rows * width,
            transcendentals=rows * HEADS * (pair_count + 1) * cluster,
        ),
        compiler_params=kernel_params(),
        name="attend_blocks",
    )(
        table,
        queries,
        pairs_buffer,
        *[pairs_buffer] * (STEP * pair_count),
        placed,
        w_out,
        w_mix,
    )


def slot_table(owner, within, capacity):
    entries = owner.shape[0]
    alike = owner[:, None] == owner[None, :]
    earlier = jnp.arange(entries)[None, :] < jnp.arange(entries)[:, None]
    ranking = jnp.sum(jnp.where(alike & earlier, 1, 0), axis=1).astype(jnp.int32)
    slots = owner * capacity + ranking
    matches = slots[None, :] == jnp.arange(SPAN * capacity, dtype=jnp.int32)[:, None]
    tables = jnp.sum(jnp.where(matches, within[None, :], 0), axis=1)
    return ranking, tables.reshape(SPAN, capacity)


def body(features, assignment, pairs, w_query, w_key, w_value, w_out, w_mix):
    rows_dev, width = features.shape
    block_count, pair_count = pairs.shape
    cluster = rows_dev // block_count
    peers = lax.axis_size("elec")
    stride = peers // SPAN
    groups = [[rest + place_ * stride for place_ in range(SPAN)] for rest in range(stride)]
    position = lax.axis_index("elec") // stride
    capacity = (block_count * pair_count + SPAN - 1) // SPAN + 1

    listed = pairs.reshape(-1)
    owner = listed // block_count // stride
    within = listed % block_count
    ranking, tables = slot_table(owner, within, capacity)
    demanded = lax.all_to_all(
        tables, "elec", split_axis=0, concat_axis=0, axis_index_groups=groups, tiled=True
    )

    placed, normed = place(
        features, assignment.reshape(block_count // SUB, 1, SUB * cluster)
    )
    blocks = normed.reshape(block_count, cluster, width)
    outgoing = pick(position.reshape(1), demanded, blocks)
    arrived = [
        lax.ppermute(piece, "elec", [(i, (i + (o + 1) * stride) % peers) for i in range(peers)])
        for o, piece in enumerate(outgoing)
    ]

    w_both = jnp.concatenate([w_key, w_value], axis=1)
    own_at = -((1 - SPAN) * capacity // block_count) * block_count
    total = own_at + block_count
    buffer = project_pairs(blocks, w_both, None, own_at, total)
    queries = project_queries(normed, w_query, cluster)
    for o, piece in enumerate(arrived):
        buffer = project_pairs(piece, w_both, buffer, o * capacity, total)
    offset = (position - owner) % SPAN
    table = jnp.where(offset == 0, own_at + within, (offset - 1) * capacity + ranking)
    return attend(table, queries, buffer, own_at, placed, w_out, w_mix, pair_count)


def solution(mesh):
    placed = (
        P(("groups", "elec"), None),
        P(("groups", "elec")),
        P(("groups", "elec"), None),
        P(),
        P(),
        P(),
        P(),
        P(),
    )
    return jax.shard_map(
        body, mesh=mesh, in_specs=placed, out_specs=P(("groups", "elec"), None), check_vma=False
    )
```

time: 346 us -> 258 us (0.75)
  waiting for transfers between devices: 192 us -> 83.5 us
  starting transfers between devices: 0.13 us -> 33.1 us
  between operations: 13.2 us -> 0.08 us
  local copies, waits for them, and re-layouts: 15.5 us -> 9.86 us
  Pallas kernels: 122 us -> 126 us
    all_gather x4 -> x0, waiting for transfers between devices: 192 us -> none  [body(): lax.all_gather(normed, 'elec', axis_index_groups=groups, axis=0, tiled=True)]
    ppermute x0 -> x7, waiting for transfers between devices: none -> 83.5 us  [body(): lax.ppermute(piece, 'elec', [(i, (i + (o + 1) * stride) % peers) for i in...]
    ppermute x0 -> x7, starting transfers between devices: none -> 26.8 us  [body(): lax.ppermute(piece, 'elec', [(i, (i + (o + 1) * stride) % peers) for i in...]
    unnamed x32 -> x21, local copies, waits for them, and re-layouts: 14.7 us -> 8.13 us
    all_to_all x0 -> x1, starting transfers between devices: none -> 6.28 us  [body(): lax.all_to_all(tables, 'elec', split_axis=0, concat_axis=0, axis_index_gr...]
    pallas_call x8 -> x12, Pallas kernels: 122 us -> 126 us  [the longest x1 76.7 us: attend(): pl.pallas_call(functools.partial(attend_kernel, pair_count=pair_count, he...]
  transfers between devices with their start and end apart: 4 -> 8, of which waited for: 4 -> 4; matrix products, arithmetic and copies ran while one was open for 1% -> 1% of each run, Pallas kernels for 27% -> 16%
where the time goes in v2:
time: 258 us; the launch traced here: 253 us
  Pallas kernels  126 us (49%)
  waiting for transfers between devices  83.5 us (32%)
  starting transfers between devices  33.1 us (13%)
  local copies, waits for them, and re-layouts  9.86 us (4%)
    ppermute x7, waiting for transfers between devices, body(): lax.ppermute(piece, 'elec', [(i, (i + (o + 1) * stride) % peers) for i in...  83.5 us
    pallas_call x1, Pallas kernels, attend(): pl.pallas_call(functools.partial(attend_kernel, pair_count=pair_count, he...  76.7 us
    pallas_call x8, Pallas kernels, project_pairs(): pl.pallas_call(key_value_kernel, grid=(blocks // per,), in_specs=in_specs...  31.5 us
    ppermute x7, starting transfers between devices, body(): lax.ppermute(piece, 'elec', [(i, (i + (o + 1) * stride) % peers) for i in...  26.8 us
    unnamed x21, local copies, waits for them, and re-layouts  8.13 us
    pallas_call x1, Pallas kernels, place(): pl.pallas_call(place_kernel, grid=(walkers,), in_specs=[local, pl.BlockSp...  6.6 us
    pallas_call x1, Pallas kernels, project_queries(): pl.pallas_call(functools.partial(query_kernel, cluster=cluster, head_widt...  6.42 us
    all_to_all x1, starting transfers between devices, body(): lax.all_to_all(tables, 'elec', split_axis=0, concat_axis=0, axis_index_gr...  6.28 us
  transfers between devices with their start and end apart: 8, of which 4 were waited for; matrix products, arithmetic and copies ran while one was open for 1% of the time, Pallas kernels for 16%

profile of v2, /device:TPU:8, one launch (start us, length us, event | category | flops | bytes accessed | tf_op | source)
XLA Modules:
  0.0 253.4 jit_solution(9573794315476785214)
XLA Ops:
  0.0 0.8 copy.21
  2.0 6.3 %all-to-all-start = ((s32[8,1,25]{2,1,0:T(1,128)}), s32[8,1,25]{2,1,0:T(1,128)S(1)}, u32[]{:S(2)}, u32[]{:S(2)}) async-start(s32[8,1,25]{2,1,0:T(1,128)} %all_to_all.7), calls=%async_computation | async-start | bytes 8192 | tf_op jit(solution)/shard_map/all_to_all | solution.py:291
  9.0 6.6 %place_rows.1 = (bf16[4096,256]{1,0:T(8,128)(2,1)S(1)}, bf16[4096,256]{1,0:T(8,128)(2,1)S(1)}) custom-call(bf16[4096,256]{1,0:T(8,128)(2,1)} %features_ref.1, s32[8,1,512]{2,1,0:T(1,128)S(1)} %bitcast.9), custom_call_target="tpu_custom_call" | custom-call | flops 1073741824 | bytes 6291456 | tf_op jit(solution)/shard_map/place_rows/pallas_call | solution.py:57
  15.6 1.3 copy-done
  16.9 5.2 %pick_blocks.1 = (bf16[25,64,256]{2,1,0:T(8,128)(2,1)S(1)}, bf16[25,64,256]{2,1,0:T(8,128)(2,1)S(1)}, bf16[25,64,256]{2,1,0:T(8,128)(2,1)}, bf16[25,64,256]{2,1,...) custom-call(s32[1]{0:T(128)} %bitcast.2.position_ref, ...), custom_call_target="tpu_custom_call" | custom-call | bytes 11468800 | tf_op jit(solution)/shard_map/pick_blocks/pallas_call | solution.py:89
  22.1 1.5 collective-permute-start.6
  23.5 1.5 collective-permute-start.5
  25.0 0.9 collective-permute-start.4
  25.9 2.9 %collective-permute-start.3 = (bf16[25,64,256]{2,1,0:T(8,128)(2,1)}, bf16[25,64,256]{2,1,0:T(8,128)(2,1)}, u32[]{:S(2)}, u32[]{:S(2)}) collective-permute-start(bf16[25,64,256]{2,1,0:T(8,128)(2,1)} %get-tuple-element.18), channel_id=1, source_target_pairs={{0,8},{1,9},{2,10},{3,11},{4,12},{5,13},{6,14},{7,15},{8,0},{9,1},... | collective-permute-start | bytes 2457608 | tf_op jit(solution)/shard_map/ppermute | solution.py:301
  28.8 1.5 collective-permute-start.2
  30.3 13.9 %collective-permute-done.6.rows_ref = bf16[25,64,256]{2,1,0:T(8,128)(2,1)S(1)} collective-permute-done((bf16[25,64,256]{2,1,0:T(8,128)(2,1)S(1)}, bf16[25,64,256]{2,1,0:T(8,128)(2,1)S(1)}, u32[]{:S(2)}, u32[]{:S(2)}) %collective-permute-start.6) | collective-permute-done | bytes 819232 | tf_op jit(solution)/shard_map/ppermute | solution.py:301
  44.2 0.9 copy-done.2
  45.0 2.0 collective-permute-start.1
  47.0 0.9 copy-done.4
  48.0 16.6 %collective-permute-start = (bf16[25,64,256]{2,1,0:T(8,128)(2,1)}, bf16[25,64,256]{2,1,0:T(8,128)(2,1)}, u32[]{:S(2)}, u32[]{:S(2)}) collective-permute-start(bf16[25,64,256]{2,1,0:T(8,128)(2,1)} %get-tuple-element.15), channel_id=1, source_target_pairs={{0,14},{1,15},{2,0},{3,1},{4,2},{5,3},{6,4},{7,5},{8,6},{9,7},{10,... | collective-permute-start | bytes 2457608 | tf_op jit(solution)/shard_map/ppermute | solution.py:301
  64.6 1.0 copy.22
  65.6 0.9 constant_dynamic-update-slice_fusion.1
  66.5 0.9 constant_dynamic-update-slice_fusion.w_ref
  67.4 1.6 copy-done.1
  69.0 4.8 %keys_values.8.rest_0_ = bf16[256,64,512]{2,1,0:T(8,128)(2,1)} custom-call(bf16[64,64,256]{2,1,0:T(8,128)(2,1)S(1)} %bitcast.6, bf16[256,512]{1,0:T(8,128)(2,1)S(1)} %constant_dynamic-update-slice_fusion.w_ref), custom_call_target="tpu_custom_call" | custom-call | flops 1073741824 | bytes 6291456 | tf_op jit(solution)/shard_map/keys_values/pallas_call | solution.py:156
  73.8 6.4 %queries.1.query_ref = bf16[64,256,256]{2,1,0:T(8,128)(2,1)} custom-call(bf16[4096,256]{1,0:T(8,128)(2,1)S(1)} %copy-done.1, bf16[256,256]{1,0:T(8,128)(2,1)S(1)} %bitcast.7), custom_call_target="tpu_custom_call" | custom-call | flops 2147483648 | bytes 10485760 | tf_op jit(solution)/shard_map/queries/pallas_call | solution.py:116
  80.2 2.9 %keys_values.9.rest_0_ = bf16[256,64,512]{2,1,0:T(8,128)(2,1)} custom-call(bf16[25,64,256]{2,1,0:T(8,128)(2,1)S(1)} %copy-done.3, bf16[256,512]{1,0:T(8,128)(2,1)S(1)} %constant_dynamic-update-slice_fusion.w_ref, bf16[256,64,512]{2,1,0:T(8,128)(2,1)} %keys_values.8.rest_0_), custom_call_target="tpu_custom_call", output_to_operand_aliasing={{}: (2, {})} | custom-call | flops 419430400 | bytes 2457600 | tf_op jit(solution)/shard_map/keys_values/pallas_call | solution.py:156
  83.1 2.9 %keys_values.10.rest_0_ = bf16[256,64,512]{2,1,0:T(8,128)(2,1)} custom-call(bf16[25,64,256]{2,1,0:T(8,128)(2,1)S(1)} %copy-done.5, bf16[256,512]{1,0:T(8,128)(2,1)S(1)} %constant_dynamic-update-slice_fusion.w_ref, bf16[256,64,512]{2,1,0:T(8,128)(2,1)} %keys_values.9.rest_0_), custom_call_target="tpu_custom_call", output_to_operand_aliasing={{}: (2, {})} | custom-call | flops 419430400 | bytes 2457600 | tf_op jit(solution)/shard_map/keys_values/pallas_call | solution.py:156
  86.0 45.6 %collective-permute-done.4.rows_ref = bf16[25,64,256]{2,1,0:T(8,128)(2,1)} collective-permute-done((bf16[25,64,256]{2,1,0:T(8,128)(2,1)}, bf16[25,64,256]{2,1,0:T(8,128)(2,1)}, u32[]{:S(2)}, u32[]{:S(2)}) %collective-permute-start.4) | collective-permute-done | bytes 819232 | tf_op jit(solution)/shard_map/ppermute | solution.py:301
  131.6 4.5 %keys_values.11.rest_0_ = bf16[256,64,512]{2,1,0:T(8,128)(2,1)} custom-call(bf16[25,64,256]{2,1,0:T(8,128)(2,1)} %collective-permute-done.4.rows_ref, bf16[256,512]{1,0:T(8,128)(2,1)S(1)} %constant_dynamic-update-slice_fusion.w_ref, bf16[256,64,512]{2,1,0:T(8,128)(2,1)} %keys_values.10.rest_0_), custom_call_target="tpu_custom_call", output_to_operand_aliasing={{}: (2, {})} | custom-call | flops 419430400 | bytes 2457600 | tf_op jit(solution)/shard_map/keys_values/pallas_call | solution.py:156
  136.1 13.1 %collective-permute-done.3.rows_ref = bf16[25,64,256]{2,1,0:T(8,128)(2,1)} collective-permute-done((bf16[25,64,256]{2,1,0:T(8,128)(2,1)}, bf16[25,64,256]{2,1,0:T(8,128)(2,1)}, u32[]{:S(2)}, u32[]{:S(2)}) %collective-permute-start.3) | collective-permute-done | bytes 819232 | tf_op jit(solution)/shard_map/ppermute | solution.py:301
  149.1 4.5 %keys_values.12.rest_0_ = bf16[256,64,512]{2,1,0:T(8,128)(2,1)} custom-call(bf16[25,64,256]{2,1,0:T(8,128)(2,1)} %collective-permute-done.3.rows_ref, bf16[256,512]{1,0:T(8,128)(2,1)S(1)} %constant_dynamic-update-slice_fusion.w_ref, bf16[256,64,512]{2,1,0:T(8,128)(2,1)} %keys_values.11.rest_0_), custom_call_target="tpu_custom_call", output_to_operand_aliasing={{}: (2, {})} | custom-call | flops 419430400 | bytes 2457600 | tf_op jit(solution)/shard_map/keys_values/pallas_call | solution.py:156
  153.6 11.0 %collective-permute-done.2.rows_ref = bf16[25,64,256]{2,1,0:T(8,128)(2,1)S(1)} collective-permute-done((bf16[25,64,256]{2,1,0:T(8,128)(2,1)}, bf16[25,64,256]{2,1,0:T(8,128)(2,1)S(1)}, u32[]{:S(2)}, u32[]{:S(2)}) %collective-permute-start.2) | collective-permute-done | bytes 819232 | tf_op jit(solution)/shard_map/ppermute | solution.py:301
  164.7 2.9 %keys_values.13.rest_0_ = bf16[256,64,512]{2,1,0:T(8,128)(2,1)} custom-call(bf16[25,64,256]{2,1,0:T(8,128)(2,1)S(1)} %collective-permute-done.2.rows_ref, bf16[256,512]{1,0:T(8,128)(2,1)S(1)} %constant_dynamic-update-slice_fusion.w_ref, bf16[256,64,512]{2,1,0:T(8,128)(2,1)} %keys_values.12.rest_0_), custom_call_target="tpu_custom_call", output_to_operand_aliasing={{}: (2, {})} | custom-call | flops 419430400 | bytes 2457600 | tf_op jit(solution)/shard_map/keys_values/pallas_call | solution.py:156
  167.6 4.5 %keys_values.14.rest_0_ = bf16[256,64,512]{2,1,0:T(8,128)(2,1)} custom-call(bf16[25,64,256]{2,1,0:T(8,128)(2,1)} %collective-permute-done.1.rows_ref, bf16[256,512]{1,0:T(8,128)(2,1)S(1)} %constant_dynamic-update-slice_fusion.w_ref, bf16[256,64,512]{2,1,0:T(8,128)(2,1)} %keys_values.13.rest_0_), custom_call_target="tpu_custom_call", output_to_operand_aliasing={{}: (2, {})} | custom-call | flops 419430400 | bytes 2457600 | tf_op jit(solution)/shard_map/keys_values/pallas_call | solution.py:156
  172.1 4.5 %keys_values.15.own_ref.rest_0_.rest_1_.rest_2_.rest_3_.rest_4_.rest_5_.rest_6_.rest_7_.rest_8_.rest_9_.rest_10_.rest_11_ = bf16[256,64,512]{2,1,0:T(8,128)(2,1)} custom-call(bf16[25,64,256]{2,1,0:T(8,128)(2,1)} %collective-permute-done.rows_ref, bf16[256,512]{1,0:T(8,128)(2,1)S(1)} %constant_dynamic-update-slice_fusion.w_ref, ...), custom_call_target="tpu_custom_call", output_to_operand_aliasing={{}: (2, {})} | custom-call | flops 419430400 | bytes 2457600 | tf_op jit(solution)/shard_map/keys_values/pallas_call | solution.py:156
  176.6 76.7 %attend_blocks.1 = bf16[4096,256]{1,0:T(8,128)(2,1)} custom-call(s32[192]{0:T(256)S(1)} %get-tuple-element.23.table_ref, bf16[64,256,256]{2,1,0:T(8,128)(2,1)} %queries.1.query_ref, bf16[256,64,512]{2,1,0:T(8,128)(2,1)} %keys_values.15.own_ref.rest_0_.rest_1_.rest_2_.rest_3_.rest_4_.rest_5_.rest_6_.rest_7_.rest_8_.rest_9_.rest_10_.rest_11_, ...), custom_call_target="tpu_custom_call" | custom-call | flops 17179869184 | bytes 25165824 | tf_op jit(solution)/shard_map/attend_blocks/pallas_call | solution.py:234
  (24 shorter events, 1.9 us)
Async XLA Ops:
  2.0 14.9 %all-to-all-start = ((s32[8,1,25]{2,1,0:T(1,128)}), s32[8,1,25]{2,1,0:T(1,128)S(1)}, u32[]{:S(2)}, u32[]{:S(2)}) async-start(s32[8,1,25]{2,1,0:T(1,128)} %all_to_all.7), calls=%async_computation | async-start | bytes 8192 | tf_op jit(solution)/shard_map/all_to_all | solution.py:291
  8.3 0.7 copy-start.8
  15.6 1.3 copy-start
  22.1 22.1 %collective-permute-start.6 = (bf16[25,64,256]{2,1,0:T(8,128)(2,1)S(1)}, bf16[25,64,256]{2,1,0:T(8,128)(2,1)S(1)}, u32[]{:S(2)}, u32[]{:S(2)}) collective-permute-start(bf16[25,64,256]{2,1,0:T(8,128)(2,1)S(1)} %get-tuple-element.21), channel_id=1, source_target_pairs={{0,2},{1,3},{2,4},{3,5},{4,6},{5,7},{6,8},{7,9},{8,10},{9,11},{10,... | collective-permute-start | bytes 2457608 | tf_op jit(solution)/shard_map/ppermute | solution.py:301
  23.5 23.5 %collective-permute-start.5 = (bf16[25,64,256]{2,1,0:T(8,128)(2,1)S(1)}, bf16[25,64,256]{2,1,0:T(8,128)(2,1)S(1)}, u32[]{:S(2)}, u32[]{:S(2)}) collective-permute-start(bf16[25,64,256]{2,1,0:T(8,128)(2,1)S(1)} %get-tuple-element.20), channel_id=1, source_target_pairs={{0,4},{1,5},{2,6},{3,7},{4,8},{5,9},{6,10},{7,11},{8,12},{9,13},{1... | collective-permute-start | bytes 2457608 | tf_op jit(solution)/shard_map/ppermute | solution.py:301
  25.0 106.6 %collective-permute-start.4 = (bf16[25,64,256]{2,1,0:T(8,128)(2,1)}, bf16[25,64,256]{2,1,0:T(8,128)(2,1)}, u32[]{:S(2)}, u32[]{:S(2)}) collective-permute-start(bf16[25,64,256]{2,1,0:T(8,128)(2,1)} %get-tuple-element.19), channel_id=1, source_target_pairs={{0,6},{1,7},{2,8},{3,9},{4,10},{5,11},{6,12},{7,13},{8,14},{9,15},... | collective-permute-start | bytes 2457608 | tf_op jit(solution)/shard_map/ppermute | solution.py:301
  25.9 123.2 %collective-permute-start.3 = (bf16[25,64,256]{2,1,0:T(8,128)(2,1)}, bf16[25,64,256]{2,1,0:T(8,128)(2,1)}, u32[]{:S(2)}, u32[]{:S(2)}) collective-permute-start(bf16[25,64,256]{2,1,0:T(8,128)(2,1)} %get-tuple-element.18), channel_id=1, source_target_pairs={{0,8},{1,9},{2,10},{3,11},{4,12},{5,13},{6,14},{7,15},{8,0},{9,1},... | collective-permute-start | bytes 2457608 | tf_op jit(solution)/shard_map/ppermute | solution.py:301
  28.8 135.8 %collective-permute-start.2 = (bf16[25,64,256]{2,1,0:T(8,128)(2,1)}, bf16[25,64,256]{2,1,0:T(8,128)(2,1)S(1)}, u32[]{:S(2)}, u32[]{:S(2)}) collective-permute-start(bf16[25,64,256]{2,1,0:T(8,128)(2,1)} %get-tuple-element.17), channel_id=1, source_target_pairs={{0,10},{1,11},{2,12},{3,13},{4,14},{5,15},{6,0},{7,1},{8,2},{9,3},... | collective-permute-start | bytes 2457608 | tf_op jit(solution)/shard_map/ppermute | solution.py:301
  44.2 0.9 copy-start.2
  45.0 122.6 %collective-permute-start.1 = (bf16[25,64,256]{2,1,0:T(8,128)(2,1)}, bf16[25,64,256]{2,1,0:T(8,128)(2,1)}, u32[]{:S(2)}, u32[]{:S(2)}) collective-permute-start(bf16[25,64,256]{2,1,0:T(8,128)(2,1)} %get-tuple-element.16), channel_id=1, source_target_pairs={{0,12},{1,13},{2,14},{3,15},{4,0},{5,1},{6,2},{7,3},{8,4},{9,5},{1... | collective-permute-start | bytes 2457608 | tf_op jit(solution)/shard_map/ppermute | solution.py:301
  47.0 0.9 copy-start.4
  48.0 124.1 %collective-permute-start = (bf16[25,64,256]{2,1,0:T(8,128)(2,1)}, bf16[25,64,256]{2,1,0:T(8,128)(2,1)}, u32[]{:S(2)}, u32[]{:S(2)}) collective-permute-start(bf16[25,64,256]{2,1,0:T(8,128)(2,1)} %get-tuple-element.15), channel_id=1, source_target_pairs={{0,14},{1,15},{2,0},{3,1},{4,2},{5,3},{6,4},{7,5},{8,6},{9,7},{10,... | collective-permute-start | bytes 2457608 | tf_op jit(solution)/shard_map/ppermute | solution.py:301
  67.4 1.6 copy-start.1
  69.0 11.2 %copy-start.3 = (bf16[25,64,256]{2,1,0:T(8,128)(2,1)S(1)}, bf16[25,64,256]{2,1,0:T(8,128)(2,1)}, u32[]{:S(2)}) copy-start(bf16[25,64,256]{2,1,0:T(8,128)(2,1)} %copy-done.2) | copy-start | bytes 2457604
  80.2 2.9 %copy-start.5 = (bf16[25,64,256]{2,1,0:T(8,128)(2,1)S(1)}, bf16[25,64,256]{2,1,0:T(8,128)(2,1)}, u32[]{:S(2)}) copy-start(bf16[25,64,256]{2,1,0:T(8,128)(2,1)} %copy-done.4) | copy-start | bytes 2457604
  172.1 4.5 %copy-start.6 = (bf16[256,256]{1,0:T(8,128)(2,1)S(1)}, bf16[256,256]{1,0:T(8,128)(2,1)}, u32[]{:S(2)}) copy-start(bf16[256,256]{1,0:T(8,128)(2,1)} %rest_13_.1) | copy-start | bytes 393220
  172.1 4.5 %copy-start.7 = (bf16[256,256]{1,0:T(8,128)(2,1)S(1)}, bf16[256,256]{1,0:T(8,128)(2,1)}, u32[]{:S(2)}) copy-start(bf16[256,256]{1,0:T(8,128)(2,1)} %rest_14_.1) | copy-start | bytes 393220

commit v3 on v2

--- a/solution.py
+++ b/solution.py
@@ -180,36 +180,48 @@
     fold_lane = lax.broadcasted_iota(jnp.int32, (cluster, tile), 1) % cluster
     fold = jnp.where(fold_row == fold_lane, 1.0, 0.0).astype(jnp.bfloat16)
     zeros = jnp.zeros((span, tile), jnp.bfloat16)
-    attended = []
-    for block in range(STEP):
+    ones = jnp.ones((16, tile), jnp.bfloat16)
+    tiles = HEADS // GROUP
+    units = [(block, t) for block in range(STEP) for t in range(tiles)]
+    keys, values = {}, {}
+
+    def gather(block):
         members = [own_ref[block]]
         members += [listed_refs[block * pair_count + j][0] for j in range(pair_count)]
-        keys = jnp.concatenate([m[:, :width] for m in members], axis=0)
-        values = jnp.concatenate([m[:, width:] for m in members], axis=0).T
-        pieces = []
-        for t in range(HEADS // GROUP):
-            lo = t * span // 128 * 128
-            picked = query_ref[block, t * span : (t + 1) * span, :]
-            ahead, behind = t * span - lo, lo + 128 - (t + 1) * span
-            stack = [zeros] * (ahead // span) + [picked] + [zeros] * (behind // span)
-            scores = jnp.dot(
-                keys[:, lo : lo + 128],
-                jnp.concatenate(stack, axis=0),
-                preferred_element_type=jnp.float32,
-            )
-            top = jnp.max(scores, axis=0, keepdims=True)
-            weights = jnp.exp(scores - top)
-            total = jnp.sum(weights, axis=0, keepdims=True)
-            result = jnp.dot(
-                values[t * span : (t + 1) * span],
-                weights.astype(jnp.bfloat16),
-                preferred_element_type=jnp.float32,
-            )
-            result = result * (1.0 / total)
-            pieces.append(jnp.where(diagonal, result, 0.0).astype(jnp.bfloat16))
-        stacked = jnp.concatenate(pieces, axis=0)
-        folded = lax.dot_general(fold, stacked, NT, preferred_element_type=jnp.float32)
-        attended.append(folded.astype(jnp.bfloat16))
+        keys[block] = jnp.concatenate([m[:, :width] for m in members], axis=0)
+        values[block] = jnp.concatenate([m[:, width:] for m in members], axis=0).T
+
+    def scores_of(block, t):
+        if t == 0:
+            gather(block)
+        lo = t * span // 128 * 128
+        picked = query_ref[block, t * span : (t + 1) * span, :]
+        ahead, behind = t * span - lo, lo + 128 - (t + 1) * span
+        stack = [zeros] * (ahead // span) + [picked] + [zeros] * (behind // span)
+        return jnp.dot(
+            keys[block][:, lo : lo + 128],
+            jnp.concatenate(stack, axis=0),
+            preferred_element_type=jnp.float32,
+        )
+
+    lead = 2
+    scores = [scores_of(*unit) for unit in units[:lead]]
+    attended, pieces = [], []
+    for at, (block, t) in enumerate(units):
+        if at + lead < len(units):
+            scores.append(scores_of(*units[at + lead]))
+        current = scores[at]
+        top = jnp.max(current, axis=0, keepdims=True)
+        weights = jnp.exp(current - top).astype(jnp.bfloat16)
+        lifted = jnp.concatenate([values[block][t * span : (t + 1) * span], ones], axis=0)
+        result = jnp.dot(lifted, weights, preferred_element_type=jnp.float32)
+        result = result[:span] * (1.0 / result[span : span + 1])
+        pieces.append(jnp.where(diagonal, result, 0.0).astype(jnp.bfloat16))
+        if t == tiles - 1:
+            stacked = jnp.concatenate(pieces, axis=0)
+            folded = lax.dot_general(fold, stacked, NT, preferred_element_type=jnp.float32)
+            attended.append(folded.astype(jnp.bfloat16))
+            pieces = []
     middle = placed_ref[...].astype(jnp.float32) + jnp.dot(
         jnp.concatenate(attended, axis=0), out_w_ref[...], preferred_element_type=jnp.float32
     )

time: 258 us -> 231 us (0.90)
  the two profiles are of different devices: /device:TPU:8 before, /device:TPU:28 now
where the time goes in v3:
time: 231 us; the launch traced here: 230 us
  waiting for transfers between devices  108 us (47%)
  Pallas kernels  98.9 us (43%)
  starting transfers between devices  13 us (6%)
  local copies, waits for them, and re-layouts  9.86 us (4%)
    ppermute x7, waiting for transfers between devices, body(): lax.ppermute(piece, 'elec', [(i, (i + (o + 1) * stride) % peers) for i in...  108 us
    pallas_call x1, Pallas kernels, attend(): pl.pallas_call(functools.partial(attend_kernel, pair_count=pair_count, he...  49.2 us
    pallas_call x8, Pallas kernels, project_pairs(): pl.pallas_call(key_value_kernel, grid=(blocks // per,), in_specs=in_specs...  31.5 us
    unnamed x21, local copies, waits for them, and re-layouts  8.13 us
    ppermute x7, starting transfers between devices, body(): lax.ppermute(piece, 'elec', [(i, (i + (o + 1) * stride) % peers) for i in...  6.99 us
    pallas_call x1, Pallas kernels, place(): pl.pallas_call(place_kernel, grid=(walkers,), in_specs=[local, pl.BlockSp...  6.59 us
    pallas_call x1, Pallas kernels, project_queries(): pl.pallas_call(functools.partial(query_kernel, cluster=cluster, head_widt...  6.42 us
    all_to_all x1, starting transfers between devices, body(): lax.all_to_all(tables, 'elec', split_axis=0, concat_axis=0, axis_index_gr...  6 us
  transfers between devices with their start and end apart: 8, of which 3 were waited for; matrix products, arithmetic and copies ran while one was open for 1% of the time, Pallas kernels for 17%

profile of v3, /device:TPU:28, one launch (start us, length us, event | category | flops | bytes accessed | tf_op | source)
XLA Modules:
  0.0 229.9 jit_solution(6914719566595969730)
XLA Ops:
  0.0 0.8 copy.21
  0.9 0.2 select_reduce_fusion.1
  1.3 0.7 all_to_all.7
  2.0 6.0 %all-to-all-start = ((s32[8,1,25]{2,1,0:T(1,128)}), s32[8,1,25]{2,1,0:T(1,128)S(1)}, u32[]{:S(2)}, u32[]{:S(2)}) async-start(s32[8,1,25]{2,1,0:T(1,128)} %all_to_all.7), calls=%async_computation | async-start | bytes 8192 | tf_op jit(solution)/shard_map/all_to_all | solution.py:303
  8.0 0.7 copy-done.8
  8.7 6.6 %place_rows.1 = (bf16[4096,256]{1,0:T(8,128)(2,1)S(1)}, bf16[4096,256]{1,0:T(8,128)(2,1)S(1)}) custom-call(bf16[4096,256]{1,0:T(8,128)(2,1)} %features_ref.1, s32[8,1,512]{2,1,0:T(1,128)S(1)} %bitcast.9), custom_call_target="tpu_custom_call" | custom-call | flops 1073741824 | bytes 6291456 | tf_op jit(solution)/shard_map/place_rows/pallas_call | solution.py:57
  15.3 1.3 copy-done
  16.6 5.2 %pick_blocks.1 = (bf16[25,64,256]{2,1,0:T(8,128)(2,1)S(1)}, bf16[25,64,256]{2,1,0:T(8,128)(2,1)S(1)}, bf16[25,64,256]{2,1,0:T(8,128)(2,1)}, bf16[25,64,256]{2,1,...) custom-call(s32[1]{0:T(128)} %bitcast.2.position_ref, ...), custom_call_target="tpu_custom_call" | custom-call | bytes 11468800 | tf_op jit(solution)/shard_map/pick_blocks/pallas_call | solution.py:89
  21.8 2.0 collective-permute-start.5
  23.8 1.5 collective-permute-start.4
  25.3 1.5 collective-permute-start.3
  26.7 1.5 collective-permute-start.2
  28.2 13.9 %collective-permute-done.6.rows_ref = bf16[25,64,256]{2,1,0:T(8,128)(2,1)S(1)} collective-permute-done((bf16[25,64,256]{2,1,0:T(8,128)(2,1)S(1)}, bf16[25,64,256]{2,1,0:T(8,128)(2,1)S(1)}, u32[]{:S(2)}, u32[]{:S(2)}) %collective-permute-start.6) | collective-permute-done | bytes 819232 | tf_op jit(solution)/shard_map/ppermute | solution.py:313
  42.1 0.9 copy-done.2
  43.0 0.6 collective-permute-start.1
  43.5 15.8 %collective-permute-done.5.rows_ref = bf16[25,64,256]{2,1,0:T(8,128)(2,1)S(1)} collective-permute-done((bf16[25,64,256]{2,1,0:T(8,128)(2,1)S(1)}, bf16[25,64,256]{2,1,0:T(8,128)(2,1)S(1)}, u32[]{:S(2)}, u32[]{:S(2)}) %collective-permute-start.5) | collective-permute-done | bytes 819232 | tf_op jit(solution)/shard_map/ppermute | solution.py:313
  59.4 0.9 copy-done.4
  60.3 1.0 copy.22
  61.3 0.9 constant_dynamic-update-slice_fusion.1
  62.2 0.9 constant_dynamic-update-slice_fusion.w_ref
  63.1 1.6 copy-done.1
  64.7 4.7 %keys_values.8.rest_0_ = bf16[256,64,512]{2,1,0:T(8,128)(2,1)} custom-call(bf16[64,64,256]{2,1,0:T(8,128)(2,1)S(1)} %bitcast.6, bf16[256,512]{1,0:T(8,128)(2,1)S(1)} %constant_dynamic-update-slice_fusion.w_ref), custom_call_target="tpu_custom_call" | custom-call | flops 1073741824 | bytes 6291456 | tf_op jit(solution)/shard_map/keys_values/pallas_call | solution.py:156
  69.5 6.4 %queries.1.query_ref = bf16[64,256,256]{2,1,0:T(8,128)(2,1)} custom-call(bf16[4096,256]{1,0:T(8,128)(2,1)S(1)} %copy-done.1, bf16[256,256]{1,0:T(8,128)(2,1)S(1)} %bitcast.7), custom_call_target="tpu_custom_call" | custom-call | flops 2147483648 | bytes 10485760 | tf_op jit(solution)/shard_map/queries/pallas_call | solution.py:116
  75.9 2.9 %keys_values.9.rest_0_ = bf16[256,64,512]{2,1,0:T(8,128)(2,1)} custom-call(bf16[25,64,256]{2,1,0:T(8,128)(2,1)S(1)} %copy-done.3, bf16[256,512]{1,0:T(8,128)(2,1)S(1)} %constant_dynamic-update-slice_fusion.w_ref, bf16[256,64,512]{2,1,0:T(8,128)(2,1)} %keys_values.8.rest_0_), custom_call_target="tpu_custom_call", output_to_operand_aliasing={{}: (2, {})} | custom-call | flops 419430400 | bytes 2457600 | tf_op jit(solution)/shard_map/keys_values/pallas_call | solution.py:156
  78.8 2.9 %keys_values.10.rest_0_ = bf16[256,64,512]{2,1,0:T(8,128)(2,1)} custom-call(bf16[25,64,256]{2,1,0:T(8,128)(2,1)S(1)} %copy-done.5, bf16[256,512]{1,0:T(8,128)(2,1)S(1)} %constant_dynamic-update-slice_fusion.w_ref, bf16[256,64,512]{2,1,0:T(8,128)(2,1)} %keys_values.9.rest_0_), custom_call_target="tpu_custom_call", output_to_operand_aliasing={{}: (2, {})} | custom-call | flops 419430400 | bytes 2457600 | tf_op jit(solution)/shard_map/keys_values/pallas_call | solution.py:156
  81.7 4.5 %keys_values.11.rest_0_ = bf16[256,64,512]{2,1,0:T(8,128)(2,1)} custom-call(bf16[25,64,256]{2,1,0:T(8,128)(2,1)} %collective-permute-done.4.rows_ref, bf16[256,512]{1,0:T(8,128)(2,1)S(1)} %constant_dynamic-update-slice_fusion.w_ref, bf16[256,64,512]{2,1,0:T(8,128)(2,1)} %keys_values.10.rest_0_), custom_call_target="tpu_custom_call", output_to_operand_aliasing={{}: (2, {})} | custom-call | flops 419430400 | bytes 2457600 | tf_op jit(solution)/shard_map/keys_values/pallas_call | solution.py:156
  86.2 78.0 %collective-permute-done.3.rows_ref = bf16[25,64,256]{2,1,0:T(8,128)(2,1)} collective-permute-done((bf16[25,64,256]{2,1,0:T(8,128)(2,1)}, bf16[25,64,256]{2,1,0:T(8,128)(2,1)}, u32[]{:S(2)}, u32[]{:S(2)}) %collective-permute-start.3) | collective-permute-done | bytes 819232 | tf_op jit(solution)/shard_map/ppermute | solution.py:313
  164.2 4.5 %keys_values.12.rest_0_ = bf16[256,64,512]{2,1,0:T(8,128)(2,1)} custom-call(bf16[25,64,256]{2,1,0:T(8,128)(2,1)} %collective-permute-done.3.rows_ref, bf16[256,512]{1,0:T(8,128)(2,1)S(1)} %constant_dynamic-update-slice_fusion.w_ref, bf16[256,64,512]{2,1,0:T(8,128)(2,1)} %keys_values.11.rest_0_), custom_call_target="tpu_custom_call", output_to_operand_aliasing={{}: (2, {})} | custom-call | flops 419430400 | bytes 2457600 | tf_op jit(solution)/shard_map/keys_values/pallas_call | solution.py:156
  168.7 2.9 %keys_values.13.rest_0_ = bf16[256,64,512]{2,1,0:T(8,128)(2,1)} custom-call(bf16[25,64,256]{2,1,0:T(8,128)(2,1)S(1)} %collective-permute-done.2.rows_ref, bf16[256,512]{1,0:T(8,128)(2,1)S(1)} %constant_dynamic-update-slice_fusion.w_ref, bf16[256,64,512]{2,1,0:T(8,128)(2,1)} %keys_values.12.rest_0_), custom_call_target="tpu_custom_call", output_to_operand_aliasing={{}: (2, {})} | custom-call | flops 419430400 | bytes 2457600 | tf_op jit(solution)/shard_map/keys_values/pallas_call | solution.py:156
  171.7 4.5 %keys_values.14.rest_0_ = bf16[256,64,512]{2,1,0:T(8,128)(2,1)} custom-call(bf16[25,64,256]{2,1,0:T(8,128)(2,1)} %collective-permute-done.1.rows_ref, bf16[256,512]{1,0:T(8,128)(2,1)S(1)} %constant_dynamic-update-slice_fusion.w_ref, bf16[256,64,512]{2,1,0:T(8,128)(2,1)} %keys_values.13.rest_0_), custom_call_target="tpu_custom_call", output_to_operand_aliasing={{}: (2, {})} | custom-call | flops 419430400 | bytes 2457600 | tf_op jit(solution)/shard_map/keys_values/pallas_call | solution.py:156
  176.2 4.5 %keys_values.15.own_ref.rest_0_.rest_1_.rest_2_.rest_3_.rest_4_.rest_5_.rest_6_.rest_7_.rest_8_.rest_9_.rest_10_.rest_11_ = bf16[256,64,512]{2,1,0:T(8,128)(2,1)} custom-call(bf16[25,64,256]{2,1,0:T(8,128)(2,1)} %collective-permute-done.rows_ref, bf16[256,512]{1,0:T(8,128)(2,1)S(1)} %constant_dynamic-update-slice_fusion.w_ref, ...), custom_call_target="tpu_custom_call", output_to_operand_aliasing={{}: (2, {})} | custom-call | flops 419430400 | bytes 2457600 | tf_op jit(solution)/shard_map/keys_values/pallas_call | solution.py:156
  180.7 49.2 %attend_blocks.1 = bf16[4096,256]{1,0:T(8,128)(2,1)} custom-call(s32[192]{0:T(256)S(1)} %get-tuple-element.23.table_ref, bf16[64,256,256]{2,1,0:T(8,128)(2,1)} %queries.1.query_ref, bf16[256,64,512]{2,1,0:T(8,128)(2,1)} %keys_values.15.own_ref.rest_0_.rest_1_.rest_2_.rest_3_.rest_4_.rest_5_.rest_6_.rest_7_.rest_8_.rest_9_.rest_10_.rest_11_, ...), custom_call_target="tpu_custom_call" | custom-call | flops 17179869184 | bytes 25165824 | tf_op jit(solution)/shard_map/attend_blocks/pallas_call | solution.py:246
  (24 shorter events, 0.4 us)
Async XLA Ops:
  2.0 14.6 %all-to-all-start = ((s32[8,1,25]{2,1,0:T(1,128)}), s32[8,1,25]{2,1,0:T(1,128)S(1)}, u32[]{:S(2)}, u32[]{:S(2)}) async-start(s32[8,1,25]{2,1,0:T(1,128)} %all_to_all.7), calls=%async_computation | async-start | bytes 8192 | tf_op jit(solution)/shard_map/all_to_all | solution.py:303
  8.0 0.7 copy-start.8
  15.3 1.3 copy-start
  21.8 20.3 %collective-permute-start.6 = (bf16[25,64,256]{2,1,0:T(8,128)(2,1)S(1)}, bf16[25,64,256]{2,1,0:T(8,128)(2,1)S(1)}, u32[]{:S(2)}, u32[]{:S(2)}) collective-permute-start(bf16[25,64,256]{2,1,0:T(8,128)(2,1)S(1)} %get-tuple-element.21), channel_id=1, source_target_pairs={{0,2},{1,3},{2,4},{3,5},{4,6},{5,7},{6,8},{7,9},{8,10},{9,11},{10,... | collective-permute-start | bytes 2457608 | tf_op jit(solution)/shard_map/ppermute | solution.py:313
  21.8 37.6 %collective-permute-start.5 = (bf16[25,64,256]{2,1,0:T(8,128)(2,1)S(1)}, bf16[25,64,256]{2,1,0:T(8,128)(2,1)S(1)}, u32[]{:S(2)}, u32[]{:S(2)}) collective-permute-start(bf16[25,64,256]{2,1,0:T(8,128)(2,1)S(1)} %get-tuple-element.20), channel_id=1, source_target_pairs={{0,4},{1,5},{2,6},{3,7},{4,8},{5,9},{6,10},{7,11},{8,12},{9,13},{1... | collective-permute-start | bytes 2457608 | tf_op jit(solution)/shard_map/ppermute | solution.py:313
  23.8 57.9 %collective-permute-start.4 = (bf16[25,64,256]{2,1,0:T(8,128)(2,1)}, bf16[25,64,256]{2,1,0:T(8,128)(2,1)}, u32[]{:S(2)}, u32[]{:S(2)}) collective-permute-start(bf16[25,64,256]{2,1,0:T(8,128)(2,1)} %get-tuple-element.19), channel_id=1, source_target_pairs={{0,6},{1,7},{2,8},{3,9},{4,10},{5,11},{6,12},{7,13},{8,14},{9,15},... | collective-permute-start | bytes 2457608 | tf_op jit(solution)/shard_map/ppermute | solution.py:313
  25.3 138.9 %collective-permute-start.3 = (bf16[25,64,256]{2,1,0:T(8,128)(2,1)}, bf16[25,64,256]{2,1,0:T(8,128)(2,1)}, u32[]{:S(2)}, u32[]{:S(2)}) collective-permute-start(bf16[25,64,256]{2,1,0:T(8,128)(2,1)} %get-tuple-element.18), channel_id=1, source_target_pairs={{0,8},{1,9},{2,10},{3,11},{4,12},{5,13},{6,14},{7,15},{8,0},{9,1},... | collective-permute-start | bytes 2457608 | tf_op jit(solution)/shard_map/ppermute | solution.py:313
  26.7 142.0 %collective-permute-start.2 = (bf16[25,64,256]{2,1,0:T(8,128)(2,1)}, bf16[25,64,256]{2,1,0:T(8,128)(2,1)S(1)}, u32[]{:S(2)}, u32[]{:S(2)}) collective-permute-start(bf16[25,64,256]{2,1,0:T(8,128)(2,1)} %get-tuple-element.17), channel_id=1, source_target_pairs={{0,10},{1,11},{2,12},{3,13},{4,14},{5,15},{6,0},{7,1},{8,2},{9,3},... | collective-permute-start | bytes 2457608 | tf_op jit(solution)/shard_map/ppermute | solution.py:313
  42.1 0.9 copy-start.2
  43.0 128.7 %collective-permute-start.1 = (bf16[25,64,256]{2,1,0:T(8,128)(2,1)}, bf16[25,64,256]{2,1,0:T(8,128)(2,1)}, u32[]{:S(2)}, u32[]{:S(2)}) collective-permute-start(bf16[25,64,256]{2,1,0:T(8,128)(2,1)} %get-tuple-element.16), channel_id=1, source_target_pairs={{0,12},{1,13},{2,14},{3,15},{4,0},{5,1},{6,2},{7,3},{8,4},{9,5},{1... | collective-permute-start | bytes 2457608 | tf_op jit(solution)/shard_map/ppermute | solution.py:313
  59.4 0.9 copy-start.4
  60.3 115.9 %collective-permute-start = (bf16[25,64,256]{2,1,0:T(8,128)(2,1)}, bf16[25,64,256]{2,1,0:T(8,128)(2,1)}, u32[]{:S(2)}, u32[]{:S(2)}) collective-permute-start(bf16[25,64,256]{2,1,0:T(8,128)(2,1)} %get-tuple-element.15), channel_id=1, source_target_pairs={{0,14},{1,15},{2,0},{3,1},{4,2},{5,3},{6,4},{7,5},{8,6},{9,7},{10,... | collective-permute-start | bytes 2457608 | tf_op jit(solution)/shard_map/ppermute | solution.py:313
  63.1 1.6 copy-start.1
  64.7 11.2 %copy-start.3 = (bf16[25,64,256]{2,1,0:T(8,128)(2,1)S(1)}, bf16[25,64,256]{2,1,0:T(8,128)(2,1)}, u32[]{:S(2)}) copy-start(bf16[25,64,256]{2,1,0:T(8,128)(2,1)} %copy-done.2) | copy-start | bytes 2457604
  75.9 2.9 %copy-start.5 = (bf16[25,64,256]{2,1,0:T(8,128)(2,1)S(1)}, bf16[25,64,256]{2,1,0:T(8,128)(2,1)}, u32[]{:S(2)}) copy-start(bf16[25,64,256]{2,1,0:T(8,128)(2,1)} %copy-done.4) | copy-start | bytes 2457604
  176.1 4.5 %copy-start.6 = (bf16[256,256]{1,0:T(8,128)(2,1)S(1)}, bf16[256,256]{1,0:T(8,128)(2,1)}, u32[]{:S(2)}) copy-start(bf16[256,256]{1,0:T(8,128)(2,1)} %rest_13_.1) | copy-start | bytes 393220
  176.2 4.5 %copy-start.7 = (bf16[256,256]{1,0:T(8,128)(2,1)S(1)}, bf16[256,256]{1,0:T(8,128)(2,1)}, u32[]{:S(2)}) copy-start(bf16[256,256]{1,0:T(8,128)(2,1)} %rest_14_.1) | copy-start | bytes 393220

commit v4 on v3

--- a/solution.py
+++ b/solution.py
@@ -34,7 +34,7 @@
     return row_head == lane_head
 
 
-def place_kernel(features_ref, assignment_ref, placed_ref, normed_ref):
+def place_kernel(features_ref, assignment_ref, normed_ref, *placed_ref):
     rows = features_ref.shape[0]
     lane = 128
     features = features_ref[...]
@@ -45,11 +45,12 @@
         chosen = jnp.concatenate([chosen] * (rows // lane), axis=1)
         one_hot = jnp.where(chosen == columns, 1.0, 0.0).astype(jnp.bfloat16)
         placed = jnp.dot(one_hot, features, preferred_element_type=jnp.float32)
-        placed_ref[pl.ds(part * lane, lane), :] = placed.astype(jnp.bfloat16)
+        if placed_ref:
+            placed_ref[0][pl.ds(part * lane, lane), :] = placed.astype(jnp.bfloat16)
         normed_ref[pl.ds(part * lane, lane), :] = layer_norm(placed).astype(jnp.bfloat16)
 
 
-def place(features, assignment):
+def place(features, assignment, outputs):
     width = features.shape[1]
     walkers, _, rows = assignment.shape
     local = pl.BlockSpec((rows, width), lambda i: (i, 0))
@@ -58,8 +59,8 @@
         place_kernel,
         grid=(walkers,),
         in_specs=[local, pl.BlockSpec((1, 1, rows), lambda i: (i, 0, 0))],
-        out_specs=[local] * 2,
-        out_shape=[out, out],
+        out_specs=[local] * outputs,
+        out_shape=[out] * outputs,
         cost_estimate=pl.CostEstimate(
             flops=2 * walkers * rows * rows * width,
             bytes_accessed=6 * walkers * rows * width,
@@ -70,33 +71,45 @@
     )(features, assignment)
 
 
-def pick_kernel(position_ref, demanded_ref, blocks_ref, *out_refs):
-    for step, out_ref in enumerate(out_refs):
-        reader = (position_ref[0] + step + 1) % SPAN
-
-        def one_slot(slot, carry, reader=reader, out_ref=out_ref):
-            out_ref[slot] = blocks_ref[demanded_ref[reader, slot]]
-            return carry
-
-        lax.fori_loop(0, out_ref.shape[0], one_slot, 0)
-
-
-def pick(position, demanded, blocks):
-    capacity = demanded.shape[1]
-    piece = jax.ShapeDtypeStruct((capacity,) + blocks.shape[1:], blocks.dtype)
+def choose(index, values):
+    result = values[-1]
+    for at in range(len(values) - 2, -1, -1):
+        result = jnp.where(index == at, values[at], result)
+    return result
+
+
+def pick_kernel(position_ref, wanted_ref, blocks_ref, *out_refs, plan, capacity):
+    position = position_ref[0]
+    for out_ref, pieces in zip(out_refs, plan, strict=True):
+        for at, (reader_of, owner_of) in enumerate(pieces):
+            reader, first = reader_of(position), owner_of(position) * capacity
+
+            def one_slot(slot, carry, out_ref=out_ref, at=at, reader=reader, first=first):
+                out_ref[at * capacity + slot] = blocks_ref[wanted_ref[reader, first + slot]]
+                return carry
+
+            lax.fori_loop(0, capacity, one_slot, 0)
+
+
+def pick(position, wanted, blocks, plan):
+    capacity = wanted.shape[1] // SPAN
+    outs = [
+        jax.ShapeDtypeStruct((len(pieces) * capacity,) + blocks.shape[1:], blocks.dtype)
+        for pieces in plan
+    ]
     smem = pl.BlockSpec(memory_space=pltpu.SMEM)
     vmem = pl.BlockSpec(memory_space=pltpu.VMEM)
     return pl.pallas_call(
-        pick_kernel,
+        functools.partial(pick_kernel, plan=plan, capacity=capacity),
         in_specs=[smem, smem, vmem],
-        out_specs=[vmem] * (SPAN - 1),
-        out_shape=[piece] * (SPAN - 1),
+        out_specs=[vmem] * len(outs),
+        out_shape=outs,
         cost_estimate=pl.CostEstimate(
-            flops=0, bytes_accessed=4 * (SPAN - 1) * piece.size, transcendentals=0
+            flops=0, bytes_accessed=4 * sum(out.size for out in outs), transcendentals=0
         ),
         compiler_params=kernel_params(),
         name="pick_blocks",
-    )(position, demanded, blocks)
+    )(position, wanted, blocks)
 
 
 def query_kernel(normed_ref, query_w_ref, query_ref, *, cluster, head_width):
@@ -140,9 +153,9 @@
     out_ref[...] = both.astype(jnp.bfloat16).reshape(out_ref.shape)
 
 
-def project_pairs(piece, w_both, so_far, at, total):
-    blocks, cluster, width = piece.shape
-    per = 5 if blocks % 5 == 0 else 8
+def project_pairs(piece, w_both, so_far, at, total, blocks):
+    _, cluster, width = piece.shape
+    per = max(n for n in range(1, 9) if blocks % n == 0 and at % n == 0)
     in_specs = [
         pl.BlockSpec((per, cluster, width), lambda i: (i, 0, 0)),
         pl.BlockSpec((width, 2 * width), lambda i: (0, 0)),
@@ -161,7 +174,9 @@
         out_shape=jax.ShapeDtypeStruct((total, cluster, 2 * width), jnp.bfloat16),
         input_output_aliases=aliases,
         cost_estimate=pl.CostEstimate(
-            flops=4 * piece.size * width, bytes_accessed=6 * piece.size, transcendentals=0
+            flops=4 * blocks * cluster * width * width,
+            bytes_accessed=6 * blocks * cluster * width,
+            transcendentals=0,
         ),
         compiler_params=kernel_params(),
         name="keys_values",
@@ -286,43 +301,139 @@
     return ranking, tables.reshape(SPAN, capacity)
 
 
+OUT = (2, 0, 3, 1)
+FROM = (1, 3, 0, 2)
+LEVELS = 4
+
+
+def position_at(z, y):
+    return 2 * z + y
+
+
+def partner(position):
+    return position ^ 1
+
+
+def onward(position):
+    return position_at(choose(position // 2, OUT), position % 2)
+
+
+def source(position):
+    return position_at(choose(position // 2, FROM), position % 2)
+
+
+def opposite(position):
+    return position_at(LEVELS - 1 - position // 2, position % 2)
+
+
+def itself(position):
+    return position
+
+
+def crossed(route):
+    return lambda position: partner(route(position))
+
+
+OWN_PLAN = (
+    ((partner, itself),),
+    ((source, itself), (crossed(source), itself)),
+    ((opposite, itself), (crossed(opposite), itself)),
+)
+PASSED_PLAN = (
+    ((partner, source), (crossed(onward), source)),
+    ((onward, source),),
+)
+
+
 def body(features, assignment, pairs, w_query, w_key, w_value, w_out, w_mix):
     rows_dev, width = features.shape
     block_count, pair_count = pairs.shape
     cluster = rows_dev // block_count
-    peers = lax.axis_size("elec")
-    stride = peers // SPAN
+    stride = lax.axis_size("elec") // SPAN
     groups = [[rest + place_ * stride for place_ in range(SPAN)] for rest in range(stride)]
     position = lax.axis_index("elec") // stride
     capacity = (block_count * pair_count + SPAN - 1) // SPAN + 1
+
+    def moved(x, moves):
+        pairs_of = [(s * stride + r, d * stride + r) for s, d in moves for r in range(stride)]
+        return lax.ppermute(x, "elec", pairs_of)
+
+    def across_z(pairs_of_z):
+        return [(position_at(s, y), position_at(d, y)) for s, d in pairs_of_z for y in range(2)]
+
+    swap = [(p, p ^ 1) for p in range(SPAN)]
+    first_moves = across_z(enumerate(OUT))
+    second_moves = across_z(enumerate(FROM))
+    middle_moves = across_z([(1, 2), (2, 1)])
+    outward_moves = across_z([(2, 3), (1, 0)])
+
+    raw = moved(features, first_moves)
+    raw_assignment = moved(assignment, first_moves)
 
     listed = pairs.reshape(-1)
     owner = listed // block_count // stride
     within = listed % block_count
     ranking, tables = slot_table(owner, within, capacity)
-    demanded = lax.all_to_all(
-        tables, "elec", split_axis=0, concat_axis=0, axis_index_groups=groups, tiled=True
-    )
-
-    placed, normed = place(
-        features, assignment.reshape(block_count // SUB, 1, SUB * cluster)
-    )
-    blocks = normed.reshape(block_count, cluster, width)
-    outgoing = pick(position.reshape(1), demanded, blocks)
-    arrived = [
-        lax.ppermute(piece, "elec", [(i, (i + (o + 1) * stride) % peers) for i in range(peers)])
-        for o, piece in enumerate(outgoing)
-    ]
+    wanted = lax.all_to_all(
+        jnp.broadcast_to(tables.reshape(1, -1), (SPAN, SPAN * capacity)),
+        "elec",
+        split_axis=0,
+        concat_axis=0,
+        axis_index_groups=groups,
+        tiled=True,
+    )
+    at_position = position.reshape(1)
+
+    walker_shape = (block_count // SUB, 1, SUB * cluster)
+    block_shape = (block_count, cluster, width)
+    normed, placed = place(features, assignment.reshape(walker_shape), 2)
+    blocks = normed.reshape(block_shape)
+    near, second, middle = pick(at_position, wanted, blocks, OWN_PLAN)
+    near = moved(near, swap)
+    second = moved(second, second_moves)
+    middle = moved(middle, middle_moves)
+
+    (passed,) = place(raw, raw_assignment.reshape(walker_shape), 1)
+    passed = passed.reshape(block_shape)
+    beside, outward = pick(at_position, wanted, passed, PASSED_PLAN)
+    outward = moved(outward, outward_moves)
+    beside = moved(beside, swap)
+    second_beside = moved(second[capacity:], swap)
+    outward_beside = moved(beside[capacity:], outward_moves)
+    middle_beside = moved(middle[capacity:], swap)
 
     w_both = jnp.concatenate([w_key, w_value], axis=1)
-    own_at = -((1 - SPAN) * capacity // block_count) * block_count
-    total = own_at + block_count
-    buffer = project_pairs(blocks, w_both, None, own_at, total)
+    pieces = [near, second, second_beside, beside, middle, outward, middle_beside, outward_beside]
+    own_at = len(pieces) * capacity
+    passed_at = own_at + block_count
+    total = passed_at + block_count
+    buffer = project_pairs(blocks, w_both, None, own_at, total, block_count)
     queries = project_queries(normed, w_query, cluster)
-    for o, piece in enumerate(arrived):
-        buffer = project_pairs(piece, w_both, buffer, o * capacity, total)
-    offset = (position - owner) % SPAN
-    table = jnp.where(offset == 0, own_at + within, (offset - 1) * capacity + ranking)
+    buffer = project_pairs(passed, w_both, buffer, passed_at, total, block_count)
+    for at, piece in enumerate(pieces):
+        buffer = project_pairs(piece, w_both, buffer, at * capacity, total, capacity)
+
+    z, y = position // 2, position % 2
+    is_end = (z == 0) | (z == LEVELS - 1)
+    z_owner, same = owner // 2, owner % 2 == y
+    from_first = z_owner == choose(z, FROM)
+    from_second = z_owner == choose(z, OUT)
+    piece_of = jnp.where(
+        z_owner == z,
+        0,
+        jnp.where(
+            from_first,
+            3,
+            jnp.where(
+                from_second,
+                jnp.where(same, 1, 2),
+                jnp.where(is_end, jnp.where(same, 5, 7), jnp.where(same, 4, 6)),
+            ),
+        ),
+    )
+    whole_at = jnp.where(z_owner == z, own_at, passed_at)
+    whole = same & ((z_owner == z) | from_first)
+    table = jnp.where(whole, whole_at + within, piece_of * capacity + ranking)
     return attend(table, queries, buffer, own_at, placed, w_out, w_mix, pair_count)
 
 

time: 231 us -> 231 us (level)
  the two profiles are of different devices: /device:TPU:28 before, /device:TPU:8 now
where the time goes in v4:
time: 231 us; the launch traced here: 230 us
  Pallas kernels  114 us (49%)
  waiting for transfers between devices  87.2 us (38%)
  starting transfers between devices  19.1 us (8%)
  local copies, waits for them, and re-layouts  9.41 us (4%)
    ppermute x10, waiting for transfers between devices, moved(): return lax.ppermute(x, 'elec', pairs_of)  54.8 us
    pallas_call x1, Pallas kernels, attend(): pl.pallas_call(functools.partial(attend_kernel, pair_count=pair_count, he...  49.4 us
    pallas_call x10, Pallas kernels, project_pairs(): pl.pallas_call(key_value_kernel, grid=(blocks // per,), in_specs=in_specs...  39.6 us
    all_to_all x1, waiting for transfers between devices, body(): lax.all_to_all(jnp.broadcast_to(tables.reshape(1, -1), (SPAN, SPAN * capa...  32.5 us
    pallas_call x2, Pallas kernels, place(): pl.pallas_call(place_kernel, grid=(walkers,), in_specs=[local, pl.BlockSp...  13.2 us
    ppermute x10, starting transfers between devices, moved(): return lax.ppermute(x, 'elec', pairs_of)  12.2 us
    all_to_all x1, starting transfers between devices, body(): lax.all_to_all(jnp.broadcast_to(tables.reshape(1, -1), (SPAN, SPAN * capa...  6.84 us
    pallas_call x1, Pallas kernels, project_queries(): pl.pallas_call(functools.partial(query_kernel, cluster=cluster, head_widt...  6.45 us
  transfers between devices with their start and end apart: 11, of which 3 were waited for; matrix products, arithmetic and copies ran while one was open for 3% of the time, Pallas kernels for 26%

profile of v4, /device:TPU:8, one launch (start us, length us, event | category | flops | bytes accessed | tf_op | source)
XLA Modules:
  0.0 230.1 jit_solution(3095139961959471177)
XLA Ops:
  0.0 0.8 copy.23
  1.9 6.8 %all-to-all-start = ((s32[8,1,200]{2,1,0:T(1,128)}), s32[8,1,200]{2,1,0:T(1,128)S(1)}, u32[]{:S(2)}, u32[]{:S(2)}) async-start(s32[8,1,200]{2,1,0:T(1,128)} %broadcast_in_dim.67), calls=%async_computation | async-start | bytes 16384 | tf_op jit(solution)/shard_map/all_to_all | solution.py:377
  9.5 6.6 %place_rows.2 = (bf16[4096,256]{1,0:T(8,128)(2,1)S(1)}, bf16[4096,256]{1,0:T(8,128)(2,1)S(1)}) custom-call(bf16[4096,256]{1,0:T(8,128)(2,1)} %features_ref.1, s32[8,1,512]{2,1,0:T(1,128)S(1)} %bitcast.17), custom_call_target="tpu_custom_call" | custom-call | flops 1073741824 | bytes 6291456 | tf_op jit(solution)/shard_map/place_rows/pallas_call | solution.py:58
  16.1 1.3 copy-done.8
  17.4 32.5 %all-to-all-done = s32[8,1,200]{2,1,0:T(1,128)S(1)} async-done(((s32[8,1,200]{2,1,0:T(1,128)}), s32[8,1,200]{2,1,0:T(1,128)S(1)}, u32[]{:S(2)}, u32[]{:S(2)}) %all-to-all-start) | async-done | bytes 6432 | tf_op jit(solution)/shard_map/all_to_all | solution.py:377
  49.9 2.9 %pick_blocks.3 = (bf16[25,64,256]{2,1,0:T(8,128)(2,1)}, bf16[50,64,256]{2,1,0:T(8,128)(2,1)S(1)}, bf16[50,64,256]{2,1,0:T(8,128)(2,1)S(1)}) custom-call(s32[1]{0:T(128)} %bitcast.2.position_ref, s32[8,200]{1,0:T(8,128)S(1)} %bitcast.14, bf16[64,64,256]{2,1,0:T(8,128)(2,1)S(1)} %bitcast.11), custom_call_target="tpu_custom_call" | custom-call | bytes 8192000 | tf_op jit(solution)/shard_map/pick_blocks/pallas_call | solution.py:102
  52.8 2.4 %collective-permute-start.7 = (bf16[50,64,256]{2,1,0:T(8,128)(2,1)S(1)}, bf16[50,64,256]{2,1,0:T(8,128)(2,1)S(1)}, u32[]{:S(2)}, u32[]{:S(2)}) collective-permute-start(bf16[50,64,256]{2,1,0:T(8,128)(2,1)S(1)} %get-tuple-element.16), channel_id=1, source_target_pairs={{0,4},{1,5},{2,6},{3,7},{4,12},{5,13},{6,14},{7,15},{8,0},{9,1},{1... | collective-permute-start | bytes 4915208 | tf_op jit(solution)/shard_map/ppermute | solution.py:359
  55.1 2.3 %collective-permute-start.4 = (bf16[50,64,256]{2,1,0:T(8,128)(2,1)S(1)}, bf16[50,64,256]{2,1,0:T(8,128)(2,1)S(1)}, u32[]{:S(2)}, u32[]{:S(2)}) collective-permute-start(bf16[50,64,256]{2,1,0:T(8,128)(2,1)S(1)} %get-tuple-element.14), channel_id=1, source_target_pairs={{4,8},{5,9},{6,10},{7,11},{8,4},{9,5},{10,6},{11,7},{20,24},{21,25... | collective-permute-start | bytes 4915208 | tf_op jit(solution)/shard_map/ppermute | solution.py:359
  57.5 6.6 %place_rows.3 = bf16[4096,256]{1,0:T(8,128)(2,1)S(1)} custom-call(bf16[4096,256]{1,0:T(8,128)(2,1)} %collective-permute-done.features_ref, s32[8,1,512]{2,1,0:T(1,128)S(1)} %bitcast.16), custom_call_target="tpu_custom_call" | custom-call | flops 1073741824 | bytes 6291456 | tf_op jit(solution)/shard_map/place_rows/pallas_call | solution.py:58
  64.1 2.3 %pick_blocks.2 = (bf16[50,64,256]{2,1,0:T(8,128)(2,1)S(1)}, bf16[25,64,256]{2,1,0:T(8,128)(2,1)}) custom-call(s32[1]{0:T(128)} %bitcast.2.position_ref, s32[8,200]{1,0:T(8,128)S(1)} %bitcast.15, bf16[64,64,256]{2,1,0:T(8,128)(2,1)S(1)} %bitcast.9), custom_call_target="tpu_custom_call" | custom-call | bytes 4915200 | tf_op jit(solution)/shard_map/pick_blocks/pallas_call | solution.py:102
  67.0 1.5 collective-permute-start.9
  68.5 22.9 %collective-permute-done.7.rows_ref = bf16[50,64,256]{2,1,0:T(8,128)(2,1)S(1)} collective-permute-done((bf16[50,64,256]{2,1,0:T(8,128)(2,1)S(1)}, bf16[50,64,256]{2,1,0:T(8,128)(2,1)S(1)}, u32[]{:S(2)}, u32[]{:S(2)}) %collective-permute-start.7) | collective-permute-done | bytes 1638432 | tf_op jit(solution)/shard_map/ppermute | solution.py:359
  91.4 1.1 slice.14
  93.0 31.9 %collective-permute-done.4.rows_ref = bf16[50,64,256]{2,1,0:T(8,128)(2,1)S(1)} collective-permute-done((bf16[50,64,256]{2,1,0:T(8,128)(2,1)S(1)}, bf16[50,64,256]{2,1,0:T(8,128)(2,1)S(1)}, u32[]{:S(2)}, u32[]{:S(2)}) %collective-permute-start.4) | collective-permute-done | bytes 1638432 | tf_op jit(solution)/shard_map/ppermute | solution.py:359
  124.9 1.1 slice.13
  126.5 2.2 collective-permute-start.6
  128.7 1.0 slice.12
  129.7 2.2 collective-permute-start.3
  132.1 0.9 constant_dynamic-update-slice_fusion.w_ref
  133.0 1.6 copy-done.1
  134.6 4.7 %keys_values.10.rest_0_ = bf16[328,64,512]{2,1,0:T(8,128)(2,1)} custom-call(bf16[64,64,256]{2,1,0:T(8,128)(2,1)S(1)} %bitcast.12, bf16[256,512]{1,0:T(8,128)(2,1)S(1)} %constant_dynamic-update-slice_fusion.w_ref), custom_call_target="tpu_custom_call" | custom-call | flops 1073741824 | bytes 6291456 | tf_op jit(solution)/shard_map/keys_values/pallas_call | solution.py:169
  139.3 6.4 %queries.1.query_ref = bf16[64,256,256]{2,1,0:T(8,128)(2,1)} custom-call(bf16[4096,256]{1,0:T(8,128)(2,1)S(1)} %copy-done.1, bf16[256,256]{1,0:T(8,128)(2,1)S(1)} %bitcast.13), custom_call_target="tpu_custom_call" | custom-call | flops 2147483648 | bytes 10485760 | tf_op jit(solution)/shard_map/queries/pallas_call | solution.py:129
  145.7 4.7 %keys_values.11.rest_0_ = bf16[328,64,512]{2,1,0:T(8,128)(2,1)} custom-call(bf16[64,64,256]{2,1,0:T(8,128)(2,1)S(1)} %bitcast.10, bf16[256,512]{1,0:T(8,128)(2,1)S(1)} %constant_dynamic-update-slice_fusion.w_ref, bf16[328,64,512]{2,1,0:T(8,128)(2,1)} %keys_values.10.rest_0_), custom_call_target="tpu_custom_call", output_to_operand_aliasing={{}: (2, {})} | custom-call | flops 1073741824 | bytes 6291456 | tf_op jit(solution)/shard_map/keys_values/pallas_call | solution.py:169
  150.4 4.6 %keys_values.12.rest_0_ = bf16[328,64,512]{2,1,0:T(8,128)(2,1)} custom-call(bf16[25,64,256]{2,1,0:T(8,128)(2,1)} %collective-permute-done.9.rows_ref, bf16[256,512]{1,0:T(8,128)(2,1)S(1)} %constant_dynamic-update-slice_fusion.w_ref, bf16[328,64,512]{2,1,0:T(8,128)(2,1)} %keys_values.11.rest_0_), custom_call_target="tpu_custom_call", output_to_operand_aliasing={{}: (2, {})} | custom-call | flops 419430400 | bytes 2457600 | tf_op jit(solution)/shard_map/keys_values/pallas_call | solution.py:169
  155.0 3.0 %keys_values.13.rest_0_ = bf16[328,64,512]{2,1,0:T(8,128)(2,1)} custom-call(bf16[50,64,256]{2,1,0:T(8,128)(2,1)S(1)} %copy-done.5, bf16[256,512]{1,0:T(8,128)(2,1)S(1)} %constant_dynamic-update-slice_fusion.w_ref, bf16[328,64,512]{2,1,0:T(8,128)(2,1)} %keys_values.12.rest_0_), custom_call_target="tpu_custom_call", output_to_operand_aliasing={{}: (2, {})} | custom-call | flops 419430400 | bytes 2457600 | tf_op jit(solution)/shard_map/keys_values/pallas_call | solution.py:169
  158.0 4.6 %keys_values.14.rest_0_ = bf16[328,64,512]{2,1,0:T(8,128)(2,1)} custom-call(bf16[25,64,256]{2,1,0:T(8,128)(2,1)} %collective-permute-done.8.rows_ref, bf16[256,512]{1,0:T(8,128)(2,1)S(1)} %constant_dynamic-update-slice_fusion.w_ref, bf16[328,64,512]{2,1,0:T(8,128)(2,1)} %keys_values.13.rest_0_), custom_call_target="tpu_custom_call", output_to_operand_aliasing={{}: (2, {})} | custom-call | flops 419430400 | bytes 2457600 | tf_op jit(solution)/shard_map/keys_values/pallas_call | solution.py:169
  162.6 3.0 %keys_values.15.rest_0_ = bf16[328,64,512]{2,1,0:T(8,128)(2,1)} custom-call(bf16[50,64,256]{2,1,0:T(8,128)(2,1)S(1)} %copy-done.7, bf16[256,512]{1,0:T(8,128)(2,1)S(1)} %constant_dynamic-update-slice_fusion.w_ref, bf16[328,64,512]{2,1,0:T(8,128)(2,1)} %keys_values.14.rest_0_), custom_call_target="tpu_custom_call", output_to_operand_aliasing={{}: (2, {})} | custom-call | flops 419430400 | bytes 2457600 | tf_op jit(solution)/shard_map/keys_values/pallas_call | solution.py:169
  165.6 2.9 %keys_values.16.rest_0_ = bf16[328,64,512]{2,1,0:T(8,128)(2,1)} custom-call(bf16[50,64,256]{2,1,0:T(8,128)(2,1)S(1)} %copy-done.3, bf16[256,512]{1,0:T(8,128)(2,1)S(1)} %constant_dynamic-update-slice_fusion.w_ref, bf16[328,64,512]{2,1,0:T(8,128)(2,1)} %keys_values.15.rest_0_), custom_call_target="tpu_custom_call", output_to_operand_aliasing={{}: (2, {})} | custom-call | flops 419430400 | bytes 2457600 | tf_op jit(solution)/shard_map/keys_values/pallas_call | solution.py:169
  168.6 4.5 %keys_values.17.rest_0_ = bf16[328,64,512]{2,1,0:T(8,128)(2,1)} custom-call(bf16[25,64,256]{2,1,0:T(8,128)(2,1)} %collective-permute-done.6.rows_ref, bf16[256,512]{1,0:T(8,128)(2,1)S(1)} %constant_dynamic-update-slice_fusion.w_ref, bf16[328,64,512]{2,1,0:T(8,128)(2,1)} %keys_values.16.rest_0_), custom_call_target="tpu_custom_call", output_to_operand_aliasing={{}: (2, {})} | custom-call | flops 419430400 | bytes 2457600 | tf_op jit(solution)/shard_map/keys_values/pallas_call | solution.py:169
  173.1 2.9 %keys_values.18.rest_0_ = bf16[328,64,512]{2,1,0:T(8,128)(2,1)} custom-call(bf16[25,64,256]{2,1,0:T(8,128)(2,1)S(1)} %collective-permute-done.5.rows_ref, bf16[256,512]{1,0:T(8,128)(2,1)S(1)} %constant_dynamic-update-slice_fusion.w_ref, bf16[328,64,512]{2,1,0:T(8,128)(2,1)} %keys_values.17.rest_0_), custom_call_target="tpu_custom_call", output_to_operand_aliasing={{}: (2, {})} | custom-call | flops 419430400 | bytes 2457600 | tf_op jit(solution)/shard_map/keys_values/pallas_call | solution.py:169
  176.0 4.7 %keys_values.19.own_ref.rest_0_.rest_1_.rest_2_.rest_3_.rest_4_.rest_5_.rest_6_.rest_7_.rest_8_.rest_9_.rest_10_.rest_11_ = bf16[328,64,512]{2,1,0:T(8,128)(2,1)} custom-call(bf16[25,64,256]{2,1,0:T(8,128)(2,1)} %collective-permute-done.3.rows_ref, bf16[256,512]{1,0:T(8,128)(2,1)S(1)} %constant_dynamic-update-slice_fusion.w_ref, ...), custom_call_target="tpu_custom_call", output_to_operand_aliasing={{}: (2, {})} | custom-call | flops 419430400 | bytes 2457600 | tf_op jit(solution)/shard_map/keys_values/pallas_call | solution.py:169
  180.7 49.4 %attend_blocks.1 = bf16[4096,256]{1,0:T(8,128)(2,1)} custom-call(s32[192]{0:T(256)S(1)} %get-tuple-element.20.table_ref, bf16[64,256,256]{2,1,0:T(8,128)(2,1)} %queries.1.query_ref, bf16[328,64,512]{2,1,0:T(8,128)(2,1)} %keys_values.19.own_ref.rest_0_.rest_1_.rest_2_.rest_3_.rest_4_.rest_5_.rest_6_.rest_7_.rest_8_.rest_9_.rest_10_.rest_11_, ...), custom_call_target="tpu_custom_call" | custom-call | flops 17179869184 | bytes 25165824 | tf_op jit(solution)/shard_map/attend_blocks/pallas_call | solution.py:261
  (50 shorter events, 3.7 us)
Async XLA Ops:
  0.0 57.5 %collective-permute-start = (bf16[4096,256]{1,0:T(8,128)(2,1)}, bf16[4096,256]{1,0:T(8,128)(2,1)}, u32[]{:S(2)}, u32[]{:S(2)}) collective-permute-start(bf16[4096,256]{1,0:T(8,128)(2,1)} %features_ref.1), channel_id=1, source_target_pairs={{0,8},{1,9},{2,10},{3,11},{4,0},{5,1},{6,2},{7,3},{8,12},{9,13},{1... | collective-permute-start | bytes 6291464 | tf_op jit(solution)/shard_map/ppermute | solution.py:359
  1.9 48.0 %all-to-all-start = ((s32[8,1,200]{2,1,0:T(1,128)}), s32[8,1,200]{2,1,0:T(1,128)S(1)}, u32[]{:S(2)}, u32[]{:S(2)}) async-start(s32[8,1,200]{2,1,0:T(1,128)} %broadcast_in_dim.67), calls=%async_computation | async-start | bytes 16384 | tf_op jit(solution)/shard_map/all_to_all | solution.py:377
  8.7 48.8 %collective-permute-start.1 = (s32[4096]{0:T(1024)}, s32[4096]{0:T(1024)S(1)}, u32[]{:S(2)}, u32[]{:S(2)}) collective-permute-start(s32[4096]{0:T(1024)} %param.9), channel_id=1, source_target_pairs={{0,8},{1,9},{2,10},{3,11},{4,0},{5,1},{6,2},{7,3},{8,12},{9,13},{1... | collective-permute-start | bytes 49160 | tf_op jit(solution)/shard_map/ppermute | solution.py:359
  8.8 0.8 copy-start.12
  16.1 1.3 copy-start.8
  17.4 40.1 %copy-start = (bf16[4096,256]{1,0:T(8,128)(2,1)}, bf16[4096,256]{1,0:T(8,128)(2,1)S(1)}, u32[]{:S(2)}) copy-start(bf16[4096,256]{1,0:T(8,128)(2,1)S(1)} %get-tuple-element.12.normed_ref) | copy-start | bytes 6291460
  52.8 38.6 %collective-permute-start.7 = (bf16[50,64,256]{2,1,0:T(8,128)(2,1)S(1)}, bf16[50,64,256]{2,1,0:T(8,128)(2,1)S(1)}, u32[]{:S(2)}, u32[]{:S(2)}) collective-permute-start(bf16[50,64,256]{2,1,0:T(8,128)(2,1)S(1)} %get-tuple-element.16), channel_id=1, source_target_pairs={{0,4},{1,5},{2,6},{3,7},{4,12},{5,13},{6,14},{7,15},{8,0},{9,1},{1... | collective-permute-start | bytes 4915208 | tf_op jit(solution)/shard_map/ppermute | solution.py:359
  55.1 69.7 %collective-permute-start.4 = (bf16[50,64,256]{2,1,0:T(8,128)(2,1)S(1)}, bf16[50,64,256]{2,1,0:T(8,128)(2,1)S(1)}, u32[]{:S(2)}, u32[]{:S(2)}) collective-permute-start(bf16[50,64,256]{2,1,0:T(8,128)(2,1)S(1)} %get-tuple-element.14), channel_id=1, source_target_pairs={{4,8},{5,9},{6,10},{7,11},{8,4},{9,5},{10,6},{11,7},{20,24},{21,25... | collective-permute-start | bytes 4915208 | tf_op jit(solution)/shard_map/ppermute | solution.py:359
  66.5 62.2 %collective-permute-start.2 = (bf16[50,64,256]{2,1,0:T(8,128)(2,1)S(1)}, bf16[50,64,256]{2,1,0:T(8,128)(2,1)S(1)}, u32[]{:S(2)}, u32[]{:S(2)}) collective-permute-start(bf16[50,64,256]{2,1,0:T(8,128)(2,1)S(1)} %get-tuple-element.13), channel_id=1, source_target_pairs={{0,2},{1,3},{2,0},{3,1},{4,6},{5,7},{6,4},{7,5},{8,10},{9,11},{10,... | collective-permute-start | bytes 4915208 | tf_op jit(solution)/shard_map/ppermute | solution.py:359
  67.0 64.9 %copy-start.13 = (bf16[256,256]{1,0:T(8,128)(2,1)S(1)}, bf16[256,256]{1,0:T(8,128)(2,1)}, u32[]{:S(2)}) copy-start(bf16[256,256]{1,0:T(8,128)(2,1)} %param.12) | copy-start | bytes 393220
  67.0 83.4 %collective-permute-start.9 = (bf16[25,64,256]{2,1,0:T(8,128)(2,1)}, bf16[25,64,256]{2,1,0:T(8,128)(2,1)}, u32[]{:S(2)}, u32[]{:S(2)}) collective-permute-start(bf16[25,64,256]{2,1,0:T(8,128)(2,1)} %get-tuple-element.17), channel_id=1, source_target_pairs={{0,2},{1,3},{2,0},{3,1},{4,6},{5,7},{6,4},{7,5},{8,10},{9,11},{10,... | collective-permute-start | bytes 2457608 | tf_op jit(solution)/shard_map/ppermute | solution.py:359
  91.4 38.3 %copy-start.4 = (bf16[50,64,256]{2,1,0:T(8,128)(2,1)}, bf16[50,64,256]{2,1,0:T(8,128)(2,1)S(1)}, u32[]{:S(2)}) copy-start(bf16[50,64,256]{2,1,0:T(8,128)(2,1)S(1)} %collective-permute-done.7.rows_ref) | copy-start | bytes 4915204
  92.5 39.5 %copy-start.14 = (bf16[256,256]{1,0:T(8,128)(2,1)S(1)}, bf16[256,256]{1,0:T(8,128)(2,1)}, u32[]{:S(2)}) copy-start(bf16[256,256]{1,0:T(8,128)(2,1)} %param.11) | copy-start | bytes 393220
  92.5 65.5 %collective-permute-start.8 = (bf16[25,64,256]{2,1,0:T(8,128)(2,1)}, bf16[25,64,256]{2,1,0:T(8,128)(2,1)}, u32[]{:S(2)}, u32[]{:S(2)}) collective-permute-start(bf16[25,64,256]{2,1,0:T(8,128)(2,1)} %slice.14), channel_id=1, source_target_pairs={{0,2},{1,3},{2,0},{3,1},{4,6},{5,7},{6,4},{7,5},{8,10},{9,11},{10,... | collective-permute-start | bytes 2457608 | tf_op jit(solution)/shard_map/ppermute | solution.py:359
  124.9 4.9 %copy-start.2 = (bf16[50,64,256]{2,1,0:T(8,128)(2,1)}, bf16[50,64,256]{2,1,0:T(8,128)(2,1)S(1)}, u32[]{:S(2)}) copy-start(bf16[50,64,256]{2,1,0:T(8,128)(2,1)S(1)} %collective-permute-done.4.rows_ref) | copy-start | bytes 4915204
  126.0 47.1 %collective-permute-start.5 = (bf16[25,64,256]{2,1,0:T(8,128)(2,1)}, bf16[25,64,256]{2,1,0:T(8,128)(2,1)S(1)}, u32[]{:S(2)}, u32[]{:S(2)}) collective-permute-start(bf16[25,64,256]{2,1,0:T(8,128)(2,1)} %slice.13), channel_id=1, source_target_pairs={{0,2},{1,3},{2,0},{3,1},{4,6},{5,7},{6,4},{7,5},{8,10},{9,11},{10,... | collective-permute-start | bytes 2457608 | tf_op jit(solution)/shard_map/ppermute | solution.py:359
  126.5 42.1 %collective-permute-start.6 = (bf16[25,64,256]{2,1,0:T(8,128)(2,1)}, bf16[25,64,256]{2,1,0:T(8,128)(2,1)}, u32[]{:S(2)}, u32[]{:S(2)}) collective-permute-start(bf16[25,64,256]{2,1,0:T(8,128)(2,1)} %get-tuple-element.15), channel_id=1, source_target_pairs={{8,12},{9,13},{10,14},{11,15},{4,0},{5,1},{6,2},{7,3},{24,28},{25,... | collective-permute-start | bytes 2457608 | tf_op jit(solution)/shard_map/ppermute | solution.py:359
  128.7 3.3 %copy-start.6 = (bf16[50,64,256]{2,1,0:T(8,128)(2,1)}, bf16[50,64,256]{2,1,0:T(8,128)(2,1)S(1)}, u32[]{:S(2)}) copy-start(bf16[50,64,256]{2,1,0:T(8,128)(2,1)S(1)} %collective-permute-done.2.rows_ref) | copy-start | bytes 4915204
  129.7 46.3 %collective-permute-start.3 = (bf16[25,64,256]{2,1,0:T(8,128)(2,1)}, bf16[25,64,256]{2,1,0:T(8,128)(2,1)}, u32[]{:S(2)}, u32[]{:S(2)}) collective-permute-start(bf16[25,64,256]{2,1,0:T(8,128)(2,1)} %slice.12), channel_id=1, source_target_pairs={{8,12},{9,13},{10,14},{11,15},{4,0},{5,1},{6,2},{7,3},{24,28},{25,... | collective-permute-start | bytes 2457608 | tf_op jit(solution)/shard_map/ppermute | solution.py:359
  133.0 1.6 copy-start.1
  150.4 4.6 %copy-start.5 = (bf16[50,64,256]{2,1,0:T(8,128)(2,1)S(1)}, bf16[50,64,256]{2,1,0:T(8,128)(2,1)}, u32[]{:S(2)}) copy-start(bf16[50,64,256]{2,1,0:T(8,128)(2,1)} %copy-done.4) | copy-start | bytes 4915204
  158.0 4.6 %copy-start.7 = (bf16[50,64,256]{2,1,0:T(8,128)(2,1)S(1)}, bf16[50,64,256]{2,1,0:T(8,128)(2,1)}, u32[]{:S(2)}) copy-start(bf16[50,64,256]{2,1,0:T(8,128)(2,1)} %copy-done.6) | copy-start | bytes 4915204
  162.6 3.0 %copy-start.3 = (bf16[50,64,256]{2,1,0:T(8,128)(2,1)S(1)}, bf16[50,64,256]{2,1,0:T(8,128)(2,1)}, u32[]{:S(2)}) copy-start(bf16[50,64,256]{2,1,0:T(8,128)(2,1)} %copy-done.2) | copy-start | bytes 4915204
  176.0 4.7 %copy-start.9 = (bf16[4096,256]{1,0:T(8,128)(2,1)S(1)}, bf16[4096,256]{1,0:T(8,128)(2,1)}, u32[]{:S(2)}) copy-start(bf16[4096,256]{1,0:T(8,128)(2,1)} %copy-done.8) | copy-start | bytes 6291460
  176.0 4.7 %copy-start.10 = (bf16[256,256]{1,0:T(8,128)(2,1)S(1)}, bf16[256,256]{1,0:T(8,128)(2,1)}, u32[]{:S(2)}) copy-start(bf16[256,256]{1,0:T(8,128)(2,1)} %rest_13_.1) | copy-start | bytes 393220
  176.0 4.7 %copy-start.11 = (bf16[256,256]{1,0:T(8,128)(2,1)S(1)}, bf16[256,256]{1,0:T(8,128)(2,1)}, u32[]{:S(2)}) copy-start(bf16[256,256]{1,0:T(8,128)(2,1)} %rest_14_.1) | copy-start | bytes 393220

commit v5 on v4

--- a/solution.py
+++ b/solution.py
@@ -12,9 +12,11 @@
 SUB = 8
 GROUP = 4
 STEP = 4
+HEAD_WALKERS = 3
 VMEM_BYTES = 48 * 1024 * 1024
 
 NT = (((1,), (1,)), ((), ()))
+SHORT = pl.CostEstimate(flops=0, bytes_accessed=0, transcendentals=0)
 
 
 def kernel_params():
@@ -34,7 +36,8 @@
     return row_head == lane_head
 
 
-def place_kernel(features_ref, assignment_ref, normed_ref, *placed_ref):
+def place_kernel(features_ref, assignment_ref, *rest, outputs):
+    normed_ref, *placed_ref = rest[len(rest) - outputs :]
     rows = features_ref.shape[0]
     lane = 128
     features = features_ref[...]
@@ -50,25 +53,47 @@
         normed_ref[pl.ds(part * lane, lane), :] = layer_norm(placed).astype(jnp.bfloat16)
 
 
-def place(features, assignment, outputs):
-    width = features.shape[1]
+def place(features, assignment, outputs, first=0, so_far=None, after=()):
+    count, width = features.shape
     walkers, _, rows = assignment.shape
-    local = pl.BlockSpec((rows, width), lambda i: (i, 0))
-    out = jax.ShapeDtypeStruct(features.shape, jnp.bfloat16)
-    return pl.pallas_call(
-        place_kernel,
-        grid=(walkers,),
-        in_specs=[local, pl.BlockSpec((1, 1, rows), lambda i: (i, 0, 0))],
-        out_specs=[local] * outputs,
+    out = jax.ShapeDtypeStruct((walkers * rows, width), jnp.bfloat16)
+    extra = [x for x in (so_far,) if x is not None] + list(after)
+    return pl.pallas_call(
+        functools.partial(place_kernel, outputs=outputs),
+        grid=(count // rows,),
+        in_specs=[
+            pl.BlockSpec((rows, width), lambda i: (i, 0)),
+            pl.BlockSpec((1, 1, rows), lambda i: (first + i, 0, 0)),
+        ]
+        + [pl.BlockSpec(memory_space=pl.ANY)] * len(extra),
+        out_specs=[pl.BlockSpec((rows, width), lambda i: (first + i, 0))] * outputs,
         out_shape=[out] * outputs,
-        cost_estimate=pl.CostEstimate(
-            flops=2 * walkers * rows * rows * width,
-            bytes_accessed=6 * walkers * rows * width,
-            transcendentals=0,
-        ),
+        input_output_aliases={} if so_far is None else {2: 0},
+        cost_estimate=SHORT,
         compiler_params=kernel_params(),
         name="place_rows",
-    )(features, assignment)
+    )(features, assignment, *extra)
+
+
+def tail_kernel(features_ref, *rest):
+    out_ref = rest[-1]
+    out_ref[...] = features_ref[...]
+
+
+def tail_rows(features, rows, first, after):
+    total, width = features.shape
+    count = total - first * rows
+    return pl.pallas_call(
+        tail_kernel,
+        grid=(count // rows,),
+        in_specs=[pl.BlockSpec((rows, width), lambda i: (first + i, 0))]
+        + [pl.BlockSpec(memory_space=pl.ANY)] * len(after),
+        out_specs=pl.BlockSpec((rows, width), lambda i: (i, 0)),
+        out_shape=jax.ShapeDtypeStruct((count, width), features.dtype),
+        cost_estimate=SHORT,
+        compiler_params=kernel_params(),
+        name="tail_rows",
+    )(features, *after)
 
 
 def choose(index, values):
@@ -78,38 +103,39 @@
     return result
 
 
-def pick_kernel(position_ref, wanted_ref, blocks_ref, *out_refs, plan, capacity):
+def pick_kernel(position_ref, wanted_ref, *rest, plan, capacity):
     position = position_ref[0]
-    for out_ref, pieces in zip(out_refs, plan, strict=True):
-        for at, (reader_of, owner_of) in enumerate(pieces):
+    for out_ref, pieces in zip(rest[len(rest) - len(plan) :], plan, strict=True):
+        for at, (blocks, reader_of, owner_of) in enumerate(pieces):
             reader, first = reader_of(position), owner_of(position) * capacity
 
-            def one_slot(slot, carry, out_ref=out_ref, at=at, reader=reader, first=first):
-                out_ref[at * capacity + slot] = blocks_ref[wanted_ref[reader, first + slot]]
+            def one_slot(slot, carry, out_ref=out_ref, at=at, blocks=blocks, reader=reader, first=first):
+                out_ref[at * capacity + slot] = rest[blocks][wanted_ref[reader, first + slot]]
                 return carry
 
             lax.fori_loop(0, capacity, one_slot, 0)
 
 
-def pick(position, wanted, blocks, plan):
+def pick(position, wanted, sources, plan, after=()):
     capacity = wanted.shape[1] // SPAN
+    block = sources[0].shape[1:]
     outs = [
-        jax.ShapeDtypeStruct((len(pieces) * capacity,) + blocks.shape[1:], blocks.dtype)
+        jax.ShapeDtypeStruct((len(pieces) * capacity,) + block, sources[0].dtype)
         for pieces in plan
     ]
     smem = pl.BlockSpec(memory_space=pltpu.SMEM)
     vmem = pl.BlockSpec(memory_space=pltpu.VMEM)
     return pl.pallas_call(
         functools.partial(pick_kernel, plan=plan, capacity=capacity),
-        in_specs=[smem, smem, vmem],
+        in_specs=[smem, smem]
+        + [vmem] * len(sources)
+        + [pl.BlockSpec(memory_space=pl.ANY)] * len(after),
         out_specs=[vmem] * len(outs),
         out_shape=outs,
-        cost_estimate=pl.CostEstimate(
-            flops=0, bytes_accessed=4 * sum(out.size for out in outs), transcendentals=0
-        ),
+        cost_estimate=SHORT,
         compiler_params=kernel_params(),
         name="pick_blocks",
-    )(position, wanted, blocks)
+    )(position, wanted, *sources, *after)
 
 
 def query_kernel(normed_ref, query_w_ref, query_ref, *, cluster, head_width):
@@ -135,11 +161,7 @@
         ],
         out_specs=pl.BlockSpec((SUB, width, GROUP * cluster), lambda i: (i, 0, 0)),
         out_shape=jax.ShapeDtypeStruct((blocks, width, GROUP * cluster), jnp.bfloat16),
-        cost_estimate=pl.CostEstimate(
-            flops=2 * rows * GROUP * width * width,
-            bytes_accessed=2 * rows * width * (GROUP + 1),
-            transcendentals=0,
-        ),
+        cost_estimate=SHORT,
         compiler_params=kernel_params(),
         name="queries",
     )(normed, w_query.T)
@@ -148,14 +170,21 @@
 def key_value_kernel(rows_ref, w_ref, *rest):
     out_ref = rest[-1]
     blocks, cluster, width = rows_ref.shape
-    rows = rows_ref[...].reshape(blocks * cluster, width)
-    both = jnp.dot(rows, w_ref[...], preferred_element_type=jnp.float32)
-    out_ref[...] = both.astype(jnp.bfloat16).reshape(out_ref.shape)
-
-
-def project_pairs(piece, w_both, so_far, at, total, blocks):
-    _, cluster, width = piece.shape
-    per = max(n for n in range(1, 9) if blocks % n == 0 and at % n == 0)
+    per = max(n for n in range(1, 9) if blocks % n == 0)
+
+    def some(at, carry):
+        here = pl.ds(at * per, per)
+        rows = rows_ref[here].reshape(per * cluster, width)
+        both = jnp.dot(rows, w_ref[...], preferred_element_type=jnp.float32)
+        out_ref[here] = both.astype(jnp.bfloat16).reshape((per,) + out_ref.shape[1:])
+        return carry
+
+    lax.fori_loop(0, blocks // per, some, 0)
+
+
+def project_pairs(piece, w_both, so_far, at, total):
+    blocks, cluster, width = piece.shape
+    per = max(n for n in range(1, 33) if blocks % n == 0 and at % n == 0)
     in_specs = [
         pl.BlockSpec((per, cluster, width), lambda i: (i, 0, 0)),
         pl.BlockSpec((width, 2 * width), lambda i: (0, 0)),
@@ -173,11 +202,7 @@
         out_specs=pl.BlockSpec((per, cluster, 2 * width), lambda i: (at // per + i, 0, 0)),
         out_shape=jax.ShapeDtypeStruct((total, cluster, 2 * width), jnp.bfloat16),
         input_output_aliases=aliases,
-        cost_estimate=pl.CostEstimate(
-            flops=4 * blocks * cluster * width * width,
-            bytes_accessed=6 * blocks * cluster * width,
-            transcendentals=0,
-        ),
+        cost_estimate=SHORT,
         compiler_params=kernel_params(),
         name="keys_values",
     )(*operands)
@@ -272,11 +297,7 @@
             out_specs=local,
         ),
         out_shape=jax.ShapeDtypeStruct((rows, width), jnp.bfloat16),
-        cost_estimate=pl.CostEstimate(
-            flops=4 * rows * HEADS * width * (pair_count + 1) * cluster,
-            bytes_accessed=24 * rows * width,
-            transcendentals=rows * HEADS * (pair_count + 1) * cluster,
-        ),
+        cost_estimate=SHORT,
         compiler_params=kernel_params(),
         name="attend_blocks",
     )(
@@ -334,15 +355,11 @@
     return lambda position: partner(route(position))
 
 
-OWN_PLAN = (
-    ((partner, itself),),
-    ((source, itself), (crossed(source), itself)),
-    ((opposite, itself), (crossed(opposite), itself)),
-)
-PASSED_PLAN = (
-    ((partner, source), (crossed(onward), source)),
-    ((onward, source),),
-)
+FIRST_PLAN = (((0, source, itself),), ((0, crossed(source), itself),))
+MIDDLE_PLAN = (((0, opposite, itself),), ((0, crossed(opposite), itself),))
+ON_PLAN = (((0, crossed(onward), source),),)
+BESIDE_PLAN = (((0, partner, itself), (1, partner, source)),)
+OUTWARD_PLAN = (((0, onward, source),),)
 
 
 def body(features, assignment, pairs, w_query, w_key, w_value, w_out, w_mix):
@@ -365,9 +382,14 @@
     first_moves = across_z(enumerate(OUT))
     second_moves = across_z(enumerate(FROM))
     middle_moves = across_z([(1, 2), (2, 1)])
+
+    def cross(moves):
+        return [(s, d ^ 1) for s, d in moves]
+
     outward_moves = across_z([(2, 3), (1, 0)])
 
-    raw = moved(features, first_moves)
+    rows = SUB * cluster
+    raw_head = moved(features[: HEAD_WALKERS * rows], first_moves)
     raw_assignment = moved(assignment, first_moves)
 
     listed = pairs.reshape(-1)
@@ -383,35 +405,45 @@
         tiled=True,
     )
     at_position = position.reshape(1)
-
-    walker_shape = (block_count // SUB, 1, SUB * cluster)
+    raw_tail = moved(tail_rows(features, rows, HEAD_WALKERS, (wanted, raw_head)), first_moves)
+
+    walker_shape = (block_count // SUB, 1, rows)
     block_shape = (block_count, cluster, width)
     normed, placed = place(features, assignment.reshape(walker_shape), 2)
     blocks = normed.reshape(block_shape)
-    near, second, middle = pick(at_position, wanted, blocks, OWN_PLAN)
-    near = moved(near, swap)
+    raw_assignment = raw_assignment.reshape(walker_shape)
+    (passed,) = place(raw_head, raw_assignment, 1)
+    second, second_cross = pick(at_position, wanted, (blocks,), FIRST_PLAN, after=(passed,))
     second = moved(second, second_moves)
-    middle = moved(middle, middle_moves)
-
-    (passed,) = place(raw, raw_assignment.reshape(walker_shape), 1)
-    passed = passed.reshape(block_shape)
-    beside, outward = pick(at_position, wanted, passed, PASSED_PLAN)
-    outward = moved(outward, outward_moves)
-    beside = moved(beside, swap)
-    second_beside = moved(second[capacity:], swap)
-    outward_beside = moved(beside[capacity:], outward_moves)
-    middle_beside = moved(middle[capacity:], swap)
+    second_cross = moved(second_cross, cross(second_moves))
 
     w_both = jnp.concatenate([w_key, w_value], axis=1)
-    pieces = [near, second, second_beside, beside, middle, outward, middle_beside, outward_beside]
-    own_at = len(pieces) * capacity
+    own_at = 8 * capacity
     passed_at = own_at + block_count
     total = passed_at + block_count
-    buffer = project_pairs(blocks, w_both, None, own_at, total, block_count)
+    buffer = project_pairs(blocks, w_both, None, own_at, total)
     queries = project_queries(normed, w_query, cluster)
-    buffer = project_pairs(passed, w_both, buffer, passed_at, total, block_count)
-    for at, piece in enumerate(pieces):
-        buffer = project_pairs(piece, w_both, buffer, at * capacity, total, capacity)
+
+    (passed,) = place(
+        raw_tail, raw_assignment, 1, first=HEAD_WALKERS, so_far=passed, after=(buffer, queries)
+    )
+    middle, middle_cross = pick(at_position, wanted, (blocks,), MIDDLE_PLAN, after=(raw_tail,))
+    middle = moved(middle, middle_moves)
+    middle_cross = moved(middle_cross, cross(middle_moves))
+    passed = passed.reshape(block_shape)
+    (on,) = pick(at_position, wanted, (passed,), ON_PLAN)
+    on = moved(on, swap)
+    (beside,) = pick(at_position, wanted, (blocks, passed), BESIDE_PLAN)
+    beside = moved(beside, swap)
+    (outward,) = pick(at_position, wanted, (passed,), OUTWARD_PLAN)
+    outward = moved(outward, outward_moves)
+    on = moved(on, outward_moves)
+
+    buffer = project_pairs(passed, w_both, buffer, passed_at, total)
+    at = 0
+    for piece in (second, second_cross, beside, outward, on, middle, middle_cross):
+        buffer = project_pairs(piece, w_both, buffer, at, total)
+        at += piece.shape[0]
 
     z, y = position // 2, position % 2
     is_end = (z == 0) | (z == LEVELS - 1)
@@ -420,14 +452,14 @@
     from_second = z_owner == choose(z, OUT)
     piece_of = jnp.where(
         z_owner == z,
-        0,
+        2,
         jnp.where(
             from_first,
             3,
             jnp.where(
                 from_second,
-                jnp.where(same, 1, 2),
-                jnp.where(is_end, jnp.where(same, 5, 7), jnp.where(same, 4, 6)),
+                jnp.where(same, 0, 1),
+                jnp.where(is_end, jnp.where(same, 4, 5), jnp.where(same, 6, 7)),
             ),
         ),
     )

time: 231 us -> 229 us (level)
  blocking collectives: 0 us -> 20 us
  waiting for transfers between devices: 87.2 us -> 77.4 us
  Pallas kernels: 114 us -> 105 us
    all_to_all x1 -> x0, waiting for transfers between devices: 32.5 us -> none  [body(): lax.all_to_all(jnp.broadcast_to(tables.reshape(1, -1), (SPAN, SPAN * capa...]
    ppermute x10 -> x11, waiting for transfers between devices: 54.8 us -> 77.4 us  [moved(): return lax.ppermute(x, 'elec', pairs_of)]
    all_to_all x0 -> x1, blocking collectives: none -> 20 us  [body(): lax.all_to_all(jnp.broadcast_to(tables.reshape(1, -1), (SPAN, SPAN * capa...]
    pallas_call x10 -> x9, Pallas kernels: 39.6 us -> 28.8 us  [project_pairs(): pl.pallas_call(key_value_kernel, grid=(blocks // per,), in_specs=in_specs...]
    all_to_all x1 -> x0, starting transfers between devices: 6.84 us -> none  [body(): lax.all_to_all(jnp.broadcast_to(tables.reshape(1, -1), (SPAN, SPAN * capa...]
    ppermute x10 -> x11, starting transfers between devices: 12.2 us -> 17.8 us  [moved(): return lax.ppermute(x, 'elec', pairs_of)]
    pallas_call x2 -> x5, Pallas kernels: 5.22 us -> 7.49 us  [pick(): pl.pallas_call(functools.partial(pick_kernel, plan=plan, capacity=capacit...]
    unnamed x34 -> x12, local copies, waits for them, and re-layouts: 4.56 us -> 5 us
  transfers between devices with their start and end apart: 11 -> 11, of which waited for: 3 -> 3; matrix products, arithmetic and copies ran while one was open for 3% -> 2% of each run, Pallas kernels for 26% -> 20%
where the time goes in v5:
time: 229 us; the launch traced here: 228 us
  Pallas kernels  105 us (46%)
  waiting for transfers between devices  77.4 us (34%)
  blocking collectives  20 us (9%)
  starting transfers between devices  17.8 us (8%)
  local copies, waits for them, and re-layouts  7.24 us (3%)
    ppermute x11, waiting for transfers between devices, moved(): return lax.ppermute(x, 'elec', pairs_of)  77.4 us
    pallas_call x1, Pallas kernels, attend(): pl.pallas_call(functools.partial(attend_kernel, pair_count=pair_count, he...  49.2 us
    pallas_call x9, Pallas kernels, project_pairs(): pl.pallas_call(key_value_kernel, grid=(blocks // per,), in_specs=in_specs...  28.8 us
    all_to_all x1, blocking collectives, body(): lax.all_to_all(jnp.broadcast_to(tables.reshape(1, -1), (SPAN, SPAN * capa...  20 us
    ppermute x11, starting transfers between devices, moved(): return lax.ppermute(x, 'elec', pairs_of)  17.8 us
    pallas_call x3, Pallas kernels, place(): pl.pallas_call(functools.partial(place_kernel, outputs=outputs), grid=(co...  10.9 us
    pallas_call x5, Pallas kernels, pick(): pl.pallas_call(functools.partial(pick_kernel, plan=plan, capacity=capacit...  7.49 us
    pallas_call x1, Pallas kernels, project_queries(): pl.pallas_call(functools.partial(query_kernel, cluster=cluster, head_widt...  6.48 us
  transfers between devices with their start and end apart: 11, of which 3 were waited for; matrix products, arithmetic and copies ran while one was open for 2% of the time, Pallas kernels for 20%

profile of v5, /device:TPU:8, one launch (start us, length us, event | category | flops | bytes accessed | tf_op | source)
XLA Modules:
  0.0 228.2 jit_solution(2222687777328824050)
XLA Ops:
  0.0 1.2 slice.3
  2.6 20.0 %all_to_all.8 = s32[8,1,200]{2,1,0:T(1,128)S(1)} all-to-all(s32[8,1,200]{2,1,0:T(1,128)S(1)} %broadcast_in_dim.67), channel_id=1, replica_groups={{0,2,4,6,8,10,12,14},{1,3,5,7,9,11,13,15},{16,18,20,22,24,26,28,30},{17..., dimensions={0} | all-to-all | bytes 12800 | tf_op jit(solution)/shard_map/all_to_all | solution.py:399
  22.6 1.6 copy-done
  24.2 2.2 tail_rows.1
  26.4 1.4 collective-permute-start.1
  27.8 1.6 collective-permute-start.4
  32.9 6.6 %place_rows.3 = (bf16[4096,256]{1,0:T(8,128)(2,1)S(1)}, bf16[4096,256]{1,0:T(8,128)(2,1)S(1)}) custom-call(bf16[4096,256]{1,0:T(8,128)(2,1)} %features_ref.3, s32[8,1,512]{2,1,0:T(1,128)S(1)} %bitcast.26), custom_call_target="tpu_custom_call" | custom-call | tf_op jit(solution)/shard_map/place_rows/pallas_call | solution.py:61
  39.5 6.5 %queries.1.rest_2_.query_ref = bf16[64,256,256]{2,1,0:T(8,128)(2,1)} custom-call(bf16[4096,256]{1,0:T(8,128)(2,1)S(1)} %get-tuple-element.11.normed_ref, bf16[256,256]{1,0:T(8,128)(2,1)S(1)} %bitcast.17), custom_call_target="tpu_custom_call" | custom-call | tf_op jit(solution)/shard_map/queries/pallas_call | solution.py:155
  46.0 4.7 %keys_values.9.rest_1_.rest_0_ = bf16[328,64,512]{2,1,0:T(8,128)(2,1)} custom-call(bf16[64,64,256]{2,1,0:T(8,128)(2,1)S(1)} %bitcast.13, bf16[256,512]{1,0:T(8,128)(2,1)S(1)} %constant_dynamic-update-slice_fusion.w_ref), custom_call_target="tpu_custom_call" | custom-call | tf_op jit(solution)/shard_map/keys_values/pallas_call | solution.py:198
  50.7 6.8 %collective-permute-done.4 = s32[4096]{0:T(1024)S(1)} collective-permute-done((s32[4096]{0:T(1024)}, s32[4096]{0:T(1024)S(1)}, u32[]{:S(2)}, u32[]{:S(2)}) %collective-permute-start.4) | collective-permute-done | bytes 16416 | tf_op jit(solution)/shard_map/ppermute | solution.py:376
  57.5 1.6 place_rows.4.rest_0_.rest_1_
  59.1 2.4 %pick_blocks.9 = (bf16[25,64,256]{2,1,0:T(8,128)(2,1)}, bf16[25,64,256]{2,1,0:T(8,128)(2,1)}) custom-call(s32[1]{0:T(128)} %bitcast.2.position_ref, s32[8,200]{1,0:T(8,128)S(1)} %bitcast.19, bf16[64,64,256]{2,1,0:T(8,128)(2,1)S(1)} %bitcast.14, bf16[4096,256]{1,0:T(8,128)(2,1)S(1)} %place_rows.4.rest_0_.rest_1_), custom_call_target="tpu_custom_call" | custom-call | tf_op jit(solution)/shard_map/pick_blocks/pallas_call | solution.py:128
  61.5 2.7 %place_rows.5 = bf16[4096,256]{1,0:T(8,128)(2,1)S(1)} custom-call(bf16[2560,256]{1,0:T(8,128)(2,1)S(1)} %collective-permute-done.1.rest_1_.features_ref, s32[8,1,512]{2,1,0:T(1,128)S(1)} %bitcast.25, bf16[4096,256]{1,0:T(8,128)(2,1)S(1)} %place_rows.4.rest_0_.rest_1_, ...), custom_call_target="tpu_custom_call", output_to_operand_aliasing={{}: (2, {})} | custom-call | tf_op jit(solution)/shard_map/place_rows/pallas_call | solution.py:61
  64.2 1.2 pick_blocks.8
  65.4 1.8 pick_blocks.6
  67.8 1.5 collective-permute-start.5
  70.5 1.8 collective-permute-start.10
  73.2 2.2 collective-permute-start.7
  76.6 61.7 %collective-permute-done.5 = bf16[25,64,256]{2,1,0:T(8,128)(2,1)} collective-permute-done((bf16[25,64,256]{2,1,0:T(8,128)(2,1)}, bf16[25,64,256]{2,1,0:T(8,128)(2,1)}, u32[]{:S(2)}, u32[]{:S(2)}) %collective-permute-start.5) | collective-permute-done | bytes 819232 | tf_op jit(solution)/shard_map/ppermute | solution.py:376
  138.2 1.9 collective-permute-start.6
  140.1 3.5 %collective-permute-start.3 = (bf16[25,64,256]{2,1,0:T(8,128)(2,1)S(1)}, bf16[25,64,256]{2,1,0:T(8,128)(2,1)S(1)}, u32[]{:S(2)}, u32[]{:S(2)}) collective-permute-start(bf16[25,64,256]{2,1,0:T(8,128)(2,1)S(1)} %get-tuple-element.13), channel_id=1, source_target_pairs={{4,8},{5,9},{6,10},{7,11},{8,4},{9,5},{10,6},{11,7},{20,24},{21,25... | collective-permute-start | bytes 2457608 | tf_op jit(solution)/shard_map/ppermute | solution.py:376
  143.6 2.3 %collective-permute-start.2 = (bf16[25,64,256]{2,1,0:T(8,128)(2,1)S(1)}, bf16[25,64,256]{2,1,0:T(8,128)(2,1)S(1)}, u32[]{:S(2)}, u32[]{:S(2)}) collective-permute-start(bf16[25,64,256]{2,1,0:T(8,128)(2,1)S(1)} %get-tuple-element.12), channel_id=1, source_target_pairs={{4,10},{5,11},{6,8},{7,9},{8,6},{9,7},{10,4},{11,5},{20,26},{21,27... | collective-permute-start | bytes 2457608 | tf_op jit(solution)/shard_map/ppermute | solution.py:376
  145.9 4.7 %keys_values.10.rest_0_ = bf16[328,64,512]{2,1,0:T(8,128)(2,1)} custom-call(bf16[64,64,256]{2,1,0:T(8,128)(2,1)S(1)} %bitcast.12, bf16[256,512]{1,0:T(8,128)(2,1)S(1)} %constant_dynamic-update-slice_fusion.w_ref, bf16[328,64,512]{2,1,0:T(8,128)(2,1)} %keys_values.9.rest_1_.rest_0_), custom_call_target="tpu_custom_call", output_to_operand_aliasing={{}: (2, {})} | custom-call | tf_op jit(solution)/shard_map/keys_values/pallas_call | solution.py:198
  150.6 2.4 %keys_values.11.rest_0_ = bf16[328,64,512]{2,1,0:T(8,128)(2,1)} custom-call(bf16[25,64,256]{2,1,0:T(8,128)(2,1)S(1)} %collective-permute-done.10.rows_ref, bf16[256,512]{1,0:T(8,128)(2,1)S(1)} %constant_dynamic-update-slice_fusion.w_ref, bf16[328,64,512]{2,1,0:T(8,128)(2,1)} %keys_values.10.rest_0_), custom_call_target="tpu_custom_call", output_to_operand_aliasing={{}: (2, {})} | custom-call | tf_op jit(solution)/shard_map/keys_values/pallas_call | solution.py:198
  153.1 2.4 %keys_values.12.rest_0_ = bf16[328,64,512]{2,1,0:T(8,128)(2,1)} custom-call(bf16[25,64,256]{2,1,0:T(8,128)(2,1)S(1)} %collective-permute-done.9.rows_ref, bf16[256,512]{1,0:T(8,128)(2,1)S(1)} %constant_dynamic-update-slice_fusion.w_ref, bf16[328,64,512]{2,1,0:T(8,128)(2,1)} %keys_values.11.rest_0_), custom_call_target="tpu_custom_call", output_to_operand_aliasing={{}: (2, {})} | custom-call | tf_op jit(solution)/shard_map/keys_values/pallas_call | solution.py:198
  155.5 4.9 %keys_values.13.rest_0_ = bf16[328,64,512]{2,1,0:T(8,128)(2,1)} custom-call(bf16[50,64,256]{2,1,0:T(8,128)(2,1)} %collective-permute-done.8.rows_ref, bf16[256,512]{1,0:T(8,128)(2,1)S(1)} %constant_dynamic-update-slice_fusion.w_ref, bf16[328,64,512]{2,1,0:T(8,128)(2,1)} %keys_values.12.rest_0_), custom_call_target="tpu_custom_call", output_to_operand_aliasing={{}: (2, {})} | custom-call | tf_op jit(solution)/shard_map/keys_values/pallas_call | solution.py:198
  160.3 2.4 %keys_values.14.rest_0_ = bf16[328,64,512]{2,1,0:T(8,128)(2,1)} custom-call(bf16[25,64,256]{2,1,0:T(8,128)(2,1)S(1)} %collective-permute-done.7.rows_ref, bf16[256,512]{1,0:T(8,128)(2,1)S(1)} %constant_dynamic-update-slice_fusion.w_ref, bf16[328,64,512]{2,1,0:T(8,128)(2,1)} %keys_values.13.rest_0_), custom_call_target="tpu_custom_call", output_to_operand_aliasing={{}: (2, {})} | custom-call | tf_op jit(solution)/shard_map/keys_values/pallas_call | solution.py:198
  162.7 2.5 %keys_values.15.rest_0_ = bf16[328,64,512]{2,1,0:T(8,128)(2,1)} custom-call(bf16[25,64,256]{2,1,0:T(8,128)(2,1)S(1)} %collective-permute-done.6.rows_ref, bf16[256,512]{1,0:T(8,128)(2,1)S(1)} %constant_dynamic-update-slice_fusion.w_ref, bf16[328,64,512]{2,1,0:T(8,128)(2,1)} %keys_values.14.rest_0_), custom_call_target="tpu_custom_call", output_to_operand_aliasing={{}: (2, {})} | custom-call | tf_op jit(solution)/shard_map/keys_values/pallas_call | solution.py:198
  165.2 2.4 %keys_values.16.rest_0_ = bf16[328,64,512]{2,1,0:T(8,128)(2,1)} custom-call(bf16[25,64,256]{2,1,0:T(8,128)(2,1)S(1)} %collective-permute-done.3.rows_ref, bf16[256,512]{1,0:T(8,128)(2,1)S(1)} %constant_dynamic-update-slice_fusion.w_ref, bf16[328,64,512]{2,1,0:T(8,128)(2,1)} %keys_values.15.rest_0_), custom_call_target="tpu_custom_call", output_to_operand_aliasing={{}: (2, {})} | custom-call | tf_op jit(solution)/shard_map/keys_values/pallas_call | solution.py:198
  167.6 8.9 %collective-permute-done.2.rows_ref = bf16[25,64,256]{2,1,0:T(8,128)(2,1)S(1)} collective-permute-done((bf16[25,64,256]{2,1,0:T(8,128)(2,1)S(1)}, bf16[25,64,256]{2,1,0:T(8,128)(2,1)S(1)}, u32[]{:S(2)}, u32[]{:S(2)}) %collective-permute-start.2) | collective-permute-done | bytes 819232 | tf_op jit(solution)/shard_map/ppermute | solution.py:376
  176.5 2.5 %keys_values.17.own_ref.rest_0_.rest_1_.rest_2_.rest_3_.rest_4_.rest_5_.rest_6_.rest_7_.rest_8_.rest_9_.rest_10_.rest_11_ = bf16[328,64,512]{2,1,0:T(8,128)(2,1)} custom-call(bf16[25,64,256]{2,1,0:T(8,128)(2,1)S(1)} %collective-permute-done.2.rows_ref, bf16[256,512]{1,0:T(8,128)(2,1)S(1)} %constant_dynamic-update-slice_fusion.w_ref, ...), custom_call_target="tpu_custom_call", output_to_operand_aliasing={{}: (2, {})} | custom-call | tf_op jit(solution)/shard_map/keys_values/pallas_call | solution.py:198
  178.9 49.2 %attend_blocks.1 = bf16[4096,256]{1,0:T(8,128)(2,1)} custom-call(s32[192]{0:T(256)S(1)} %get-tuple-element.18.table_ref, bf16[64,256,256]{2,1,0:T(8,128)(2,1)} %queries.1.rest_2_.query_ref, bf16[328,64,512]{2,1,0:T(8,128)(2,1)} %keys_values.17.own_ref.rest_0_.rest_1_.rest_2_.rest_3_.rest_4_.rest_5_.rest_6_.rest_7_.rest_8_.rest_9_.rest_10_.rest_11_, ...), custom_call_target="tpu_custom_call" | custom-call | tf_op jit(solution)/shard_map/attend_blocks/pallas_call | solution.py:286
  (31 shorter events, 8.7 us)
Async XLA Ops:
  1.2 21.5 %collective-permute-start = (bf16[1536,256]{1,0:T(8,128)(2,1)S(1)}, bf16[1536,256]{1,0:T(8,128)(2,1)S(1)}, u32[]{:S(2)}, u32[]{:S(2)}) collective-permute-start(bf16[1536,256]{1,0:T(8,128)(2,1)S(1)} %slice.3), channel_id=1, source_target_pairs={{0,8},{1,9},{2,10},{3,11},{4,0},{5,1},{6,2},{7,3},{8,12},{9,13},{1... | collective-permute-start | bytes 2359304 | tf_op jit(solution)/shard_map/ppermute | solution.py:376
  22.6 1.6 copy-start
  26.4 35.1 %collective-permute-start.1 = (bf16[2560,256]{1,0:T(8,128)(2,1)}, bf16[2560,256]{1,0:T(8,128)(2,1)S(1)}, u32[]{:S(2)}, u32[]{:S(2)}) collective-permute-start(bf16[2560,256]{1,0:T(8,128)(2,1)} %tail_rows.1), channel_id=1, source_target_pairs={{0,8},{1,9},{2,10},{3,11},{4,0},{5,1},{6,2},{7,3},{8,12},{9,13},{1... | collective-permute-start | bytes 3932168 | tf_op jit(solution)/shard_map/ppermute | solution.py:376
  27.8 29.7 %collective-permute-start.4 = (s32[4096]{0:T(1024)}, s32[4096]{0:T(1024)S(1)}, u32[]{:S(2)}, u32[]{:S(2)}) collective-permute-start(s32[4096]{0:T(1024)} %param.9), channel_id=1, source_target_pairs={{0,8},{1,9},{2,10},{3,11},{4,0},{5,1},{6,2},{7,3},{8,12},{9,13},{1... | collective-permute-start | bytes 49160 | tf_op jit(solution)/shard_map/ppermute | solution.py:376
  32.2 0.7 copy-start.3
  67.3 88.2 %collective-permute-start.8 = (bf16[50,64,256]{2,1,0:T(8,128)(2,1)S(1)}, bf16[50,64,256]{2,1,0:T(8,128)(2,1)}, u32[]{:S(2)}, u32[]{:S(2)}) collective-permute-start(bf16[50,64,256]{2,1,0:T(8,128)(2,1)S(1)} %pick_blocks.8), channel_id=1, source_target_pairs={{0,2},{1,3},{2,0},{3,1},{4,6},{5,7},{6,4},{7,5},{8,10},{9,11},{10,... | collective-permute-start | bytes 4915208 | tf_op jit(solution)/shard_map/ppermute | solution.py:376
  67.8 70.4 %collective-permute-start.5 = (bf16[25,64,256]{2,1,0:T(8,128)(2,1)}, bf16[25,64,256]{2,1,0:T(8,128)(2,1)}, u32[]{:S(2)}, u32[]{:S(2)}) collective-permute-start(bf16[25,64,256]{2,1,0:T(8,128)(2,1)} %pick_blocks.6), channel_id=1, source_target_pairs={{0,2},{1,3},{2,0},{3,1},{4,6},{5,7},{6,4},{7,5},{8,10},{9,11},{10,... | collective-permute-start | bytes 2457608 | tf_op jit(solution)/shard_map/ppermute | solution.py:376
  69.3 70.8 %collective-permute-start.9 = (bf16[25,64,256]{2,1,0:T(8,128)(2,1)}, bf16[25,64,256]{2,1,0:T(8,128)(2,1)S(1)}, u32[]{:S(2)}, u32[]{:S(2)}) collective-permute-start(bf16[25,64,256]{2,1,0:T(8,128)(2,1)} %get-tuple-element.14), channel_id=1, source_target_pairs={{0,6},{1,7},{2,4},{3,5},{4,14},{5,15},{6,12},{7,13},{8,2},{9,3},{1... | collective-permute-start | bytes 2457608 | tf_op jit(solution)/shard_map/ppermute | solution.py:376
  70.5 73.1 %collective-permute-start.10 = (bf16[25,64,256]{2,1,0:T(8,128)(2,1)}, bf16[25,64,256]{2,1,0:T(8,128)(2,1)S(1)}, u32[]{:S(2)}, u32[]{:S(2)}) collective-permute-start(bf16[25,64,256]{2,1,0:T(8,128)(2,1)} %get-tuple-element.15), channel_id=1, source_target_pairs={{0,4},{1,5},{2,6},{3,7},{4,12},{5,13},{6,14},{7,15},{8,0},{9,1},{1... | collective-permute-start | bytes 2457608 | tf_op jit(solution)/shard_map/ppermute | solution.py:376
  73.2 87.2 %collective-permute-start.7 = (bf16[25,64,256]{2,1,0:T(8,128)(2,1)S(1)}, bf16[25,64,256]{2,1,0:T(8,128)(2,1)S(1)}, u32[]{:S(2)}, u32[]{:S(2)}) collective-permute-start(bf16[25,64,256]{2,1,0:T(8,128)(2,1)S(1)} %pick_blocks.7), channel_id=1, source_target_pairs={{8,12},{9,13},{10,14},{11,15},{4,0},{5,1},{6,2},{7,3},{24,28},{25,... | collective-permute-start | bytes 2457608 | tf_op jit(solution)/shard_map/ppermute | solution.py:376
  138.2 24.5 %collective-permute-start.6 = (bf16[25,64,256]{2,1,0:T(8,128)(2,1)}, bf16[25,64,256]{2,1,0:T(8,128)(2,1)S(1)}, u32[]{:S(2)}, u32[]{:S(2)}) collective-permute-start(bf16[25,64,256]{2,1,0:T(8,128)(2,1)} %collective-permute-done.5), channel_id=1, source_target_pairs={{8,12},{9,13},{10,14},{11,15},{4,0},{5,1},{6,2},{7,3},{24,28},{25,... | collective-permute-start | bytes 2457608 | tf_op jit(solution)/shard_map/ppermute | solution.py:376
  140.1 25.1 %collective-permute-start.3 = (bf16[25,64,256]{2,1,0:T(8,128)(2,1)S(1)}, bf16[25,64,256]{2,1,0:T(8,128)(2,1)S(1)}, u32[]{:S(2)}, u32[]{:S(2)}) collective-permute-start(bf16[25,64,256]{2,1,0:T(8,128)(2,1)S(1)} %get-tuple-element.13), channel_id=1, source_target_pairs={{4,8},{5,9},{6,10},{7,11},{8,4},{9,5},{10,6},{11,7},{20,24},{21,25... | collective-permute-start | bytes 2457608 | tf_op jit(solution)/shard_map/ppermute | solution.py:376
  143.6 32.9 %collective-permute-start.2 = (bf16[25,64,256]{2,1,0:T(8,128)(2,1)S(1)}, bf16[25,64,256]{2,1,0:T(8,128)(2,1)S(1)}, u32[]{:S(2)}, u32[]{:S(2)}) collective-permute-start(bf16[25,64,256]{2,1,0:T(8,128)(2,1)S(1)} %get-tuple-element.12), channel_id=1, source_target_pairs={{4,10},{5,11},{6,8},{7,9},{8,6},{9,7},{10,4},{11,5},{20,26},{21,27... | collective-permute-start | bytes 2457608 | tf_op jit(solution)/shard_map/ppermute | solution.py:376
  167.6 11.4 %copy-start.1 = (bf16[256,256]{1,0:T(8,128)(2,1)S(1)}, bf16[256,256]{1,0:T(8,128)(2,1)}, u32[]{:S(2)}) copy-start(bf16[256,256]{1,0:T(8,128)(2,1)} %rest_13_.1) | copy-start | bytes 393220
  167.6 11.4 %copy-start.2 = (bf16[256,256]{1,0:T(8,128)(2,1)S(1)}, bf16[256,256]{1,0:T(8,128)(2,1)}, u32[]{:S(2)}) copy-start(bf16[256,256]{1,0:T(8,128)(2,1)} %rest_14_.1) | copy-start | bytes 393220

commit v6 on v5

v6 whole, which is shorter than its diff:
```python
import functools

import jax
import jax.numpy as jnp
from jax import lax
from jax.experimental import pallas as pl
from jax.experimental.pallas import tpu as pltpu
from jax.sharding import PartitionSpec as P

HEADS = 16
SPAN = 8
SUB = 8
GROUP = 4
STEP = 4
VMEM_BYTES = 48 * 1024 * 1024

NT = (((1,), (1,)), ((), ()))


def lasting(us):
    return pl.CostEstimate(flops=int(us * 1.15e9), bytes_accessed=0, transcendentals=0)


def kernel_params():
    return pltpu.CompilerParams(vmem_limit_bytes=VMEM_BYTES)


def layer_norm(rows):
    mean = jnp.mean(rows, axis=-1, keepdims=True)
    centred = rows - mean
    variance = jnp.mean(centred * centred, axis=-1, keepdims=True)
    return centred * lax.rsqrt(variance + 1e-05)


def head_mask(shape, head_width, cluster):
    row_head = lax.broadcasted_iota(jnp.int32, shape, 0) // head_width % GROUP
    lane_head = lax.broadcasted_iota(jnp.int32, shape, 1) // cluster
    return row_head == lane_head


def place_kernel(features_ref, assignment_ref, after_ref, placed_ref, normed_ref):
    rows = features_ref.shape[0]
    lane = 128
    features = features_ref[...]
    columns = lax.broadcasted_iota(jnp.int32, (lane, rows), 1)
    for part in range(rows // lane):
        chosen = assignment_ref[0, :, part * lane : (part + 1) * lane] & (rows - 1)
        chosen = jnp.broadcast_to(chosen, (lane, lane)).T
        chosen = jnp.concatenate([chosen] * (rows // lane), axis=1)
        one_hot = jnp.where(chosen == columns, 1.0, 0.0).astype(jnp.bfloat16)
        placed = jnp.dot(one_hot, features, preferred_element_type=jnp.float32)
        placed_ref[pl.ds(part * lane, lane), :] = placed.astype(jnp.bfloat16)
        normed_ref[pl.ds(part * lane, lane), :] = layer_norm(placed).astype(jnp.bfloat16)


def place(features, assignment, after):
    width = features.shape[1]
    walkers, _, rows = assignment.shape
    local = pl.BlockSpec((rows, width), lambda i: (i, 0))
    out = jax.ShapeDtypeStruct(features.shape, jnp.bfloat16)
    return pl.pallas_call(
        place_kernel,
        grid=(walkers,),
        in_specs=[
            local,
            pl.BlockSpec((1, 1, rows), lambda i: (i, 0, 0)),
            pl.BlockSpec(memory_space=pl.ANY),
        ],
        out_specs=[local] * 2,
        out_shape=[out, out],
        cost_estimate=lasting(7),
        compiler_params=kernel_params(),
        name="place_rows",
    )(features, assignment, after)


def choose(index, values):
    result = values[-1]
    for at in range(len(values) - 2, -1, -1):
        result = jnp.where(index == at, values[at], result)
    return result


def pick_kernel(position_ref, wanted_ref, *rest, plan, capacity):
    position = position_ref[0]
    for out_ref, pieces in zip(rest[len(rest) - len(plan) :], plan, strict=True):
        for at, (blocks, reader_of, owner_of) in enumerate(pieces):
            reader, first = reader_of(position), owner_of(position) * capacity

            def one_slot(slot, carry, out_ref=out_ref, at=at, blocks=blocks, reader=reader, first=first):
                out_ref[at * capacity + slot] = rest[blocks][wanted_ref[reader, first + slot]]
                return carry

            lax.fori_loop(0, capacity, one_slot, 0)


def pick(position, wanted, sources, plan, after=()):
    capacity = wanted.shape[1] // SPAN
    block = sources[0].shape[1:]
    outs = [
        jax.ShapeDtypeStruct((len(pieces) * capacity,) + block, sources[0].dtype)
        for pieces in plan
    ]
    smem = pl.BlockSpec(memory_space=pltpu.SMEM)
    vmem = pl.BlockSpec(memory_space=pltpu.VMEM)
    return pl.pallas_call(
        functools.partial(pick_kernel, plan=plan, capacity=capacity),
        in_specs=[smem, smem]
        + [vmem] * len(sources)
        + [pl.BlockSpec(memory_space=pl.ANY)] * len(after),
        out_specs=[vmem] * len(outs),
        out_shape=outs,
        cost_estimate=lasting(1.5),
        compiler_params=kernel_params(),
        name="pick_blocks",
    )(position, wanted, *sources, *after)


def query_kernel(normed_ref, query_w_ref, query_ref, *, cluster, head_width):
    width = normed_ref.shape[1]
    mask = head_mask((width, GROUP * cluster), head_width, cluster)
    for block in range(query_ref.shape[0]):
        own = normed_ref[pl.ds(block * cluster, cluster), :]
        own = jnp.concatenate([own] * GROUP, axis=0)
        query = lax.dot_general(query_w_ref[...], own, NT, preferred_element_type=jnp.float32)
        query = query.astype(jnp.bfloat16) * jnp.bfloat16(1.0 / head_width**0.5)
        query_ref[block] = jnp.where(mask, query, jnp.bfloat16(0.0))


def project_queries(normed, w_query, cluster):
    rows, width = normed.shape
    blocks = rows // cluster
    return pl.pallas_call(
        functools.partial(query_kernel, cluster=cluster, head_width=width // HEADS),
        grid=(blocks // SUB,),
        in_specs=[
            pl.BlockSpec((SUB * cluster, width), lambda i: (i, 0)),
            pl.BlockSpec((width, width), lambda i: (0, 0)),
        ],
        out_specs=pl.BlockSpec((SUB, width, GROUP * cluster), lambda i: (i, 0, 0)),
        out_shape=jax.ShapeDtypeStruct((blocks, width, GROUP * cluster), jnp.bfloat16),
        cost_estimate=lasting(6.5),
        compiler_params=kernel_params(),
        name="queries",
    )(normed, w_query.T)


def key_value_kernel(rows_ref, w_ref, *rest):
    out_ref = rest[-1]
    blocks, cluster, width = rows_ref.shape
    per = max(n for n in range(1, 9) if blocks % n == 0)

    def some(at, carry):
        here = pl.ds(at * per, per)
        rows = rows_ref[here].reshape(per * cluster, width)
        both = jnp.dot(rows, w_ref[...], preferred_element_type=jnp.float32)
        out_ref[here] = both.astype(jnp.bfloat16).reshape((per,) + out_ref.shape[1:])
        return carry

    lax.fori_loop(0, blocks // per, some, 0)


def project_pairs(piece, w_both, so_far, at, total):
    blocks, cluster, width = piece.shape
    per = max(n for n in range(1, 33) if blocks % n == 0 and at % n == 0)
    in_specs = [
        pl.BlockSpec((per, cluster, width), lambda i: (i, 0, 0)),
        pl.BlockSpec((width, 2 * width), lambda i: (0, 0)),
    ]
    operands = [piece, w_both]
    aliases = {}
    if so_far is not None:
        in_specs.append(pl.BlockSpec(memory_space=pl.ANY))
        operands.append(so_far)
        aliases = {2: 0}
    return pl.pallas_call(
        key_value_kernel,
        grid=(blocks // per,),
        in_specs=in_specs,
        out_specs=pl.BlockSpec((per, cluster, 2 * width), lambda i: (at // per + i, 0, 0)),
        out_shape=jax.ShapeDtypeStruct((total, cluster, 2 * width), jnp.bfloat16),
        input_output_aliases=aliases,
        cost_estimate=lasting(blocks / 12),
        compiler_params=kernel_params(),
        name="keys_values",
    )(*operands)


def attend_kernel(range_ref, order_ref, table_ref, *rest, pair_count, head_width):
    step = pl.program_id(0)
    count = range_ref[1]

    @pl.when(step < count)
    def _():
        attend_step(
            step, range_ref[0], count, order_ref, *rest, pair_count=pair_count, head_width=head_width
        )


def attend_step(step, begin, count, order_ref, *rest, pair_count, head_width):
    query_refs, rest = rest[:STEP], rest[STEP:]
    own_refs, rest = rest[:STEP], rest[STEP:]
    listed_refs, rest = rest[: STEP * pair_count], rest[STEP * pair_count :]
    placed_refs, rest = rest[:STEP], rest[STEP:]
    out_w_ref, mix_ref, *_, mixed_ref, done_ref, sems = rest
    cluster, width = placed_refs[0].shape
    span = GROUP * head_width
    tile = GROUP * cluster
    diagonal = head_mask((span, tile), head_width, cluster)
    fold_row = lax.broadcasted_iota(jnp.int32, (cluster, tile), 0)
    fold_lane = lax.broadcasted_iota(jnp.int32, (cluster, tile), 1) % cluster
    fold = jnp.where(fold_row == fold_lane, 1.0, 0.0).astype(jnp.bfloat16)
    zeros = jnp.zeros((span, tile), jnp.bfloat16)
    ones = jnp.ones((16, tile), jnp.bfloat16)
    tiles = HEADS // GROUP
    units = [(block, t) for block in range(STEP) for t in range(tiles)]
    keys, values = {}, {}

    def gather(block):
        members = [own_refs[block][0]]
        members += [listed_refs[block * pair_count + j][0] for j in range(pair_count)]
        keys[block] = jnp.concatenate([m[:, :width] for m in members], axis=0)
        values[block] = jnp.concatenate([m[:, width:] for m in members], axis=0).T

    def scores_of(block, t):
        if t == 0:
            gather(block)
        lo = t * span // 128 * 128
        picked = query_refs[block][0, t * span : (t + 1) * span, :]
        ahead, behind = t * span - lo, lo + 128 - (t + 1) * span
        stack = [zeros] * (ahead // span) + [picked] + [zeros] * (behind // span)
        return jnp.dot(
            keys[block][:, lo : lo + 128],
            jnp.concatenate(stack, axis=0),
            preferred_element_type=jnp.float32,
        )

    lead = 2
    scores = [scores_of(*unit) for unit in units[:lead]]
    attended, pieces = [], []
    for at, (block, t) in enumerate(units):
        if at + lead < len(units):
            scores.append(scores_of(*units[at + lead]))
        current = scores[at]
        top = jnp.max(current, axis=0, keepdims=True)
        weights = jnp.exp(current - top).astype(jnp.bfloat16)
        lifted = jnp.concatenate([values[block][t * span : (t + 1) * span], ones], axis=0)
        result = jnp.dot(lifted, weights, preferred_element_type=jnp.float32)
        result = result[:span] * (1.0 / result[span : span + 1])
        pieces.append(jnp.where(diagonal, result, 0.0).astype(jnp.bfloat16))
        if t == tiles - 1:
            stacked = jnp.concatenate(pieces, axis=0)
            folded = lax.dot_general(fold, stacked, NT, preferred_element_type=jnp.float32)
            attended.append(folded.astype(jnp.bfloat16))
            pieces = []
    placed = jnp.concatenate([ref[...] for ref in placed_refs], axis=0)
    middle = placed.astype(jnp.float32) + jnp.dot(
        jnp.concatenate(attended, axis=0), out_w_ref[...], preferred_element_type=jnp.float32
    )
    middle = middle.astype(jnp.bfloat16).astype(jnp.float32)
    second = layer_norm(middle).astype(jnp.bfloat16)
    mixed = middle + jnp.tanh(jnp.dot(second, mix_ref[...], preferred_element_type=jnp.float32))

    def copies(of_step):
        for block in range(STEP):
            row = order_ref[(begin + of_step) * STEP + block] * cluster
            yield pltpu.make_async_copy(
                done_ref.at[pl.ds(block * cluster, cluster), :],
                mixed_ref.at[pl.ds(pl.multiple_of(row, cluster), cluster), :],
                sems.at[block],
            )

    @pl.when(step > 0)
    def _():
        for copy in copies(step - 1):
            copy.wait()

    done_ref[...] = mixed.astype(jnp.bfloat16)
    for copy in copies(step):
        copy.start()

    @pl.when(step == count - 1)
    def _():
        for copy in copies(step):
            copy.wait()


def attend(begin, count, order, table, queries, buffer, own_at, placed, w_out, w_mix, so_far=None):
    rows, width = placed.shape
    blocks, _, tile = queries.shape
    cluster = rows // blocks
    pair_count = table.shape[0] // blocks
    whole = pl.BlockSpec((width, width), lambda i, f, o, t: (0, 0))

    def reader(i, j, f, o):
        step = f[0] + jnp.minimum(i, jnp.maximum(f[1] - 1, 0))
        return o[step * STEP + j]

    def listed(j, n):
        return pl.BlockSpec(
            (1, cluster, 2 * width),
            lambda i, f, o, t: (t[reader(i, j, f, o) * pair_count + n], 0, 0),
        )

    each = range(STEP)
    in_specs = [
        pl.BlockSpec((1, width, tile), lambda i, f, o, t, j=j: (reader(i, j, f, o), 0, 0))
        for j in each
    ]
    in_specs += [
        pl.BlockSpec(
            (1, cluster, 2 * width), lambda i, f, o, t, j=j: (own_at + reader(i, j, f, o), 0, 0)
        )
        for j in each
    ]
    in_specs += [listed(j, n) for j in each for n in range(pair_count)]
    in_specs += [
        pl.BlockSpec((cluster, width), lambda i, f, o, t, j=j: (reader(i, j, f, o), 0)) for j in each
    ]
    in_specs += [whole, whole]
    operands = [queries] * STEP + [buffer] * (STEP + STEP * pair_count) + [placed] * STEP
    operands += [w_out, w_mix]
    aliases = {}
    if so_far is not None:
        aliases = {3 + len(operands): 0}
        in_specs.append(pl.BlockSpec(memory_space=pl.ANY))
        operands.append(so_far)
    return pl.pallas_call(
        functools.partial(attend_kernel, pair_count=pair_count, head_width=width // HEADS),
        grid_spec=pltpu.PrefetchScalarGridSpec(
            num_scalar_prefetch=3,
            grid=(blocks // STEP,),
            in_specs=in_specs,
            out_specs=pl.BlockSpec(memory_space=pl.ANY),
            scratch_shapes=[
                pltpu.VMEM((STEP * cluster, width), jnp.bfloat16),
                pltpu.SemaphoreType.DMA((STEP,)),
            ],
        ),
        out_shape=jax.ShapeDtypeStruct((rows, width), jnp.bfloat16),
        input_output_aliases=aliases,
        cost_estimate=lasting(25),
        compiler_params=kernel_params(),
        name="attend_blocks",
    )(jnp.stack([begin, count]).astype(jnp.int32), order, table, *operands)


def slot_tables(owner, within, capacity):
    readers, entries = owner.shape
    alike = owner[:, :, None] == owner[:, None, :]
    earlier = jnp.arange(entries)[None, :] < jnp.arange(entries)[:, None]
    ranking = jnp.sum(jnp.where(alike & earlier, 1, 0), axis=2).astype(jnp.int32)
    slots = owner * capacity + ranking
    every = jnp.arange(SPAN * capacity, dtype=jnp.int32)
    matches = slots[:, None, :] == every[None, :, None]
    return ranking, jnp.sum(jnp.where(matches, within[:, None, :], 0), axis=2).astype(jnp.int32)


def early_first(early):
    count = jnp.sum(early.astype(jnp.int32))
    blocks = jnp.arange(early.shape[0], dtype=jnp.int32)
    before = blocks[None, :] < blocks[:, None]
    ahead = jnp.sum(jnp.where(before & (early[None, :] == early[:, None]), 1, 0), axis=1)
    place_ = jnp.where(early, ahead, count + ahead)
    order = jnp.sum(jnp.where(place_[None, :] == blocks[:, None], blocks[None, :], 0), axis=1)
    return order.astype(jnp.int32), count


OUT = (2, 0, 3, 1)
FROM = (1, 3, 0, 2)
LEVELS = 4


def position_at(z, y):
    return 2 * z + y


def partner(position):
    return position ^ 1


def onward(position):
    return position_at(choose(position // 2, OUT), position % 2)


def source(position):
    return position_at(choose(position // 2, FROM), position % 2)


def opposite(position):
    return position_at(LEVELS - 1 - position // 2, position % 2)


def itself(position):
    return position


def crossed(route):
    return lambda position: partner(route(position))


SECOND_PLAN = (((0, source, itself), (1, source, partner)),)
MIDDLE_PLAN = (((0, opposite, itself), (1, opposite, partner)),)
PASSED_PLAN = (((0, crossed(onward), source),), ((0, partner, source),), ((0, onward, source),))


def body(features, assignment, pairs, w_query, w_key, w_value, w_out, w_mix):
    rows_dev, width = features.shape
    block_count, pair_count = pairs.shape
    cluster = rows_dev // block_count
    stride = lax.axis_size("elec") // SPAN
    groups = [[rest + place_ * stride for place_ in range(SPAN)] for rest in range(stride)]
    position = lax.axis_index("elec") // stride
    at_position = position.reshape(1)
    capacity = (block_count * pair_count + SPAN - 1) // SPAN + 1

    def moved(x, moves):
        pairs_of = [(s * stride + r, d * stride + r) for s, d in moves for r in range(stride)]
        return lax.ppermute(x, "elec", pairs_of)

    def across_z(pairs_of_z):
        return [(position_at(s, y), position_at(d, y)) for s, d in pairs_of_z for y in range(2)]

    swap = [(p, p ^ 1) for p in range(SPAN)]
    first_moves = across_z(enumerate(OUT))
    second_moves = across_z(enumerate(FROM))
    middle_moves = across_z([(1, 2), (2, 1)])
    outward_moves = across_z([(2, 3), (1, 0)])

    all_pairs = lax.all_to_all(
        jnp.broadcast_to(pairs.reshape(1, -1), (SPAN, block_count * pair_count)),
        "elec",
        split_axis=0,
        concat_axis=0,
        axis_index_groups=groups,
        tiled=True,
    )
    shape = (block_count // SUB, 1, SUB * cluster)
    placed, normed = place(features, assignment.reshape(shape), all_pairs)
    blocks = normed.reshape(block_count, cluster, width)
    passed = moved(blocks, first_moves)
    beside = moved(blocks, swap)

    w_both = jnp.concatenate([w_key, w_value], axis=1)
    own_at = 8 * capacity
    passed_at = own_at + block_count
    beside_at = passed_at + block_count
    total = beside_at + block_count
    buffer = project_pairs(blocks, w_both, None, own_at, total)
    queries = project_queries(normed, w_query, cluster)
    _, wanted = slot_tables(
        all_pairs // block_count // stride, all_pairs % block_count, capacity
    )

    (second,) = pick(at_position, wanted, (blocks, beside), SECOND_PLAN)
    second = moved(second, second_moves)
    on, near, outward = pick(at_position, wanted, (passed,), PASSED_PLAN)
    on = moved(on, swap)
    near = moved(near, swap)
    outward = moved(outward, outward_moves)
    (middle,) = pick(at_position, wanted, (blocks, beside), MIDDLE_PLAN, after=(on,))
    on = moved(on, outward_moves)
    middle = moved(middle, middle_moves)

    buffer = project_pairs(beside, w_both, buffer, beside_at, total)
    buffer = project_pairs(passed, w_both, buffer, passed_at, total)
    buffer = project_pairs(near, w_both, buffer, 0, total)
    buffer = project_pairs(second, w_both, buffer, capacity, total)

    listed = pairs.reshape(-1)
    owner = listed // block_count // stride
    within = listed % block_count
    (ranking,), _ = slot_tables(owner[None], within[None], capacity)
    z, y = position // 2, position % 2
    is_end = (z == 0) | (z == LEVELS - 1)
    z_owner, same = owner // 2, owner % 2 == y
    from_first = z_owner == choose(z, FROM)
    late = z_owner == LEVELS - 1 - z
    piece_of = jnp.where(
        from_first,
        0,
        jnp.where(
            late,
            jnp.where(is_end, jnp.where(same, 3, 4), jnp.where(same, 5, 6)),
            jnp.where(same, 1, 2),
        ),
    )
    whole_at = jnp.where(z_owner == z, jnp.where(same, own_at, beside_at), passed_at)
    whole = (z_owner == z) | (from_first & same)
    table = jnp.where(whole, whole_at + within, piece_of * capacity + ranking)

    early = ~jnp.any(late.reshape(block_count, pair_count), axis=1)
    order, early_count = early_first(early)
    steps = block_count // STEP
    early_steps = jnp.minimum(early_count // STEP, steps - 1)
    shared = (order, table, queries)
    rest = (own_at, placed, w_out, w_mix)
    mixed = attend(jnp.zeros_like(early_steps), early_steps, *shared, buffer, *rest)
    for piece, at in ((outward, 3), (on, 4), (middle, 5)):
        buffer = project_pairs(piece, w_both, buffer, at * capacity, total)
    return attend(early_steps, steps - early_steps, *shared, buffer, *rest, so_far=mixed)


def solution(mesh):
    placed = (
        P(("groups", "elec"), None),
        P(("groups", "elec")),
        P(("groups", "elec"), None),
        P(),
        P(),
        P(),
        P(),
        P(),
    )
    return jax.shard_map(
        body, mesh=mesh, in_specs=placed, out_specs=P(("groups", "elec"), None), check_vma=False
    )
```

time: 229 us -> 204 us (0.89)
  waiting for transfers between devices: 77.4 us -> 45.8 us
  Pallas kernels: 105 us -> 126 us
  blocking collectives: 20 us -> 0 us
  local copies, waits for them, and re-layouts: 7.24 us -> 3.26 us
  other arithmetic: 0.37 us -> 4.09 us
  between operations: 0.24 us -> 2.95 us
    ppermute x11 -> x8, waiting for transfers between devices: 77.4 us -> 45.8 us  [moved(): return lax.ppermute(x, 'elec', pairs_of)]
    all_to_all x1 -> x0, blocking collectives: 20 us -> none  [body(): lax.all_to_all(jnp.broadcast_to(tables.reshape(1, -1), (SPAN, SPAN * capa...]
    pallas_call x1 -> x2, Pallas kernels: 49.2 us -> 61.1 us  [attend(): pl.pallas_call(functools.partial(attend_kernel, pair_count=pair_count, he...]
    pallas_call x9 -> x8, Pallas kernels: 28.8 us -> 39.2 us  [project_pairs(): pl.pallas_call(key_value_kernel, grid=(blocks // per,), in_specs=in_specs...]
    all_to_all x0 -> x1, starting transfers between devices: none -> 6.28 us  [body(): lax.all_to_all(jnp.broadcast_to(pairs.reshape(1, -1), (SPAN, block_count...]
    pallas_call x4 -> x1, Pallas kernels: 13.1 us -> 7.68 us  [place(): pl.pallas_call(place_kernel, grid=(walkers,), in_specs=[local, pl.BlockSp...]
    ppermute x11 -> x8, starting transfers between devices: 17.8 us -> 13.3 us  [moved(): return lax.ppermute(x, 'elec', pairs_of)]
    unnamed x12 -> x13, local copies, waits for them, and re-layouts: 5 us -> 2.51 us
  transfers between devices with their start and end apart: 11 -> 9, of which waited for: 3 -> 2; matrix products, arithmetic and copies ran while one was open for 2% -> 2% of each run, Pallas kernels for 20% -> 39%
where the time goes in v6:
time: 204 us; the launch traced here: 202 us
  Pallas kernels  126 us (62%)
  waiting for transfers between devices  45.8 us (22%)
  starting transfers between devices  19.5 us (10%)
  other arithmetic  4.09 us (2%)
  local copies, waits for them, and re-layouts  3.26 us (2%)
  between operations  2.95 us (1%)
    pallas_call x2, Pallas kernels, attend(): pl.pallas_call(functools.partial(attend_kernel, pair_count=pair_count, he...  61.1 us
    ppermute x8, waiting for transfers between devices, moved(): return lax.ppermute(x, 'elec', pairs_of)  45.8 us
    pallas_call x8, Pallas kernels, project_pairs(): pl.pallas_call(key_value_kernel, grid=(blocks // per,), in_specs=in_specs...  39.2 us
    ppermute x8, starting transfers between devices, moved(): return lax.ppermute(x, 'elec', pairs_of)  13.3 us
    pallas_call x3, Pallas kernels, pick(): pl.pallas_call(functools.partial(pick_kernel, plan=plan, capacity=capacit...  9.95 us
    pallas_call x1, Pallas kernels, project_queries(): pl.pallas_call(functools.partial(query_kernel, cluster=cluster, head_widt...  8.33 us
    pallas_call x1, Pallas kernels, place(): pl.pallas_call(place_kernel, grid=(walkers,), in_specs=[local, pl.BlockSp...  7.68 us
    all_to_all x1, starting transfers between devices, body(): lax.all_to_all(jnp.broadcast_to(pairs.reshape(1, -1), (SPAN, block_count...  6.28 us
  transfers between devices with their start and end apart: 9, of which 2 were waited for; matrix products, arithmetic and copies ran while one was open for 2% of the time, Pallas kernels for 39%

profile of v6, /device:TPU:8, one launch (start us, length us, event | category | flops | bytes accessed | tf_op | source)
XLA Modules:
  0.0 201.9 jit_solution(15057533812826978855)
XLA Ops:
  0.0 0.8 copy.22
  1.5 6.3 %all-to-all-start = ((s32[8,1,192]{2,1,0:T(1,128)}), s32[8,1,192]{2,1,0:T(1,128)S(1)}, u32[]{:S(2)}, u32[]{:S(2)}) async-start(s32[8,1,192]{2,1,0:T(1,128)} %broadcast_in_dim.105), calls=%async_computation | async-start | bytes 16384 | tf_op jit(solution)/shard_map/all_to_all | solution.py:430
  7.8 0.7 fusion.19
  8.6 0.7 convert_reduce_fusion
  9.3 0.9 constant_dynamic-update-slice_fusion.1
  10.4 0.7 add_select_fusion.8
  13.9 0.7 select_reduce_fusion.1
  14.7 0.7 copy-done.2
  15.4 7.7 %place_rows.1 = (bf16[4096,256]{1,0:T(8,128)(2,1)S(1)}, bf16[4096,256]{1,0:T(8,128)(2,1)}) custom-call(bf16[4096,256]{1,0:T(8,128)(2,1)} %features_ref.1, s32[8,1,512]{2,1,0:T(1,128)S(1)} %bitcast.21, s32[8,192]{1,0:T(8,128)S(1)} %get-tuple-element.17.after_ref), custom_call_target="tpu_custom_call" | custom-call | flops 8049999872 | tf_op jit(solution)/shard_map/place_rows/pallas_call | solution.py:61
  23.1 1.5 collective-permute-start
  24.6 0.6 collective-permute-start.1
  26.3 7.1 %keys_values.8.rest_0_ = bf16[392,64,512]{2,1,0:T(8,128)(2,1)} custom-call(bf16[64,64,256]{2,1,0:T(8,128)(2,1)} %bitcast.9.rest_0_.rows_ref, bf16[256,512]{1,0:T(8,128)(2,1)S(1)} %constant_dynamic-update-slice_fusion.w_ref), custom_call_target="tpu_custom_call" | custom-call | flops 6133333504 | tf_op jit(solution)/shard_map/keys_values/pallas_call | solution.py:176
  33.4 8.3 %queries.1.rest_0_.rest_1_.rest_2_.rest_3_ = bf16[64,256,256]{2,1,0:T(8,128)(2,1)} custom-call(bf16[4096,256]{1,0:T(8,128)(2,1)} %get-tuple-element.10.normed_ref, bf16[256,256]{1,0:T(8,128)(2,1)S(1)} %bitcast.20), custom_call_target="tpu_custom_call" | custom-call | flops 7474999808 | tf_op jit(solution)/shard_map/queries/pallas_call | solution.py:133
  41.7 28.5 %collective-permute-done.rest_1_.rows_ref = bf16[64,64,256]{2,1,0:T(8,128)(2,1)} collective-permute-done((bf16[64,64,256]{2,1,0:T(8,128)(2,1)}, bf16[64,64,256]{2,1,0:T(8,128)(2,1)}, u32[]{:S(2)}, u32[]{:S(2)}) %collective-permute-start) | collective-permute-done | bytes 2097184 | tf_op jit(solution)/shard_map/ppermute | solution.py:419
  70.2 2.7 %pick_blocks.5 = bf16[50,64,256]{2,1,0:T(8,128)(2,1)S(1)} custom-call(s32[1]{0:T(128)} %bitcast.4.position_ref, s32[8,200]{1,0:T(8,128)S(1)} %select_reduce_fusion.wanted_ref, bf16[64,64,256]{2,1,0:T(8,128)(2,1)} %bitcast.9.rest_0_.rows_ref, bf16[64,64,256]{2,1,0:T(8,128)(2,1)} %collective-permute-done.rest_1_.rows_ref), custom_call_target="tpu_custom_call" | custom-call | flops 1724999936 | tf_op jit(solution)/shard_map/pick_blocks/pallas_call | solution.py:106
  72.9 2.4 %collective-permute-start.6 = (bf16[50,64,256]{2,1,0:T(8,128)(2,1)S(1)}, bf16[50,64,256]{2,1,0:T(8,128)(2,1)S(1)}, u32[]{:S(2)}, u32[]{:S(2)}) collective-permute-start(bf16[50,64,256]{2,1,0:T(8,128)(2,1)S(1)} %pick_blocks.5), channel_id=1, source_target_pairs={{0,4},{1,5},{2,6},{3,7},{4,12},{5,13},{6,14},{7,15},{8,0},{9,1},{1... | collective-permute-start | bytes 4915208 | tf_op jit(solution)/shard_map/ppermute | solution.py:419
  75.4 3.3 %pick_blocks.3 = (bf16[25,64,256]{2,1,0:T(8,128)(2,1)S(1)}, bf16[25,64,256]{2,1,0:T(8,128)(2,1)S(1)}, bf16[25,64,256]{2,1,0:T(8,128)(2,1)}) custom-call(s32[1]{0:T(128)} %bitcast.4.position_ref, s32[8,200]{1,0:T(8,128)S(1)} %select_reduce_fusion.wanted_ref, bf16[64,64,256]{2,1,0:T(8,128)(2,1)} %collective-permute-done.1.rest_0_.rows_ref), custom_call_target="tpu_custom_call" | custom-call | flops 1724999936 | tf_op jit(solution)/shard_map/pick_blocks/pallas_call | solution.py:106
  78.7 1.5 collective-permute-start.7
  80.1 2.4 %collective-permute-start.5 = (bf16[25,64,256]{2,1,0:T(8,128)(2,1)}, bf16[25,64,256]{2,1,0:T(8,128)(2,1)}, u32[]{:S(2)}, u32[]{:S(2)}) collective-permute-start(bf16[25,64,256]{2,1,0:T(8,128)(2,1)} %get-tuple-element.12), channel_id=1, source_target_pairs={{8,12},{9,13},{10,14},{11,15},{4,0},{5,1},{6,2},{7,3},{24,28},{25,... | collective-permute-start | bytes 2457608 | tf_op jit(solution)/shard_map/ppermute | solution.py:419
  83.1 7.1 %keys_values.9.rest_0_ = bf16[392,64,512]{2,1,0:T(8,128)(2,1)} custom-call(bf16[64,64,256]{2,1,0:T(8,128)(2,1)} %collective-permute-done.rest_1_.rows_ref, bf16[256,512]{1,0:T(8,128)(2,1)S(1)} %constant_dynamic-update-slice_fusion.w_ref, bf16[392,64,512]{2,1,0:T(8,128)(2,1)} %keys_values.8.rest_0_), custom_call_target="tpu_custom_call", output_to_operand_aliasing={{}: (2, {})} | custom-call | flops 6133333504 | tf_op jit(solution)/shard_map/keys_values/pallas_call | solution.py:176
  90.2 7.0 %keys_values.10.rest_0_ = bf16[392,64,512]{2,1,0:T(8,128)(2,1)} custom-call(bf16[64,64,256]{2,1,0:T(8,128)(2,1)} %collective-permute-done.1.rest_0_.rows_ref, bf16[256,512]{1,0:T(8,128)(2,1)S(1)} %constant_dynamic-update-slice_fusion.w_ref, bf16[392,64,512]{2,1,0:T(8,128)(2,1)} %keys_values.9.rest_0_), custom_call_target="tpu_custom_call", output_to_operand_aliasing={{}: (2, {})} | custom-call | flops 6133333504 | tf_op jit(solution)/shard_map/keys_values/pallas_call | solution.py:176
  97.3 17.3 %collective-permute-done.2.rest_2_ = bf16[25,64,256]{2,1,0:T(8,128)(2,1)} collective-permute-done((bf16[25,64,256]{2,1,0:T(8,128)(2,1)S(1)}, bf16[25,64,256]{2,1,0:T(8,128)(2,1)}, u32[]{:S(2)}, u32[]{:S(2)}) %collective-permute-start.2) | collective-permute-done | bytes 819232 | tf_op jit(solution)/shard_map/ppermute | solution.py:419
  114.5 3.9 %pick_blocks.4 = bf16[50,64,256]{2,1,0:T(8,128)(2,1)} custom-call(s32[1]{0:T(128)} %bitcast.4.position_ref, s32[8,200]{1,0:T(8,128)S(1)} %select_reduce_fusion.wanted_ref, bf16[64,64,256]{2,1,0:T(8,128)(2,1)} %bitcast.9.rest_0_.rows_ref, bf16[64,64,256]{2,1,0:T(8,128)(2,1)} %collective-permute-done.rest_1_.rows_ref, ...), custom_call_target="tpu_custom_call" | custom-call | flops 1724999936 | tf_op jit(solution)/shard_map/pick_blocks/pallas_call | solution.py:106
  118.5 1.9 collective-permute-start.3
  120.4 2.4 %collective-permute-start.4 = (bf16[25,64,256]{2,1,0:T(8,128)(2,1)}, bf16[25,64,256]{2,1,0:T(8,128)(2,1)}, u32[]{:S(2)}, u32[]{:S(2)}) collective-permute-start(bf16[25,64,256]{2,1,0:T(8,128)(2,1)} %collective-permute-done.2.rest_2_), channel_id=1, source_target_pairs={{8,12},{9,13},{10,14},{11,15},{4,0},{5,1},{6,2},{7,3},{24,28},{25,... | collective-permute-start | bytes 2457608 | tf_op jit(solution)/shard_map/ppermute | solution.py:419
  122.8 2.4 %keys_values.11.rest_0_ = bf16[392,64,512]{2,1,0:T(8,128)(2,1)} custom-call(bf16[25,64,256]{2,1,0:T(8,128)(2,1)S(1)} %collective-permute-done.7.rows_ref, bf16[256,512]{1,0:T(8,128)(2,1)S(1)} %constant_dynamic-update-slice_fusion.w_ref, bf16[392,64,512]{2,1,0:T(8,128)(2,1)} %keys_values.10.rest_0_), custom_call_target="tpu_custom_call", output_to_operand_aliasing={{}: (2, {})} | custom-call | flops 2395833344 | tf_op jit(solution)/shard_map/keys_values/pallas_call | solution.py:176
  125.2 3.7 %keys_values.12.rest_0_.rest_4_.rest_5_.rest_6_.rest_7_.rest_8_.rest_9_.rest_10_.rest_11_.rest_12_.rest_13_.rest_14_.rest_15_.rest_16_.rest_17_.rest_18_.rest_19_ = bf16[392,64,512]{2,1,0:T(8,128)(2,1)} custom-call(bf16[50,64,256]{2,1,0:T(8,128)(2,1)S(1)} %collective-permute-done.6.rows_ref, ...), custom_call_target="tpu_custom_call", output_to_operand_aliasing={{}: (2, {})} | custom-call | flops 4791666688 | tf_op jit(solution)/shard_map/keys_values/pallas_call | solution.py:176
  128.9 25.2 %attend_blocks.2.rest_26_ = bf16[4096,256]{1,0:T(8,128)(2,1)} custom-call(s32[2]{0:T(128)S(1)} %get-tuple-element.19.range_ref, s32[64]{0:T(128)S(1)} %select_reduce_fusion.3.order_ref, s32[192]{0:T(256)S(1)} %or_select_fusion.table_ref, bf16[64,256,256]{2,1,0:T(8,128)(2,1)} %queries.1.rest_0_.rest_1_.rest_2_.rest_3_, ...), custom_call_target="tpu_custom_call" | custom-call | flops 28750000128 | tf_op jit(solution)/shard_map/attend_blocks/pallas_call | solution.py:328
  154.1 3.6 %keys_values.13.rest_0_ = bf16[392,64,512]{2,1,0:T(8,128)(2,1)} custom-call(bf16[25,64,256]{2,1,0:T(8,128)(2,1)} %collective-permute-done.5.rows_ref, bf16[256,512]{1,0:T(8,128)(2,1)S(1)} %constant_dynamic-update-slice_fusion.w_ref, ...), custom_call_target="tpu_custom_call", output_to_operand_aliasing={{}: (2, {})} | custom-call | flops 2395833344 | tf_op jit(solution)/shard_map/keys_values/pallas_call | solution.py:176
  157.7 3.5 %keys_values.14.rest_0_ = bf16[392,64,512]{2,1,0:T(8,128)(2,1)} custom-call(bf16[25,64,256]{2,1,0:T(8,128)(2,1)} %collective-permute-done.4.rows_ref, bf16[256,512]{1,0:T(8,128)(2,1)S(1)} %constant_dynamic-update-slice_fusion.w_ref, bf16[392,64,512]{2,1,0:T(8,128)(2,1)} %keys_values.13.rest_0_), custom_call_target="tpu_custom_call", output_to_operand_aliasing={{}: (2, {})} | custom-call | flops 2395833344 | tf_op jit(solution)/shard_map/keys_values/pallas_call | solution.py:176
  161.2 4.8 %keys_values.15.rest_4_.rest_5_.rest_6_.rest_7_.rest_8_.rest_9_.rest_10_.rest_11_.rest_12_.rest_13_.rest_14_.rest_15_.rest_16_.rest_17_.rest_18_.rest_19_ = bf16[392,64,512]{2,1,0:T(8,128)(2,1)} custom-call(bf16[50,64,256]{2,1,0:T(8,128)(2,1)} %collective-permute-done.3.rows_ref, ...), custom_call_target="tpu_custom_call", output_to_operand_aliasing={{}: (2, {})} | custom-call | flops 4791666688 | tf_op jit(solution)/shard_map/keys_values/pallas_call | solution.py:176
  166.0 35.9 %attend_blocks.3 = bf16[4096,256]{1,0:T(8,128)(2,1)} custom-call(s32[2]{0:T(128)S(1)} %get-tuple-element.18.range_ref, s32[64]{0:T(128)S(1)} %select_reduce_fusion.3.order_ref, s32[192]{0:T(256)S(1)} %or_select_fusion.table_ref, bf16[64,256,256]{2,1,0:T(8,128)(2,1)} %queries.1.rest_0_.rest_1_.rest_2_.rest_3_, ...), custom_call_target="tpu_custom_call", output_to_operand_aliasing={{}: (29, {})} | custom-call | flops 28750000128 | tf_op jit(solution)/shard_map/attend_blocks/pallas_call | solution.py:328
  (33 shorter events, 2.7 us)
Async XLA Ops:
  1.5 12.4 %all-to-all-start = ((s32[8,1,192]{2,1,0:T(1,128)}), s32[8,1,192]{2,1,0:T(1,128)S(1)}, u32[]{:S(2)}, u32[]{:S(2)}) async-start(s32[8,1,192]{2,1,0:T(1,128)} %broadcast_in_dim.105), calls=%async_computation | async-start | bytes 16384 | tf_op jit(solution)/shard_map/all_to_all | solution.py:430
  14.7 0.7 copy-start.2
  15.4 10.0 %copy-start.3 = (bf16[256,256]{1,0:T(8,128)(2,1)S(1)}, bf16[256,256]{1,0:T(8,128)(2,1)}, u32[]{:S(2)}) copy-start(bf16[256,256]{1,0:T(8,128)(2,1)} %param.11) | copy-start | bytes 393220
  15.4 10.1 %copy-start.4 = (bf16[256,256]{1,0:T(8,128)(2,1)S(1)}, bf16[256,256]{1,0:T(8,128)(2,1)}, u32[]{:S(2)}) copy-start(bf16[256,256]{1,0:T(8,128)(2,1)} %param.13) | copy-start | bytes 393220
  23.1 47.1 %collective-permute-start = (bf16[64,64,256]{2,1,0:T(8,128)(2,1)}, bf16[64,64,256]{2,1,0:T(8,128)(2,1)}, u32[]{:S(2)}, u32[]{:S(2)}) collective-permute-start(bf16[64,64,256]{2,1,0:T(8,128)(2,1)} %bitcast.9.rest_0_.rows_ref), channel_id=1, source_target_pairs={{0,2},{1,3},{2,0},{3,1},{4,6},{5,7},{6,4},{7,5},{8,10},{9,11},{10,... | collective-permute-start | bytes 6291464 | tf_op jit(solution)/shard_map/ppermute | solution.py:419
  24.6 50.7 %collective-permute-start.1 = (bf16[64,64,256]{2,1,0:T(8,128)(2,1)}, bf16[64,64,256]{2,1,0:T(8,128)(2,1)}, u32[]{:S(2)}, u32[]{:S(2)}) collective-permute-start(bf16[64,64,256]{2,1,0:T(8,128)(2,1)} %bitcast.9.rest_0_.rows_ref), channel_id=1, source_target_pairs={{0,8},{1,9},{2,10},{3,11},{4,0},{5,1},{6,2},{7,3},{8,12},{9,13},{1... | collective-permute-start | bytes 6291464 | tf_op jit(solution)/shard_map/ppermute | solution.py:419
  72.9 52.3 %collective-permute-start.6 = (bf16[50,64,256]{2,1,0:T(8,128)(2,1)S(1)}, bf16[50,64,256]{2,1,0:T(8,128)(2,1)S(1)}, u32[]{:S(2)}, u32[]{:S(2)}) collective-permute-start(bf16[50,64,256]{2,1,0:T(8,128)(2,1)S(1)} %pick_blocks.5), channel_id=1, source_target_pairs={{0,4},{1,5},{2,6},{3,7},{4,12},{5,13},{6,14},{7,15},{8,0},{9,1},{1... | collective-permute-start | bytes 4915208 | tf_op jit(solution)/shard_map/ppermute | solution.py:419
  78.7 44.1 %collective-permute-start.7 = (bf16[25,64,256]{2,1,0:T(8,128)(2,1)S(1)}, bf16[25,64,256]{2,1,0:T(8,128)(2,1)S(1)}, u32[]{:S(2)}, u32[]{:S(2)}) collective-permute-start(bf16[25,64,256]{2,1,0:T(8,128)(2,1)S(1)} %get-tuple-element.13), channel_id=1, source_target_pairs={{0,2},{1,3},{2,0},{3,1},{4,6},{5,7},{6,4},{7,5},{8,10},{9,11},{10,... | collective-permute-start | bytes 2457608 | tf_op jit(solution)/shard_map/ppermute | solution.py:419
  80.1 74.0 %collective-permute-start.5 = (bf16[25,64,256]{2,1,0:T(8,128)(2,1)}, bf16[25,64,256]{2,1,0:T(8,128)(2,1)}, u32[]{:S(2)}, u32[]{:S(2)}) collective-permute-start(bf16[25,64,256]{2,1,0:T(8,128)(2,1)} %get-tuple-element.12), channel_id=1, source_target_pairs={{8,12},{9,13},{10,14},{11,15},{4,0},{5,1},{6,2},{7,3},{24,28},{25,... | collective-permute-start | bytes 2457608 | tf_op jit(solution)/shard_map/ppermute | solution.py:419
  82.6 32.0 %collective-permute-start.2 = (bf16[25,64,256]{2,1,0:T(8,128)(2,1)S(1)}, bf16[25,64,256]{2,1,0:T(8,128)(2,1)}, u32[]{:S(2)}, u32[]{:S(2)}) collective-permute-start(bf16[25,64,256]{2,1,0:T(8,128)(2,1)S(1)} %get-tuple-element.11), channel_id=1, source_target_pairs={{0,2},{1,3},{2,0},{3,1},{4,6},{5,7},{6,4},{7,5},{8,10},{9,11},{10,... | collective-permute-start | bytes 2457608 | tf_op jit(solution)/shard_map/ppermute | solution.py:419
  118.5 42.8 %collective-permute-start.3 = (bf16[50,64,256]{2,1,0:T(8,128)(2,1)}, bf16[50,64,256]{2,1,0:T(8,128)(2,1)}, u32[]{:S(2)}, u32[]{:S(2)}) collective-permute-start(bf16[50,64,256]{2,1,0:T(8,128)(2,1)} %pick_blocks.4), channel_id=1, source_target_pairs={{4,8},{5,9},{6,10},{7,11},{8,4},{9,5},{10,6},{11,7},{20,24},{21,25... | collective-permute-start | bytes 4915208 | tf_op jit(solution)/shard_map/ppermute | solution.py:419
  120.4 37.3 %collective-permute-start.4 = (bf16[25,64,256]{2,1,0:T(8,128)(2,1)}, bf16[25,64,256]{2,1,0:T(8,128)(2,1)}, u32[]{:S(2)}, u32[]{:S(2)}) collective-permute-start(bf16[25,64,256]{2,1,0:T(8,128)(2,1)} %collective-permute-done.2.rest_2_), channel_id=1, source_target_pairs={{8,12},{9,13},{10,14},{11,15},{4,0},{5,1},{6,2},{7,3},{24,28},{25,... | collective-permute-start | bytes 2457608 | tf_op jit(solution)/shard_map/ppermute | solution.py:419
  125.2 3.7 %copy-start = (bf16[256,256]{1,0:T(8,128)(2,1)S(1)}, bf16[256,256]{1,0:T(8,128)(2,1)}, u32[]{:S(2)}) copy-start(bf16[256,256]{1,0:T(8,128)(2,1)} %rest_24_.3) | copy-start | bytes 393220
  125.2 3.7 %copy-start.1 = (bf16[256,256]{1,0:T(8,128)(2,1)S(1)}, bf16[256,256]{1,0:T(8,128)(2,1)}, u32[]{:S(2)}) copy-start(bf16[256,256]{1,0:T(8,128)(2,1)} %rest_25_.3) | copy-start | bytes 393220

commit v7 on v6

--- a/solution.py
+++ b/solution.py
@@ -38,7 +38,7 @@
     return row_head == lane_head
 
 
-def place_kernel(features_ref, assignment_ref, after_ref, placed_ref, normed_ref):
+def place_kernel(features_ref, assignment_ref, placed_ref, normed_ref):
     rows = features_ref.shape[0]
     lane = 128
     features = features_ref[...]
@@ -53,7 +53,7 @@
         normed_ref[pl.ds(part * lane, lane), :] = layer_norm(placed).astype(jnp.bfloat16)
 
 
-def place(features, assignment, after):
+def place(features, assignment):
     width = features.shape[1]
     walkers, _, rows = assignment.shape
     local = pl.BlockSpec((rows, width), lambda i: (i, 0))
@@ -61,17 +61,13 @@
     return pl.pallas_call(
         place_kernel,
         grid=(walkers,),
-        in_specs=[
-            local,
-            pl.BlockSpec((1, 1, rows), lambda i: (i, 0, 0)),
-            pl.BlockSpec(memory_space=pl.ANY),
-        ],
+        in_specs=[local, pl.BlockSpec((1, 1, rows), lambda i: (i, 0, 0))],
         out_specs=[local] * 2,
         out_shape=[out, out],
         cost_estimate=lasting(7),
         compiler_params=kernel_params(),
         name="place_rows",
-    )(features, assignment, after)
+    )(features, assignment)
 
 
 def choose(index, values):
@@ -162,7 +158,7 @@
 
 def project_pairs(piece, w_both, so_far, at, total):
     blocks, cluster, width = piece.shape
-    per = max(n for n in range(1, 33) if blocks % n == 0 and at % n == 0)
+    per = max(n for n in range(1, 26) if blocks % n == 0 and at % n == 0)
     in_specs = [
         pl.BlockSpec((per, cluster, width), lambda i: (i, 0, 0)),
         pl.BlockSpec((width, 2 * width), lambda i: (0, 0)),
@@ -186,24 +182,80 @@
     )(*operands)
 
 
-def attend_kernel(range_ref, order_ref, table_ref, *rest, pair_count, head_width):
-    step = pl.program_id(0)
-    count = range_ref[1]
-
-    @pl.when(step < count)
+def attend_kernel(
+    range_ref,
+    order_ref,
+    table_ref,
+    query_ref,
+    buffer_ref,
+    placed_ref,
+    out_w_ref,
+    mix_ref,
+    *rest,
+    own_at,
+    head_width,
+):
+    mixed_ref, query_buf, pair_buf, placed_buf, done_buf, in_sems, out_sems = rest[-7:]
+    begin, count = range_ref[0], range_ref[1]
+    pair_count = pair_buf.shape[2] - 1
+
+    def fetches(step, slot):
+        for j in range(STEP):
+            block = order_ref[step * STEP + j]
+            sources = [(query_ref.at[block], query_buf.at[slot, j])]
+            sources.append((placed_ref.at[block], placed_buf.at[slot, j]))
+            sources.append((buffer_ref.at[own_at + block], pair_buf.at[slot, j, 0]))
+            for n in range(pair_count):
+                listed = table_ref[block * pair_count + n]
+                sources.append((buffer_ref.at[listed], pair_buf.at[slot, j, 1 + n]))
+            for n, (source_, target) in enumerate(sources):
+                sem = in_sems.at[slot, j * (pair_count + 3) + n]
+                yield pltpu.make_async_copy(source_, target, sem)
+
+    def stores(step):
+        for j in range(STEP):
+            target = mixed_ref.at[order_ref[step * STEP + j]]
+            yield pltpu.make_async_copy(done_buf.at[j], target, out_sems.at[j])
+
+    def one_step(i, carry):
+        slot = i % 2
+        for copy in fetches(begin + jnp.minimum(i + 1, count - 1), 1 - slot):
+            copy.start()
+        for copy in fetches(begin + i, slot):
+            copy.wait()
+        mixed = attend_step(
+            query_buf.at[slot],
+            pair_buf.at[slot],
+            placed_buf.at[slot],
+            out_w_ref,
+            mix_ref,
+            head_width,
+        )
+
+        @pl.when(i > 0)
+        def _():
+            for copy in stores(begin + i - 1):
+                copy.wait()
+
+        done_buf[...] = mixed.reshape(done_buf.shape)
+        for copy in stores(begin + i):
+            copy.start()
+        return carry
+
+    @pl.when(count > 0)
     def _():
-        attend_step(
-            step, range_ref[0], count, order_ref, *rest, pair_count=pair_count, head_width=head_width
-        )
-
-
-def attend_step(step, begin, count, order_ref, *rest, pair_count, head_width):
-    query_refs, rest = rest[:STEP], rest[STEP:]
-    own_refs, rest = rest[:STEP], rest[STEP:]
-    listed_refs, rest = rest[: STEP * pair_count], rest[STEP * pair_count :]
-    placed_refs, rest = rest[:STEP], rest[STEP:]
-    out_w_ref, mix_ref, *_, mixed_ref, done_ref, sems = rest
-    cluster, width = placed_refs[0].shape
+        for copy in fetches(begin, 0):
+            copy.start()
+        lax.fori_loop(0, count, one_step, 0)
+        for copy in fetches(begin + count - 1, count % 2):
+            copy.wait()
+        for copy in stores(begin + count - 1):
+            copy.wait()
+
+
+def attend_step(query_ref, pair_ref, placed_ref, out_w_ref, mix_ref, head_width):
+    _, members_count, cluster, _ = pair_ref.shape
+    width = placed_ref.shape[2]
     span = GROUP * head_width
     tile = GROUP * cluster
     diagonal = head_mask((span, tile), head_width, cluster)
@@ -217,8 +269,7 @@
     keys, values = {}, {}
 
     def gather(block):
-        members = [own_refs[block][0]]
-        members += [listed_refs[block * pair_count + j][0] for j in range(pair_count)]
+        members = [pair_ref[block, n] for n in range(members_count)]
         keys[block] = jnp.concatenate([m[:, :width] for m in members], axis=0)
         values[block] = jnp.concatenate([m[:, width:] for m in members], axis=0).T
 
@@ -226,7 +277,7 @@
         if t == 0:
             gather(block)
         lo = t * span // 128 * 128
-        picked = query_refs[block][0, t * span : (t + 1) * span, :]
+        picked = query_ref[block, t * span : (t + 1) * span, :]
         ahead, behind = t * span - lo, lo + 128 - (t + 1) * span
         stack = [zeros] * (ahead // span) + [picked] + [zeros] * (behind // span)
         return jnp.dot(
@@ -253,117 +304,68 @@
             folded = lax.dot_general(fold, stacked, NT, preferred_element_type=jnp.float32)
             attended.append(folded.astype(jnp.bfloat16))
             pieces = []
-    placed = jnp.concatenate([ref[...] for ref in placed_refs], axis=0)
+    placed = placed_ref[...].reshape(STEP * cluster, width)
     middle = placed.astype(jnp.float32) + jnp.dot(
         jnp.concatenate(attended, axis=0), out_w_ref[...], preferred_element_type=jnp.float32
     )
     middle = middle.astype(jnp.bfloat16).astype(jnp.float32)
     second = layer_norm(middle).astype(jnp.bfloat16)
     mixed = middle + jnp.tanh(jnp.dot(second, mix_ref[...], preferred_element_type=jnp.float32))
-
-    def copies(of_step):
-        for block in range(STEP):
-            row = order_ref[(begin + of_step) * STEP + block] * cluster
-            yield pltpu.make_async_copy(
-                done_ref.at[pl.ds(block * cluster, cluster), :],
-                mixed_ref.at[pl.ds(pl.multiple_of(row, cluster), cluster), :],
-                sems.at[block],
-            )
-
-    @pl.when(step > 0)
-    def _():
-        for copy in copies(step - 1):
-            copy.wait()
-
-    done_ref[...] = mixed.astype(jnp.bfloat16)
-    for copy in copies(step):
-        copy.start()
-
-    @pl.when(step == count - 1)
-    def _():
-        for copy in copies(step):
-            copy.wait()
+    return mixed.astype(jnp.bfloat16)
 
 
 def attend(begin, count, order, table, queries, buffer, own_at, placed, w_out, w_mix, so_far=None):
-    rows, width = placed.shape
-    blocks, _, tile = queries.shape
-    cluster = rows // blocks
+    blocks, cluster, width = placed.shape
     pair_count = table.shape[0] // blocks
-    whole = pl.BlockSpec((width, width), lambda i, f, o, t: (0, 0))
-
-    def reader(i, j, f, o):
-        step = f[0] + jnp.minimum(i, jnp.maximum(f[1] - 1, 0))
-        return o[step * STEP + j]
-
-    def listed(j, n):
-        return pl.BlockSpec(
-            (1, cluster, 2 * width),
-            lambda i, f, o, t: (t[reader(i, j, f, o) * pair_count + n], 0, 0),
-        )
-
-    each = range(STEP)
-    in_specs = [
-        pl.BlockSpec((1, width, tile), lambda i, f, o, t, j=j: (reader(i, j, f, o), 0, 0))
-        for j in each
-    ]
-    in_specs += [
-        pl.BlockSpec(
-            (1, cluster, 2 * width), lambda i, f, o, t, j=j: (own_at + reader(i, j, f, o), 0, 0)
-        )
-        for j in each
-    ]
-    in_specs += [listed(j, n) for j in each for n in range(pair_count)]
-    in_specs += [
-        pl.BlockSpec((cluster, width), lambda i, f, o, t, j=j: (reader(i, j, f, o), 0)) for j in each
-    ]
-    in_specs += [whole, whole]
-    operands = [queries] * STEP + [buffer] * (STEP + STEP * pair_count) + [placed] * STEP
-    operands += [w_out, w_mix]
+    smem = pl.BlockSpec(memory_space=pltpu.SMEM)
+    vmem = pl.BlockSpec(memory_space=pltpu.VMEM)
+    hbm = pl.BlockSpec(memory_space=pl.ANY)
+    in_specs = [smem, smem, smem, hbm, hbm, hbm, vmem, vmem]
+    operands = [queries, buffer, placed, w_out, w_mix]
     aliases = {}
     if so_far is not None:
-        aliases = {3 + len(operands): 0}
-        in_specs.append(pl.BlockSpec(memory_space=pl.ANY))
+        aliases = {len(in_specs): 0}
+        in_specs.append(hbm)
         operands.append(so_far)
     return pl.pallas_call(
-        functools.partial(attend_kernel, pair_count=pair_count, head_width=width // HEADS),
-        grid_spec=pltpu.PrefetchScalarGridSpec(
-            num_scalar_prefetch=3,
-            grid=(blocks // STEP,),
-            in_specs=in_specs,
-            out_specs=pl.BlockSpec(memory_space=pl.ANY),
-            scratch_shapes=[
-                pltpu.VMEM((STEP * cluster, width), jnp.bfloat16),
-                pltpu.SemaphoreType.DMA((STEP,)),
-            ],
-        ),
-        out_shape=jax.ShapeDtypeStruct((rows, width), jnp.bfloat16),
+        functools.partial(attend_kernel, own_at=own_at, head_width=width // HEADS),
+        in_specs=in_specs,
+        out_specs=hbm,
+        out_shape=jax.ShapeDtypeStruct(placed.shape, jnp.bfloat16),
+        scratch_shapes=[
+            pltpu.VMEM((2, STEP) + queries.shape[1:], jnp.bfloat16),
+            pltpu.VMEM((2, STEP, pair_count + 1, cluster, 2 * width), jnp.bfloat16),
+            pltpu.VMEM((2, STEP, cluster, width), jnp.bfloat16),
+            pltpu.VMEM((STEP, cluster, width), jnp.bfloat16),
+            pltpu.SemaphoreType.DMA((2, STEP * (pair_count + 3))),
+            pltpu.SemaphoreType.DMA((STEP,)),
+        ],
         input_output_aliases=aliases,
-        cost_estimate=lasting(25),
+        cost_estimate=lasting(20),
         compiler_params=kernel_params(),
         name="attend_blocks",
     )(jnp.stack([begin, count]).astype(jnp.int32), order, table, *operands)
 
 
 def slot_tables(owner, within, capacity):
-    readers, entries = owner.shape
-    alike = owner[:, :, None] == owner[:, None, :]
+    entries = owner.shape[0]
+    alike = owner[:, None] == owner[None, :]
     earlier = jnp.arange(entries)[None, :] < jnp.arange(entries)[:, None]
-    ranking = jnp.sum(jnp.where(alike & earlier, 1, 0), axis=2).astype(jnp.int32)
+    ranking = jnp.sum(jnp.where(alike & earlier, 1, 0), axis=1).astype(jnp.int32)
     slots = owner * capacity + ranking
-    every = jnp.arange(SPAN * capacity, dtype=jnp.int32)
-    matches = slots[:, None, :] == every[None, :, None]
-    return ranking, jnp.sum(jnp.where(matches, within[:, None, :], 0), axis=2).astype(jnp.int32)
-
-
-def early_first(early):
-    count = jnp.sum(early.astype(jnp.int32))
-    blocks = jnp.arange(early.shape[0], dtype=jnp.int32)
-    before = blocks[None, :] < blocks[:, None]
-    ahead = jnp.sum(jnp.where(before & (early[None, :] == early[:, None]), 1, 0), axis=1)
-    place_ = jnp.where(early, ahead, count + ahead)
-    order = jnp.sum(jnp.where(place_[None, :] == blocks[:, None], blocks[None, :], 0), axis=1)
-    return order.astype(jnp.int32), count
+    matches = slots[None, :] == jnp.arange(SPAN * capacity, dtype=jnp.int32)[:, None]
+    return ranking, jnp.sum(jnp.where(matches, within[None, :], 0), axis=1).astype(jnp.int32)
+
+
+def by_class(classes, count):
+    blocks = jnp.arange(classes.shape[0], dtype=jnp.int32)
+    before = (classes[None, :] < classes[:, None]) | (
+        (classes[None, :] == classes[:, None]) & (blocks[None, :] < blocks[:, None])
+    )
+    rank = jnp.sum(jnp.where(before, 1, 0), axis=1)
+    order = jnp.sum(jnp.where(rank[None, :] == blocks[:, None], blocks[None, :], 0), axis=1)
+    ends = [jnp.sum(jnp.where(classes <= c, 1, 0)).astype(jnp.int32) for c in range(count)]
+    return order.astype(jnp.int32), ends
 
 
 OUT = (2, 0, 3, 1)
@@ -400,8 +402,10 @@
 
 
 SECOND_PLAN = (((0, source, itself), (1, source, partner)),)
-MIDDLE_PLAN = (((0, opposite, itself), (1, opposite, partner)),)
-PASSED_PLAN = (((0, crossed(onward), source),), ((0, partner, source),), ((0, onward, source),))
+MIDDLE_PLAN = (((0, opposite, itself),),)
+MIDDLE_CROSS_PLAN = (((0, opposite, partner),),)
+ON_PLAN = (((0, crossed(onward), source),), ((0, onward, source),))
+NEAR_PLAN = (((0, partner, source),),)
 
 
 def body(features, assignment, pairs, w_query, w_key, w_value, w_out, w_mix):
@@ -427,16 +431,20 @@
     middle_moves = across_z([(1, 2), (2, 1)])
     outward_moves = across_z([(2, 3), (1, 0)])
 
-    all_pairs = lax.all_to_all(
-        jnp.broadcast_to(pairs.reshape(1, -1), (SPAN, block_count * pair_count)),
+    listed = pairs.reshape(-1)
+    owner = listed // block_count // stride
+    within = listed % block_count
+    ranking, tables = slot_tables(owner, within, capacity)
+    wanted = lax.all_to_all(
+        jnp.broadcast_to(tables[None], (SPAN, SPAN * capacity)),
         "elec",
         split_axis=0,
         concat_axis=0,
         axis_index_groups=groups,
         tiled=True,
     )
-    shape = (block_count // SUB, 1, SUB * cluster)
-    placed, normed = place(features, assignment.reshape(shape), all_pairs)
+
+    placed, normed = place(features, assignment.reshape(block_count // SUB, 1, SUB * cluster))
     blocks = normed.reshape(block_count, cluster, width)
     passed = moved(blocks, first_moves)
     beside = moved(blocks, swap)
@@ -448,29 +456,27 @@
     total = beside_at + block_count
     buffer = project_pairs(blocks, w_both, None, own_at, total)
     queries = project_queries(normed, w_query, cluster)
-    _, wanted = slot_tables(
-        all_pairs // block_count // stride, all_pairs % block_count, capacity
-    )
 
     (second,) = pick(at_position, wanted, (blocks, beside), SECOND_PLAN)
     second = moved(second, second_moves)
-    on, near, outward = pick(at_position, wanted, (passed,), PASSED_PLAN)
+    on, outward = pick(at_position, wanted, (passed,), ON_PLAN)
     on = moved(on, swap)
+    outward = moved(outward, outward_moves)
+    (near,) = pick(at_position, wanted, (passed,), NEAR_PLAN, after=(on,))
     near = moved(near, swap)
-    outward = moved(outward, outward_moves)
-    (middle,) = pick(at_position, wanted, (blocks, beside), MIDDLE_PLAN, after=(on,))
+    (middle,) = pick(at_position, wanted, (blocks,), MIDDLE_PLAN, after=(on,))
+    middle = moved(middle, middle_moves)
     on = moved(on, outward_moves)
-    middle = moved(middle, middle_moves)
+    (middle_cross,) = pick(
+        at_position, wanted, (beside,), MIDDLE_CROSS_PLAN, after=(second,)
+    )
+    middle_cross = moved(middle_cross, middle_moves)
 
     buffer = project_pairs(beside, w_both, buffer, beside_at, total)
     buffer = project_pairs(passed, w_both, buffer, passed_at, total)
     buffer = project_pairs(near, w_both, buffer, 0, total)
     buffer = project_pairs(second, w_both, buffer, capacity, total)
 
-    listed = pairs.reshape(-1)
-    owner = listed // block_count // stride
-    within = listed % block_count
-    (ranking,), _ = slot_tables(owner[None], within[None], capacity)
     z, y = position // 2, position % 2
     is_end = (z == 0) | (z == LEVELS - 1)
     z_owner, same = owner // 2, owner % 2 == y
@@ -489,16 +495,19 @@
     whole = (z_owner == z) | (from_first & same)
     table = jnp.where(whole, whole_at + within, piece_of * capacity + ranking)
 
-    early = ~jnp.any(late.reshape(block_count, pair_count), axis=1)
-    order, early_count = early_first(early)
-    steps = block_count // STEP
-    early_steps = jnp.minimum(early_count // STEP, steps - 1)
+    arrival = jnp.where(late, jnp.where(same | is_end, 1, 2), 0)
+    order, ends = by_class(jnp.max(arrival.reshape(block_count, pair_count), axis=1), 2)
+    marks = [0, ends[0] // STEP, ends[1] // STEP, block_count // STEP]
+    phases = [(marks[n], marks[n + 1] - marks[n]) for n in range(3)]
     shared = (order, table, queries)
-    rest = (own_at, placed, w_out, w_mix)
-    mixed = attend(jnp.zeros_like(early_steps), early_steps, *shared, buffer, *rest)
+    rest = (own_at, placed.reshape(blocks.shape), w_out, w_mix)
+    mixed = attend(*phases[0], *shared, buffer, *rest)
     for piece, at in ((outward, 3), (on, 4), (middle, 5)):
         buffer = project_pairs(piece, w_both, buffer, at * capacity, total)
-    return attend(early_steps, steps - early_steps, *shared, buffer, *rest, so_far=mixed)
+    mixed = attend(*phases[1], *shared, buffer, *rest, so_far=mixed)
+    buffer = project_pairs(middle_cross, w_both, buffer, 6 * capacity, total)
+    mixed = attend(*phases[2], *shared, buffer, *rest, so_far=mixed)
+    return mixed.reshape(rows_dev, width)
 
 
 def solution(mesh):

time: 204 us -> 182 us (0.89)
  waiting for transfers between devices: 45.8 us -> 32.8 us
  Pallas kernels: 126 us -> 115 us
  other arithmetic: 4.09 us -> 1.59 us
  between operations: 2.95 us -> 5.18 us
    ppermute x8 -> x9, waiting for transfers between devices: 45.8 us -> 13.7 us  [moved(): return lax.ppermute(x, 'elec', pairs_of)]
    all_to_all x1, waiting for transfers between devices: 0.01 us -> 19.2 us  [body(): lax.all_to_all(jnp.broadcast_to(tables[None], (SPAN, SPAN * capacity)), '...]
    pallas_call x2 -> x3, Pallas kernels: 61.1 us -> 55.8 us  [attend(): pl.pallas_call(functools.partial(attend_kernel, own_at=own_at, head_width...]
    pallas_call x8 -> x9, Pallas kernels: 39.2 us -> 34.6 us  [project_pairs(): pl.pallas_call(key_value_kernel, grid=(blocks // per,), in_specs=in_specs...]
    ppermute x8 -> x9, starting transfers between devices: 13.3 us -> 14.7 us  [moved(): return lax.ppermute(x, 'elec', pairs_of)]
    pallas_call x3 -> x5, Pallas kernels: 9.95 us -> 8.85 us  [pick(): pl.pallas_call(functools.partial(pick_kernel, plan=plan, capacity=capacit...]
  transfers between devices with their start and end apart: 9 -> 10, of which waited for: 2 -> 3; matrix products, arithmetic and copies ran while one was open for 2% -> 1% of each run, Pallas kernels for 39% -> 47%
where the time goes in v7:
time: 182 us; the launch traced here: 178 us
  Pallas kernels  115 us (63%)
  waiting for transfers between devices  32.8 us (18%)
  starting transfers between devices  20.5 us (11%)
  between operations  5.18 us (3%)
  local copies, waits for them, and re-layouts  3.01 us (2%)
    pallas_call x3, Pallas kernels, attend(): pl.pallas_call(functools.partial(attend_kernel, own_at=own_at, head_width...  55.8 us
    pallas_call x9, Pallas kernels, project_pairs(): pl.pallas_call(key_value_kernel, grid=(blocks // per,), in_specs=in_specs...  34.6 us
    all_to_all x1, waiting for transfers between devices, body(): lax.all_to_all(jnp.broadcast_to(tables[None], (SPAN, SPAN * capacity)), '...  19.2 us
    ppermute x9, starting transfers between devices, moved(): return lax.ppermute(x, 'elec', pairs_of)  14.7 us
    ppermute x9, waiting for transfers between devices, moved(): return lax.ppermute(x, 'elec', pairs_of)  13.7 us
    pallas_call x5, Pallas kernels, pick(): pl.pallas_call(functools.partial(pick_kernel, plan=plan, capacity=capacit...  8.85 us
    pallas_call x1, Pallas kernels, project_queries(): pl.pallas_call(functools.partial(query_kernel, cluster=cluster, head_widt...  8.33 us
    pallas_call x1, Pallas kernels, place(): pl.pallas_call(place_kernel, grid=(walkers,), in_specs=[local, pl.BlockSp...  7.7 us
  transfers between devices with their start and end apart: 10, of which 3 were waited for; matrix products, arithmetic and copies ran while one was open for 1% of the time, Pallas kernels for 47%

profile of v7, /device:TPU:8, one launch (start us, length us, event | category | flops | bytes accessed | tf_op | source)
XLA Modules:
  0.0 178.4 jit_solution(4983056010145224911)
XLA Ops:
  0.0 0.7 copy-done.2
  0.7 7.7 %place_rows.1 = (bf16[4096,256]{1,0:T(8,128)(2,1)S(1)}, bf16[4096,256]{1,0:T(8,128)(2,1)}) custom-call(bf16[4096,256]{1,0:T(8,128)(2,1)} %features_ref.1, s32[8,1,512]{2,1,0:T(1,128)S(1)} %bitcast.19), custom_call_target="tpu_custom_call" | custom-call | flops 8049999872 | tf_op jit(solution)/shard_map/place_rows/pallas_call | solution.py:61
  8.4 1.3 copy-done.3
  9.7 2.0 %collective-permute-start = (bf16[64,64,256]{2,1,0:T(8,128)(2,1)}, bf16[64,64,256]{2,1,0:T(8,128)(2,1)S(1)}, u32[]{:S(2)}, u32[]{:S(2)}) collective-permute-start(bf16[64,64,256]{2,1,0:T(8,128)(2,1)} %bitcast.5.rest_0_.rows_ref), channel_id=1, source_target_pairs={{0,2},{1,3},{2,0},{3,1},{4,6},{5,7},{6,4},{7,5},{8,10},{9,11},{10,... | collective-permute-start | bytes 6291464 | tf_op jit(solution)/shard_map/ppermute | solution.py:423
  13.0 5.8 %all-to-all-start = ((s32[8,1,200]{2,1,0:T(1,128)}), s32[8,1,200]{2,1,0:T(1,128)S(1)}, u32[]{:S(2)}, u32[]{:S(2)}) async-start(s32[8,1,200]{2,1,0:T(1,128)} %broadcast_in_dim.108), calls=%async_computation | async-start | bytes 16384 | tf_op jit(solution)/shard_map/all_to_all | solution.py:438
  18.8 0.7 fusion.14
  24.8 7.1 %keys_values.9.rest_0_ = bf16[392,64,512]{2,1,0:T(8,128)(2,1)} custom-call(bf16[64,64,256]{2,1,0:T(8,128)(2,1)} %bitcast.5.rest_0_.rows_ref, bf16[256,512]{1,0:T(8,128)(2,1)S(1)} %constant_dynamic-update-slice_fusion.w_ref), custom_call_target="tpu_custom_call" | custom-call | flops 6133333504 | tf_op jit(solution)/shard_map/keys_values/pallas_call | solution.py:172
  31.9 8.3 %queries.1.query_ref = bf16[64,256,256]{2,1,0:T(8,128)(2,1)} custom-call(bf16[4096,256]{1,0:T(8,128)(2,1)} %get-tuple-element.9.normed_ref, bf16[256,256]{1,0:T(8,128)(2,1)S(1)} %bitcast.13), custom_call_target="tpu_custom_call" | custom-call | flops 7474999808 | tf_op jit(solution)/shard_map/queries/pallas_call | solution.py:129
  40.3 19.2 %all-to-all-done = s32[8,1,200]{2,1,0:T(1,128)S(1)} async-done(((s32[8,1,200]{2,1,0:T(1,128)}), s32[8,1,200]{2,1,0:T(1,128)S(1)}, u32[]{:S(2)}, u32[]{:S(2)}) %all-to-all-start) | async-done | bytes 6432 | tf_op jit(solution)/shard_map/all_to_all | solution.py:438
  59.4 2.1 %pick_blocks.7 = (bf16[25,64,256]{2,1,0:T(8,128)(2,1)S(1)}, bf16[25,64,256]{2,1,0:T(8,128)(2,1)S(1)}) custom-call(s32[1]{0:T(128)} %bitcast.4.position_ref, s32[8,200]{1,0:T(8,128)S(1)} %bitcast.14, bf16[64,64,256]{2,1,0:T(8,128)(2,1)} %collective-permute-done.3.rest_0_.rows_ref), custom_call_target="tpu_custom_call" | custom-call | flops 1724999936 | tf_op jit(solution)/shard_map/pick_blocks/pallas_call | solution.py:102
  62.2 2.1 %pick_blocks.5 = bf16[50,64,256]{2,1,0:T(8,128)(2,1)S(1)} custom-call(s32[1]{0:T(128)} %bitcast.4.position_ref, s32[8,200]{1,0:T(8,128)S(1)} %bitcast.15, bf16[64,64,256]{2,1,0:T(8,128)(2,1)} %bitcast.5.rest_0_.rows_ref, bf16[64,64,256]{2,1,0:T(8,128)(2,1)S(1)} %collective-permute-done.rest_1_.rest_0_.rows_ref), custom_call_target="tpu_custom_call" | custom-call | flops 1724999936 | tf_op jit(solution)/shard_map/pick_blocks/pallas_call | solution.py:102
  64.3 2.4 %collective-permute-start.1 = (bf16[50,64,256]{2,1,0:T(8,128)(2,1)S(1)}, bf16[50,64,256]{2,1,0:T(8,128)(2,1)S(1)}, u32[]{:S(2)}, u32[]{:S(2)}) collective-permute-start(bf16[50,64,256]{2,1,0:T(8,128)(2,1)S(1)} %pick_blocks.5), channel_id=1, source_target_pairs={{0,4},{1,5},{2,6},{3,7},{4,12},{5,13},{6,14},{7,15},{8,0},{9,1},{1... | collective-permute-start | bytes 4915208 | tf_op jit(solution)/shard_map/ppermute | solution.py:423
  66.9 1.6 collective-permute-start.7
  68.5 4.7 %keys_values.10.rest_0_ = bf16[392,64,512]{2,1,0:T(8,128)(2,1)} custom-call(bf16[64,64,256]{2,1,0:T(8,128)(2,1)S(1)} %collective-permute-done.rest_1_.rest_0_.rows_ref, bf16[256,512]{1,0:T(8,128)(2,1)S(1)} %constant_dynamic-update-slice_fusion.w_ref, bf16[392,64,512]{2,1,0:T(8,128)(2,1)} %keys_values.9.rest_0_), custom_call_target="tpu_custom_call", output_to_operand_aliasing={{}: (2, {})} | custom-call | flops 6133333504 | tf_op jit(solution)/shard_map/keys_values/pallas_call | solution.py:172
  73.3 7.6 %collective-permute-done.4.rest_1_ = bf16[25,64,256]{2,1,0:T(8,128)(2,1)S(1)} collective-permute-done((bf16[25,64,256]{2,1,0:T(8,128)(2,1)S(1)}, bf16[25,64,256]{2,1,0:T(8,128)(2,1)S(1)}, u32[]{:S(2)}, u32[]{:S(2)}) %collective-permute-start.4) | collective-permute-done | bytes 819232 | tf_op jit(solution)/shard_map/ppermute | solution.py:423
  80.8 1.9 %pick_blocks.9 = bf16[25,64,256]{2,1,0:T(8,128)(2,1)S(1)} custom-call(s32[1]{0:T(128)} %bitcast.4.position_ref, s32[8,200]{1,0:T(8,128)S(1)} %bitcast.16, bf16[64,64,256]{2,1,0:T(8,128)(2,1)} %collective-permute-done.3.rest_0_.rows_ref, bf16[25,64,256]{2,1,0:T(8,128)(2,1)S(1)} %collective-permute-done.4.rest_1_), custom_call_target="tpu_custom_call" | custom-call | flops 1724999936 | tf_op jit(solution)/shard_map/pick_blocks/pallas_call | solution.py:102
  83.3 7.0 %keys_values.11.rest_0_ = bf16[392,64,512]{2,1,0:T(8,128)(2,1)} custom-call(bf16[64,64,256]{2,1,0:T(8,128)(2,1)} %collective-permute-done.3.rest_0_.rows_ref, bf16[256,512]{1,0:T(8,128)(2,1)S(1)} %constant_dynamic-update-slice_fusion.w_ref, bf16[392,64,512]{2,1,0:T(8,128)(2,1)} %keys_values.10.rest_0_), custom_call_target="tpu_custom_call", output_to_operand_aliasing={{}: (2, {})} | custom-call | flops 6133333504 | tf_op jit(solution)/shard_map/keys_values/pallas_call | solution.py:172
  90.3 1.9 %pick_blocks.8 = bf16[25,64,256]{2,1,0:T(8,128)(2,1)S(1)} custom-call(s32[1]{0:T(128)} %bitcast.4.position_ref, s32[8,200]{1,0:T(8,128)S(1)} %bitcast.17, bf16[64,64,256]{2,1,0:T(8,128)(2,1)} %bitcast.5.rest_0_.rows_ref, bf16[25,64,256]{2,1,0:T(8,128)(2,1)S(1)} %collective-permute-done.4.rest_1_), custom_call_target="tpu_custom_call" | custom-call | flops 1724999936 | tf_op jit(solution)/shard_map/pick_blocks/pallas_call | solution.py:102
  92.2 3.4 %collective-permute-start.5 = (bf16[25,64,256]{2,1,0:T(8,128)(2,1)S(1)}, bf16[25,64,256]{2,1,0:T(8,128)(2,1)S(1)}, u32[]{:S(2)}, u32[]{:S(2)}) collective-permute-start(bf16[25,64,256]{2,1,0:T(8,128)(2,1)S(1)} %pick_blocks.8), channel_id=1, source_target_pairs={{4,8},{5,9},{6,10},{7,11},{8,4},{9,5},{10,6},{11,7},{20,24},{21,25... | collective-permute-start | bytes 2457608 | tf_op jit(solution)/shard_map/ppermute | solution.py:423
  95.6 1.3 collective-permute-start.6
  97.0 6.0 %collective-permute-done.1.rest_1_.rows_ref = bf16[50,64,256]{2,1,0:T(8,128)(2,1)S(1)} collective-permute-done((bf16[50,64,256]{2,1,0:T(8,128)(2,1)S(1)}, bf16[50,64,256]{2,1,0:T(8,128)(2,1)S(1)}, u32[]{:S(2)}, u32[]{:S(2)}) %collective-permute-start.1) | collective-permute-done | bytes 1638432 | tf_op jit(solution)/shard_map/ppermute | solution.py:423
  103.0 0.9 pick_blocks.6
  104.0 2.7 %collective-permute-start.2 = (bf16[25,64,256]{2,1,0:T(8,128)(2,1)S(1)}, bf16[25,64,256]{2,1,0:T(8,128)(2,1)S(1)}, u32[]{:S(2)}, u32[]{:S(2)}) collective-permute-start(bf16[25,64,256]{2,1,0:T(8,128)(2,1)S(1)} %pick_blocks.6), channel_id=1, source_target_pairs={{4,8},{5,9},{6,10},{7,11},{8,4},{9,5},{10,6},{11,7},{20,24},{21,25... | collective-permute-start | bytes 2457608 | tf_op jit(solution)/shard_map/ppermute | solution.py:423
  106.7 2.4 %keys_values.12.rest_0_ = bf16[392,64,512]{2,1,0:T(8,128)(2,1)} custom-call(bf16[25,64,256]{2,1,0:T(8,128)(2,1)S(1)} %collective-permute-done.8.rows_ref, bf16[256,512]{1,0:T(8,128)(2,1)S(1)} %constant_dynamic-update-slice_fusion.w_ref, bf16[392,64,512]{2,1,0:T(8,128)(2,1)} %keys_values.11.rest_0_), custom_call_target="tpu_custom_call", output_to_operand_aliasing={{}: (2, {})} | custom-call | flops 2395833344 | tf_op jit(solution)/shard_map/keys_values/pallas_call | solution.py:172
  109.1 3.6 %keys_values.13.rest_0_.buffer_ref = bf16[392,64,512]{2,1,0:T(8,128)(2,1)} custom-call(bf16[50,64,256]{2,1,0:T(8,128)(2,1)S(1)} %collective-permute-done.1.rest_1_.rows_ref, bf16[256,512]{1,0:T(8,128)(2,1)S(1)} %constant_dynamic-update-slice_fusion.w_ref, bf16[392,64,512]{2,1,0:T(8,128)(2,1)} %keys_values.12.rest_0_), custom_call_target="tpu_custom_call", output_to_operand_aliasing={{}: (2, {})} | custom-call | flops 4791666688 | tf_op jit(solution)/shard_map/keys_values/pallas_call | solution.py:172
  112.8 20.6 %attend_blocks.3.rest_0_ = bf16[64,64,256]{2,1,0:T(8,128)(2,1)} custom-call(s32[2]{0:T(128)S(1)} %pad_add_fusion.2.range_ref, s32[64]{0:T(128)S(1)} %select_reduce_fusion.2.order_ref, s32[192]{0:T(256)S(1)} %get-tuple-element.16.table_ref, bf16[64,256,256]{2,1,0:T(8,128)(2,1)} %queries.1.query_ref, bf16[392,64,512]{2,1,0:T(8,128)(2,1)} %keys_values.13.rest_0_.buffer_ref, ...), custom_call_target="tpu_custom_call" | custom-call | flops 23000000512 | tf_op jit(solution)/shard_map/attend_blocks/pallas_call | solution.py:330
  133.3 2.5 %keys_values.14.rest_0_ = bf16[392,64,512]{2,1,0:T(8,128)(2,1)} custom-call(bf16[25,64,256]{2,1,0:T(8,128)(2,1)S(1)} %collective-permute-done.7.rows_ref, bf16[256,512]{1,0:T(8,128)(2,1)S(1)} %constant_dynamic-update-slice_fusion.w_ref, bf16[392,64,512]{2,1,0:T(8,128)(2,1)} %keys_values.13.rest_0_.buffer_ref), custom_call_target="tpu_custom_call", output_to_operand_aliasing={{}: (2, {})} | custom-call | flops 2395833344 | tf_op jit(solution)/shard_map/keys_values/pallas_call | solution.py:172
  135.8 2.4 %keys_values.15.rest_0_ = bf16[392,64,512]{2,1,0:T(8,128)(2,1)} custom-call(bf16[25,64,256]{2,1,0:T(8,128)(2,1)S(1)} %collective-permute-done.6.rows_ref, bf16[256,512]{1,0:T(8,128)(2,1)S(1)} %constant_dynamic-update-slice_fusion.w_ref, bf16[392,64,512]{2,1,0:T(8,128)(2,1)} %keys_values.14.rest_0_), custom_call_target="tpu_custom_call", output_to_operand_aliasing={{}: (2, {})} | custom-call | flops 2395833344 | tf_op jit(solution)/shard_map/keys_values/pallas_call | solution.py:172
  138.2 2.5 %keys_values.16.rest_0_.buffer_ref = bf16[392,64,512]{2,1,0:T(8,128)(2,1)} custom-call(bf16[25,64,256]{2,1,0:T(8,128)(2,1)S(1)} %collective-permute-done.5.rows_ref, bf16[256,512]{1,0:T(8,128)(2,1)S(1)} %constant_dynamic-update-slice_fusion.w_ref, bf16[392,64,512]{2,1,0:T(8,128)(2,1)} %keys_values.15.rest_0_), custom_call_target="tpu_custom_call", output_to_operand_aliasing={{}: (2, {})} | custom-call | flops 2395833344 | tf_op jit(solution)/shard_map/keys_values/pallas_call | solution.py:172
  140.7 14.6 %attend_blocks.4.rest_0_ = bf16[64,64,256]{2,1,0:T(8,128)(2,1)} custom-call(s32[2]{0:T(128)S(1)} %pad_add_fusion.1.range_ref, s32[64]{0:T(128)S(1)} %select_reduce_fusion.2.order_ref, s32[192]{0:T(256)S(1)} %get-tuple-element.16.table_ref, bf16[64,256,256]{2,1,0:T(8,128)(2,1)} %queries.1.query_ref, ...), custom_call_target="tpu_custom_call", output_to_operand_aliasing={{}: (8, {})} | custom-call | flops 23000000512 | tf_op jit(solution)/shard_map/attend_blocks/pallas_call | solution.py:330
  155.4 2.4 %keys_values.17.buffer_ref = bf16[392,64,512]{2,1,0:T(8,128)(2,1)} custom-call(bf16[25,64,256]{2,1,0:T(8,128)(2,1)S(1)} %collective-permute-done.2.rows_ref, bf16[256,512]{1,0:T(8,128)(2,1)S(1)} %constant_dynamic-update-slice_fusion.w_ref, bf16[392,64,512]{2,1,0:T(8,128)(2,1)} %keys_values.16.rest_0_.buffer_ref), custom_call_target="tpu_custom_call", output_to_operand_aliasing={{}: (2, {})} | custom-call | flops 2395833344 | tf_op jit(solution)/shard_map/keys_values/pallas_call | solution.py:172
  157.8 20.6 %attend_blocks.5 = bf16[64,64,256]{2,1,0:T(8,128)(2,1)} custom-call(s32[2]{0:T(128)S(1)} %pad_add_fusion.range_ref, s32[64]{0:T(128)S(1)} %select_reduce_fusion.2.order_ref, s32[192]{0:T(256)S(1)} %get-tuple-element.16.table_ref, bf16[64,256,256]{2,1,0:T(8,128)(2,1)} %queries.1.query_ref, ...), custom_call_target="tpu_custom_call", output_to_operand_aliasing={{}: (8, {})} | custom-call | flops 23000000512 | tf_op jit(solution)/shard_map/attend_blocks/pallas_call | solution.py:330
  (43 shorter events, 3.1 us)
Async XLA Ops:
  0.0 0.7 copy-start.2
  0.7 11.0 %copy-start.8 = (s32[64,3]{0,1:T(4,128)S(1)}, s32[64,3]{0,1:T(4,128)}, u32[]{:S(2)}) copy-start(s32[64,3]{0,1:T(4,128)} %param.10) | copy-start | bytes 2308
  0.7 23.6 %copy-start.5 = (bf16[256,256]{1,0:T(8,128)(2,1)S(1)}, bf16[256,256]{1,0:T(8,128)(2,1)}, u32[]{:S(2)}) copy-start(bf16[256,256]{1,0:T(8,128)(2,1)} %param.11) | copy-start | bytes 393220
  0.7 24.0 %copy-start.6 = (bf16[256,256]{1,0:T(8,128)(2,1)S(1)}, bf16[256,256]{1,0:T(8,128)(2,1)}, u32[]{:S(2)}) copy-start(bf16[256,256]{1,0:T(8,128)(2,1)} %param.12) | copy-start | bytes 393220
  0.7 24.1 %copy-start.7 = (bf16[256,256]{1,0:T(8,128)(2,1)S(1)}, bf16[256,256]{1,0:T(8,128)(2,1)}, u32[]{:S(2)}) copy-start(bf16[256,256]{1,0:T(8,128)(2,1)} %param.13) | copy-start | bytes 393220
  8.4 1.3 copy-start.3
  9.7 49.7 %collective-permute-start.3 = (bf16[64,64,256]{2,1,0:T(8,128)(2,1)}, bf16[64,64,256]{2,1,0:T(8,128)(2,1)}, u32[]{:S(2)}, u32[]{:S(2)}) collective-permute-start(bf16[64,64,256]{2,1,0:T(8,128)(2,1)} %bitcast.5.rest_0_.rows_ref), channel_id=1, source_target_pairs={{0,8},{1,9},{2,10},{3,11},{4,0},{5,1},{6,2},{7,3},{8,12},{9,13},{1... | collective-permute-start | bytes 6291464 | tf_op jit(solution)/shard_map/ppermute | solution.py:423
  9.7 52.4 %collective-permute-start = (bf16[64,64,256]{2,1,0:T(8,128)(2,1)}, bf16[64,64,256]{2,1,0:T(8,128)(2,1)S(1)}, u32[]{:S(2)}, u32[]{:S(2)}) collective-permute-start(bf16[64,64,256]{2,1,0:T(8,128)(2,1)} %bitcast.5.rest_0_.rows_ref), channel_id=1, source_target_pairs={{0,2},{1,3},{2,0},{3,1},{4,6},{5,7},{6,4},{7,5},{8,10},{9,11},{10,... | collective-permute-start | bytes 6291464 | tf_op jit(solution)/shard_map/ppermute | solution.py:423
  13.0 46.5 %all-to-all-start = ((s32[8,1,200]{2,1,0:T(1,128)}), s32[8,1,200]{2,1,0:T(1,128)S(1)}, u32[]{:S(2)}, u32[]{:S(2)}) async-start(s32[8,1,200]{2,1,0:T(1,128)} %broadcast_in_dim.108), calls=%async_computation | async-start | bytes 16384 | tf_op jit(solution)/shard_map/all_to_all | solution.py:438
  61.6 19.3 %collective-permute-start.4 = (bf16[25,64,256]{2,1,0:T(8,128)(2,1)S(1)}, bf16[25,64,256]{2,1,0:T(8,128)(2,1)S(1)}, u32[]{:S(2)}, u32[]{:S(2)}) collective-permute-start(bf16[25,64,256]{2,1,0:T(8,128)(2,1)S(1)} %get-tuple-element.10), channel_id=1, source_target_pairs={{0,2},{1,3},{2,0},{3,1},{4,6},{5,7},{6,4},{7,5},{8,10},{9,11},{10,... | collective-permute-start | bytes 2457608 | tf_op jit(solution)/shard_map/ppermute | solution.py:423
  64.3 38.7 %collective-permute-start.1 = (bf16[50,64,256]{2,1,0:T(8,128)(2,1)S(1)}, bf16[50,64,256]{2,1,0:T(8,128)(2,1)S(1)}, u32[]{:S(2)}, u32[]{:S(2)}) collective-permute-start(bf16[50,64,256]{2,1,0:T(8,128)(2,1)S(1)} %pick_blocks.5), channel_id=1, source_target_pairs={{0,4},{1,5},{2,6},{3,7},{4,12},{5,13},{6,14},{7,15},{8,0},{9,1},{1... | collective-permute-start | bytes 4915208 | tf_op jit(solution)/shard_map/ppermute | solution.py:423
  66.9 66.4 %collective-permute-start.7 = (bf16[25,64,256]{2,1,0:T(8,128)(2,1)S(1)}, bf16[25,64,256]{2,1,0:T(8,128)(2,1)S(1)}, u32[]{:S(2)}, u32[]{:S(2)}) collective-permute-start(bf16[25,64,256]{2,1,0:T(8,128)(2,1)S(1)} %get-tuple-element.11), channel_id=1, source_target_pairs={{8,12},{9,13},{10,14},{11,15},{4,0},{5,1},{6,2},{7,3},{24,28},{25,... | collective-permute-start | bytes 2457608 | tf_op jit(solution)/shard_map/ppermute | solution.py:423
  82.7 24.0 %collective-permute-start.8 = (bf16[25,64,256]{2,1,0:T(8,128)(2,1)S(1)}, bf16[25,64,256]{2,1,0:T(8,128)(2,1)S(1)}, u32[]{:S(2)}, u32[]{:S(2)}) collective-permute-start(bf16[25,64,256]{2,1,0:T(8,128)(2,1)S(1)} %pick_blocks.9), channel_id=1, source_target_pairs={{0,2},{1,3},{2,0},{3,1},{4,6},{5,7},{6,4},{7,5},{8,10},{9,11},{10,... | collective-permute-start | bytes 2457608 | tf_op jit(solution)/shard_map/ppermute | solution.py:423
  92.2 46.0 %collective-permute-start.5 = (bf16[25,64,256]{2,1,0:T(8,128)(2,1)S(1)}, bf16[25,64,256]{2,1,0:T(8,128)(2,1)S(1)}, u32[]{:S(2)}, u32[]{:S(2)}) collective-permute-start(bf16[25,64,256]{2,1,0:T(8,128)(2,1)S(1)} %pick_blocks.8), channel_id=1, source_target_pairs={{4,8},{5,9},{6,10},{7,11},{8,4},{9,5},{10,6},{11,7},{20,24},{21,25... | collective-permute-start | bytes 2457608 | tf_op jit(solution)/shard_map/ppermute | solution.py:423
  95.6 40.2 %collective-permute-start.6 = (bf16[25,64,256]{2,1,0:T(8,128)(2,1)S(1)}, bf16[25,64,256]{2,1,0:T(8,128)(2,1)S(1)}, u32[]{:S(2)}, u32[]{:S(2)}) collective-permute-start(bf16[25,64,256]{2,1,0:T(8,128)(2,1)S(1)} %collective-permute-done.4.rest_1_), channel_id=1, source_target_pairs={{8,12},{9,13},{10,14},{11,15},{4,0},{5,1},{6,2},{7,3},{24,28},{25,... | collective-permute-start | bytes 2457608 | tf_op jit(solution)/shard_map/ppermute | solution.py:423
  104.0 51.4 %collective-permute-start.2 = (bf16[25,64,256]{2,1,0:T(8,128)(2,1)S(1)}, bf16[25,64,256]{2,1,0:T(8,128)(2,1)S(1)}, u32[]{:S(2)}, u32[]{:S(2)}) collective-permute-start(bf16[25,64,256]{2,1,0:T(8,128)(2,1)S(1)} %pick_blocks.6), channel_id=1, source_target_pairs={{4,8},{5,9},{6,10},{7,11},{8,4},{9,5},{10,6},{11,7},{20,24},{21,25... | collective-permute-start | bytes 2457608 | tf_op jit(solution)/shard_map/ppermute | solution.py:423
  109.1 3.6 %copy-start = (bf16[256,256]{1,0:T(8,128)(2,1)S(1)}, bf16[256,256]{1,0:T(8,128)(2,1)}, u32[]{:S(2)}) copy-start(bf16[256,256]{1,0:T(8,128)(2,1)} %out_w_ref.5) | copy-start | bytes 393220
  109.1 3.6 %copy-start.1 = (bf16[256,256]{1,0:T(8,128)(2,1)S(1)}, bf16[256,256]{1,0:T(8,128)(2,1)}, u32[]{:S(2)}) copy-start(bf16[256,256]{1,0:T(8,128)(2,1)} %mix_ref.5) | copy-start | bytes 393220
  109.1 3.6 %copy-start.4 = (bf16[4096,256]{1,0:T(8,128)(2,1)S(1)}, bf16[4096,256]{1,0:T(8,128)(2,1)}, u32[]{:S(2)}) copy-start(bf16[4096,256]{1,0:T(8,128)(2,1)} %copy-done.3) | copy-start | bytes 6291460

commit v8 on v7

--- a/solution.py
+++ b/solution.py
@@ -1,4 +1,5 @@
 import functools
+import math
 
 import jax
 import jax.numpy as jnp
@@ -12,6 +13,7 @@
 SUB = 8
 GROUP = 4
 STEP = 4
+SCORES_AHEAD, WEIGHTS_AHEAD = 3, 1
 VMEM_BYTES = 48 * 1024 * 1024
 
 NT = (((1,), (1,)), ((), ()))
@@ -119,8 +121,8 @@
         own = normed_ref[pl.ds(block * cluster, cluster), :]
         own = jnp.concatenate([own] * GROUP, axis=0)
         query = lax.dot_general(query_w_ref[...], own, NT, preferred_element_type=jnp.float32)
-        query = query.astype(jnp.bfloat16) * jnp.bfloat16(1.0 / head_width**0.5)
-        query_ref[block] = jnp.where(mask, query, jnp.bfloat16(0.0))
+        query = query * (math.log2(math.e) / head_width**0.5)
+        query_ref[block] = jnp.where(mask, query, 0.0).astype(jnp.bfloat16)
 
 
 def project_queries(normed, w_query, cluster):
@@ -286,24 +288,34 @@
             preferred_element_type=jnp.float32,
         )
 
-    lead = 2
-    scores = [scores_of(*unit) for unit in units[:lead]]
-    attended, pieces = [], []
-    for at, (block, t) in enumerate(units):
-        if at + lead < len(units):
-            scores.append(scores_of(*units[at + lead]))
-        current = scores[at]
-        top = jnp.max(current, axis=0, keepdims=True)
-        weights = jnp.exp(current - top).astype(jnp.bfloat16)
+    def weights_of(scores):
+        top = jnp.max(scores, axis=0, keepdims=True)
+        return jnp.exp2(scores - top).astype(jnp.bfloat16)
+
+    def product_of(block, t, weights):
         lifted = jnp.concatenate([values[block][t * span : (t + 1) * span], ones], axis=0)
-        result = jnp.dot(lifted, weights, preferred_element_type=jnp.float32)
-        result = result[:span] * (1.0 / result[span : span + 1])
-        pieces.append(jnp.where(diagonal, result, 0.0).astype(jnp.bfloat16))
-        if t == tiles - 1:
-            stacked = jnp.concatenate(pieces, axis=0)
-            folded = lax.dot_general(fold, stacked, NT, preferred_element_type=jnp.float32)
-            attended.append(folded.astype(jnp.bfloat16))
-            pieces = []
+        return jnp.dot(lifted, weights, preferred_element_type=jnp.float32)
+
+    def scaled(product):
+        result = product[:span] * (1.0 / product[span : span + 1])
+        return jnp.where(diagonal, result, 0.0).astype(jnp.bfloat16)
+
+    count = len(units)
+    scores, weights, products, pieces, attended = {}, {}, {}, [], []
+    for at in range(-SCORES_AHEAD, count + 1):
+        if at + SCORES_AHEAD < count:
+            scores[at + SCORES_AHEAD] = scores_of(*units[at + SCORES_AHEAD])
+        if 0 <= at + WEIGHTS_AHEAD < count:
+            weights[at + WEIGHTS_AHEAD] = weights_of(scores.pop(at + WEIGHTS_AHEAD))
+        if 0 <= at < count:
+            products[at] = product_of(*units[at], weights.pop(at))
+        if at > 0:
+            pieces.append(scaled(products.pop(at - 1)))
+            if len(pieces) == tiles:
+                stacked = jnp.concatenate(pieces, axis=0)
+                folded = lax.dot_general(fold, stacked, NT, preferred_element_type=jnp.float32)
+                attended.append(folded.astype(jnp.bfloat16))
+                pieces = []
     placed = placed_ref[...].reshape(STEP * cluster, width)
     middle = placed.astype(jnp.float32) + jnp.dot(
         jnp.concatenate(attended, axis=0), out_w_ref[...], preferred_element_type=jnp.float32

time: 182 us -> 177 us (0.973)
  the two profiles are of different devices: /device:TPU:8 before, /device:TPU:0 now
where the time goes in v8:
time: 177 us
  Pallas kernels  104 us (59%)
  waiting for transfers between devices  47.3 us (27%)
  starting transfers between devices  15.1 us (9%)
  between operations  5.19 us (3%)
  local copies, waits for them, and re-layouts  3.01 us (2%)
    pallas_call x3, Pallas kernels, attend(): pl.pallas_call(functools.partial(attend_kernel, own_at=own_at, head_width...  44.8 us
    pallas_call x9, Pallas kernels, project_pairs(): pl.pallas_call(key_value_kernel, grid=(blocks // per,), in_specs=in_specs...  34.6 us
    ppermute x9, waiting for transfers between devices, moved(): return lax.ppermute(x, 'elec', pairs_of)  26.9 us
    all_to_all x1, waiting for transfers between devices, body(): lax.all_to_all(jnp.broadcast_to(tables[None], (SPAN, SPAN * capacity)), '...  20.4 us
    ppermute x9, starting transfers between devices, moved(): return lax.ppermute(x, 'elec', pairs_of)  11.8 us
    pallas_call x5, Pallas kernels, pick(): pl.pallas_call(functools.partial(pick_kernel, plan=plan, capacity=capacit...  8.85 us
    pallas_call x1, Pallas kernels, project_queries(): pl.pallas_call(functools.partial(query_kernel, cluster=cluster, head_widt...  8.34 us
    pallas_call x1, Pallas kernels, place(): pl.pallas_call(place_kernel, grid=(walkers,), in_specs=[local, pl.BlockSp...  7.7 us
  transfers between devices with their start and end apart: 10, of which 4 were waited for; matrix products, arithmetic and copies ran while one was open for 1% of the time, Pallas kernels for 53%

profile of v8, /device:TPU:0, one launch (start us, length us, event | category | flops | bytes accessed | tf_op | source)
XLA Modules:
  0.0 176.5 jit_solution(2171850526016287936)
XLA Ops:
  0.0 0.7 copy-done.2
  0.7 7.7 %place_rows.1 = (bf16[4096,256]{1,0:T(8,128)(2,1)S(1)}, bf16[4096,256]{1,0:T(8,128)(2,1)}) custom-call(bf16[4096,256]{1,0:T(8,128)(2,1)} %features_ref.1, s32[8,1,512]{2,1,0:T(1,128)S(1)} %bitcast.19), custom_call_target="tpu_custom_call" | custom-call | flops 8049999872 | tf_op jit(solution)/shard_map/place_rows/pallas_call | solution.py:63
  8.4 1.3 copy-done.3
  9.7 4.0 %collective-permute-start.3 = (bf16[64,64,256]{2,1,0:T(8,128)(2,1)}, bf16[64,64,256]{2,1,0:T(8,128)(2,1)}, u32[]{:S(2)}, u32[]{:S(2)}) collective-permute-start(bf16[64,64,256]{2,1,0:T(8,128)(2,1)} %bitcast.5.rest_0_.rows_ref), channel_id=1, source_target_pairs={{0,8},{1,9},{2,10},{3,11},{4,0},{5,1},{6,2},{7,3},{8,12},{9,13},{1... | collective-permute-start | bytes 6291464 | tf_op jit(solution)/shard_map/ppermute | solution.py:435
  13.8 1.5 collective-permute-start
  16.5 3.3 %all-to-all-start = ((s32[8,1,200]{2,1,0:T(1,128)}), s32[8,1,200]{2,1,0:T(1,128)S(1)}, u32[]{:S(2)}, u32[]{:S(2)}) async-start(s32[8,1,200]{2,1,0:T(1,128)} %broadcast_in_dim.108), calls=%async_computation | async-start | bytes 16384 | tf_op jit(solution)/shard_map/all_to_all | solution.py:450
  25.9 7.1 %keys_values.9.rest_0_ = bf16[392,64,512]{2,1,0:T(8,128)(2,1)} custom-call(bf16[64,64,256]{2,1,0:T(8,128)(2,1)} %bitcast.5.rest_0_.rows_ref, bf16[256,512]{1,0:T(8,128)(2,1)S(1)} %constant_dynamic-update-slice_fusion.w_ref), custom_call_target="tpu_custom_call" | custom-call | flops 6133333504 | tf_op jit(solution)/shard_map/keys_values/pallas_call | solution.py:174
  33.0 8.3 %queries.1.query_ref = bf16[64,256,256]{2,1,0:T(8,128)(2,1)} custom-call(bf16[4096,256]{1,0:T(8,128)(2,1)} %get-tuple-element.9.normed_ref, bf16[256,256]{1,0:T(8,128)(2,1)S(1)} %bitcast.13), custom_call_target="tpu_custom_call" | custom-call | flops 7474999808 | tf_op jit(solution)/shard_map/queries/pallas_call | solution.py:131
  41.4 20.4 %all-to-all-done = s32[8,1,200]{2,1,0:T(1,128)S(1)} async-done(((s32[8,1,200]{2,1,0:T(1,128)}), s32[8,1,200]{2,1,0:T(1,128)S(1)}, u32[]{:S(2)}, u32[]{:S(2)}) %all-to-all-start) | async-done | bytes 6432 | tf_op jit(solution)/shard_map/all_to_all | solution.py:450
  61.8 2.1 %pick_blocks.7 = (bf16[25,64,256]{2,1,0:T(8,128)(2,1)S(1)}, bf16[25,64,256]{2,1,0:T(8,128)(2,1)S(1)}) custom-call(s32[1]{0:T(128)} %bitcast.4.position_ref, s32[8,200]{1,0:T(8,128)S(1)} %bitcast.14, bf16[64,64,256]{2,1,0:T(8,128)(2,1)} %collective-permute-done.3.rest_0_.rows_ref), custom_call_target="tpu_custom_call" | custom-call | flops 1724999936 | tf_op jit(solution)/shard_map/pick_blocks/pallas_call | solution.py:104
  63.9 1.0 collective-permute-start.4
  64.9 2.1 %pick_blocks.5 = bf16[50,64,256]{2,1,0:T(8,128)(2,1)S(1)} custom-call(s32[1]{0:T(128)} %bitcast.4.position_ref, s32[8,200]{1,0:T(8,128)S(1)} %bitcast.15, bf16[64,64,256]{2,1,0:T(8,128)(2,1)} %bitcast.5.rest_0_.rows_ref, bf16[64,64,256]{2,1,0:T(8,128)(2,1)S(1)} %collective-permute-done.rest_1_.rest_0_.rows_ref), custom_call_target="tpu_custom_call" | custom-call | flops 1724999936 | tf_op jit(solution)/shard_map/pick_blocks/pallas_call | solution.py:104
  67.5 1.3 collective-permute-start.7
  68.8 4.7 %keys_values.10.rest_0_ = bf16[392,64,512]{2,1,0:T(8,128)(2,1)} custom-call(bf16[64,64,256]{2,1,0:T(8,128)(2,1)S(1)} %collective-permute-done.rest_1_.rest_0_.rows_ref, bf16[256,512]{1,0:T(8,128)(2,1)S(1)} %constant_dynamic-update-slice_fusion.w_ref, bf16[392,64,512]{2,1,0:T(8,128)(2,1)} %keys_values.9.rest_0_), custom_call_target="tpu_custom_call", output_to_operand_aliasing={{}: (2, {})} | custom-call | flops 6133333504 | tf_op jit(solution)/shard_map/keys_values/pallas_call | solution.py:174
  73.6 9.2 %collective-permute-done.4.rest_1_ = bf16[25,64,256]{2,1,0:T(8,128)(2,1)S(1)} collective-permute-done((bf16[25,64,256]{2,1,0:T(8,128)(2,1)S(1)}, bf16[25,64,256]{2,1,0:T(8,128)(2,1)S(1)}, u32[]{:S(2)}, u32[]{:S(2)}) %collective-permute-start.4) | collective-permute-done | bytes 819232 | tf_op jit(solution)/shard_map/ppermute | solution.py:435
  82.8 1.9 %pick_blocks.9 = bf16[25,64,256]{2,1,0:T(8,128)(2,1)S(1)} custom-call(s32[1]{0:T(128)} %bitcast.4.position_ref, s32[8,200]{1,0:T(8,128)S(1)} %bitcast.16, bf16[64,64,256]{2,1,0:T(8,128)(2,1)} %collective-permute-done.3.rest_0_.rows_ref, bf16[25,64,256]{2,1,0:T(8,128)(2,1)S(1)} %collective-permute-done.4.rest_1_), custom_call_target="tpu_custom_call" | custom-call | flops 1724999936 | tf_op jit(solution)/shard_map/pick_blocks/pallas_call | solution.py:104
  84.7 0.9 collective-permute-start.8
  85.6 7.0 %keys_values.11.rest_0_ = bf16[392,64,512]{2,1,0:T(8,128)(2,1)} custom-call(bf16[64,64,256]{2,1,0:T(8,128)(2,1)} %collective-permute-done.3.rest_0_.rows_ref, bf16[256,512]{1,0:T(8,128)(2,1)S(1)} %constant_dynamic-update-slice_fusion.w_ref, bf16[392,64,512]{2,1,0:T(8,128)(2,1)} %keys_values.10.rest_0_), custom_call_target="tpu_custom_call", output_to_operand_aliasing={{}: (2, {})} | custom-call | flops 6133333504 | tf_op jit(solution)/shard_map/keys_values/pallas_call | solution.py:174
  92.6 1.9 %pick_blocks.8 = bf16[25,64,256]{2,1,0:T(8,128)(2,1)S(1)} custom-call(s32[1]{0:T(128)} %bitcast.4.position_ref, s32[8,200]{1,0:T(8,128)S(1)} %bitcast.17, bf16[64,64,256]{2,1,0:T(8,128)(2,1)} %bitcast.5.rest_0_.rows_ref, bf16[25,64,256]{2,1,0:T(8,128)(2,1)S(1)} %collective-permute-done.4.rest_1_), custom_call_target="tpu_custom_call" | custom-call | flops 1724999936 | tf_op jit(solution)/shard_map/pick_blocks/pallas_call | solution.py:104
  95.2 1.3 collective-permute-start.6
  96.5 10.3 %collective-permute-done.1.rest_1_.rows_ref = bf16[50,64,256]{2,1,0:T(8,128)(2,1)S(1)} collective-permute-done((bf16[50,64,256]{2,1,0:T(8,128)(2,1)S(1)}, bf16[50,64,256]{2,1,0:T(8,128)(2,1)S(1)}, u32[]{:S(2)}, u32[]{:S(2)}) %collective-permute-start.1) | collective-permute-done | bytes 1638432 | tf_op jit(solution)/shard_map/ppermute | solution.py:435
  106.8 0.9 pick_blocks.6
  108.4 2.4 %keys_values.12.rest_0_ = bf16[392,64,512]{2,1,0:T(8,128)(2,1)} custom-call(bf16[25,64,256]{2,1,0:T(8,128)(2,1)S(1)} %collective-permute-done.8.rows_ref, bf16[256,512]{1,0:T(8,128)(2,1)S(1)} %constant_dynamic-update-slice_fusion.w_ref, bf16[392,64,512]{2,1,0:T(8,128)(2,1)} %keys_values.11.rest_0_), custom_call_target="tpu_custom_call", output_to_operand_aliasing={{}: (2, {})} | custom-call | flops 2395833344 | tf_op jit(solution)/shard_map/keys_values/pallas_call | solution.py:174
  110.8 3.6 %keys_values.13.rest_0_.buffer_ref = bf16[392,64,512]{2,1,0:T(8,128)(2,1)} custom-call(bf16[50,64,256]{2,1,0:T(8,128)(2,1)S(1)} %collective-permute-done.1.rest_1_.rows_ref, bf16[256,512]{1,0:T(8,128)(2,1)S(1)} %constant_dynamic-update-slice_fusion.w_ref, bf16[392,64,512]{2,1,0:T(8,128)(2,1)} %keys_values.12.rest_0_), custom_call_target="tpu_custom_call", output_to_operand_aliasing={{}: (2, {})} | custom-call | flops 4791666688 | tf_op jit(solution)/shard_map/keys_values/pallas_call | solution.py:174
  114.5 14.7 %attend_blocks.3.rest_0_ = bf16[64,64,256]{2,1,0:T(8,128)(2,1)} custom-call(s32[2]{0:T(128)S(1)} %pad_add_fusion.2.range_ref, s32[64]{0:T(128)S(1)} %select_reduce_fusion.2.order_ref, s32[192]{0:T(256)S(1)} %get-tuple-element.16.table_ref, bf16[64,256,256]{2,1,0:T(8,128)(2,1)} %queries.1.query_ref, bf16[392,64,512]{2,1,0:T(8,128)(2,1)} %keys_values.13.rest_0_.buffer_ref, ...), custom_call_target="tpu_custom_call" | custom-call | flops 23000000512 | tf_op jit(solution)/shard_map/attend_blocks/pallas_call | solution.py:342
  129.3 2.4 %keys_values.14.rest_0_ = bf16[392,64,512]{2,1,0:T(8,128)(2,1)} custom-call(bf16[25,64,256]{2,1,0:T(8,128)(2,1)S(1)} %collective-permute-done.7.rows_ref, bf16[256,512]{1,0:T(8,128)(2,1)S(1)} %constant_dynamic-update-slice_fusion.w_ref, bf16[392,64,512]{2,1,0:T(8,128)(2,1)} %keys_values.13.rest_0_.buffer_ref), custom_call_target="tpu_custom_call", output_to_operand_aliasing={{}: (2, {})} | custom-call | flops 2395833344 | tf_op jit(solution)/shard_map/keys_values/pallas_call | solution.py:174
  131.7 7.4 %collective-permute-done.6.rows_ref = bf16[25,64,256]{2,1,0:T(8,128)(2,1)S(1)} collective-permute-done((bf16[25,64,256]{2,1,0:T(8,128)(2,1)S(1)}, bf16[25,64,256]{2,1,0:T(8,128)(2,1)S(1)}, u32[]{:S(2)}, u32[]{:S(2)}) %collective-permute-start.6) | collective-permute-done | bytes 819232 | tf_op jit(solution)/shard_map/ppermute | solution.py:435
  139.1 2.4 %keys_values.15.rest_0_ = bf16[392,64,512]{2,1,0:T(8,128)(2,1)} custom-call(bf16[25,64,256]{2,1,0:T(8,128)(2,1)S(1)} %collective-permute-done.6.rows_ref, bf16[256,512]{1,0:T(8,128)(2,1)S(1)} %constant_dynamic-update-slice_fusion.w_ref, bf16[392,64,512]{2,1,0:T(8,128)(2,1)} %keys_values.14.rest_0_), custom_call_target="tpu_custom_call", output_to_operand_aliasing={{}: (2, {})} | custom-call | flops 2395833344 | tf_op jit(solution)/shard_map/keys_values/pallas_call | solution.py:174
  141.5 2.5 %keys_values.16.rest_0_.buffer_ref = bf16[392,64,512]{2,1,0:T(8,128)(2,1)} custom-call(bf16[25,64,256]{2,1,0:T(8,128)(2,1)S(1)} %collective-permute-done.5.rows_ref, bf16[256,512]{1,0:T(8,128)(2,1)S(1)} %constant_dynamic-update-slice_fusion.w_ref, bf16[392,64,512]{2,1,0:T(8,128)(2,1)} %keys_values.15.rest_0_), custom_call_target="tpu_custom_call", output_to_operand_aliasing={{}: (2, {})} | custom-call | flops 2395833344 | tf_op jit(solution)/shard_map/keys_values/pallas_call | solution.py:174
  144.0 29.0 %attend_blocks.4.rest_0_ = bf16[64,64,256]{2,1,0:T(8,128)(2,1)} custom-call(s32[2]{0:T(128)S(1)} %pad_add_fusion.1.range_ref, s32[64]{0:T(128)S(1)} %select_reduce_fusion.2.order_ref, s32[192]{0:T(256)S(1)} %get-tuple-element.16.table_ref, bf16[64,256,256]{2,1,0:T(8,128)(2,1)} %queries.1.query_ref, ...), custom_call_target="tpu_custom_call", output_to_operand_aliasing={{}: (8, {})} | custom-call | flops 23000000512 | tf_op jit(solution)/shard_map/attend_blocks/pallas_call | solution.py:342
  173.1 2.4 %keys_values.17.buffer_ref = bf16[392,64,512]{2,1,0:T(8,128)(2,1)} custom-call(bf16[25,64,256]{2,1,0:T(8,128)(2,1)S(1)} %collective-permute-done.2.rows_ref, bf16[256,512]{1,0:T(8,128)(2,1)S(1)} %constant_dynamic-update-slice_fusion.w_ref, bf16[392,64,512]{2,1,0:T(8,128)(2,1)} %keys_values.16.rest_0_.buffer_ref), custom_call_target="tpu_custom_call", output_to_operand_aliasing={{}: (2, {})} | custom-call | flops 2395833344 | tf_op jit(solution)/shard_map/keys_values/pallas_call | solution.py:174
  175.5 1.0 attend_blocks.5
  (43 shorter events, 4.4 us)
Async XLA Ops:
  0.0 0.7 copy-start.2
  0.7 14.6 %copy-start.8 = (s32[64,3]{0,1:T(4,128)S(1)}, s32[64,3]{0,1:T(4,128)}, u32[]{:S(2)}) copy-start(s32[64,3]{0,1:T(4,128)} %param.10) | copy-start | bytes 2308
  0.7 24.7 %copy-start.5 = (bf16[256,256]{1,0:T(8,128)(2,1)S(1)}, bf16[256,256]{1,0:T(8,128)(2,1)}, u32[]{:S(2)}) copy-start(bf16[256,256]{1,0:T(8,128)(2,1)} %param.11) | copy-start | bytes 393220
  0.7 25.1 %copy-start.6 = (bf16[256,256]{1,0:T(8,128)(2,1)S(1)}, bf16[256,256]{1,0:T(8,128)(2,1)}, u32[]{:S(2)}) copy-start(bf16[256,256]{1,0:T(8,128)(2,1)} %param.12) | copy-start | bytes 393220
  0.7 25.2 %copy-start.7 = (bf16[256,256]{1,0:T(8,128)(2,1)S(1)}, bf16[256,256]{1,0:T(8,128)(2,1)}, u32[]{:S(2)}) copy-start(bf16[256,256]{1,0:T(8,128)(2,1)} %param.13) | copy-start | bytes 393220
  8.4 1.3 copy-start.3
  9.7 52.1 %collective-permute-start.3 = (bf16[64,64,256]{2,1,0:T(8,128)(2,1)}, bf16[64,64,256]{2,1,0:T(8,128)(2,1)}, u32[]{:S(2)}, u32[]{:S(2)}) collective-permute-start(bf16[64,64,256]{2,1,0:T(8,128)(2,1)} %bitcast.5.rest_0_.rows_ref), channel_id=1, source_target_pairs={{0,8},{1,9},{2,10},{3,11},{4,0},{5,1},{6,2},{7,3},{8,12},{9,13},{1... | collective-permute-start | bytes 6291464 | tf_op jit(solution)/shard_map/ppermute | solution.py:435
  13.8 51.1 %collective-permute-start = (bf16[64,64,256]{2,1,0:T(8,128)(2,1)}, bf16[64,64,256]{2,1,0:T(8,128)(2,1)S(1)}, u32[]{:S(2)}, u32[]{:S(2)}) collective-permute-start(bf16[64,64,256]{2,1,0:T(8,128)(2,1)} %bitcast.5.rest_0_.rows_ref), channel_id=1, source_target_pairs={{0,2},{1,3},{2,0},{3,1},{4,6},{5,7},{6,4},{7,5},{8,10},{9,11},{10,... | collective-permute-start | bytes 6291464 | tf_op jit(solution)/shard_map/ppermute | solution.py:435
  16.5 45.3 %all-to-all-start = ((s32[8,1,200]{2,1,0:T(1,128)}), s32[8,1,200]{2,1,0:T(1,128)S(1)}, u32[]{:S(2)}, u32[]{:S(2)}) async-start(s32[8,1,200]{2,1,0:T(1,128)} %broadcast_in_dim.108), calls=%async_computation | async-start | bytes 16384 | tf_op jit(solution)/shard_map/all_to_all | solution.py:450
  63.9 18.9 %collective-permute-start.4 = (bf16[25,64,256]{2,1,0:T(8,128)(2,1)S(1)}, bf16[25,64,256]{2,1,0:T(8,128)(2,1)S(1)}, u32[]{:S(2)}, u32[]{:S(2)}) collective-permute-start(bf16[25,64,256]{2,1,0:T(8,128)(2,1)S(1)} %get-tuple-element.10), channel_id=1, source_target_pairs={{0,2},{1,3},{2,0},{3,1},{4,6},{5,7},{6,4},{7,5},{8,10},{9,11},{10,... | collective-permute-start | bytes 2457608 | tf_op jit(solution)/shard_map/ppermute | solution.py:435
  67.0 39.7 %collective-permute-start.1 = (bf16[50,64,256]{2,1,0:T(8,128)(2,1)S(1)}, bf16[50,64,256]{2,1,0:T(8,128)(2,1)S(1)}, u32[]{:S(2)}, u32[]{:S(2)}) collective-permute-start(bf16[50,64,256]{2,1,0:T(8,128)(2,1)S(1)} %pick_blocks.5), channel_id=1, source_target_pairs={{0,4},{1,5},{2,6},{3,7},{4,12},{5,13},{6,14},{7,15},{8,0},{9,1},{1... | collective-permute-start | bytes 4915208 | tf_op jit(solution)/shard_map/ppermute | solution.py:435
  67.5 61.7 %collective-permute-start.7 = (bf16[25,64,256]{2,1,0:T(8,128)(2,1)S(1)}, bf16[25,64,256]{2,1,0:T(8,128)(2,1)S(1)}, u32[]{:S(2)}, u32[]{:S(2)}) collective-permute-start(bf16[25,64,256]{2,1,0:T(8,128)(2,1)S(1)} %get-tuple-element.11), channel_id=1, source_target_pairs={{8,12},{9,13},{10,14},{11,15},{4,0},{5,1},{6,2},{7,3},{24,28},{25,... | collective-permute-start | bytes 2457608 | tf_op jit(solution)/shard_map/ppermute | solution.py:435
  84.7 23.7 %collective-permute-start.8 = (bf16[25,64,256]{2,1,0:T(8,128)(2,1)S(1)}, bf16[25,64,256]{2,1,0:T(8,128)(2,1)S(1)}, u32[]{:S(2)}, u32[]{:S(2)}) collective-permute-start(bf16[25,64,256]{2,1,0:T(8,128)(2,1)S(1)} %pick_blocks.9), channel_id=1, source_target_pairs={{0,2},{1,3},{2,0},{3,1},{4,6},{5,7},{6,4},{7,5},{8,10},{9,11},{10,... | collective-permute-start | bytes 2457608 | tf_op jit(solution)/shard_map/ppermute | solution.py:435
  94.5 47.0 %collective-permute-start.5 = (bf16[25,64,256]{2,1,0:T(8,128)(2,1)S(1)}, bf16[25,64,256]{2,1,0:T(8,128)(2,1)S(1)}, u32[]{:S(2)}, u32[]{:S(2)}) collective-permute-start(bf16[25,64,256]{2,1,0:T(8,128)(2,1)S(1)} %pick_blocks.8), channel_id=1, source_target_pairs={{4,8},{5,9},{6,10},{7,11},{8,4},{9,5},{10,6},{11,7},{20,24},{21,25... | collective-permute-start | bytes 2457608 | tf_op jit(solution)/shard_map/ppermute | solution.py:435
  95.2 43.9 %collective-permute-start.6 = (bf16[25,64,256]{2,1,0:T(8,128)(2,1)S(1)}, bf16[25,64,256]{2,1,0:T(8,128)(2,1)S(1)}, u32[]{:S(2)}, u32[]{:S(2)}) collective-permute-start(bf16[25,64,256]{2,1,0:T(8,128)(2,1)S(1)} %collective-permute-done.4.rest_1_), channel_id=1, source_target_pairs={{8,12},{9,13},{10,14},{11,15},{4,0},{5,1},{6,2},{7,3},{24,28},{25,... | collective-permute-start | bytes 2457608 | tf_op jit(solution)/shard_map/ppermute | solution.py:435
  107.7 65.4 %collective-permute-start.2 = (bf16[25,64,256]{2,1,0:T(8,128)(2,1)S(1)}, bf16[25,64,256]{2,1,0:T(8,128)(2,1)S(1)}, u32[]{:S(2)}, u32[]{:S(2)}) collective-permute-start(bf16[25,64,256]{2,1,0:T(8,128)(2,1)S(1)} %pick_blocks.6), channel_id=1, source_target_pairs={{4,8},{5,9},{6,10},{7,11},{8,4},{9,5},{10,6},{11,7},{20,24},{21,25... | collective-permute-start | bytes 2457608 | tf_op jit(solution)/shard_map/ppermute | solution.py:435
  110.8 3.7 %copy-start = (bf16[256,256]{1,0:T(8,128)(2,1)S(1)}, bf16[256,256]{1,0:T(8,128)(2,1)}, u32[]{:S(2)}) copy-start(bf16[256,256]{1,0:T(8,128)(2,1)} %out_w_ref.5) | copy-start | bytes 393220
  110.8 3.7 %copy-start.1 = (bf16[256,256]{1,0:T(8,128)(2,1)S(1)}, bf16[256,256]{1,0:T(8,128)(2,1)}, u32[]{:S(2)}) copy-start(bf16[256,256]{1,0:T(8,128)(2,1)} %mix_ref.5) | copy-start | bytes 393220
  110.8 3.7 %copy-start.4 = (bf16[4096,256]{1,0:T(8,128)(2,1)S(1)}, bf16[4096,256]{1,0:T(8,128)(2,1)}, u32[]{:S(2)}) copy-start(bf16[4096,256]{1,0:T(8,128)(2,1)} %copy-done.3) | copy-start | bytes 6291460

commit v9 on v8

--- a/solution.py
+++ b/solution.py
@@ -143,45 +143,34 @@
     )(normed, w_query.T)
 
 
-def key_value_kernel(rows_ref, w_ref, *rest):
-    out_ref = rest[-1]
-    blocks, cluster, width = rows_ref.shape
-    per = max(n for n in range(1, 9) if blocks % n == 0)
-
-    def some(at, carry):
-        here = pl.ds(at * per, per)
-        rows = rows_ref[here].reshape(per * cluster, width)
-        both = jnp.dot(rows, w_ref[...], preferred_element_type=jnp.float32)
-        out_ref[here] = both.astype(jnp.bfloat16).reshape((per,) + out_ref.shape[1:])
-        return carry
-
-    lax.fori_loop(0, blocks // per, some, 0)
-
-
-def project_pairs(piece, w_both, so_far, at, total):
-    blocks, cluster, width = piece.shape
-    per = max(n for n in range(1, 26) if blocks % n == 0 and at % n == 0)
-    in_specs = [
-        pl.BlockSpec((per, cluster, width), lambda i: (i, 0, 0)),
-        pl.BlockSpec((width, 2 * width), lambda i: (0, 0)),
+def collect_kernel(*refs, places):
+    buffer_ref, sems = refs[-2:]
+    copy_pieces(refs[: len(places)], buffer_ref, places, sems)
+
+
+def copy_pieces(piece_refs, buffer_ref, places, sems):
+    copies = [
+        pltpu.make_async_copy(piece, buffer_ref.at[pl.ds(at, piece.shape[0])], sems.at[n])
+        for n, (piece, at) in enumerate(zip(piece_refs, places, strict=True))
     ]
-    operands = [piece, w_both]
-    aliases = {}
-    if so_far is not None:
-        in_specs.append(pl.BlockSpec(memory_space=pl.ANY))
-        operands.append(so_far)
-        aliases = {2: 0}
+    for copy in copies:
+        copy.start()
+    for copy in copies:
+        copy.wait()
+
+
+def collect(pieces, places, total):
+    hbm = pl.BlockSpec(memory_space=pl.ANY)
     return pl.pallas_call(
-        key_value_kernel,
-        grid=(blocks // per,),
-        in_specs=in_specs,
-        out_specs=pl.BlockSpec((per, cluster, 2 * width), lambda i: (at // per + i, 0, 0)),
-        out_shape=jax.ShapeDtypeStruct((total, cluster, 2 * width), jnp.bfloat16),
-        input_output_aliases=aliases,
-        cost_estimate=lasting(blocks / 12),
+        functools.partial(collect_kernel, places=places),
+        in_specs=[hbm] * len(pieces),
+        out_specs=hbm,
+        out_shape=jax.ShapeDtypeStruct((total,) + pieces[0].shape[1:], pieces[0].dtype),
+        scratch_shapes=[pltpu.SemaphoreType.DMA((len(pieces),))],
+        cost_estimate=lasting(4),
         compiler_params=kernel_params(),
-        name="keys_values",
-    )(*operands)
+        name="collect_blocks",
+    )(*pieces)
 
 
 def attend_kernel(
@@ -189,27 +178,29 @@
     order_ref,
     table_ref,
     query_ref,
-    buffer_ref,
     placed_ref,
-    out_w_ref,
-    mix_ref,
     *rest,
     own_at,
     head_width,
+    places,
 ):
-    mixed_ref, query_buf, pair_buf, placed_buf, done_buf, in_sems, out_sems = rest[-7:]
+    weight_refs, rest = rest[:4], rest[4:]
+    piece_refs = rest[: len(places)]
+    mixed_ref, buffer_ref, query_buf, member_buf, placed_buf = rest[-11:-6]
+    attended_buf, before_buf, done_buf, in_sems, out_sems, piece_sems = rest[-6:]
     begin, count = range_ref[0], range_ref[1]
-    pair_count = pair_buf.shape[2] - 1
+    pair_count = member_buf.shape[2] - 1
+    copy_pieces(piece_refs, buffer_ref, places, piece_sems)
 
     def fetches(step, slot):
         for j in range(STEP):
             block = order_ref[step * STEP + j]
             sources = [(query_ref.at[block], query_buf.at[slot, j])]
             sources.append((placed_ref.at[block], placed_buf.at[slot, j]))
-            sources.append((buffer_ref.at[own_at + block], pair_buf.at[slot, j, 0]))
+            sources.append((buffer_ref.at[own_at + block], member_buf.at[slot, j, 0]))
             for n in range(pair_count):
                 listed = table_ref[block * pair_count + n]
-                sources.append((buffer_ref.at[listed], pair_buf.at[slot, j, 1 + n]))
+                sources.append((buffer_ref.at[listed], member_buf.at[slot, j, 1 + n]))
             for n, (source_, target) in enumerate(sources):
                 sem = in_sems.at[slot, j * (pair_count + 3) + n]
                 yield pltpu.make_async_copy(source_, target, sem)
@@ -218,6 +209,9 @@
         for j in range(STEP):
             target = mixed_ref.at[order_ref[step * STEP + j]]
             yield pltpu.make_async_copy(done_buf.at[j], target, out_sems.at[j])
+
+    def finish():
+        return finish_step(before_buf[...], attended_buf[...], *weight_refs[2:])
 
     def one_step(i, carry):
         slot = i % 2
@@ -225,39 +219,61 @@
             copy.start()
         for copy in fetches(begin + i, slot):
             copy.wait()
-        mixed = attend_step(
-            query_buf.at[slot],
-            pair_buf.at[slot],
-            placed_buf.at[slot],
-            out_w_ref,
-            mix_ref,
-            head_width,
+        attended, mixed = attend_step(
+            query_buf.at[slot], member_buf.at[slot], *weight_refs[:2], head_width, finish
         )
+
+        @pl.when(i > 1)
+        def _():
+            for copy in stores(begin + i - 2):
+                copy.wait()
+
+        done_buf[...] = mixed.reshape(done_buf.shape)
+        attended_buf[...] = attended
+        before_buf[...] = placed_buf[slot].reshape(before_buf.shape)
 
         @pl.when(i > 0)
         def _():
             for copy in stores(begin + i - 1):
-                copy.wait()
-
-        done_buf[...] = mixed.reshape(done_buf.shape)
-        for copy in stores(begin + i):
-            copy.start()
+                copy.start()
+
         return carry
 
     @pl.when(count > 0)
     def _():
         for copy in fetches(begin, 0):
             copy.start()
+        attended_buf[...] = jnp.zeros_like(attended_buf)
+        before_buf[...] = jnp.zeros_like(before_buf)
         lax.fori_loop(0, count, one_step, 0)
         for copy in fetches(begin + count - 1, count % 2):
             copy.wait()
+        mixed = finish()
+
+        @pl.when(count > 1)
+        def _():
+            for copy in stores(begin + count - 2):
+                copy.wait()
+
+        done_buf[...] = mixed.reshape(done_buf.shape)
+        for copy in stores(begin + count - 1):
+            copy.start()
         for copy in stores(begin + count - 1):
             copy.wait()
 
 
-def attend_step(query_ref, pair_ref, placed_ref, out_w_ref, mix_ref, head_width):
-    _, members_count, cluster, _ = pair_ref.shape
-    width = placed_ref.shape[2]
+def finish_step(placed, attended, out_w_ref, mix_ref):
+    middle = placed.astype(jnp.float32) + jnp.dot(
+        attended, out_w_ref[...], preferred_element_type=jnp.float32
+    )
+    middle = middle.astype(jnp.bfloat16).astype(jnp.float32)
+    second = layer_norm(middle).astype(jnp.bfloat16)
+    mixed = middle + jnp.tanh(jnp.dot(second, mix_ref[...], preferred_element_type=jnp.float32))
+    return mixed.astype(jnp.bfloat16)
+
+
+def attend_step(query_ref, member_ref, key_w_ref, value_w_ref, head_width, meanwhile):
+    _, members_count, cluster, width = member_ref.shape
     span = GROUP * head_width
     tile = GROUP * cluster
     diagonal = head_mask((span, tile), head_width, cluster)
@@ -271,9 +287,11 @@
     keys, values = {}, {}
 
     def gather(block):
-        members = [pair_ref[block, n] for n in range(members_count)]
-        keys[block] = jnp.concatenate([m[:, :width] for m in members], axis=0)
-        values[block] = jnp.concatenate([m[:, width:] for m in members], axis=0).T
+        members = member_ref[block].reshape(members_count * cluster, width)
+        key = jnp.dot(members, key_w_ref[...], preferred_element_type=jnp.float32)
+        keys[block] = key.astype(jnp.bfloat16)
+        value = lax.dot_general(value_w_ref[...], members, NT, preferred_element_type=jnp.float32)
+        values[block] = value.astype(jnp.bfloat16)
 
     def scores_of(block, t):
         if t == 0:
@@ -303,6 +321,8 @@
     count = len(units)
     scores, weights, products, pieces, attended = {}, {}, {}, [], []
     for at in range(-SCORES_AHEAD, count + 1):
+        if at == 0:
+            other = meanwhile()
         if at + SCORES_AHEAD < count:
             scores[at + SCORES_AHEAD] = scores_of(*units[at + SCORES_AHEAD])
         if 0 <= at + WEIGHTS_AHEAD < count:
@@ -316,44 +336,46 @@
                 folded = lax.dot_general(fold, stacked, NT, preferred_element_type=jnp.float32)
                 attended.append(folded.astype(jnp.bfloat16))
                 pieces = []
-    placed = placed_ref[...].reshape(STEP * cluster, width)
-    middle = placed.astype(jnp.float32) + jnp.dot(
-        jnp.concatenate(attended, axis=0), out_w_ref[...], preferred_element_type=jnp.float32
-    )
-    middle = middle.astype(jnp.bfloat16).astype(jnp.float32)
-    second = layer_norm(middle).astype(jnp.bfloat16)
-    mixed = middle + jnp.tanh(jnp.dot(second, mix_ref[...], preferred_element_type=jnp.float32))
-    return mixed.astype(jnp.bfloat16)
-
-
-def attend(begin, count, order, table, queries, buffer, own_at, placed, w_out, w_mix, so_far=None):
+    return jnp.concatenate(attended, axis=0), other
+
+
+def attend(begin, count, order, table, queries, placed, weights, buffer, pieces, places, own_at, so_far):
     blocks, cluster, width = placed.shape
     pair_count = table.shape[0] // blocks
     smem = pl.BlockSpec(memory_space=pltpu.SMEM)
     vmem = pl.BlockSpec(memory_space=pltpu.VMEM)
     hbm = pl.BlockSpec(memory_space=pl.ANY)
-    in_specs = [smem, smem, smem, hbm, hbm, hbm, vmem, vmem]
-    operands = [queries, buffer, placed, w_out, w_mix]
-    aliases = {}
+    in_specs = [smem, smem, smem, hbm, hbm] + [vmem] * 4 + [hbm] * (len(pieces) + 1)
+    aliases = {len(in_specs) - 1: 1}
+    operands = [queries, placed, *weights, *pieces, buffer]
     if so_far is not None:
-        aliases = {len(in_specs): 0}
+        aliases[len(in_specs)] = 0
         in_specs.append(hbm)
         operands.append(so_far)
+    kernel = functools.partial(
+        attend_kernel, own_at=own_at, head_width=width // HEADS, places=places
+    )
     return pl.pallas_call(
-        functools.partial(attend_kernel, own_at=own_at, head_width=width // HEADS),
+        kernel,
         in_specs=in_specs,
-        out_specs=hbm,
-        out_shape=jax.ShapeDtypeStruct(placed.shape, jnp.bfloat16),
+        out_specs=[hbm, hbm],
+        out_shape=[
+            jax.ShapeDtypeStruct(placed.shape, jnp.bfloat16),
+            jax.ShapeDtypeStruct(buffer.shape, jnp.bfloat16),
+        ],
         scratch_shapes=[
             pltpu.VMEM((2, STEP) + queries.shape[1:], jnp.bfloat16),
-            pltpu.VMEM((2, STEP, pair_count + 1, cluster, 2 * width), jnp.bfloat16),
+            pltpu.VMEM((2, STEP, pair_count + 1, cluster, width), jnp.bfloat16),
             pltpu.VMEM((2, STEP, cluster, width), jnp.bfloat16),
+            pltpu.VMEM((STEP * cluster, width), jnp.bfloat16),
+            pltpu.VMEM((STEP * cluster, width), jnp.bfloat16),
             pltpu.VMEM((STEP, cluster, width), jnp.bfloat16),
             pltpu.SemaphoreType.DMA((2, STEP * (pair_count + 3))),
             pltpu.SemaphoreType.DMA((STEP,)),
+            pltpu.SemaphoreType.DMA((len(pieces),)),
         ],
         input_output_aliases=aliases,
-        cost_estimate=lasting(20),
+        cost_estimate=lasting(18),
         compiler_params=kernel_params(),
         name="attend_blocks",
     )(jnp.stack([begin, count]).astype(jnp.int32), order, table, *operands)
@@ -461,13 +483,11 @@
     passed = moved(blocks, first_moves)
     beside = moved(blocks, swap)
 
-    w_both = jnp.concatenate([w_key, w_value], axis=1)
-    own_at = 8 * capacity
+    queries = project_queries(normed, w_query, cluster)
+    own_at = 7 * capacity
     passed_at = own_at + block_count
     beside_at = passed_at + block_count
     total = beside_at + block_count
-    buffer = project_pairs(blocks, w_both, None, own_at, total)
-    queries = project_queries(normed, w_query, cluster)
 
     (second,) = pick(at_position, wanted, (blocks, beside), SECOND_PLAN)
     second = moved(second, second_moves)
@@ -484,10 +504,7 @@
     )
     middle_cross = moved(middle_cross, middle_moves)
 
-    buffer = project_pairs(beside, w_both, buffer, beside_at, total)
-    buffer = project_pairs(passed, w_both, buffer, passed_at, total)
-    buffer = project_pairs(near, w_both, buffer, 0, total)
-    buffer = project_pairs(second, w_both, buffer, capacity, total)
+    buffer = collect((blocks, passed, beside), (own_at, passed_at, beside_at), total)
 
     z, y = position // 2, position % 2
     is_end = (z == 0) | (z == LEVELS - 1)
@@ -511,14 +528,18 @@
     order, ends = by_class(jnp.max(arrival.reshape(block_count, pair_count), axis=1), 2)
     marks = [0, ends[0] // STEP, ends[1] // STEP, block_count // STEP]
     phases = [(marks[n], marks[n + 1] - marks[n]) for n in range(3)]
-    shared = (order, table, queries)
-    rest = (own_at, placed.reshape(blocks.shape), w_out, w_mix)
-    mixed = attend(*phases[0], *shared, buffer, *rest)
-    for piece, at in ((outward, 3), (on, 4), (middle, 5)):
-        buffer = project_pairs(piece, w_both, buffer, at * capacity, total)
-    mixed = attend(*phases[1], *shared, buffer, *rest, so_far=mixed)
-    buffer = project_pairs(middle_cross, w_both, buffer, 6 * capacity, total)
-    mixed = attend(*phases[2], *shared, buffer, *rest, so_far=mixed)
+    weights = (w_key, w_value.T, w_out, w_mix)
+    shared = (order, table, queries, placed.reshape(blocks.shape), weights)
+    arrivals = (
+        ((near, 0), (second, 1)),
+        ((outward, 3), (on, 4), (middle, 5)),
+        ((middle_cross, 6),),
+    )
+    mixed = None
+    for phase, arrived in zip(phases, arrivals, strict=True):
+        pieces = [piece for piece, _ in arrived]
+        places = tuple(at * capacity for _, at in arrived)
+        mixed, buffer = attend(*phase, *shared, buffer, pieces, places, own_at, mixed)
     return mixed.reshape(rows_dev, width)
 
 

time: 177 us -> 351 us (1.98)
  the two profiles are of different devices: /device:TPU:0 before, /device:TPU:8 now
where the time goes in v9:
time: 351 us; the launch traced here: 350 us
  Pallas kernels  277 us (79%)
  waiting for transfers between devices  39.4 us (11%)
  starting transfers between devices  21.9 us (6%)
  between operations  5.22 us (1%)
  local copies, waits for them, and re-layouts  4.71 us (1%)
    pallas_call x1, Pallas kernels, collect(): pl.pallas_call(functools.partial(collect_kernel, places=places), in_specs...  192 us
    pallas_call x3, Pallas kernels, attend(): pl.pallas_call(kernel, in_specs=in_specs, out_specs=[hbm, hbm], out_shape...  58.7 us
    all_to_all x1, waiting for transfers between devices, body(): lax.all_to_all(jnp.broadcast_to(tables[None], (SPAN, SPAN * capacity)), '...  34.4 us
    ppermute x9, starting transfers between devices, moved(): return lax.ppermute(x, 'elec', pairs_of)  16.1 us
    pallas_call x5, Pallas kernels, pick(): pl.pallas_call(functools.partial(pick_kernel, plan=plan, capacity=capacit...  10.7 us
    pallas_call x1, Pallas kernels, project_queries(): pl.pallas_call(functools.partial(query_kernel, cluster=cluster, head_widt...  8.29 us
    pallas_call x1, Pallas kernels, place(): pl.pallas_call(place_kernel, grid=(walkers,), in_specs=[local, pl.BlockSp...  7.69 us
  transfers between devices with their start and end apart: 10, of which 2 were waited for; matrix products, arithmetic and copies ran while one was open for 1% of the time, Pallas kernels for 71%

profile of v9, /device:TPU:8, one launch (start us, length us, event | category | flops | bytes accessed | tf_op | source)
XLA Modules:
  0.0 350.0 jit_solution(10634489908862547096)
XLA Ops:
  0.0 0.7 copy-done.5
  0.7 7.7 %place_rows.1 = (bf16[4096,256]{1,0:T(8,128)(2,1)S(1)}, bf16[4096,256]{1,0:T(8,128)(2,1)}) custom-call(bf16[4096,256]{1,0:T(8,128)(2,1)} %features_ref.1, s32[8,1,512]{2,1,0:T(1,128)S(1)} %bitcast.23), custom_call_target="tpu_custom_call" | custom-call | flops 8049999872 | tf_op jit(solution)/shard_map/place_rows/pallas_call | solution.py:63
  8.4 1.3 copy-done.6
  9.8 2.0 collective-permute-start
  11.8 0.1 reshape.148
  12.0 0.2 select_reduce_fusion.1
  12.2 0.1 select_reduce_fusion
  12.3 0.6 broadcast_in_dim.108
  12.9 5.8 %all-to-all-start = ((s32[8,1,200]{2,1,0:T(1,128)}), s32[8,1,200]{2,1,0:T(1,128)S(1)}, u32[]{:S(2)}, u32[]{:S(2)}) async-start(s32[8,1,200]{2,1,0:T(1,128)} %broadcast_in_dim.108), calls=%async_computation | async-start | bytes 16384 | tf_op jit(solution)/shard_map/all_to_all | solution.py:472
  18.8 0.7 fusion.14
  24.4 0.2 select_reduce_fusion.3
  24.6 0.1 select_reduce_fusion.2.order_ref
  25.0 34.4 %all-to-all-done = s32[8,1,200]{2,1,0:T(1,128)S(1)} async-done(((s32[8,1,200]{2,1,0:T(1,128)}), s32[8,1,200]{2,1,0:T(1,128)S(1)}, u32[]{:S(2)}, u32[]{:S(2)}) %all-to-all-start) | async-done | bytes 6432 | tf_op jit(solution)/shard_map/all_to_all | solution.py:472
  59.5 2.1 pick_blocks.7
  61.6 0.6 collective-permute-start.5
  62.2 2.9 pick_blocks.5
  65.1 2.4 collective-permute-start.1
  67.6 8.3 %queries.1.query_ref = bf16[64,256,256]{2,1,0:T(8,128)(2,1)} custom-call(bf16[4096,256]{1,0:T(8,128)(2,1)} %get-tuple-element.14.normed_ref, bf16[256,256]{1,0:T(8,128)(2,1)S(1)} %bitcast.17), custom_call_target="tpu_custom_call" | custom-call | flops 7474999808 | tf_op jit(solution)/shard_map/queries/pallas_call | solution.py:131
  75.9 5.0 %collective-permute-done.5.rest_1_ = bf16[25,64,256]{2,1,0:T(8,128)(2,1)S(1)} collective-permute-done((bf16[25,64,256]{2,1,0:T(8,128)(2,1)S(1)}, bf16[25,64,256]{2,1,0:T(8,128)(2,1)S(1)}, u32[]{:S(2)}, u32[]{:S(2)}) %collective-permute-start.5) | collective-permute-done | bytes 819232 | tf_op jit(solution)/shard_map/ppermute | solution.py:457
  80.8 2.8 pick_blocks.9
  83.6 0.5 collective-permute-start.8
  84.2 3.2 collective-permute-start.4
  87.5 191.7 %collect_blocks.1.rest_6_ = bf16[367,64,256]{2,1,0:T(8,128)(2,1)} custom-call(bf16[64,64,256]{2,1,0:T(8,128)(2,1)} %bitcast.7.rest_0_.refs_0_, bf16[64,64,256]{2,1,0:T(8,128)(2,1)} %collective-permute-done.3.rest_0_.refs_1_, bf16[64,64,256]{2,1,0:T(8,128)(2,1)} %copy-done), custom_call_target="tpu_custom_call" | custom-call | flops 4600000000 | tf_op jit(solution)/shard_map/collect_blocks/pallas_call | solution.py:164
  279.2 2.0 pick_blocks.8
  281.3 3.3 collective-permute-start.7
  284.6 1.3 collective-permute-start.6
  285.9 0.9 pick_blocks.6
  286.9 2.7 collective-permute-start.2
  289.6 24.4 %attend_blocks.3 = (bf16[64,64,256]{2,1,0:T(8,128)(2,1)}, bf16[367,64,256]{2,1,0:T(8,128)(2,1)}) custom-call(s32[2]{0:T(128)S(1)} %pad_add_fusion.2.range_ref, s32[64]{0:T(128)S(1)} %select_reduce_fusion.2.order_ref, s32[192]{0:T(256)S(1)} %get-tuple-element.26.table_ref, bf16[64,256,256]{2,1,0:T(8,128)(2,1)} %queries.1.query_ref, ...), custom_call_target="tpu_custom_call", output_to_operand_aliasing={{1}: (11, {})} | custom-call | flops 20700000256 | tf_op jit(solution)/shard_map/attend_blocks/pallas_call | solution.py:358
  314.1 1.6 copy-done.8
  315.7 13.2 %attend_blocks.4 = (bf16[64,64,256]{2,1,0:T(8,128)(2,1)}, bf16[367,64,256]{2,1,0:T(8,128)(2,1)}) custom-call(s32[2]{0:T(128)S(1)} %pad_add_fusion.1.range_ref, s32[64]{0:T(128)S(1)} %select_reduce_fusion.2.order_ref, s32[192]{0:T(256)S(1)} %get-tuple-element.26.table_ref, ...), custom_call_target="tpu_custom_call", output_to_operand_aliasing={{1}: (12, {}), {0}: (13, {})} | custom-call | flops 20700000256 | tf_op jit(solution)/shard_map/attend_blocks/pallas_call | solution.py:358
  328.9 21.1 %attend_blocks.5 = (bf16[64,64,256]{2,1,0:T(8,128)(2,1)}, bf16[367,64,256]{2,1,0:T(8,128)(2,1)}) custom-call(s32[2]{0:T(128)S(1)} %pad_add_fusion.range_ref, s32[64]{0:T(128)S(1)} %select_reduce_fusion.2.order_ref, s32[192]{0:T(256)S(1)} %get-tuple-element.26.table_ref, ...), custom_call_target="tpu_custom_call", output_to_operand_aliasing={{1}: (10, {}), {0}: (11, {})} | custom-call | flops 20700000256 | tf_op jit(solution)/shard_map/attend_blocks/pallas_call | solution.py:358
  (40 shorter events, 0.7 us)
Async XLA Ops:
  0.0 0.7 copy-start.5
  0.7 11.0 %copy-start.11 = (s32[64,3]{0,1:T(4,128)S(1)}, s32[64,3]{0,1:T(4,128)}, u32[]{:S(2)}) copy-start(s32[64,3]{0,1:T(4,128)} %param.10) | copy-start | bytes 2308
  0.7 24.1 %copy-start.9 = (bf16[256,256]{1,0:T(8,128)(2,1)S(1)}, bf16[256,256]{1,0:T(8,128)(2,1)}, u32[]{:S(2)}) copy-start(bf16[256,256]{1,0:T(8,128)(2,1)} %param.11) | copy-start | bytes 393220
  0.7 24.2 %copy-start.10 = (bf16[256,256]{1,0:T(8,128)(2,1)S(1)}, bf16[256,256]{1,0:T(8,128)(2,1)}, u32[]{:S(2)}) copy-start(bf16[256,256]{1,0:T(8,128)(2,1)} %param.13) | copy-start | bytes 393220
  8.4 1.3 copy-start.6
  9.7 49.7 %collective-permute-start.3 = (bf16[64,64,256]{2,1,0:T(8,128)(2,1)}, bf16[64,64,256]{2,1,0:T(8,128)(2,1)}, u32[]{:S(2)}, u32[]{:S(2)}) collective-permute-start(bf16[64,64,256]{2,1,0:T(8,128)(2,1)} %bitcast.7.rest_0_.refs_0_), channel_id=1, source_target_pairs={{0,8},{1,9},{2,10},{3,11},{4,0},{5,1},{6,2},{7,3},{8,12},{9,13},{1... | collective-permute-start | bytes 6291464 | tf_op jit(solution)/shard_map/ppermute | solution.py:457
  9.8 52.4 %collective-permute-start = (bf16[64,64,256]{2,1,0:T(8,128)(2,1)}, bf16[64,64,256]{2,1,0:T(8,128)(2,1)S(1)}, u32[]{:S(2)}, u32[]{:S(2)}) collective-permute-start(bf16[64,64,256]{2,1,0:T(8,128)(2,1)} %bitcast.7.rest_0_.refs_0_), channel_id=1, source_target_pairs={{0,2},{1,3},{2,0},{3,1},{4,6},{5,7},{6,4},{7,5},{8,10},{9,11},{10,... | collective-permute-start | bytes 6291464 | tf_op jit(solution)/shard_map/ppermute | solution.py:457
  12.9 46.5 %all-to-all-start = ((s32[8,1,200]{2,1,0:T(1,128)}), s32[8,1,200]{2,1,0:T(1,128)S(1)}, u32[]{:S(2)}, u32[]{:S(2)}) async-start(s32[8,1,200]{2,1,0:T(1,128)} %broadcast_in_dim.108), calls=%async_computation | async-start | bytes 16384 | tf_op jit(solution)/shard_map/all_to_all | solution.py:472
  61.6 19.3 %collective-permute-start.5 = (bf16[25,64,256]{2,1,0:T(8,128)(2,1)S(1)}, bf16[25,64,256]{2,1,0:T(8,128)(2,1)S(1)}, u32[]{:S(2)}, u32[]{:S(2)}) collective-permute-start(bf16[25,64,256]{2,1,0:T(8,128)(2,1)S(1)} %get-tuple-element.17), channel_id=1, source_target_pairs={{0,2},{1,3},{2,0},{3,1},{4,6},{5,7},{6,4},{7,5},{8,10},{9,11},{10,... | collective-permute-start | bytes 2457608 | tf_op jit(solution)/shard_map/ppermute | solution.py:457
  62.2 2.9 copy-start
  65.1 220.9 %collective-permute-start.1 = (bf16[50,64,256]{2,1,0:T(8,128)(2,1)S(1)}, bf16[50,64,256]{2,1,0:T(8,128)(2,1)S(1)}, u32[]{:S(2)}, u32[]{:S(2)}) collective-permute-start(bf16[50,64,256]{2,1,0:T(8,128)(2,1)S(1)} %pick_blocks.5), channel_id=1, source_target_pairs={{0,4},{1,5},{2,6},{3,7},{4,12},{5,13},{6,14},{7,15},{8,0},{9,1},{1... | collective-permute-start | bytes 4915208 | tf_op jit(solution)/shard_map/ppermute | solution.py:457
  83.6 205.9 %collective-permute-start.8 = (bf16[25,64,256]{2,1,0:T(8,128)(2,1)}, bf16[25,64,256]{2,1,0:T(8,128)(2,1)S(1)}, u32[]{:S(2)}, u32[]{:S(2)}) collective-permute-start(bf16[25,64,256]{2,1,0:T(8,128)(2,1)} %pick_blocks.9), channel_id=1, source_target_pairs={{0,2},{1,3},{2,0},{3,1},{4,6},{5,7},{6,4},{7,5},{8,10},{9,11},{10,... | collective-permute-start | bytes 2457608 | tf_op jit(solution)/shard_map/ppermute | solution.py:457
  84.2 229.8 %collective-permute-start.4 = (bf16[25,64,256]{2,1,0:T(8,128)(2,1)S(1)}, bf16[25,64,256]{2,1,0:T(8,128)(2,1)S(1)}, u32[]{:S(2)}, u32[]{:S(2)}) collective-permute-start(bf16[25,64,256]{2,1,0:T(8,128)(2,1)S(1)} %get-tuple-element.16), channel_id=1, source_target_pairs={{8,12},{9,13},{10,14},{11,15},{4,0},{5,1},{6,2},{7,3},{24,28},{25,... | collective-permute-start | bytes 2457608 | tf_op jit(solution)/shard_map/ppermute | solution.py:457
  279.2 6.7 %copy-start.1 = (bf16[64,64,256]{2,1,0:T(8,128)(2,1)S(1)}, bf16[64,64,256]{2,1,0:T(8,128)(2,1)}, u32[]{:S(2)}) copy-start(bf16[64,64,256]{2,1,0:T(8,128)(2,1)} %copy-done) | copy-start | bytes 6291460
  281.2 8.4 %copy-start.2 = (bf16[256,256]{1,0:T(8,128)(2,1)S(1)}, bf16[256,256]{1,0:T(8,128)(2,1)}, u32[]{:S(2)}) copy-start(bf16[256,256]{1,0:T(8,128)(2,1)} %rest_0_.5) | copy-start | bytes 393220
  281.2 8.4 %copy-start.3 = (bf16[256,256]{1,0:T(8,128)(2,1)S(1)}, bf16[256,256]{1,0:T(8,128)(2,1)}, u32[]{:S(2)}) copy-start(bf16[256,256]{1,0:T(8,128)(2,1)} %rest_2_.5) | copy-start | bytes 393220
  281.2 8.3 %copy-start.4 = (bf16[256,256]{1,0:T(8,128)(2,1)S(1)}, bf16[256,256]{1,0:T(8,128)(2,1)}, u32[]{:S(2)}) copy-start(bf16[256,256]{1,0:T(8,128)(2,1)} %rest_3_.5) | copy-start | bytes 393220
  281.2 8.3 %copy-start.7 = (bf16[4096,256]{1,0:T(8,128)(2,1)S(1)}, bf16[4096,256]{1,0:T(8,128)(2,1)}, u32[]{:S(2)}) copy-start(bf16[4096,256]{1,0:T(8,128)(2,1)} %copy-done.6) | copy-start | bytes 6291460
  281.3 32.8 %collective-permute-start.7 = (bf16[25,64,256]{2,1,0:T(8,128)(2,1)S(1)}, bf16[25,64,256]{2,1,0:T(8,128)(2,1)S(1)}, u32[]{:S(2)}, u32[]{:S(2)}) collective-permute-start(bf16[25,64,256]{2,1,0:T(8,128)(2,1)S(1)} %pick_blocks.8), channel_id=1, source_target_pairs={{4,8},{5,9},{6,10},{7,11},{8,4},{9,5},{10,6},{11,7},{20,24},{21,25... | collective-permute-start | bytes 2457608 | tf_op jit(solution)/shard_map/ppermute | solution.py:457
  284.6 29.5 %collective-permute-start.6 = (bf16[25,64,256]{2,1,0:T(8,128)(2,1)S(1)}, bf16[25,64,256]{2,1,0:T(8,128)(2,1)S(1)}, u32[]{:S(2)}, u32[]{:S(2)}) collective-permute-start(bf16[25,64,256]{2,1,0:T(8,128)(2,1)S(1)} %collective-permute-done.5.rest_1_), channel_id=1, source_target_pairs={{8,12},{9,13},{10,14},{11,15},{4,0},{5,1},{6,2},{7,3},{24,28},{25,... | collective-permute-start | bytes 2457608 | tf_op jit(solution)/shard_map/ppermute | solution.py:457
  286.9 42.0 %collective-permute-start.2 = (bf16[25,64,256]{2,1,0:T(8,128)(2,1)S(1)}, bf16[25,64,256]{2,1,0:T(8,128)(2,1)S(1)}, u32[]{:S(2)}, u32[]{:S(2)}) collective-permute-start(bf16[25,64,256]{2,1,0:T(8,128)(2,1)S(1)} %pick_blocks.6), channel_id=1, source_target_pairs={{4,8},{5,9},{6,10},{7,11},{8,4},{9,5},{10,6},{11,7},{20,24},{21,25... | collective-permute-start | bytes 2457608 | tf_op jit(solution)/shard_map/ppermute | solution.py:457
  314.1 1.6 copy-start.8

commit v10 on v9

--- a/solution.py
+++ b/solution.py
@@ -160,11 +160,10 @@
 
 
 def collect(pieces, places, total):
-    hbm = pl.BlockSpec(memory_space=pl.ANY)
     return pl.pallas_call(
         functools.partial(collect_kernel, places=places),
-        in_specs=[hbm] * len(pieces),
-        out_specs=hbm,
+        in_specs=[pl.BlockSpec(memory_space=pltpu.VMEM)] * len(pieces),
+        out_specs=pl.BlockSpec(memory_space=pl.ANY),
         out_shape=jax.ShapeDtypeStruct((total,) + pieces[0].shape[1:], pieces[0].dtype),
         scratch_shapes=[pltpu.SemaphoreType.DMA((len(pieces),))],
         cost_estimate=lasting(4),
@@ -345,7 +344,7 @@
     smem = pl.BlockSpec(memory_space=pltpu.SMEM)
     vmem = pl.BlockSpec(memory_space=pltpu.VMEM)
     hbm = pl.BlockSpec(memory_space=pl.ANY)
-    in_specs = [smem, smem, smem, hbm, hbm] + [vmem] * 4 + [hbm] * (len(pieces) + 1)
+    in_specs = [smem, smem, smem, hbm, hbm] + [vmem] * (4 + len(pieces)) + [hbm]
     aliases = {len(in_specs) - 1: 1}
     operands = [queries, placed, *weights, *pieces, buffer]
     if so_far is not None:

time: 351 us -> 178 us (0.51)
  the two profiles are of different devices: /device:TPU:8 before, /device:TPU:0 now
where the time goes in v10:
time: 178 us; the launch traced here: 176 us
  Pallas kernels  88.6 us (50%)
  waiting for transfers between devices  61 us (34%)
  starting transfers between devices  15.2 us (9%)
  between operations  5.2 us (3%)
  local copies, waits for them, and re-layouts  4.72 us (3%)
    pallas_call x3, Pallas kernels, attend(): pl.pallas_call(kernel, in_specs=in_specs, out_specs=[hbm, hbm], out_shape...  56.4 us
    all_to_all x1, waiting for transfers between devices, body(): lax.all_to_all(jnp.broadcast_to(tables[None], (SPAN, SPAN * capacity)), '...  35.7 us
    ppermute x9, waiting for transfers between devices, moved(): return lax.ppermute(x, 'elec', pairs_of)  25.3 us
    ppermute x9, starting transfers between devices, moved(): return lax.ppermute(x, 'elec', pairs_of)  11.8 us
    pallas_call x5, Pallas kernels, pick(): pl.pallas_call(functools.partial(pick_kernel, plan=plan, capacity=capacit...  10.7 us
    pallas_call x1, Pallas kernels, project_queries(): pl.pallas_call(functools.partial(query_kernel, cluster=cluster, head_widt...  8.29 us
    pallas_call x1, Pallas kernels, place(): pl.pallas_call(place_kernel, grid=(walkers,), in_specs=[local, pl.BlockSp...  7.69 us
    pallas_call x1, Pallas kernels, collect(): pl.pallas_call(functools.partial(collect_kernel, places=places), in_specs...  5.55 us
  transfers between devices with their start and end apart: 10, of which 4 were waited for; matrix products, arithmetic and copies ran while one was open for 2% of the time, Pallas kernels for 45%

profile of v10, /device:TPU:0, one launch (start us, length us, event | category | flops | bytes accessed | tf_op | source)
XLA Modules:
  0.0 176.3 jit_solution(15032207412594802998)
XLA Ops:
  0.0 0.7 copy-done.5
  0.7 7.7 %place_rows.1 = (bf16[4096,256]{1,0:T(8,128)(2,1)S(1)}, bf16[4096,256]{1,0:T(8,128)(2,1)}) custom-call(bf16[4096,256]{1,0:T(8,128)(2,1)} %features_ref.1, s32[8,1,512]{2,1,0:T(1,128)S(1)} %bitcast.23), custom_call_target="tpu_custom_call" | custom-call | flops 8049999872 | tf_op jit(solution)/shard_map/place_rows/pallas_call | solution.py:63
  8.4 1.3 copy-done.6
  9.7 4.0 %collective-permute-start.3 = (bf16[64,64,256]{2,1,0:T(8,128)(2,1)}, bf16[64,64,256]{2,1,0:T(8,128)(2,1)}, u32[]{:S(2)}, u32[]{:S(2)}) collective-permute-start(bf16[64,64,256]{2,1,0:T(8,128)(2,1)} %bitcast.7.rest_0_.refs_0_), channel_id=1, source_target_pairs={{0,8},{1,9},{2,10},{3,11},{4,0},{5,1},{6,2},{7,3},{8,12},{9,13},{1... | collective-permute-start | bytes 6291464 | tf_op jit(solution)/shard_map/ppermute | solution.py:456
  13.8 1.5 collective-permute-start
  15.6 0.2 select_reduce_fusion.1
  15.9 0.6 broadcast_in_dim.108
  16.5 3.3 %all-to-all-start = ((s32[8,1,200]{2,1,0:T(1,128)}), s32[8,1,200]{2,1,0:T(1,128)S(1)}, u32[]{:S(2)}, u32[]{:S(2)}) async-start(s32[8,1,200]{2,1,0:T(1,128)} %broadcast_in_dim.108), calls=%async_computation | async-start | bytes 16384 | tf_op jit(solution)/shard_map/all_to_all | solution.py:471
  19.9 0.7 fusion.14
  25.5 0.2 select_reduce_fusion.3
  26.1 35.7 %all-to-all-done = s32[8,1,200]{2,1,0:T(1,128)S(1)} async-done(((s32[8,1,200]{2,1,0:T(1,128)}), s32[8,1,200]{2,1,0:T(1,128)S(1)}, u32[]{:S(2)}, u32[]{:S(2)}) %all-to-all-start) | async-done | bytes 6432 | tf_op jit(solution)/shard_map/all_to_all | solution.py:471
  61.8 2.1 %pick_blocks.7 = (bf16[25,64,256]{2,1,0:T(8,128)(2,1)S(1)}, bf16[25,64,256]{2,1,0:T(8,128)(2,1)S(1)}) custom-call(s32[1]{0:T(128)} %bitcast.6.position_ref, s32[8,200]{1,0:T(8,128)S(1)} %bitcast.18, bf16[64,64,256]{2,1,0:T(8,128)(2,1)} %collective-permute-done.3.rest_0_.refs_1_), custom_call_target="tpu_custom_call" | custom-call | flops 1724999936 | tf_op jit(solution)/shard_map/pick_blocks/pallas_call | solution.py:104
  63.9 1.0 collective-permute-start.5
  64.9 2.9 %pick_blocks.5 = bf16[50,64,256]{2,1,0:T(8,128)(2,1)S(1)} custom-call(s32[1]{0:T(128)} %bitcast.6.position_ref, s32[8,200]{1,0:T(8,128)S(1)} %bitcast.19, bf16[64,64,256]{2,1,0:T(8,128)(2,1)} %bitcast.7.rest_0_.refs_0_, bf16[64,64,256]{2,1,0:T(8,128)(2,1)S(1)} %collective-permute-done.rest_1_.rest_0_.refs_2_), custom_call_target="tpu_custom_call" | custom-call | flops 1724999936 | tf_op jit(solution)/shard_map/pick_blocks/pallas_call | solution.py:104
  67.8 0.3 collective-permute-start.1
  68.2 8.3 %queries.1.query_ref = bf16[64,256,256]{2,1,0:T(8,128)(2,1)} custom-call(bf16[4096,256]{1,0:T(8,128)(2,1)} %get-tuple-element.14.normed_ref, bf16[256,256]{1,0:T(8,128)(2,1)S(1)} %bitcast.17), custom_call_target="tpu_custom_call" | custom-call | flops 7474999808 | tf_op jit(solution)/shard_map/queries/pallas_call | solution.py:131
  76.5 6.3 %collective-permute-done.5.rest_1_ = bf16[25,64,256]{2,1,0:T(8,128)(2,1)S(1)} collective-permute-done((bf16[25,64,256]{2,1,0:T(8,128)(2,1)S(1)}, bf16[25,64,256]{2,1,0:T(8,128)(2,1)S(1)}, u32[]{:S(2)}, u32[]{:S(2)}) %collective-permute-start.5) | collective-permute-done | bytes 819232 | tf_op jit(solution)/shard_map/ppermute | solution.py:456
  82.8 2.8 %pick_blocks.9 = bf16[25,64,256]{2,1,0:T(8,128)(2,1)} custom-call(s32[1]{0:T(128)} %bitcast.6.position_ref, s32[8,200]{1,0:T(8,128)S(1)} %bitcast.20, bf16[64,64,256]{2,1,0:T(8,128)(2,1)} %collective-permute-done.3.rest_0_.refs_1_, bf16[25,64,256]{2,1,0:T(8,128)(2,1)S(1)} %collective-permute-done.5.rest_1_), custom_call_target="tpu_custom_call" | custom-call | flops 1724999936 | tf_op jit(solution)/shard_map/pick_blocks/pallas_call | solution.py:104
  85.6 0.8 collective-permute-start.8
  86.5 1.3 collective-permute-start.4
  87.8 5.5 %collect_blocks.1.rest_6_ = bf16[367,64,256]{2,1,0:T(8,128)(2,1)} custom-call(bf16[64,64,256]{2,1,0:T(8,128)(2,1)} %bitcast.7.rest_0_.refs_0_, bf16[64,64,256]{2,1,0:T(8,128)(2,1)} %collective-permute-done.3.rest_0_.refs_1_, bf16[64,64,256]{2,1,0:T(8,128)(2,1)} %copy-done), custom_call_target="tpu_custom_call" | custom-call | flops 4600000000 | tf_op jit(solution)/shard_map/collect_blocks/pallas_call | solution.py:163
  93.4 2.0 %pick_blocks.8 = bf16[25,64,256]{2,1,0:T(8,128)(2,1)S(1)} custom-call(s32[1]{0:T(128)} %bitcast.6.position_ref, s32[8,200]{1,0:T(8,128)S(1)} %bitcast.21, bf16[64,64,256]{2,1,0:T(8,128)(2,1)} %bitcast.7.rest_0_.refs_0_, bf16[25,64,256]{2,1,0:T(8,128)(2,1)S(1)} %collective-permute-done.5.rest_1_), custom_call_target="tpu_custom_call" | custom-call | flops 1724999936 | tf_op jit(solution)/shard_map/pick_blocks/pallas_call | solution.py:104
  95.4 0.8 collective-permute-start.7
  96.3 1.3 collective-permute-start.6
  97.6 10.0 %collective-permute-done.1.rest_1_.rest_5_ = bf16[50,64,256]{2,1,0:T(8,128)(2,1)S(1)} collective-permute-done((bf16[50,64,256]{2,1,0:T(8,128)(2,1)S(1)}, bf16[50,64,256]{2,1,0:T(8,128)(2,1)S(1)}, u32[]{:S(2)}, u32[]{:S(2)}) %collective-permute-start.1) | collective-permute-done | bytes 1638432 | tf_op jit(solution)/shard_map/ppermute | solution.py:456
  107.5 0.9 pick_blocks.6
  108.5 0.7 collective-permute-start.2
  109.2 21.6 %attend_blocks.3 = (bf16[64,64,256]{2,1,0:T(8,128)(2,1)}, bf16[367,64,256]{2,1,0:T(8,128)(2,1)}) custom-call(s32[2]{0:T(128)S(1)} %pad_add_fusion.2.range_ref, s32[64]{0:T(128)S(1)} %select_reduce_fusion.2.order_ref, s32[192]{0:T(256)S(1)} %get-tuple-element.26.table_ref, bf16[64,256,256]{2,1,0:T(8,128)(2,1)} %queries.1.query_ref, ...), custom_call_target="tpu_custom_call", output_to_operand_aliasing={{1}: (11, {})} | custom-call | flops 20700000256 | tf_op jit(solution)/shard_map/attend_blocks/pallas_call | solution.py:357
  130.9 9.0 %collective-permute-done.6.rest_5_ = bf16[25,64,256]{2,1,0:T(8,128)(2,1)S(1)} collective-permute-done((bf16[25,64,256]{2,1,0:T(8,128)(2,1)S(1)}, bf16[25,64,256]{2,1,0:T(8,128)(2,1)S(1)}, u32[]{:S(2)}, u32[]{:S(2)}) %collective-permute-start.6) | collective-permute-done | bytes 819232 | tf_op jit(solution)/shard_map/ppermute | solution.py:456
  139.9 1.6 copy-done.8
  141.5 32.8 %attend_blocks.4 = (bf16[64,64,256]{2,1,0:T(8,128)(2,1)}, bf16[367,64,256]{2,1,0:T(8,128)(2,1)}) custom-call(s32[2]{0:T(128)S(1)} %pad_add_fusion.1.range_ref, s32[64]{0:T(128)S(1)} %select_reduce_fusion.2.order_ref, s32[192]{0:T(256)S(1)} %get-tuple-element.26.table_ref, ...), custom_call_target="tpu_custom_call", output_to_operand_aliasing={{1}: (12, {}), {0}: (13, {})} | custom-call | flops 20700000256 | tf_op jit(solution)/shard_map/attend_blocks/pallas_call | solution.py:357
  174.3 1.9 %attend_blocks.5 = (bf16[64,64,256]{2,1,0:T(8,128)(2,1)}, bf16[367,64,256]{2,1,0:T(8,128)(2,1)}) custom-call(s32[2]{0:T(128)S(1)} %pad_add_fusion.range_ref, s32[64]{0:T(128)S(1)} %select_reduce_fusion.2.order_ref, s32[192]{0:T(256)S(1)} %get-tuple-element.26.table_ref, ...), custom_call_target="tpu_custom_call", output_to_operand_aliasing={{1}: (10, {}), {0}: (11, {})} | custom-call | flops 20700000256 | tf_op jit(solution)/shard_map/attend_blocks/pallas_call | solution.py:357
  (40 shorter events, 1.1 us)
Async XLA Ops:
  0.0 0.7 copy-start.5
  0.7 14.6 %copy-start.11 = (s32[64,3]{0,1:T(4,128)S(1)}, s32[64,3]{0,1:T(4,128)}, u32[]{:S(2)}) copy-start(s32[64,3]{0,1:T(4,128)} %param.10) | copy-start | bytes 2308
  0.7 25.2 %copy-start.9 = (bf16[256,256]{1,0:T(8,128)(2,1)S(1)}, bf16[256,256]{1,0:T(8,128)(2,1)}, u32[]{:S(2)}) copy-start(bf16[256,256]{1,0:T(8,128)(2,1)} %param.11) | copy-start | bytes 393220
  0.7 25.3 %copy-start.10 = (bf16[256,256]{1,0:T(8,128)(2,1)S(1)}, bf16[256,256]{1,0:T(8,128)(2,1)}, u32[]{:S(2)}) copy-start(bf16[256,256]{1,0:T(8,128)(2,1)} %param.13) | copy-start | bytes 393220
  8.4 1.3 copy-start.6
  9.7 52.1 %collective-permute-start.3 = (bf16[64,64,256]{2,1,0:T(8,128)(2,1)}, bf16[64,64,256]{2,1,0:T(8,128)(2,1)}, u32[]{:S(2)}, u32[]{:S(2)}) collective-permute-start(bf16[64,64,256]{2,1,0:T(8,128)(2,1)} %bitcast.7.rest_0_.refs_0_), channel_id=1, source_target_pairs={{0,8},{1,9},{2,10},{3,11},{4,0},{5,1},{6,2},{7,3},{8,12},{9,13},{1... | collective-permute-start | bytes 6291464 | tf_op jit(solution)/shard_map/ppermute | solution.py:456
  13.8 51.1 %collective-permute-start = (bf16[64,64,256]{2,1,0:T(8,128)(2,1)}, bf16[64,64,256]{2,1,0:T(8,128)(2,1)S(1)}, u32[]{:S(2)}, u32[]{:S(2)}) collective-permute-start(bf16[64,64,256]{2,1,0:T(8,128)(2,1)} %bitcast.7.rest_0_.refs_0_), channel_id=1, source_target_pairs={{0,2},{1,3},{2,0},{3,1},{4,6},{5,7},{6,4},{7,5},{8,10},{9,11},{10,... | collective-permute-start | bytes 6291464 | tf_op jit(solution)/shard_map/ppermute | solution.py:456
  16.5 45.3 %all-to-all-start = ((s32[8,1,200]{2,1,0:T(1,128)}), s32[8,1,200]{2,1,0:T(1,128)S(1)}, u32[]{:S(2)}, u32[]{:S(2)}) async-start(s32[8,1,200]{2,1,0:T(1,128)} %broadcast_in_dim.108), calls=%async_computation | async-start | bytes 16384 | tf_op jit(solution)/shard_map/all_to_all | solution.py:471
  63.9 18.9 %collective-permute-start.5 = (bf16[25,64,256]{2,1,0:T(8,128)(2,1)S(1)}, bf16[25,64,256]{2,1,0:T(8,128)(2,1)S(1)}, u32[]{:S(2)}, u32[]{:S(2)}) collective-permute-start(bf16[25,64,256]{2,1,0:T(8,128)(2,1)S(1)} %get-tuple-element.17), channel_id=1, source_target_pairs={{0,2},{1,3},{2,0},{3,1},{4,6},{5,7},{6,4},{7,5},{8,10},{9,11},{10,... | collective-permute-start | bytes 2457608 | tf_op jit(solution)/shard_map/ppermute | solution.py:456
  64.9 2.9 %copy-start = (bf16[64,64,256]{2,1,0:T(8,128)(2,1)}, bf16[64,64,256]{2,1,0:T(8,128)(2,1)S(1)}, u32[]{:S(2)}) copy-start(bf16[64,64,256]{2,1,0:T(8,128)(2,1)S(1)} %collective-permute-done.rest_1_.rest_0_.refs_2_) | copy-start | bytes 6291460
  67.8 39.7 %collective-permute-start.1 = (bf16[50,64,256]{2,1,0:T(8,128)(2,1)S(1)}, bf16[50,64,256]{2,1,0:T(8,128)(2,1)S(1)}, u32[]{:S(2)}, u32[]{:S(2)}) collective-permute-start(bf16[50,64,256]{2,1,0:T(8,128)(2,1)S(1)} %pick_blocks.5), channel_id=1, source_target_pairs={{0,4},{1,5},{2,6},{3,7},{4,12},{5,13},{6,14},{7,15},{8,0},{9,1},{1... | collective-permute-start | bytes 4915208 | tf_op jit(solution)/shard_map/ppermute | solution.py:456
  85.6 23.6 %collective-permute-start.8 = (bf16[25,64,256]{2,1,0:T(8,128)(2,1)}, bf16[25,64,256]{2,1,0:T(8,128)(2,1)S(1)}, u32[]{:S(2)}, u32[]{:S(2)}) collective-permute-start(bf16[25,64,256]{2,1,0:T(8,128)(2,1)} %pick_blocks.9), channel_id=1, source_target_pairs={{0,2},{1,3},{2,0},{3,1},{4,6},{5,7},{6,4},{7,5},{8,10},{9,11},{10,... | collective-permute-start | bytes 2457608 | tf_op jit(solution)/shard_map/ppermute | solution.py:456
  86.5 44.4 %collective-permute-start.4 = (bf16[25,64,256]{2,1,0:T(8,128)(2,1)S(1)}, bf16[25,64,256]{2,1,0:T(8,128)(2,1)S(1)}, u32[]{:S(2)}, u32[]{:S(2)}) collective-permute-start(bf16[25,64,256]{2,1,0:T(8,128)(2,1)S(1)} %get-tuple-element.16), channel_id=1, source_target_pairs={{8,12},{9,13},{10,14},{11,15},{4,0},{5,1},{6,2},{7,3},{24,28},{25,... | collective-permute-start | bytes 2457608 | tf_op jit(solution)/shard_map/ppermute | solution.py:456
  93.3 14.2 %copy-start.1 = (bf16[64,64,256]{2,1,0:T(8,128)(2,1)S(1)}, bf16[64,64,256]{2,1,0:T(8,128)(2,1)}, u32[]{:S(2)}) copy-start(bf16[64,64,256]{2,1,0:T(8,128)(2,1)} %copy-done) | copy-start | bytes 6291460
  95.4 13.8 %copy-start.2 = (bf16[256,256]{1,0:T(8,128)(2,1)S(1)}, bf16[256,256]{1,0:T(8,128)(2,1)}, u32[]{:S(2)}) copy-start(bf16[256,256]{1,0:T(8,128)(2,1)} %rest_0_.5) | copy-start | bytes 393220
  95.4 13.8 %copy-start.3 = (bf16[256,256]{1,0:T(8,128)(2,1)S(1)}, bf16[256,256]{1,0:T(8,128)(2,1)}, u32[]{:S(2)}) copy-start(bf16[256,256]{1,0:T(8,128)(2,1)} %rest_2_.5) | copy-start | bytes 393220
  95.4 13.8 %copy-start.4 = (bf16[256,256]{1,0:T(8,128)(2,1)S(1)}, bf16[256,256]{1,0:T(8,128)(2,1)}, u32[]{:S(2)}) copy-start(bf16[256,256]{1,0:T(8,128)(2,1)} %rest_3_.5) | copy-start | bytes 393220
  95.4 13.8 %copy-start.7 = (bf16[4096,256]{1,0:T(8,128)(2,1)S(1)}, bf16[4096,256]{1,0:T(8,128)(2,1)}, u32[]{:S(2)}) copy-start(bf16[4096,256]{1,0:T(8,128)(2,1)} %copy-done.6) | copy-start | bytes 6291460
  95.4 35.5 %collective-permute-start.7 = (bf16[25,64,256]{2,1,0:T(8,128)(2,1)S(1)}, bf16[25,64,256]{2,1,0:T(8,128)(2,1)S(1)}, u32[]{:S(2)}, u32[]{:S(2)}) collective-permute-start(bf16[25,64,256]{2,1,0:T(8,128)(2,1)S(1)} %pick_blocks.8), channel_id=1, source_target_pairs={{4,8},{5,9},{6,10},{7,11},{8,4},{9,5},{10,6},{11,7},{20,24},{21,25... | collective-permute-start | bytes 2457608 | tf_op jit(solution)/shard_map/ppermute | solution.py:456
  96.3 43.6 %collective-permute-start.6 = (bf16[25,64,256]{2,1,0:T(8,128)(2,1)S(1)}, bf16[25,64,256]{2,1,0:T(8,128)(2,1)S(1)}, u32[]{:S(2)}, u32[]{:S(2)}) collective-permute-start(bf16[25,64,256]{2,1,0:T(8,128)(2,1)S(1)} %collective-permute-done.5.rest_1_), channel_id=1, source_target_pairs={{8,12},{9,13},{10,14},{11,15},{4,0},{5,1},{6,2},{7,3},{24,28},{25,... | collective-permute-start | bytes 2457608 | tf_op jit(solution)/shard_map/ppermute | solution.py:456
  108.5 65.9 %collective-permute-start.2 = (bf16[25,64,256]{2,1,0:T(8,128)(2,1)S(1)}, bf16[25,64,256]{2,1,0:T(8,128)(2,1)S(1)}, u32[]{:S(2)}, u32[]{:S(2)}) collective-permute-start(bf16[25,64,256]{2,1,0:T(8,128)(2,1)S(1)} %pick_blocks.6), channel_id=1, source_target_pairs={{4,8},{5,9},{6,10},{7,11},{8,4},{9,5},{10,6},{11,7},{20,24},{21,25... | collective-permute-start | bytes 2457608 | tf_op jit(solution)/shard_map/ppermute | solution.py:456
  139.9 1.6 copy-start.8

commit v11 on v10

--- a/solution.py
+++ b/solution.py
@@ -13,7 +13,7 @@
 SUB = 8
 GROUP = 4
 STEP = 4
-SCORES_AHEAD, WEIGHTS_AHEAD = 3, 1
+SCORES_AHEAD, WEIGHTS_AHEAD = 2, 1
 VMEM_BYTES = 48 * 1024 * 1024
 
 NT = (((1,), (1,)), ((), ()))
@@ -40,36 +40,41 @@
     return row_head == lane_head
 
 
-def place_kernel(features_ref, assignment_ref, placed_ref, normed_ref):
-    rows = features_ref.shape[0]
+def place_kernel(features_ref, assignment_ref, *rest, outputs):
+    normed_ref, *placed_ref = rest[len(rest) - outputs :]
+    walkers, _, rows = assignment_ref.shape
     lane = 128
-    features = features_ref[...]
     columns = lax.broadcasted_iota(jnp.int32, (lane, rows), 1)
-    for part in range(rows // lane):
-        chosen = assignment_ref[0, :, part * lane : (part + 1) * lane] & (rows - 1)
-        chosen = jnp.broadcast_to(chosen, (lane, lane)).T
-        chosen = jnp.concatenate([chosen] * (rows // lane), axis=1)
-        one_hot = jnp.where(chosen == columns, 1.0, 0.0).astype(jnp.bfloat16)
-        placed = jnp.dot(one_hot, features, preferred_element_type=jnp.float32)
-        placed_ref[pl.ds(part * lane, lane), :] = placed.astype(jnp.bfloat16)
-        normed_ref[pl.ds(part * lane, lane), :] = layer_norm(placed).astype(jnp.bfloat16)
-
-
-def place(features, assignment):
+    for walker in range(walkers):
+        features = features_ref[walker * rows : (walker + 1) * rows, :]
+        for part in range(rows // lane):
+            chosen = assignment_ref[walker, :, part * lane : (part + 1) * lane] & (rows - 1)
+            chosen = jnp.broadcast_to(chosen, (lane, lane)).T
+            chosen = jnp.concatenate([chosen] * (rows // lane), axis=1)
+            one_hot = jnp.where(chosen == columns, 1.0, 0.0).astype(jnp.bfloat16)
+            placed = jnp.dot(one_hot, features, preferred_element_type=jnp.float32)
+            here = pl.ds(walker * rows + part * lane, lane)
+            if placed_ref:
+                placed_ref[0][here, :] = placed.astype(jnp.bfloat16)
+            normed_ref[here, :] = layer_norm(placed).astype(jnp.bfloat16)
+
+
+def place(features, assignment, outputs, after=()):
     width = features.shape[1]
     walkers, _, rows = assignment.shape
-    local = pl.BlockSpec((rows, width), lambda i: (i, 0))
+    local = pl.BlockSpec((2 * rows, width), lambda i: (i, 0))
     out = jax.ShapeDtypeStruct(features.shape, jnp.bfloat16)
     return pl.pallas_call(
-        place_kernel,
-        grid=(walkers,),
-        in_specs=[local, pl.BlockSpec((1, 1, rows), lambda i: (i, 0, 0))],
-        out_specs=[local] * 2,
-        out_shape=[out, out],
+        functools.partial(place_kernel, outputs=outputs),
+        grid=(walkers // 2,),
+        in_specs=[local, pl.BlockSpec((2, 1, rows), lambda i: (i, 0, 0))]
+        + [pl.BlockSpec(memory_space=pl.ANY)] * len(after),
+        out_specs=[local] * outputs,
+        out_shape=[out] * outputs,
         cost_estimate=lasting(7),
         compiler_params=kernel_params(),
         name="place_rows",
-    )(features, assignment)
+    )(features, assignment, *after)
 
 
 def choose(index, values):
@@ -281,8 +286,7 @@
     fold = jnp.where(fold_row == fold_lane, 1.0, 0.0).astype(jnp.bfloat16)
     zeros = jnp.zeros((span, tile), jnp.bfloat16)
     ones = jnp.ones((16, tile), jnp.bfloat16)
-    tiles = HEADS // GROUP
-    units = [(block, t) for block in range(STEP) for t in range(tiles)]
+    units = [(block, pair) for block in range(STEP) for pair in range(HEADS // GROUP // 2)]
     keys, values = {}, {}
 
     def gather(block):
@@ -292,26 +296,34 @@
         value = lax.dot_general(value_w_ref[...], members, NT, preferred_element_type=jnp.float32)
         values[block] = value.astype(jnp.bfloat16)
 
-    def scores_of(block, t):
-        if t == 0:
+    def scores_of(block, pair):
+        if pair == 0:
             gather(block)
-        lo = t * span // 128 * 128
-        picked = query_ref[block, t * span : (t + 1) * span, :]
-        ahead, behind = t * span - lo, lo + 128 - (t + 1) * span
-        stack = [zeros] * (ahead // span) + [picked] + [zeros] * (behind // span)
+        first = query_ref[block, pair * 2 * span : (pair * 2 + 1) * span, :]
+        other = query_ref[block, (pair * 2 + 1) * span : (pair + 1) * 2 * span, :]
+        both = jnp.concatenate(
+            [
+                jnp.concatenate([first, zeros], axis=1),
+                jnp.concatenate([zeros, other], axis=1),
+            ],
+            axis=0,
+        )
         return jnp.dot(
-            keys[block][:, lo : lo + 128],
-            jnp.concatenate(stack, axis=0),
+            keys[block][:, pair * 2 * span : (pair + 1) * 2 * span],
+            both,
             preferred_element_type=jnp.float32,
         )
 
     def weights_of(scores):
         top = jnp.max(scores, axis=0, keepdims=True)
-        return jnp.exp2(scores - top).astype(jnp.bfloat16)
-
-    def product_of(block, t, weights):
-        lifted = jnp.concatenate([values[block][t * span : (t + 1) * span], ones], axis=0)
-        return jnp.dot(lifted, weights, preferred_element_type=jnp.float32)
+        return jnp.exp2((scores - top).astype(jnp.bfloat16))
+
+    def products_of(block, pair, weights):
+        for half in range(2):
+            t = pair * 2 + half
+            lifted = jnp.concatenate([values[block][t * span : (t + 1) * span], ones], axis=0)
+            here = weights[:, half * tile : (half + 1) * tile]
+            yield jnp.dot(lifted, here, preferred_element_type=jnp.float32)
 
     def scaled(product):
         result = product[:span] * (1.0 / product[span : span + 1])
@@ -321,21 +333,21 @@
     scores, weights, products, pieces, attended = {}, {}, {}, [], []
     for at in range(-SCORES_AHEAD, count + 1):
         if at == 0:
-            other = meanwhile()
+            finished = meanwhile()
         if at + SCORES_AHEAD < count:
             scores[at + SCORES_AHEAD] = scores_of(*units[at + SCORES_AHEAD])
         if 0 <= at + WEIGHTS_AHEAD < count:
             weights[at + WEIGHTS_AHEAD] = weights_of(scores.pop(at + WEIGHTS_AHEAD))
         if 0 <= at < count:
-            products[at] = product_of(*units[at], weights.pop(at))
+            products[at] = list(products_of(*units[at], weights.pop(at)))
         if at > 0:
-            pieces.append(scaled(products.pop(at - 1)))
-            if len(pieces) == tiles:
+            pieces += [scaled(product) for product in products.pop(at - 1)]
+            if len(pieces) == HEADS // GROUP:
                 stacked = jnp.concatenate(pieces, axis=0)
                 folded = lax.dot_general(fold, stacked, NT, preferred_element_type=jnp.float32)
                 attended.append(folded.astype(jnp.bfloat16))
                 pieces = []
-    return jnp.concatenate(attended, axis=0), other
+    return jnp.concatenate(attended, axis=0), finished
 
 
 def attend(begin, count, order, table, queries, placed, weights, buffer, pieces, places, own_at, so_far):
@@ -464,6 +476,8 @@
     middle_moves = across_z([(1, 2), (2, 1)])
     outward_moves = across_z([(2, 3), (1, 0)])
 
+    raw_passed, to_passed = moved(features, first_moves), moved(assignment, first_moves)
+
     listed = pairs.reshape(-1)
     owner = listed // block_count // stride
     within = listed % block_count
@@ -477,17 +491,19 @@
         tiled=True,
     )
 
-    placed, normed = place(features, assignment.reshape(block_count // SUB, 1, SUB * cluster))
-    blocks = normed.reshape(block_count, cluster, width)
-    passed = moved(blocks, first_moves)
-    beside = moved(blocks, swap)
-
+    shape = (block_count // SUB, 1, SUB * cluster)
+    block_shape = (block_count, cluster, width)
+    normed, placed = place(features, assignment.reshape(shape), 2)
+    blocks = normed.reshape(block_shape)
     queries = project_queries(normed, w_query, cluster)
     own_at = 7 * capacity
     passed_at = own_at + block_count
     beside_at = passed_at + block_count
     total = beside_at + block_count
 
+    beside = moved(blocks, swap)
+    (passed,) = place(raw_passed, to_passed.reshape(shape), 1, after=(queries,))
+    passed = passed.reshape(block_shape)
     (second,) = pick(at_position, wanted, (blocks, beside), SECOND_PLAN)
     second = moved(second, second_moves)
     on, outward = pick(at_position, wanted, (passed,), ON_PLAN)

time: 178 us -> 181 us (1.017)
  the two profiles are of different devices: /device:TPU:0 before, /device:TPU:8 now
where the time goes in v11:
time: 181 us; the launch traced here: 178 us
  Pallas kernels  92 us (51%)
  waiting for transfers between devices  49 us (27%)
  starting transfers between devices  24.3 us (13%)
  local copies, waits for them, and re-layouts  6.3 us (3%)
  between operations  5.21 us (3%)
    pallas_call x3, Pallas kernels, attend(): pl.pallas_call(kernel, in_specs=in_specs, out_specs=[hbm, hbm], out_shape...  57.2 us
    all_to_all x1, waiting for transfers between devices, body(): lax.all_to_all(jnp.broadcast_to(tables[None], (SPAN, SPAN * capacity)), '...  31.2 us
    ppermute x10, starting transfers between devices, moved(): return lax.ppermute(x, 'elec', pairs_of)  19.5 us
    ppermute x10, waiting for transfers between devices, moved(): return lax.ppermute(x, 'elec', pairs_of)  17.8 us
    pallas_call x2, Pallas kernels, place(): pl.pallas_call(functools.partial(place_kernel, outputs=outputs), grid=(wa...  11.7 us
    pallas_call x5, Pallas kernels, pick(): pl.pallas_call(functools.partial(pick_kernel, plan=plan, capacity=capacit...  9.94 us
    pallas_call x1, Pallas kernels, project_queries(): pl.pallas_call(functools.partial(query_kernel, cluster=cluster, head_widt...  8.31 us
    unnamed x36, local copies, waits for them, and re-layouts  5.56 us
  transfers between devices with their start and end apart: 11, of which 4 were waited for; matrix products, arithmetic and copies ran while one was open for 1% of the time, Pallas kernels for 40%

profile of v11, /device:TPU:8, one launch (start us, length us, event | category | flops | bytes accessed | tf_op | source)
XLA Modules:
  0.0 178.4 jit_solution(15798578563456932770)
XLA Ops:
  0.0 3.0 %collective-permute-start.3 = (bf16[4096,256]{1,0:T(8,128)(2,1)}, bf16[4096,256]{1,0:T(8,128)(2,1)}, u32[]{:S(2)}, u32[]{:S(2)}) collective-permute-start(bf16[4096,256]{1,0:T(8,128)(2,1)} %features_ref.1), channel_id=1, source_target_pairs={{0,8},{1,9},{2,10},{3,11},{4,0},{5,1},{6,2},{7,3},{8,12},{9,13},{1... | collective-permute-start | bytes 6291464 | tf_op jit(solution)/shard_map/ppermute | solution.py:468
  3.0 0.7 copy-done.10
  3.8 6.3 %place_rows.2 = (bf16[4096,256]{1,0:T(8,128)(2,1)}, bf16[4096,256]{1,0:T(8,128)(2,1)S(1)}) custom-call(bf16[4096,256]{1,0:T(8,128)(2,1)} %features_ref.1, s32[8,1,512]{2,1,0:T(1,128)S(1)} %bitcast.28), custom_call_target="tpu_custom_call" | custom-call | flops 8049999872 | tf_op jit(solution)/shard_map/place_rows/pallas_call | solution.py:67
  10.1 1.3 copy-done.11
  11.4 1.5 collective-permute-start
  13.6 0.6 broadcast_in_dim.108
  14.2 4.8 %all-to-all-start = ((s32[8,1,200]{2,1,0:T(1,128)}), s32[8,1,200]{2,1,0:T(1,128)S(1)}, u32[]{:S(2)}, u32[]{:S(2)}) async-start(s32[8,1,200]{2,1,0:T(1,128)} %broadcast_in_dim.108), calls=%async_computation | async-start | bytes 16384 | tf_op jit(solution)/shard_map/all_to_all | solution.py:485
  19.1 8.3 %queries.1.rest_0_.query_ref = bf16[64,256,256]{2,1,0:T(8,128)(2,1)} custom-call(bf16[4096,256]{1,0:T(8,128)(2,1)} %get-tuple-element.14.normed_ref, bf16[256,256]{1,0:T(8,128)(2,1)S(1)} %bitcast.22), custom_call_target="tpu_custom_call" | custom-call | flops 7474999808 | tf_op jit(solution)/shard_map/queries/pallas_call | solution.py:136
  27.4 31.2 %all-to-all-done = s32[8,1,200]{2,1,0:T(1,128)S(1)} async-done(((s32[8,1,200]{2,1,0:T(1,128)}), s32[8,1,200]{2,1,0:T(1,128)S(1)}, u32[]{:S(2)}, u32[]{:S(2)}) %all-to-all-start) | async-done | bytes 6432 | tf_op jit(solution)/shard_map/all_to_all | solution.py:485
  58.6 5.3 %place_rows.3 = bf16[4096,256]{1,0:T(8,128)(2,1)S(1)} custom-call(bf16[4096,256]{1,0:T(8,128)(2,1)} %collective-permute-done.3.features_ref, s32[8,1,512]{2,1,0:T(1,128)S(1)} %bitcast.29, bf16[64,256,256]{2,1,0:T(8,128)(2,1)} %queries.1.rest_0_.query_ref), custom_call_target="tpu_custom_call" | custom-call | flops 8049999872 | tf_op jit(solution)/shard_map/place_rows/pallas_call | solution.py:67
  63.9 2.1 %pick_blocks.7 = (bf16[25,64,256]{2,1,0:T(8,128)(2,1)}, bf16[25,64,256]{2,1,0:T(8,128)(2,1)S(1)}) custom-call(s32[1]{0:T(128)} %bitcast.6.position_ref, s32[8,200]{1,0:T(8,128)S(1)} %bitcast.23, bf16[64,64,256]{2,1,0:T(8,128)(2,1)S(1)} %bitcast.16), custom_call_target="tpu_custom_call" | custom-call | flops 1724999936 | tf_op jit(solution)/shard_map/pick_blocks/pallas_call | solution.py:109
  66.0 1.5 collective-permute-start.6
  67.5 4.0 %pick_blocks.5 = bf16[50,64,256]{2,1,0:T(8,128)(2,1)} custom-call(s32[1]{0:T(128)} %bitcast.6.position_ref, s32[8,200]{1,0:T(8,128)S(1)} %bitcast.24, bf16[64,64,256]{2,1,0:T(8,128)(2,1)} %bitcast.7.rest_0_.refs_0_, bf16[64,64,256]{2,1,0:T(8,128)(2,1)S(1)} %collective-permute-done.rest_1_.rest_0_.refs_2_), custom_call_target="tpu_custom_call" | custom-call | flops 1724999936 | tf_op jit(solution)/shard_map/pick_blocks/pallas_call | solution.py:109
  71.5 0.3 collective-permute-start.1
  71.9 0.7 fusion.14
  77.9 6.8 %collective-permute-done.6.rest_1_ = bf16[25,64,256]{2,1,0:T(8,128)(2,1)S(1)} collective-permute-done((bf16[25,64,256]{2,1,0:T(8,128)(2,1)}, bf16[25,64,256]{2,1,0:T(8,128)(2,1)S(1)}, u32[]{:S(2)}, u32[]{:S(2)}) %collective-permute-start.6) | collective-permute-done | bytes 819232 | tf_op jit(solution)/shard_map/ppermute | solution.py:468
  84.7 1.6 copy-done.3
  86.3 0.9 pick_blocks.9
  87.2 1.6 collective-permute-start.9
  88.9 3.5 %collective-permute-start.5 = (bf16[25,64,256]{2,1,0:T(8,128)(2,1)S(1)}, bf16[25,64,256]{2,1,0:T(8,128)(2,1)S(1)}, u32[]{:S(2)}, u32[]{:S(2)}) collective-permute-start(bf16[25,64,256]{2,1,0:T(8,128)(2,1)S(1)} %copy-done.6), channel_id=1, source_target_pairs={{8,12},{9,13},{10,14},{11,15},{4,0},{5,1},{6,2},{7,3},{24,28},{25,... | collective-permute-start | bytes 2457608 | tf_op jit(solution)/shard_map/ppermute | solution.py:468
  92.4 4.9 %collect_blocks.1.rest_6_ = bf16[367,64,256]{2,1,0:T(8,128)(2,1)} custom-call(bf16[64,64,256]{2,1,0:T(8,128)(2,1)} %bitcast.7.rest_0_.refs_0_, bf16[64,64,256]{2,1,0:T(8,128)(2,1)S(1)} %bitcast.18, bf16[64,64,256]{2,1,0:T(8,128)(2,1)} %copy-done), custom_call_target="tpu_custom_call" | custom-call | flops 4600000000 | tf_op jit(solution)/shard_map/collect_blocks/pallas_call | solution.py:168
  97.3 2.0 %pick_blocks.8 = bf16[25,64,256]{2,1,0:T(8,128)(2,1)S(1)} custom-call(s32[1]{0:T(128)} %bitcast.6.position_ref, s32[8,200]{1,0:T(8,128)S(1)} %bitcast.26, bf16[64,64,256]{2,1,0:T(8,128)(2,1)} %bitcast.7.rest_0_.refs_0_, bf16[25,64,256]{2,1,0:T(8,128)(2,1)S(1)} %collective-permute-done.6.rest_1_), custom_call_target="tpu_custom_call" | custom-call | flops 1724999936 | tf_op jit(solution)/shard_map/pick_blocks/pallas_call | solution.py:109
  99.4 2.1 %collective-permute-start.8 = (bf16[25,64,256]{2,1,0:T(8,128)(2,1)S(1)}, bf16[25,64,256]{2,1,0:T(8,128)(2,1)S(1)}, u32[]{:S(2)}, u32[]{:S(2)}) collective-permute-start(bf16[25,64,256]{2,1,0:T(8,128)(2,1)S(1)} %pick_blocks.8), channel_id=1, source_target_pairs={{4,8},{5,9},{6,10},{7,11},{8,4},{9,5},{10,6},{11,7},{20,24},{21,25... | collective-permute-start | bytes 2457608 | tf_op jit(solution)/shard_map/ppermute | solution.py:468
  101.4 1.3 collective-permute-start.7
  102.8 5.7 %collective-permute-done.1.rest_1_.rest_5_ = bf16[50,64,256]{2,1,0:T(8,128)(2,1)} collective-permute-done((bf16[50,64,256]{2,1,0:T(8,128)(2,1)}, bf16[50,64,256]{2,1,0:T(8,128)(2,1)}, u32[]{:S(2)}, u32[]{:S(2)}) %collective-permute-start.1) | collective-permute-done | bytes 1638432 | tf_op jit(solution)/shard_map/ppermute | solution.py:468
  108.5 0.9 pick_blocks.6
  109.4 4.6 %collective-permute-start.2 = (bf16[25,64,256]{2,1,0:T(8,128)(2,1)S(1)}, bf16[25,64,256]{2,1,0:T(8,128)(2,1)S(1)}, u32[]{:S(2)}, u32[]{:S(2)}) collective-permute-start(bf16[25,64,256]{2,1,0:T(8,128)(2,1)S(1)} %pick_blocks.6), channel_id=1, source_target_pairs={{4,8},{5,9},{6,10},{7,11},{8,4},{9,5},{10,6},{11,7},{20,24},{21,25... | collective-permute-start | bytes 2457608 | tf_op jit(solution)/shard_map/ppermute | solution.py:468
  114.1 1.6 copy-done.12
  115.7 21.6 %attend_blocks.3 = (bf16[64,64,256]{2,1,0:T(8,128)(2,1)}, bf16[367,64,256]{2,1,0:T(8,128)(2,1)}) custom-call(s32[2]{0:T(128)S(1)} %pad_add_fusion.2.range_ref, s32[64]{0:T(128)S(1)} %select_reduce_fusion.2.order_ref, s32[192]{0:T(256)S(1)} %get-tuple-element.26.table_ref, ...), custom_call_target="tpu_custom_call", output_to_operand_aliasing={{1}: (11, {})} | custom-call | flops 20700000256 | tf_op jit(solution)/shard_map/attend_blocks/pallas_call | solution.py:369
  137.3 5.3 %collective-permute-done.7.rest_5_ = bf16[25,64,256]{2,1,0:T(8,128)(2,1)S(1)} collective-permute-done((bf16[25,64,256]{2,1,0:T(8,128)(2,1)S(1)}, bf16[25,64,256]{2,1,0:T(8,128)(2,1)S(1)}, u32[]{:S(2)}, u32[]{:S(2)}) %collective-permute-start.7) | collective-permute-done | bytes 819232 | tf_op jit(solution)/shard_map/ppermute | solution.py:468
  142.6 15.4 %attend_blocks.4 = (bf16[64,64,256]{2,1,0:T(8,128)(2,1)}, bf16[367,64,256]{2,1,0:T(8,128)(2,1)}) custom-call(s32[2]{0:T(128)S(1)} %pad_add_fusion.1.range_ref, s32[64]{0:T(128)S(1)} %select_reduce_fusion.2.order_ref, s32[192]{0:T(256)S(1)} %get-tuple-element.26.table_ref, ...), custom_call_target="tpu_custom_call", output_to_operand_aliasing={{1}: (12, {}), {0}: (13, {})} | custom-call | flops 20700000256 | tf_op jit(solution)/shard_map/attend_blocks/pallas_call | solution.py:369
  158.0 20.2 %attend_blocks.5 = (bf16[64,64,256]{2,1,0:T(8,128)(2,1)}, bf16[367,64,256]{2,1,0:T(8,128)(2,1)}) custom-call(s32[2]{0:T(128)S(1)} %pad_add_fusion.range_ref, s32[64]{0:T(128)S(1)} %select_reduce_fusion.2.order_ref, s32[192]{0:T(256)S(1)} %get-tuple-element.26.table_ref, ...), custom_call_target="tpu_custom_call", output_to_operand_aliasing={{1}: (10, {}), {0}: (11, {})} | custom-call | flops 20700000256 | tf_op jit(solution)/shard_map/attend_blocks/pallas_call | solution.py:369
  (51 shorter events, 1.4 us)
Async XLA Ops:
  0.0 58.6 %collective-permute-start.4 = (s32[4096]{0:T(1024)}, s32[4096]{0:T(1024)S(1)}, u32[]{:S(2)}, u32[]{:S(2)}) collective-permute-start(s32[4096]{0:T(1024)} %param.9), channel_id=1, source_target_pairs={{0,8},{1,9},{2,10},{3,11},{4,0},{5,1},{6,2},{7,3},{8,12},{9,13},{1... | collective-permute-start | bytes 49160 | tf_op jit(solution)/shard_map/ppermute | solution.py:468
  0.0 58.6 %collective-permute-start.3 = (bf16[4096,256]{1,0:T(8,128)(2,1)}, bf16[4096,256]{1,0:T(8,128)(2,1)}, u32[]{:S(2)}, u32[]{:S(2)}) collective-permute-start(bf16[4096,256]{1,0:T(8,128)(2,1)} %features_ref.1), channel_id=1, source_target_pairs={{0,8},{1,9},{2,10},{3,11},{4,0},{5,1},{6,2},{7,3},{8,12},{9,13},{1... | collective-permute-start | bytes 6291464 | tf_op jit(solution)/shard_map/ppermute | solution.py:468
  3.0 0.7 copy-start.10
  3.8 9.2 %copy-start.15 = (s32[64,3]{0,1:T(4,128)S(1)}, s32[64,3]{0,1:T(4,128)}, u32[]{:S(2)}) copy-start(s32[64,3]{0,1:T(4,128)} %param.10) | copy-start | bytes 2308
  3.8 15.2 %copy-start.13 = (bf16[256,256]{1,0:T(8,128)(2,1)S(1)}, bf16[256,256]{1,0:T(8,128)(2,1)}, u32[]{:S(2)}) copy-start(bf16[256,256]{1,0:T(8,128)(2,1)} %param.11) | copy-start | bytes 393220
  10.1 1.3 copy-start.11
  11.4 56.1 %collective-permute-start = (bf16[64,64,256]{2,1,0:T(8,128)(2,1)}, bf16[64,64,256]{2,1,0:T(8,128)(2,1)S(1)}, u32[]{:S(2)}, u32[]{:S(2)}) collective-permute-start(bf16[64,64,256]{2,1,0:T(8,128)(2,1)} %bitcast.7.rest_0_.refs_0_), channel_id=1, source_target_pairs={{0,2},{1,3},{2,0},{3,1},{4,6},{5,7},{6,4},{7,5},{8,10},{9,11},{10,... | collective-permute-start | bytes 6291464 | tf_op jit(solution)/shard_map/ppermute | solution.py:468
  14.2 44.3 %all-to-all-start = ((s32[8,1,200]{2,1,0:T(1,128)}), s32[8,1,200]{2,1,0:T(1,128)S(1)}, u32[]{:S(2)}, u32[]{:S(2)}) async-start(s32[8,1,200]{2,1,0:T(1,128)} %broadcast_in_dim.108), calls=%async_computation | async-start | bytes 16384 | tf_op jit(solution)/shard_map/all_to_all | solution.py:485
  63.9 2.1 %copy-start.2 = (bf16[4096,256]{1,0:T(8,128)(2,1)}, bf16[4096,256]{1,0:T(8,128)(2,1)S(1)}, u32[]{:S(2)}) copy-start(bf16[4096,256]{1,0:T(8,128)(2,1)S(1)} %place_rows.3) | copy-start | bytes 6291460
  66.0 5.5 %copy-start.5 = (bf16[25,64,256]{2,1,0:T(8,128)(2,1)}, bf16[25,64,256]{2,1,0:T(8,128)(2,1)S(1)}, u32[]{:S(2)}) copy-start(bf16[25,64,256]{2,1,0:T(8,128)(2,1)S(1)} %get-tuple-element.16) | copy-start | bytes 2457604
  66.0 11.3 %copy-start.14 = (bf16[256,256]{1,0:T(8,128)(2,1)S(1)}, bf16[256,256]{1,0:T(8,128)(2,1)}, u32[]{:S(2)}) copy-start(bf16[256,256]{1,0:T(8,128)(2,1)} %param.13) | copy-start | bytes 393220
  66.0 18.7 %collective-permute-start.6 = (bf16[25,64,256]{2,1,0:T(8,128)(2,1)}, bf16[25,64,256]{2,1,0:T(8,128)(2,1)S(1)}, u32[]{:S(2)}, u32[]{:S(2)}) collective-permute-start(bf16[25,64,256]{2,1,0:T(8,128)(2,1)} %get-tuple-element.17), channel_id=1, source_target_pairs={{0,2},{1,3},{2,0},{3,1},{4,6},{5,7},{6,4},{7,5},{8,10},{9,11},{10,... | collective-permute-start | bytes 2457608 | tf_op jit(solution)/shard_map/ppermute | solution.py:468
  67.5 4.0 %copy-start = (bf16[64,64,256]{2,1,0:T(8,128)(2,1)}, bf16[64,64,256]{2,1,0:T(8,128)(2,1)S(1)}, u32[]{:S(2)}) copy-start(bf16[64,64,256]{2,1,0:T(8,128)(2,1)S(1)} %collective-permute-done.rest_1_.rest_0_.refs_2_) | copy-start | bytes 6291460
  71.5 37.0 %collective-permute-start.1 = (bf16[50,64,256]{2,1,0:T(8,128)(2,1)}, bf16[50,64,256]{2,1,0:T(8,128)(2,1)}, u32[]{:S(2)}, u32[]{:S(2)}) collective-permute-start(bf16[50,64,256]{2,1,0:T(8,128)(2,1)} %pick_blocks.5), channel_id=1, source_target_pairs={{0,4},{1,5},{2,6},{3,7},{4,12},{5,13},{6,14},{7,15},{8,0},{9,1},{1... | collective-permute-start | bytes 4915208 | tf_op jit(solution)/shard_map/ppermute | solution.py:468
  84.7 1.6 copy-start.3
  86.3 2.6 %copy-start.6 = (bf16[25,64,256]{2,1,0:T(8,128)(2,1)S(1)}, bf16[25,64,256]{2,1,0:T(8,128)(2,1)}, u32[]{:S(2)}) copy-start(bf16[25,64,256]{2,1,0:T(8,128)(2,1)} %copy-done.5) | copy-start | bytes 2457604
  86.3 6.1 %copy-start.4 = (bf16[4096,256]{1,0:T(8,128)(2,1)S(1)}, bf16[4096,256]{1,0:T(8,128)(2,1)}, u32[]{:S(2)}) copy-start(bf16[4096,256]{1,0:T(8,128)(2,1)} %copy-done.2) | copy-start | bytes 6291460
  87.2 26.8 %collective-permute-start.9 = (bf16[25,64,256]{2,1,0:T(8,128)(2,1)S(1)}, bf16[25,64,256]{2,1,0:T(8,128)(2,1)S(1)}, u32[]{:S(2)}, u32[]{:S(2)}) collective-permute-start(bf16[25,64,256]{2,1,0:T(8,128)(2,1)S(1)} %pick_blocks.9), channel_id=1, source_target_pairs={{0,2},{1,3},{2,0},{3,1},{4,6},{5,7},{6,4},{7,5},{8,10},{9,11},{10,... | collective-permute-start | bytes 2457608 | tf_op jit(solution)/shard_map/ppermute | solution.py:468
  88.9 48.4 %collective-permute-start.5 = (bf16[25,64,256]{2,1,0:T(8,128)(2,1)S(1)}, bf16[25,64,256]{2,1,0:T(8,128)(2,1)S(1)}, u32[]{:S(2)}, u32[]{:S(2)}) collective-permute-start(bf16[25,64,256]{2,1,0:T(8,128)(2,1)S(1)} %copy-done.6), channel_id=1, source_target_pairs={{8,12},{9,13},{10,14},{11,15},{4,0},{5,1},{6,2},{7,3},{24,28},{25,... | collective-permute-start | bytes 2457608 | tf_op jit(solution)/shard_map/ppermute | solution.py:468
  97.3 11.2 %copy-start.1 = (bf16[64,64,256]{2,1,0:T(8,128)(2,1)S(1)}, bf16[64,64,256]{2,1,0:T(8,128)(2,1)}, u32[]{:S(2)}) copy-start(bf16[64,64,256]{2,1,0:T(8,128)(2,1)} %copy-done) | copy-start | bytes 6291460
  99.3 14.7 %copy-start.7 = (bf16[256,256]{1,0:T(8,128)(2,1)S(1)}, bf16[256,256]{1,0:T(8,128)(2,1)}, u32[]{:S(2)}) copy-start(bf16[256,256]{1,0:T(8,128)(2,1)} %rest_0_.5) | copy-start | bytes 393220
  99.3 14.7 %copy-start.8 = (bf16[256,256]{1,0:T(8,128)(2,1)S(1)}, bf16[256,256]{1,0:T(8,128)(2,1)}, u32[]{:S(2)}) copy-start(bf16[256,256]{1,0:T(8,128)(2,1)} %rest_2_.5) | copy-start | bytes 393220
  99.3 14.7 %copy-start.9 = (bf16[256,256]{1,0:T(8,128)(2,1)S(1)}, bf16[256,256]{1,0:T(8,128)(2,1)}, u32[]{:S(2)}) copy-start(bf16[256,256]{1,0:T(8,128)(2,1)} %rest_3_.5) | copy-start | bytes 393220
  99.4 37.9 %collective-permute-start.8 = (bf16[25,64,256]{2,1,0:T(8,128)(2,1)S(1)}, bf16[25,64,256]{2,1,0:T(8,128)(2,1)S(1)}, u32[]{:S(2)}, u32[]{:S(2)}) collective-permute-start(bf16[25,64,256]{2,1,0:T(8,128)(2,1)S(1)} %pick_blocks.8), channel_id=1, source_target_pairs={{4,8},{5,9},{6,10},{7,11},{8,4},{9,5},{10,6},{11,7},{20,24},{21,25... | collective-permute-start | bytes 2457608 | tf_op jit(solution)/shard_map/ppermute | solution.py:468
  101.4 41.2 %collective-permute-start.7 = (bf16[25,64,256]{2,1,0:T(8,128)(2,1)S(1)}, bf16[25,64,256]{2,1,0:T(8,128)(2,1)S(1)}, u32[]{:S(2)}, u32[]{:S(2)}) collective-permute-start(bf16[25,64,256]{2,1,0:T(8,128)(2,1)S(1)} %collective-permute-done.6.rest_1_), channel_id=1, source_target_pairs={{8,12},{9,13},{10,14},{11,15},{4,0},{5,1},{6,2},{7,3},{24,28},{25,... | collective-permute-start | bytes 2457608 | tf_op jit(solution)/shard_map/ppermute | solution.py:468
  109.4 48.6 %collective-permute-start.2 = (bf16[25,64,256]{2,1,0:T(8,128)(2,1)S(1)}, bf16[25,64,256]{2,1,0:T(8,128)(2,1)S(1)}, u32[]{:S(2)}, u32[]{:S(2)}) collective-permute-start(bf16[25,64,256]{2,1,0:T(8,128)(2,1)S(1)} %pick_blocks.6), channel_id=1, source_target_pairs={{4,8},{5,9},{6,10},{7,11},{8,4},{9,5},{10,6},{11,7},{20,24},{21,25... | collective-permute-start | bytes 2457608 | tf_op jit(solution)/shard_map/ppermute | solution.py:468
  114.1 1.6 copy-start.12

commit v12 on v11

--- a/solution.py
+++ b/solution.py
@@ -40,8 +40,7 @@
     return row_head == lane_head
 
 
-def place_kernel(features_ref, assignment_ref, *rest, outputs):
-    normed_ref, *placed_ref = rest[len(rest) - outputs :]
+def place_kernel(features_ref, assignment_ref, placed_ref, normed_ref):
     walkers, _, rows = assignment_ref.shape
     lane = 128
     columns = lax.broadcasted_iota(jnp.int32, (lane, rows), 1)
@@ -54,27 +53,25 @@
             one_hot = jnp.where(chosen == columns, 1.0, 0.0).astype(jnp.bfloat16)
             placed = jnp.dot(one_hot, features, preferred_element_type=jnp.float32)
             here = pl.ds(walker * rows + part * lane, lane)
-            if placed_ref:
-                placed_ref[0][here, :] = placed.astype(jnp.bfloat16)
+            placed_ref[here, :] = placed.astype(jnp.bfloat16)
             normed_ref[here, :] = layer_norm(placed).astype(jnp.bfloat16)
 
 
-def place(features, assignment, outputs, after=()):
+def place(features, assignment):
     width = features.shape[1]
     walkers, _, rows = assignment.shape
     local = pl.BlockSpec((2 * rows, width), lambda i: (i, 0))
     out = jax.ShapeDtypeStruct(features.shape, jnp.bfloat16)
     return pl.pallas_call(
-        functools.partial(place_kernel, outputs=outputs),
+        place_kernel,
         grid=(walkers // 2,),
-        in_specs=[local, pl.BlockSpec((2, 1, rows), lambda i: (i, 0, 0))]
-        + [pl.BlockSpec(memory_space=pl.ANY)] * len(after),
-        out_specs=[local] * outputs,
-        out_shape=[out] * outputs,
-        cost_estimate=lasting(7),
+        in_specs=[local, pl.BlockSpec((2, 1, rows), lambda i: (i, 0, 0))],
+        out_specs=[local] * 2,
+        out_shape=[out] * 2,
+        cost_estimate=lasting(6),
         compiler_params=kernel_params(),
         name="place_rows",
-    )(features, assignment, *after)
+    )(features, assignment)
 
 
 def choose(index, values):
@@ -119,33 +116,86 @@
     )(position, wanted, *sources, *after)
 
 
-def query_kernel(normed_ref, query_w_ref, query_ref, *, cluster, head_width):
-    width = normed_ref.shape[1]
-    mask = head_mask((width, GROUP * cluster), head_width, cluster)
-    for block in range(query_ref.shape[0]):
-        own = normed_ref[pl.ds(block * cluster, cluster), :]
-        own = jnp.concatenate([own] * GROUP, axis=0)
-        query = lax.dot_general(query_w_ref[...], own, NT, preferred_element_type=jnp.float32)
-        query = query * (math.log2(math.e) / head_width**0.5)
-        query_ref[block] = jnp.where(mask, query, 0.0).astype(jnp.bfloat16)
-
-
-def project_queries(normed, w_query, cluster):
+def tiles_of(query, first, span):
+    one = query[first : first + span]
+    two = query[first + span : first + 2 * span]
+    zeros = jnp.zeros_like(one)
+    return jnp.concatenate(
+        [jnp.concatenate([one, zeros], axis=1), jnp.concatenate([zeros, two], axis=1)], axis=0
+    )
+
+
+def own_kernel(
+    normed_ref, query_w_ref, key_w_ref, value_w_ref, query_ref, own_ref, stats_ref, *, head_width
+):
+    blocks, width, tile = query_ref.shape
+    cluster = tile // GROUP
+    span = GROUP * head_width
+    mask = head_mask((width, tile), head_width, cluster)
+    scale = math.log2(math.e) / head_width**0.5
+    ones = jnp.ones((16, cluster), jnp.bfloat16)
+    rows = normed_ref[...]
+    keys = jnp.dot(rows, key_w_ref[...], preferred_element_type=jnp.float32).astype(jnp.bfloat16)
+    queries = []
+    for block in range(blocks):
+        own = rows[block * cluster : (block + 1) * cluster]
+        tiled = jnp.concatenate([own] * GROUP, axis=0)
+        query = lax.dot_general(query_w_ref[...], tiled, NT, preferred_element_type=jnp.float32)
+        query = jnp.where(mask, query * scale, 0.0).astype(jnp.bfloat16)
+        query_ref[block] = query
+        queries.append(query)
+    for block in range(blocks):
+        own = rows[block * cluster : (block + 1) * cluster]
+        value = lax.dot_general(value_w_ref[...], own, NT, preferred_element_type=jnp.float32)
+        value = value.astype(jnp.bfloat16)
+        tops, totals = [], []
+        for pair in range(HEADS // GROUP // 2):
+            first = pair * 2 * span
+            scores = jnp.dot(
+                keys[block * cluster : (block + 1) * cluster, first : first + 2 * span],
+                tiles_of(queries[block], first, span),
+                preferred_element_type=jnp.float32,
+            )
+            top = jnp.max(scores, axis=0, keepdims=True)
+            weights = jnp.exp2(scores - top).astype(jnp.bfloat16)
+            for half in range(2):
+                at = first + half * span
+                here = slice(half * tile, (half + 1) * tile)
+                lifted = jnp.concatenate([value[at : at + span], ones], axis=0)
+                product = jnp.dot(lifted, weights[:, here], preferred_element_type=jnp.float32)
+                total = product[span : span + 1]
+                result = jnp.where(mask[:span], product[:span] * (1.0 / total), 0.0)
+                own_ref[block, at : at + span, :] = result.astype(jnp.bfloat16)
+                tops.append(top[:, here])
+                totals.append(total)
+        stats_ref[block] = jnp.concatenate(tops + totals, axis=0)
+
+
+def own_part(normed, w_query, w_key, w_value, cluster):
     rows, width = normed.shape
     blocks = rows // cluster
+    tile = GROUP * cluster
+    tiles = HEADS // GROUP
+    whole = pl.BlockSpec((width, width), lambda i: (0, 0))
+    square = pl.BlockSpec((STEP, width, tile), lambda i: (i, 0, 0))
     return pl.pallas_call(
-        functools.partial(query_kernel, cluster=cluster, head_width=width // HEADS),
-        grid=(blocks // SUB,),
-        in_specs=[
-            pl.BlockSpec((SUB * cluster, width), lambda i: (i, 0)),
-            pl.BlockSpec((width, width), lambda i: (0, 0)),
+        functools.partial(own_kernel, head_width=width // HEADS),
+        grid=(blocks // STEP,),
+        in_specs=[pl.BlockSpec((STEP * cluster, width), lambda i: (i, 0)), whole, whole, whole],
+        out_specs=[
+            square,
+            square,
+            pl.BlockSpec((STEP, 2 * tiles, tile), lambda i: (i, 0, 0)),
         ],
-        out_specs=pl.BlockSpec((SUB, width, GROUP * cluster), lambda i: (i, 0, 0)),
-        out_shape=jax.ShapeDtypeStruct((blocks, width, GROUP * cluster), jnp.bfloat16),
-        cost_estimate=lasting(6.5),
+        out_shape=[
+            jax.ShapeDtypeStruct((blocks, width, tile), jnp.bfloat16),
+            jax.ShapeDtypeStruct((blocks, width, tile), jnp.bfloat16),
+            jax.ShapeDtypeStruct((blocks, 2 * tiles, tile), jnp.float32),
+        ],
+        cost_estimate=lasting(20),
         compiler_params=kernel_params(),
-        name="queries",
-    )(normed, w_query.T)
+        name="own_blocks",
+    )(normed, w_query.T, w_key, w_value.T)
 
 
 def collect_kernel(*refs, places):
@@ -182,31 +232,33 @@
     order_ref,
     table_ref,
     query_ref,
+    own_ref,
+    stats_ref,
     placed_ref,
     *rest,
-    own_at,
     head_width,
     places,
 ):
     weight_refs, rest = rest[:4], rest[4:]
     piece_refs = rest[: len(places)]
-    mixed_ref, buffer_ref, query_buf, member_buf, placed_buf = rest[-11:-6]
+    mixed_ref, buffer_ref, query_buf, own_buf, stats_buf, member_buf, placed_buf = rest[-13:-6]
     attended_buf, before_buf, done_buf, in_sems, out_sems, piece_sems = rest[-6:]
     begin, count = range_ref[0], range_ref[1]
-    pair_count = member_buf.shape[2] - 1
+    pair_count = member_buf.shape[2]
     copy_pieces(piece_refs, buffer_ref, places, piece_sems)
 
     def fetches(step, slot):
         for j in range(STEP):
             block = order_ref[step * STEP + j]
             sources = [(query_ref.at[block], query_buf.at[slot, j])]
+            sources.append((own_ref.at[block], own_buf.at[slot, j]))
+            sources.append((stats_ref.at[block], stats_buf.at[slot, j]))
             sources.append((placed_ref.at[block], placed_buf.at[slot, j]))
-            sources.append((buffer_ref.at[own_at + block], member_buf.at[slot, j, 0]))
             for n in range(pair_count):
                 listed = table_ref[block * pair_count + n]
-                sources.append((buffer_ref.at[listed], member_buf.at[slot, j, 1 + n]))
+                sources.append((buffer_ref.at[listed], member_buf.at[slot, j, n]))
             for n, (source_, target) in enumerate(sources):
-                sem = in_sems.at[slot, j * (pair_count + 3) + n]
+                sem = in_sems.at[slot, j * (pair_count + 4) + n]
                 yield pltpu.make_async_copy(source_, target, sem)
 
     def stores(step):
@@ -224,7 +276,13 @@
         for copy in fetches(begin + i, slot):
             copy.wait()
         attended, mixed = attend_step(
-            query_buf.at[slot], member_buf.at[slot], *weight_refs[:2], head_width, finish
+            query_buf.at[slot],
+            own_buf.at[slot],
+            stats_buf.at[slot],
+            member_buf.at[slot],
+            *weight_refs[:2],
+            head_width,
+            finish,
         )
 
         @pl.when(i > 1)
@@ -276,7 +334,9 @@
     return mixed.astype(jnp.bfloat16)
 
 
-def attend_step(query_ref, member_ref, key_w_ref, value_w_ref, head_width, meanwhile):
+def attend_step(
+    query_ref, own_ref, stats_ref, member_ref, key_w_ref, value_w_ref, head_width, meanwhile
+):
     _, members_count, cluster, width = member_ref.shape
     span = GROUP * head_width
     tile = GROUP * cluster
@@ -284,8 +344,8 @@
     fold_row = lax.broadcasted_iota(jnp.int32, (cluster, tile), 0)
     fold_lane = lax.broadcasted_iota(jnp.int32, (cluster, tile), 1) % cluster
     fold = jnp.where(fold_row == fold_lane, 1.0, 0.0).astype(jnp.bfloat16)
-    zeros = jnp.zeros((span, tile), jnp.bfloat16)
-    ones = jnp.ones((16, tile), jnp.bfloat16)
+    ones = jnp.ones((16, members_count * cluster), jnp.bfloat16)
+    tiles = HEADS // GROUP
     units = [(block, pair) for block in range(STEP) for pair in range(HEADS // GROUP // 2)]
     keys, values = {}, {}
 
@@ -299,34 +359,34 @@
     def scores_of(block, pair):
         if pair == 0:
             gather(block)
-        first = query_ref[block, pair * 2 * span : (pair * 2 + 1) * span, :]
-        other = query_ref[block, (pair * 2 + 1) * span : (pair + 1) * 2 * span, :]
-        both = jnp.concatenate(
-            [
-                jnp.concatenate([first, zeros], axis=1),
-                jnp.concatenate([zeros, other], axis=1),
-            ],
-            axis=0,
-        )
+        first = pair * 2 * span
         return jnp.dot(
-            keys[block][:, pair * 2 * span : (pair + 1) * 2 * span],
-            both,
+            keys[block][:, first : first + 2 * span],
+            tiles_of(query_ref[block], first, span),
             preferred_element_type=jnp.float32,
         )
 
-    def weights_of(scores):
-        top = jnp.max(scores, axis=0, keepdims=True)
-        return jnp.exp2((scores - top).astype(jnp.bfloat16))
-
-    def products_of(block, pair, weights):
+    def weights_of(block, pair, scores):
+        own_top = jnp.concatenate(
+            [stats_ref[block, t : t + 1, :] for t in (2 * pair, 2 * pair + 1)], axis=1
+        )
+        top = jnp.maximum(jnp.max(scores, axis=0, keepdims=True), own_top)
+        weights = jnp.exp2((scores - top).astype(jnp.bfloat16))
+        return weights, jnp.exp2(own_top - top)
+
+    def products_of(block, pair, weights, own_factor):
         for half in range(2):
             t = pair * 2 + half
+            here = slice(half * tile, (half + 1) * tile)
             lifted = jnp.concatenate([values[block][t * span : (t + 1) * span], ones], axis=0)
-            here = weights[:, half * tile : (half + 1) * tile]
-            yield jnp.dot(lifted, here, preferred_element_type=jnp.float32)
-
-    def scaled(product):
-        result = product[:span] * (1.0 / product[span : span + 1])
+            product = jnp.dot(lifted, weights[:, here], preferred_element_type=jnp.float32)
+            yield block, t, product, own_factor[:, here]
+
+    def scaled(block, t, product, own_factor):
+        own_total = stats_ref[block, tiles + t : tiles + t + 1, :] * own_factor
+        inverse = 1.0 / (product[span : span + 1] + own_total)
+        own = own_ref[block, t * span : (t + 1) * span, :].astype(jnp.float32)
+        result = product[:span] * inverse + own * (own_total * inverse)
         return jnp.where(diagonal, result, 0.0).astype(jnp.bfloat16)
 
     count = len(units)
@@ -337,12 +397,13 @@
         if at + SCORES_AHEAD < count:
             scores[at + SCORES_AHEAD] = scores_of(*units[at + SCORES_AHEAD])
         if 0 <= at + WEIGHTS_AHEAD < count:
-            weights[at + WEIGHTS_AHEAD] = weights_of(scores.pop(at + WEIGHTS_AHEAD))
+            ahead = at + WEIGHTS_AHEAD
+            weights[ahead] = weights_of(*units[ahead], scores.pop(ahead))
         if 0 <= at < count:
-            products[at] = list(products_of(*units[at], weights.pop(at)))
+            products[at] = list(products_of(*units[at], *weights.pop(at)))
         if at > 0:
-            pieces += [scaled(product) for product in products.pop(at - 1)]
-            if len(pieces) == HEADS // GROUP:
+            pieces += [scaled(*product) for product in products.pop(at - 1)]
+            if len(pieces) == tiles:
                 stacked = jnp.concatenate(pieces, axis=0)
                 folded = lax.dot_general(fold, stacked, NT, preferred_element_type=jnp.float32)
                 attended.append(folded.astype(jnp.bfloat16))
@@ -350,21 +411,21 @@
     return jnp.concatenate(attended, axis=0), finished
 
 
-def attend(begin, count, order, table, queries, placed, weights, buffer, pieces, places, own_at, so_far):
+def attend(begin, count, order, table, own, placed, weights, buffer, pieces, places, so_far):
     blocks, cluster, width = placed.shape
     pair_count = table.shape[0] // blocks
     smem = pl.BlockSpec(memory_space=pltpu.SMEM)
     vmem = pl.BlockSpec(memory_space=pltpu.VMEM)
     hbm = pl.BlockSpec(memory_space=pl.ANY)
-    in_specs = [smem, smem, smem, hbm, hbm] + [vmem] * (4 + len(pieces)) + [hbm]
+    in_specs = [smem] * 3 + [hbm] * (len(own) + 1) + [vmem] * (4 + len(pieces)) + [hbm]
     aliases = {len(in_specs) - 1: 1}
-    operands = [queries, placed, *weights, *pieces, buffer]
+    operands = [*own, placed, *weights, *pieces, buffer]
     if so_far is not None:
         aliases[len(in_specs)] = 0
         in_specs.append(hbm)
         operands.append(so_far)
     kernel = functools.partial(
-        attend_kernel, own_at=own_at, head_width=width // HEADS, places=places
+        attend_kernel, head_width=width // HEADS, places=places
     )
     return pl.pallas_call(
         kernel,
@@ -375,13 +436,13 @@
             jax.ShapeDtypeStruct(buffer.shape, jnp.bfloat16),
         ],
         scratch_shapes=[
-            pltpu.VMEM((2, STEP) + queries.shape[1:], jnp.bfloat16),
-            pltpu.VMEM((2, STEP, pair_count + 1, cluster, width), jnp.bfloat16),
+            *[pltpu.VMEM((2, STEP) + x.shape[1:], x.dtype) for x in own],
+            pltpu.VMEM((2, STEP, pair_count, cluster, width), jnp.bfloat16),
             pltpu.VMEM((2, STEP, cluster, width), jnp.bfloat16),
             pltpu.VMEM((STEP * cluster, width), jnp.bfloat16),
             pltpu.VMEM((STEP * cluster, width), jnp.bfloat16),
             pltpu.VMEM((STEP, cluster, width), jnp.bfloat16),
-            pltpu.SemaphoreType.DMA((2, STEP * (pair_count + 3))),
+            pltpu.SemaphoreType.DMA((2, STEP * (pair_count + 4))),
             pltpu.SemaphoreType.DMA((STEP,)),
             pltpu.SemaphoreType.DMA((len(pieces),)),
         ],
@@ -475,8 +536,6 @@
     second_moves = across_z(enumerate(FROM))
     middle_moves = across_z([(1, 2), (2, 1)])
     outward_moves = across_z([(2, 3), (1, 0)])
-
-    raw_passed, to_passed = moved(features, first_moves), moved(assignment, first_moves)
 
     listed = pairs.reshape(-1)
     owner = listed // block_count // stride
@@ -493,20 +552,19 @@
 
     shape = (block_count // SUB, 1, SUB * cluster)
     block_shape = (block_count, cluster, width)
-    normed, placed = place(features, assignment.reshape(shape), 2)
+    placed, normed = place(features, assignment.reshape(shape))
     blocks = normed.reshape(block_shape)
-    queries = project_queries(normed, w_query, cluster)
+    own = own_part(normed, w_query, w_key, w_value, cluster)
     own_at = 7 * capacity
     passed_at = own_at + block_count
     beside_at = passed_at + block_count
     total = beside_at + block_count
 
     beside = moved(blocks, swap)
-    (passed,) = place(raw_passed, to_passed.reshape(shape), 1, after=(queries,))
-    passed = passed.reshape(block_shape)
-    (second,) = pick(at_position, wanted, (blocks, beside), SECOND_PLAN)
+    passed = moved(blocks, first_moves)
+    (second,) = pick(at_position, wanted, (blocks, beside), SECOND_PLAN, after=own[2:])
     second = moved(second, second_moves)
-    on, outward = pick(at_position, wanted, (passed,), ON_PLAN)
+    on, outward = pick(at_position, wanted, (passed,), ON_PLAN, after=own[2:])
     on = moved(on, swap)
     outward = moved(outward, outward_moves)
     (near,) = pick(at_position, wanted, (passed,), NEAR_PLAN, after=(on,))
@@ -544,7 +602,7 @@
     marks = [0, ends[0] // STEP, ends[1] // STEP, block_count // STEP]
     phases = [(marks[n], marks[n + 1] - marks[n]) for n in range(3)]
     weights = (w_key, w_value.T, w_out, w_mix)
-    shared = (order, table, queries, placed.reshape(blocks.shape), weights)
+    shared = (order, table, own, placed.reshape(blocks.shape), weights)
     arrivals = (
         ((near, 0), (second, 1)),
         ((outward, 3), (on, 4), (middle, 5)),
@@ -554,7 +612,7 @@
     for phase, arrived in zip(phases, arrivals, strict=True):
         pieces = [piece for piece, _ in arrived]
         places = tuple(at * capacity for _, at in arrived)
-        mixed, buffer = attend(*phase, *shared, buffer, pieces, places, own_at, mixed)
+        mixed, buffer = attend(*phase, *shared, buffer, pieces, places, mixed)
     return mixed.reshape(rows_dev, width)
 
 

time: 181 us -> 177 us (0.978)
  the two profiles are of different devices: /device:TPU:8 before, /device:TPU:1 now
where the time goes in v12:
time: 177 us; the launch traced here: 176 us
  Pallas kernels  103 us (58%)
  waiting for transfers between devices  45 us (25%)
  starting transfers between devices  13.3 us (8%)
  local copies, waits for them, and re-layouts  8 us (5%)
  between operations  5.5 us (3%)
    pallas_call x3, Pallas kernels, attend(): pl.pallas_call(kernel, in_specs=in_specs, out_specs=[hbm, hbm], out_shape...  49.7 us
    ppermute x9, waiting for transfers between devices, moved(): return lax.ppermute(x, 'elec', pairs_of)  33.5 us
    pallas_call x1, Pallas kernels, own_part(): pl.pallas_call(functools.partial(own_kernel, head_width=width // HEADS),...  29.6 us
    pallas_call x5, Pallas kernels, pick(): pl.pallas_call(functools.partial(pick_kernel, plan=plan, capacity=capacit...  11.7 us
    all_to_all x1, waiting for transfers between devices, body(): lax.all_to_all(jnp.broadcast_to(tables[None], (SPAN, SPAN * capacity)), '...  11.6 us
    ppermute x9, starting transfers between devices, moved(): return lax.ppermute(x, 'elec', pairs_of)  10.1 us
    unnamed x36, local copies, waits for them, and re-layouts  7.26 us
    pallas_call x1, Pallas kernels, place(): pl.pallas_call(place_kernel, grid=(walkers // 2,), in_specs=[local, pl.Bl...  6.37 us
  transfers between devices with their start and end apart: 10, of which 5 were waited for; matrix products, arithmetic and copies ran while one was open for 2% of the time, Pallas kernels for 54%

profile of v12, /device:TPU:1, one launch (start us, length us, event | category | flops | bytes accessed | tf_op | source)
XLA Modules:
  0.0 176.4 jit_solution(2849054243276259263)
XLA Ops:
  0.0 0.7 copy-done.7
  0.7 6.4 %place_rows.1 = (bf16[4096,256]{1,0:T(8,128)(2,1)S(1)}, bf16[4096,256]{1,0:T(8,128)(2,1)}) custom-call(bf16[4096,256]{1,0:T(8,128)(2,1)} %features_ref.1, s32[8,1,512]{2,1,0:T(1,128)S(1)} %bitcast.24), custom_call_target="tpu_custom_call" | custom-call | flops 6899999744 | tf_op jit(solution)/shard_map/place_rows/pallas_call | solution.py:65
  7.1 1.4 copy-done.8
  8.5 3.1 %collective-permute-start.3 = (bf16[64,64,256]{2,1,0:T(8,128)(2,1)}, bf16[64,64,256]{2,1,0:T(8,128)(2,1)}, u32[]{:S(2)}, u32[]{:S(2)}) collective-permute-start(bf16[64,64,256]{2,1,0:T(8,128)(2,1)} %bitcast.7.rest_0_.refs_0_), channel_id=1, source_target_pairs={{0,8},{1,9},{2,10},{3,11},{4,0},{5,1},{6,2},{7,3},{8,12},{9,13},{1... | collective-permute-start | bytes 6291464 | tf_op jit(solution)/shard_map/ppermute | solution.py:529
  11.6 1.2 collective-permute-start
  13.5 0.6 broadcast_in_dim.108
  14.1 3.3 %all-to-all-start = ((s32[8,1,200]{2,1,0:T(1,128)}), s32[8,1,200]{2,1,0:T(1,128)S(1)}, u32[]{:S(2)}, u32[]{:S(2)}) async-start(s32[8,1,200]{2,1,0:T(1,128)} %broadcast_in_dim.108), calls=%async_computation | async-start | bytes 16384 | tf_op jit(solution)/shard_map/all_to_all | solution.py:544
  17.6 29.6 %own_blocks.1 = (bf16[64,256,256]{2,1,0:T(8,128)(2,1)}, bf16[64,256,256]{2,1,0:T(8,128)(2,1)}, f32[64,8,256]{2,1,0:T(8,128)S(1)}) custom-call(bf16[4096,256]{1,0:T(8,128)(2,1)} %get-tuple-element.17.normed_ref, bf16[256,256]{1,0:T(8,128)(2,1)S(1)} %bitcast.18, bf16[256,256]{1,0:T(8,128)(2,1)S(1)} %copy-done.4, bf16[256,256]{1,0:T(8,128)(2,1)S(1)} %bitcast.14), custom_call_target="tpu_custom_call" | custom-call | flops 23000000512 | tf_op jit(solution)/shard_map/own_blocks/pallas_call | solution.py:181
  47.2 11.6 %all-to-all-done = s32[8,1,200]{2,1,0:T(1,128)S(1)} async-done(((s32[8,1,200]{2,1,0:T(1,128)}), s32[8,1,200]{2,1,0:T(1,128)S(1)}, u32[]{:S(2)}, u32[]{:S(2)}) %all-to-all-start) | async-done | bytes 6432 | tf_op jit(solution)/shard_map/all_to_all | solution.py:544
  58.7 3.0 %pick_blocks.7 = (bf16[25,64,256]{2,1,0:T(8,128)(2,1)}, bf16[25,64,256]{2,1,0:T(8,128)(2,1)S(1)}) custom-call(s32[1]{0:T(128)} %bitcast.6.position_ref, s32[8,200]{1,0:T(8,128)S(1)} %bitcast.19, bf16[64,64,256]{2,1,0:T(8,128)(2,1)} %collective-permute-done.3.rest_0_.refs_1_, f32[64,8,256]{2,1,0:T(8,128)S(1)} %get-tuple-element.20.rest_2_.rest_1_.stats_ref), custom_call_target="tpu_custom_call" | custom-call | flops 1724999936 | tf_op jit(solution)/shard_map/pick_blocks/pallas_call | solution.py:106
  61.8 0.9 copy-done.2
  62.7 0.6 collective-permute-start.5
  63.3 1.3 copy-done
  64.6 1.0 copy-done.11
  65.6 3.9 %pick_blocks.5 = bf16[50,64,256]{2,1,0:T(8,128)(2,1)} custom-call(s32[1]{0:T(128)} %bitcast.6.position_ref, s32[8,200]{1,0:T(8,128)S(1)} %bitcast.20, bf16[64,64,256]{2,1,0:T(8,128)(2,1)} %bitcast.7.rest_0_.refs_0_, bf16[64,64,256]{2,1,0:T(8,128)(2,1)} %copy-done, f32[64,8,256]{2,1,0:T(8,128)S(1)} %copy-done.11), custom_call_target="tpu_custom_call" | custom-call | flops 1724999936 | tf_op jit(solution)/shard_map/pick_blocks/pallas_call | solution.py:106
  70.0 0.7 fusion.14
  76.4 4.4 %collective-permute-done.5.rest_1_ = bf16[25,64,256]{2,1,0:T(8,128)(2,1)S(1)} collective-permute-done((bf16[25,64,256]{2,1,0:T(8,128)(2,1)}, bf16[25,64,256]{2,1,0:T(8,128)(2,1)S(1)}, u32[]{:S(2)}, u32[]{:S(2)}) %collective-permute-start.5) | collective-permute-done | bytes 819232 | tf_op jit(solution)/shard_map/ppermute | solution.py:529
  80.8 1.9 %pick_blocks.9 = bf16[25,64,256]{2,1,0:T(8,128)(2,1)S(1)} custom-call(s32[1]{0:T(128)} %bitcast.6.position_ref, s32[8,200]{1,0:T(8,128)S(1)} %bitcast.21, bf16[64,64,256]{2,1,0:T(8,128)(2,1)} %collective-permute-done.3.rest_0_.refs_1_, bf16[25,64,256]{2,1,0:T(8,128)(2,1)S(1)} %collective-permute-done.5.rest_1_), custom_call_target="tpu_custom_call" | custom-call | flops 1724999936 | tf_op jit(solution)/shard_map/pick_blocks/pallas_call | solution.py:106
  82.7 0.5 collective-permute-start.8
  83.3 1.3 collective-permute-start.4
  84.6 5.5 %collect_blocks.1.rest_6_ = bf16[367,64,256]{2,1,0:T(8,128)(2,1)} custom-call(bf16[64,64,256]{2,1,0:T(8,128)(2,1)} %bitcast.7.rest_0_.refs_0_, bf16[64,64,256]{2,1,0:T(8,128)(2,1)} %collective-permute-done.3.rest_0_.refs_1_, bf16[64,64,256]{2,1,0:T(8,128)(2,1)} %copy-done), custom_call_target="tpu_custom_call" | custom-call | flops 4600000000 | tf_op jit(solution)/shard_map/collect_blocks/pallas_call | solution.py:218
  90.1 2.0 %pick_blocks.8 = bf16[25,64,256]{2,1,0:T(8,128)(2,1)S(1)} custom-call(s32[1]{0:T(128)} %bitcast.6.position_ref, s32[8,200]{1,0:T(8,128)S(1)} %bitcast.22, bf16[64,64,256]{2,1,0:T(8,128)(2,1)} %bitcast.7.rest_0_.refs_0_, bf16[25,64,256]{2,1,0:T(8,128)(2,1)S(1)} %collective-permute-done.5.rest_1_), custom_call_target="tpu_custom_call" | custom-call | flops 1724999936 | tf_op jit(solution)/shard_map/pick_blocks/pallas_call | solution.py:106
  92.2 0.8 collective-permute-start.7
  93.0 1.3 collective-permute-start.6
  94.3 11.4 %collective-permute-done.1.rest_1_.rest_5_ = bf16[50,64,256]{2,1,0:T(8,128)(2,1)S(1)} collective-permute-done((bf16[50,64,256]{2,1,0:T(8,128)(2,1)}, bf16[50,64,256]{2,1,0:T(8,128)(2,1)S(1)}, u32[]{:S(2)}, u32[]{:S(2)}) %collective-permute-start.1) | collective-permute-done | bytes 1638432 | tf_op jit(solution)/shard_map/ppermute | solution.py:529
  105.7 0.9 pick_blocks.6
  106.7 0.7 collective-permute-start.2
  107.4 1.6 copy-done.9
  109.0 16.8 %attend_blocks.3 = (bf16[64,64,256]{2,1,0:T(8,128)(2,1)}, bf16[367,64,256]{2,1,0:T(8,128)(2,1)}) custom-call(s32[2]{0:T(128)S(1)} %pad_add_fusion.2.range_ref, s32[64]{0:T(128)S(1)} %select_reduce_fusion.2.order_ref, s32[192]{0:T(256)S(1)} %get-tuple-element.32.table_ref, ...), custom_call_target="tpu_custom_call", output_to_operand_aliasing={{1}: (13, {})} | custom-call | flops 20700000256 | tf_op jit(solution)/shard_map/attend_blocks/pallas_call | solution.py:430
  125.9 17.6 %collective-permute-done.6.rest_5_ = bf16[25,64,256]{2,1,0:T(8,128)(2,1)S(1)} collective-permute-done((bf16[25,64,256]{2,1,0:T(8,128)(2,1)S(1)}, bf16[25,64,256]{2,1,0:T(8,128)(2,1)S(1)}, u32[]{:S(2)}, u32[]{:S(2)}) %collective-permute-start.6) | collective-permute-done | bytes 819232 | tf_op jit(solution)/shard_map/ppermute | solution.py:529
  143.4 30.9 %attend_blocks.4 = (bf16[64,64,256]{2,1,0:T(8,128)(2,1)}, bf16[367,64,256]{2,1,0:T(8,128)(2,1)}) custom-call(s32[2]{0:T(128)S(1)} %pad_add_fusion.1.range_ref, s32[64]{0:T(128)S(1)} %select_reduce_fusion.2.order_ref, s32[192]{0:T(256)S(1)} %get-tuple-element.32.table_ref, ...), custom_call_target="tpu_custom_call", output_to_operand_aliasing={{1}: (14, {}), {0}: (15, {})} | custom-call | flops 20700000256 | tf_op jit(solution)/shard_map/attend_blocks/pallas_call | solution.py:430
  174.4 2.0 %attend_blocks.5 = (bf16[64,64,256]{2,1,0:T(8,128)(2,1)}, bf16[367,64,256]{2,1,0:T(8,128)(2,1)}) custom-call(s32[2]{0:T(128)S(1)} %pad_add_fusion.range_ref, s32[64]{0:T(128)S(1)} %select_reduce_fusion.2.order_ref, s32[192]{0:T(256)S(1)} %get-tuple-element.32.table_ref, ...), custom_call_target="tpu_custom_call", output_to_operand_aliasing={{1}: (12, {}), {0}: (13, {})} | custom-call | flops 20700000256 | tf_op jit(solution)/shard_map/attend_blocks/pallas_call | solution.py:430
  (48 shorter events, 2.0 us)
Async XLA Ops:
  0.0 0.7 copy-start.7
  0.7 12.1 %copy-start.15 = (s32[64,3]{0,1:T(4,128)S(1)}, s32[64,3]{0,1:T(4,128)}, u32[]{:S(2)}) copy-start(s32[64,3]{0,1:T(4,128)} %param.10) | copy-start | bytes 2308
  0.7 16.6 %copy-start.13 = (bf16[256,256]{1,0:T(8,128)(2,1)S(1)}, bf16[256,256]{1,0:T(8,128)(2,1)}, u32[]{:S(2)}) copy-start(bf16[256,256]{1,0:T(8,128)(2,1)} %param.11) | copy-start | bytes 393220
  0.7 16.7 %copy-start.14 = (bf16[256,256]{1,0:T(8,128)(2,1)S(1)}, bf16[256,256]{1,0:T(8,128)(2,1)}, u32[]{:S(2)}) copy-start(bf16[256,256]{1,0:T(8,128)(2,1)} %param.13) | copy-start | bytes 393220
  0.7 16.8 %copy-start.4 = (bf16[256,256]{1,0:T(8,128)(2,1)S(1)}, bf16[256,256]{1,0:T(8,128)(2,1)}, u32[]{:S(2)}) copy-start(bf16[256,256]{1,0:T(8,128)(2,1)} %rest_0_.5) | copy-start | bytes 393220
  7.1 1.4 copy-start.8
  8.5 50.3 %collective-permute-start.3 = (bf16[64,64,256]{2,1,0:T(8,128)(2,1)}, bf16[64,64,256]{2,1,0:T(8,128)(2,1)}, u32[]{:S(2)}, u32[]{:S(2)}) collective-permute-start(bf16[64,64,256]{2,1,0:T(8,128)(2,1)} %bitcast.7.rest_0_.refs_0_), channel_id=1, source_target_pairs={{0,8},{1,9},{2,10},{3,11},{4,0},{5,1},{6,2},{7,3},{8,12},{9,13},{1... | collective-permute-start | bytes 6291464 | tf_op jit(solution)/shard_map/ppermute | solution.py:529
  11.6 51.7 %collective-permute-start = (bf16[64,64,256]{2,1,0:T(8,128)(2,1)}, bf16[64,64,256]{2,1,0:T(8,128)(2,1)S(1)}, u32[]{:S(2)}, u32[]{:S(2)}) collective-permute-start(bf16[64,64,256]{2,1,0:T(8,128)(2,1)} %bitcast.7.rest_0_.refs_0_), channel_id=1, source_target_pairs={{0,2},{1,3},{2,0},{3,1},{4,6},{5,7},{6,4},{7,5},{8,10},{9,11},{10,... | collective-permute-start | bytes 6291464 | tf_op jit(solution)/shard_map/ppermute | solution.py:529
  14.1 44.7 %all-to-all-start = ((s32[8,1,200]{2,1,0:T(1,128)}), s32[8,1,200]{2,1,0:T(1,128)S(1)}, u32[]{:S(2)}, u32[]{:S(2)}) async-start(s32[8,1,200]{2,1,0:T(1,128)} %broadcast_in_dim.108), calls=%async_computation | async-start | bytes 16384 | tf_op jit(solution)/shard_map/all_to_all | solution.py:544
  47.2 14.6 %copy-start.10 = (f32[64,8,256]{2,1,0:T(8,128)}, f32[64,8,256]{2,1,0:T(8,128)S(1)}, u32[]{:S(2)}) copy-start(f32[64,8,256]{2,1,0:T(8,128)S(1)} %get-tuple-element.20.rest_2_.rest_1_.stats_ref) | copy-start | bytes 1572868
  61.8 0.9 copy-start.2
  62.7 18.1 %collective-permute-start.5 = (bf16[25,64,256]{2,1,0:T(8,128)(2,1)}, bf16[25,64,256]{2,1,0:T(8,128)(2,1)S(1)}, u32[]{:S(2)}, u32[]{:S(2)}) collective-permute-start(bf16[25,64,256]{2,1,0:T(8,128)(2,1)} %get-tuple-element.23), channel_id=1, source_target_pairs={{0,2},{1,3},{2,0},{3,1},{4,6},{5,7},{6,4},{7,5},{8,10},{9,11},{10,... | collective-permute-start | bytes 2457608 | tf_op jit(solution)/shard_map/ppermute | solution.py:529
  63.3 1.3 copy-start
  64.6 1.0 copy-start.11
  69.5 36.2 %collective-permute-start.1 = (bf16[50,64,256]{2,1,0:T(8,128)(2,1)}, bf16[50,64,256]{2,1,0:T(8,128)(2,1)S(1)}, u32[]{:S(2)}, u32[]{:S(2)}) collective-permute-start(bf16[50,64,256]{2,1,0:T(8,128)(2,1)} %pick_blocks.5), channel_id=1, source_target_pairs={{0,4},{1,5},{2,6},{3,7},{4,12},{5,13},{6,14},{7,15},{8,0},{9,1},{1... | collective-permute-start | bytes 4915208 | tf_op jit(solution)/shard_map/ppermute | solution.py:529
  76.4 6.9 %copy-start.3 = (bf16[25,64,256]{2,1,0:T(8,128)(2,1)S(1)}, bf16[25,64,256]{2,1,0:T(8,128)(2,1)}, u32[]{:S(2)}) copy-start(bf16[25,64,256]{2,1,0:T(8,128)(2,1)} %copy-done.2) | copy-start | bytes 2457604
  82.7 24.7 %collective-permute-start.8 = (bf16[25,64,256]{2,1,0:T(8,128)(2,1)S(1)}, bf16[25,64,256]{2,1,0:T(8,128)(2,1)S(1)}, u32[]{:S(2)}, u32[]{:S(2)}) collective-permute-start(bf16[25,64,256]{2,1,0:T(8,128)(2,1)S(1)} %pick_blocks.9), channel_id=1, source_target_pairs={{0,2},{1,3},{2,0},{3,1},{4,6},{5,7},{6,4},{7,5},{8,10},{9,11},{10,... | collective-permute-start | bytes 2457608 | tf_op jit(solution)/shard_map/ppermute | solution.py:529
  83.3 42.6 %collective-permute-start.4 = (bf16[25,64,256]{2,1,0:T(8,128)(2,1)S(1)}, bf16[25,64,256]{2,1,0:T(8,128)(2,1)S(1)}, u32[]{:S(2)}, u32[]{:S(2)}) collective-permute-start(bf16[25,64,256]{2,1,0:T(8,128)(2,1)S(1)} %copy-done.3), channel_id=1, source_target_pairs={{8,12},{9,13},{10,14},{11,15},{4,0},{5,1},{6,2},{7,3},{24,28},{25,... | collective-permute-start | bytes 2457608 | tf_op jit(solution)/shard_map/ppermute | solution.py:529
  90.1 15.6 %copy-start.1 = (bf16[64,64,256]{2,1,0:T(8,128)(2,1)S(1)}, bf16[64,64,256]{2,1,0:T(8,128)(2,1)}, u32[]{:S(2)}) copy-start(bf16[64,64,256]{2,1,0:T(8,128)(2,1)} %copy-done) | copy-start | bytes 6291460
  92.2 15.3 %copy-start.5 = (bf16[256,256]{1,0:T(8,128)(2,1)S(1)}, bf16[256,256]{1,0:T(8,128)(2,1)}, u32[]{:S(2)}) copy-start(bf16[256,256]{1,0:T(8,128)(2,1)} %rest_2_.5) | copy-start | bytes 393220
  92.2 15.3 %copy-start.6 = (bf16[256,256]{1,0:T(8,128)(2,1)S(1)}, bf16[256,256]{1,0:T(8,128)(2,1)}, u32[]{:S(2)}) copy-start(bf16[256,256]{1,0:T(8,128)(2,1)} %rest_3_.5) | copy-start | bytes 393220
  92.2 15.3 %copy-start.12 = (f32[64,8,256]{2,1,0:T(8,128)S(1)}, f32[64,8,256]{2,1,0:T(8,128)}, u32[]{:S(2)}) copy-start(f32[64,8,256]{2,1,0:T(8,128)} %copy-done.10) | copy-start | bytes 1572868
  92.2 33.7 %collective-permute-start.7 = (bf16[25,64,256]{2,1,0:T(8,128)(2,1)S(1)}, bf16[25,64,256]{2,1,0:T(8,128)(2,1)S(1)}, u32[]{:S(2)}, u32[]{:S(2)}) collective-permute-start(bf16[25,64,256]{2,1,0:T(8,128)(2,1)S(1)} %pick_blocks.8), channel_id=1, source_target_pairs={{4,8},{5,9},{6,10},{7,11},{8,4},{9,5},{10,6},{11,7},{20,24},{21,25... | collective-permute-start | bytes 2457608 | tf_op jit(solution)/shard_map/ppermute | solution.py:529
  93.0 50.4 %collective-permute-start.6 = (bf16[25,64,256]{2,1,0:T(8,128)(2,1)S(1)}, bf16[25,64,256]{2,1,0:T(8,128)(2,1)S(1)}, u32[]{:S(2)}, u32[]{:S(2)}) collective-permute-start(bf16[25,64,256]{2,1,0:T(8,128)(2,1)S(1)} %collective-permute-done.5.rest_1_), channel_id=1, source_target_pairs={{8,12},{9,13},{10,14},{11,15},{4,0},{5,1},{6,2},{7,3},{24,28},{25,... | collective-permute-start | bytes 2457608 | tf_op jit(solution)/shard_map/ppermute | solution.py:529
  106.7 67.7 %collective-permute-start.2 = (bf16[25,64,256]{2,1,0:T(8,128)(2,1)S(1)}, bf16[25,64,256]{2,1,0:T(8,128)(2,1)S(1)}, u32[]{:S(2)}, u32[]{:S(2)}) collective-permute-start(bf16[25,64,256]{2,1,0:T(8,128)(2,1)S(1)} %pick_blocks.6), channel_id=1, source_target_pairs={{4,8},{5,9},{6,10},{7,11},{8,4},{9,5},{10,6},{11,7},{20,24},{21,25... | collective-permute-start | bytes 2457608 | tf_op jit(solution)/shard_map/ppermute | solution.py:529
  107.4 1.6 copy-start.9

commit v13 on v12

--- a/solution.py
+++ b/solution.py
@@ -125,9 +125,8 @@
     )
 
 
-def own_kernel(
-    normed_ref, query_w_ref, key_w_ref, value_w_ref, query_ref, own_ref, stats_ref, *, head_width
-):
+def own_kernel(normed_ref, query_w_ref, key_w_ref, value_w_ref, *rest, head_width):
+    query_ref, own_ref, stats_ref = rest[-3:]
     blocks, width, tile = query_ref.shape
     cluster = tile // GROUP
     span = GROUP * head_width
@@ -171,31 +170,41 @@
         stats_ref[block] = jnp.concatenate(tops + totals, axis=0)
 
 
-def own_part(normed, w_query, w_key, w_value, cluster):
+def own_part(normed, w_query, w_key, w_value, cluster, half, so_far, after):
     rows, width = normed.shape
     blocks = rows // cluster
     tile = GROUP * cluster
     tiles = HEADS // GROUP
+    steps = blocks // STEP // 2
+    first = half * steps
     whole = pl.BlockSpec((width, width), lambda i: (0, 0))
-    square = pl.BlockSpec((STEP, width, tile), lambda i: (i, 0, 0))
+    square = pl.BlockSpec((STEP, width, tile), lambda i: (first + i, 0, 0))
+    extra = [*so_far, *after]
     return pl.pallas_call(
         functools.partial(own_kernel, head_width=width // HEADS),
-        grid=(blocks // STEP,),
-        in_specs=[pl.BlockSpec((STEP * cluster, width), lambda i: (i, 0)), whole, whole, whole],
+        grid=(steps,),
+        in_specs=[
+            pl.BlockSpec((STEP * cluster, width), lambda i: (first + i, 0)),
+            whole,
+            whole,
+            whole,
+        ]
+        + [pl.BlockSpec(memory_space=pl.ANY)] * len(extra),
         out_specs=[
             square,
             square,
-            pl.BlockSpec((STEP, 2 * tiles, tile), lambda i: (i, 0, 0)),
+            pl.BlockSpec((STEP, 2 * tiles, tile), lambda i: (first + i, 0, 0)),
         ],
         out_shape=[
             jax.ShapeDtypeStruct((blocks, width, tile), jnp.bfloat16),
             jax.ShapeDtypeStruct((blocks, width, tile), jnp.bfloat16),
             jax.ShapeDtypeStruct((blocks, 2 * tiles, tile), jnp.float32),
         ],
-        cost_estimate=lasting(20),
+        input_output_aliases={4 + n: n for n in range(len(so_far))},
+        cost_estimate=lasting(15),
         compiler_params=kernel_params(),
         name="own_blocks",
-    )(normed, w_query.T, w_key, w_value.T)
+    )(normed, w_query.T, w_key, w_value.T, *extra)
 
 
 def collect_kernel(*refs, places):
@@ -239,7 +248,7 @@
     head_width,
     places,
 ):
-    weight_refs, rest = rest[:4], rest[4:]
+    weight_refs, rest = rest[:3], rest[3:]
     piece_refs = rest[: len(places)]
     mixed_ref, buffer_ref, query_buf, own_buf, stats_buf, member_buf, placed_buf = rest[-13:-6]
     attended_buf, before_buf, done_buf, in_sems, out_sems, piece_sems = rest[-6:]
@@ -267,7 +276,7 @@
             yield pltpu.make_async_copy(done_buf.at[j], target, out_sems.at[j])
 
     def finish():
-        return finish_step(before_buf[...], attended_buf[...], *weight_refs[2:])
+        return finish_step(before_buf[...], attended_buf[...], *weight_refs[1:])
 
     def one_step(i, carry):
         slot = i % 2
@@ -280,7 +289,7 @@
             own_buf.at[slot],
             stats_buf.at[slot],
             member_buf.at[slot],
-            *weight_refs[:2],
+            weight_refs[0],
             head_width,
             finish,
         )
@@ -335,33 +344,25 @@
 
 
 def attend_step(
-    query_ref, own_ref, stats_ref, member_ref, key_w_ref, value_w_ref, head_width, meanwhile
+    query_ref, own_ref, stats_ref, member_ref, pair_w_ref, head_width, meanwhile
 ):
     _, members_count, cluster, width = member_ref.shape
     span = GROUP * head_width
     tile = GROUP * cluster
     diagonal = head_mask((span, tile), head_width, cluster)
-    fold_row = lax.broadcasted_iota(jnp.int32, (cluster, tile), 0)
-    fold_lane = lax.broadcasted_iota(jnp.int32, (cluster, tile), 1) % cluster
-    fold = jnp.where(fold_row == fold_lane, 1.0, 0.0).astype(jnp.bfloat16)
     ones = jnp.ones((16, members_count * cluster), jnp.bfloat16)
     tiles = HEADS // GROUP
     units = [(block, pair) for block in range(STEP) for pair in range(HEADS // GROUP // 2)]
-    keys, values = {}, {}
-
-    def gather(block):
-        members = member_ref[block].reshape(members_count * cluster, width)
-        key = jnp.dot(members, key_w_ref[...], preferred_element_type=jnp.float32)
-        keys[block] = key.astype(jnp.bfloat16)
-        value = lax.dot_general(value_w_ref[...], members, NT, preferred_element_type=jnp.float32)
-        values[block] = value.astype(jnp.bfloat16)
+    listed = member_ref[...].reshape(STEP * members_count * cluster, width)
+    both = jnp.dot(listed, pair_w_ref[...], preferred_element_type=jnp.float32)
+    both = both.astype(jnp.bfloat16).reshape(STEP, members_count * cluster, 2 * width)
+    finished = meanwhile()
+    values = [both[block, :, width:].T for block in range(STEP)]
 
     def scores_of(block, pair):
-        if pair == 0:
-            gather(block)
         first = pair * 2 * span
         return jnp.dot(
-            keys[block][:, first : first + 2 * span],
+            both[block, :, first : first + 2 * span],
             tiles_of(query_ref[block], first, span),
             preferred_element_type=jnp.float32,
         )
@@ -387,13 +388,19 @@
         inverse = 1.0 / (product[span : span + 1] + own_total)
         own = own_ref[block, t * span : (t + 1) * span, :].astype(jnp.float32)
         result = product[:span] * inverse + own * (own_total * inverse)
-        return jnp.where(diagonal, result, 0.0).astype(jnp.bfloat16)
+        result = jnp.where(diagonal, result, 0.0)
+        return result[:, : tile // 2] + result[:, tile // 2 :]
+
+    def rows_of(pieces):
+        first, other = (jnp.concatenate(of, axis=0) for of in pieces)
+        left = lax.broadcasted_iota(jnp.int32, first.shape, 1) < cluster
+        first = first + pltpu.roll(first, cluster, 1)
+        other = other + pltpu.roll(other, cluster, 1)
+        return jnp.where(left, first, other).T.astype(jnp.bfloat16)
 
     count = len(units)
     scores, weights, products, pieces, attended = {}, {}, {}, [], []
     for at in range(-SCORES_AHEAD, count + 1):
-        if at == 0:
-            finished = meanwhile()
         if at + SCORES_AHEAD < count:
             scores[at + SCORES_AHEAD] = scores_of(*units[at + SCORES_AHEAD])
         if 0 <= at + WEIGHTS_AHEAD < count:
@@ -403,10 +410,8 @@
             products[at] = list(products_of(*units[at], *weights.pop(at)))
         if at > 0:
             pieces += [scaled(*product) for product in products.pop(at - 1)]
-            if len(pieces) == tiles:
-                stacked = jnp.concatenate(pieces, axis=0)
-                folded = lax.dot_general(fold, stacked, NT, preferred_element_type=jnp.float32)
-                attended.append(folded.astype(jnp.bfloat16))
+            if len(pieces) == 2 * tiles:
+                attended.append(rows_of((pieces[:tiles], pieces[tiles:])))
                 pieces = []
     return jnp.concatenate(attended, axis=0), finished
 
@@ -417,7 +422,7 @@
     smem = pl.BlockSpec(memory_space=pltpu.SMEM)
     vmem = pl.BlockSpec(memory_space=pltpu.VMEM)
     hbm = pl.BlockSpec(memory_space=pl.ANY)
-    in_specs = [smem] * 3 + [hbm] * (len(own) + 1) + [vmem] * (4 + len(pieces)) + [hbm]
+    in_specs = [smem] * 3 + [hbm] * (len(own) + 1) + [vmem] * (3 + len(pieces)) + [hbm]
     aliases = {len(in_specs) - 1: 1}
     operands = [*own, placed, *weights, *pieces, buffer]
     if so_far is not None:
@@ -507,7 +512,8 @@
     return lambda position: partner(route(position))
 
 
-SECOND_PLAN = (((0, source, itself), (1, source, partner)),)
+SECOND_PLAN = (((0, source, itself),),)
+SECOND_CROSS_PLAN = (((0, source, partner),),)
 MIDDLE_PLAN = (((0, opposite, itself),),)
 MIDDLE_CROSS_PLAN = (((0, opposite, partner),),)
 ON_PLAN = (((0, crossed(onward), source),), ((0, onward, source),))
@@ -541,20 +547,15 @@
     owner = listed // block_count // stride
     within = listed % block_count
     ranking, tables = slot_tables(owner, within, capacity)
-    wanted = lax.all_to_all(
-        jnp.broadcast_to(tables[None], (SPAN, SPAN * capacity)),
-        "elec",
-        split_axis=0,
-        concat_axis=0,
-        axis_index_groups=groups,
-        tiled=True,
-    )
+    wanted = lax.all_gather(tables, "elec", axis_index_groups=groups)
 
     shape = (block_count // SUB, 1, SUB * cluster)
     block_shape = (block_count, cluster, width)
     placed, normed = place(features, assignment.reshape(shape))
     blocks = normed.reshape(block_shape)
-    own = own_part(normed, w_query, w_key, w_value, cluster)
+    own_operands = (normed, w_query, w_key, w_value, cluster)
+    own = own_part(*own_operands, 0, (), (tables,))
+    own = own_part(*own_operands, 1, own, (wanted,))
     own_at = 7 * capacity
     passed_at = own_at + block_count
     beside_at = passed_at + block_count
@@ -562,18 +563,20 @@
 
     beside = moved(blocks, swap)
     passed = moved(blocks, first_moves)
-    (second,) = pick(at_position, wanted, (blocks, beside), SECOND_PLAN, after=own[2:])
+    (second,) = pick(at_position, wanted, (blocks,), SECOND_PLAN, after=own[2:])
     second = moved(second, second_moves)
+    (second_cross,) = pick(at_position, wanted, (beside,), SECOND_CROSS_PLAN, after=own[2:])
+    second_cross = moved(second_cross, second_moves)
     on, outward = pick(at_position, wanted, (passed,), ON_PLAN, after=own[2:])
     on = moved(on, swap)
     outward = moved(outward, outward_moves)
+    (middle,) = pick(at_position, wanted, (blocks,), MIDDLE_PLAN, after=(second,))
+    middle = moved(middle, middle_moves)
     (near,) = pick(at_position, wanted, (passed,), NEAR_PLAN, after=(on,))
     near = moved(near, swap)
-    (middle,) = pick(at_position, wanted, (blocks,), MIDDLE_PLAN, after=(on,))
-    middle = moved(middle, middle_moves)
     on = moved(on, outward_moves)
     (middle_cross,) = pick(
-        at_position, wanted, (beside,), MIDDLE_CROSS_PLAN, after=(second,)
+        at_position, wanted, (beside,), MIDDLE_CROSS_PLAN, after=(second_cross,)
     )
     middle_cross = moved(middle_cross, middle_moves)
 
@@ -601,10 +604,10 @@
     order, ends = by_class(jnp.max(arrival.reshape(block_count, pair_count), axis=1), 2)
     marks = [0, ends[0] // STEP, ends[1] // STEP, block_count // STEP]
     phases = [(marks[n], marks[n + 1] - marks[n]) for n in range(3)]
-    weights = (w_key, w_value.T, w_out, w_mix)
+    weights = (jnp.concatenate([w_key, w_value], axis=1), w_out, w_mix)
     shared = (order, table, own, placed.reshape(blocks.shape), weights)
     arrivals = (
-        ((near, 0), (second, 1)),
+        ((near, 0), (second, 1), (second_cross, 2)),
         ((outward, 3), (on, 4), (middle, 5)),
         ((middle_cross, 6),),
     )

time: 177 us -> 186 us (1.051)
  the two profiles are of different devices: /device:TPU:1 before, /device:TPU:8 now
where the time goes in v13:
time: 186 us; the launch traced here: 184 us
  Pallas kernels  103 us (55%)
  blocking collectives  34.1 us (18%)
  starting transfers between devices  15.8 us (8%)
  waiting for transfers between devices  15.3 us (8%)
  local copies, waits for them, and re-layouts  8.43 us (5%)
  between operations  6.07 us (3%)
    pallas_call x3, Pallas kernels, attend(): pl.pallas_call(kernel, in_specs=in_specs, out_specs=[hbm, hbm], out_shape...  48.6 us
    unnamed x1, blocking collectives  34.1 us
    pallas_call x2, Pallas kernels, own_part(): pl.pallas_call(functools.partial(own_kernel, head_width=width // HEADS),...  31.2 us
    ppermute x10, starting transfers between devices, moved(): return lax.ppermute(x, 'elec', pairs_of)  15.8 us
    ppermute x10, waiting for transfers between devices, moved(): return lax.ppermute(x, 'elec', pairs_of)  15.3 us
    pallas_call x6, Pallas kernels, pick(): pl.pallas_call(functools.partial(pick_kernel, plan=plan, capacity=capacit...  11.4 us
    unnamed x43, local copies, waits for them, and re-layouts  8.21 us
    pallas_call x1, Pallas kernels, place(): pl.pallas_call(place_kernel, grid=(walkers // 2,), in_specs=[local, pl.Bl...  6.36 us
  transfers between devices with their start and end apart: 10, of which 2 were waited for; matrix products, arithmetic and copies ran while one was open for 2% of the time, Pallas kernels for 44%

profile of v13, /device:TPU:8, one launch (start us, length us, event | category | flops | bytes accessed | tf_op | source)
XLA Modules:
  0.0 184.3 jit_solution(12723552131560893473)
XLA Ops:
  0.0 0.7 copy-done.7
  0.7 6.4 %place_rows.1 = (bf16[4096,256]{1,0:T(8,128)(2,1)S(1)}, bf16[4096,256]{1,0:T(8,128)(2,1)}) custom-call(bf16[4096,256]{1,0:T(8,128)(2,1)} %features_ref.1, s32[8,1,512]{2,1,0:T(1,128)S(1)} %bitcast.16), custom_call_target="tpu_custom_call" | custom-call | flops 6899999744 | tf_op jit(solution)/shard_map/place_rows/pallas_call | solution.py:65
  7.1 1.3 copy-done.8
  8.4 1.5 collective-permute-start
  11.3 15.6 %own_blocks.2 = (bf16[64,256,256]{2,1,0:T(8,128)(2,1)}, bf16[64,256,256]{2,1,0:T(8,128)(2,1)}, f32[64,8,256]{2,1,0:T(8,128)S(1)}) custom-call(bf16[4096,256]{1,0:T(8,128)(2,1)} %get-tuple-element.20.normed_ref, bf16[256,256]{1,0:T(8,128)(2,1)S(1)} %bitcast.12, bf16[256,256]{1,0:T(8,128)(2,1)S(1)} %copy-done.2, bf16[256,256]{1,0:T(8,128)(2,1)S(1)} %bitcast.14, ...), custom_call_target="tpu_custom_call" | custom-call | flops 17250000896 | tf_op jit(solution)/shard_map/own_blocks/pallas_call | solution.py:183
  28.4 34.1 %all-reduce = s32[1600]{0:T(1024)S(1)} all-reduce(s32[1600]{0:T(1024)S(1)} %dynamic-update-slice), channel_id=2, replica_groups={{0,2,4,6,8,10,12,14},{1,3,5,7,9,11,13,15},{16,18,20,22,24,26,28,30},{17..., use_global_device_ids=true, to_apply=%add | all-reduce | flops 1600 | bytes 12800
  62.6 15.6 %own_blocks.3 = (bf16[64,256,256]{2,1,0:T(8,128)(2,1)}, bf16[64,256,256]{2,1,0:T(8,128)(2,1)}, f32[64,8,256]{2,1,0:T(8,128)S(1)}) custom-call(bf16[4096,256]{1,0:T(8,128)(2,1)} %get-tuple-element.20.normed_ref, bf16[256,256]{1,0:T(8,128)(2,1)S(1)} %bitcast.13, ...), custom_call_target="tpu_custom_call", output_to_operand_aliasing={{0}: (4, {}), {1}: (5, {}), {2}: (6, {})} | custom-call | flops 17250000896 | tf_op jit(solution)/shard_map/own_blocks/pallas_call | solution.py:183
  78.3 2.8 %pick_blocks.9 = bf16[25,64,256]{2,1,0:T(8,128)(2,1)} custom-call(s32[1]{0:T(128)} %bitcast.7.position_ref, s32[8,200]{1,0:T(8,128)S(1)} %reshape.148.rest_3_.wanted_ref, bf16[64,64,256]{2,1,0:T(8,128)(2,1)} %bitcast.8.rest_0_.refs_0_, f32[64,8,256]{2,1,0:T(8,128)S(1)} %get-tuple-element.26.rest_1_.stats_ref), custom_call_target="tpu_custom_call" | custom-call | flops 1724999936 | tf_op jit(solution)/shard_map/pick_blocks/pallas_call | solution.py:106
  81.0 0.8 copy-done.10
  82.4 0.7 fusion.14
  88.1 1.0 copy-done.11
  89.1 3.0 %pick_blocks.8 = (bf16[25,64,256]{2,1,0:T(8,128)(2,1)}, bf16[25,64,256]{2,1,0:T(8,128)(2,1)S(1)}) custom-call(s32[1]{0:T(128)} %bitcast.7.position_ref, s32[8,200]{1,0:T(8,128)S(1)} %reshape.148.rest_3_.wanted_ref, bf16[64,64,256]{2,1,0:T(8,128)(2,1)} %collective-permute-done.3.rest_0_.refs_1_, f32[64,8,256]{2,1,0:T(8,128)S(1)} %copy-done.11), custom_call_target="tpu_custom_call" | custom-call | flops 1724999936 | tf_op jit(solution)/shard_map/pick_blocks/pallas_call | solution.py:106
  92.1 0.9 copy-done.3
  93.0 1.4 collective-permute-start.5
  94.9 1.1 copy-done.12
  96.0 0.9 pick_blocks.6
  97.0 1.6 collective-permute-start.1
  98.6 12.5 %collective-permute-done.5.rest_1_ = bf16[25,64,256]{2,1,0:T(8,128)(2,1)} collective-permute-done((bf16[25,64,256]{2,1,0:T(8,128)(2,1)}, bf16[25,64,256]{2,1,0:T(8,128)(2,1)}, u32[]{:S(2)}, u32[]{:S(2)}) %collective-permute-start.5) | collective-permute-done | bytes 819232 | tf_op jit(solution)/shard_map/ppermute | solution.py:535
  111.1 1.9 %pick_blocks.11 = bf16[25,64,256]{2,1,0:T(8,128)(2,1)S(1)} custom-call(s32[1]{0:T(128)} %bitcast.7.position_ref, s32[8,200]{1,0:T(8,128)S(1)} %reshape.148.rest_3_.wanted_ref, bf16[64,64,256]{2,1,0:T(8,128)(2,1)} %collective-permute-done.3.rest_0_.refs_1_, bf16[25,64,256]{2,1,0:T(8,128)(2,1)} %collective-permute-done.5.rest_1_), custom_call_target="tpu_custom_call" | custom-call | flops 1724999936 | tf_op jit(solution)/shard_map/pick_blocks/pallas_call | solution.py:106
  113.0 1.5 collective-permute-start.9
  114.5 1.9 %pick_blocks.10 = bf16[25,64,256]{2,1,0:T(8,128)(2,1)S(1)} custom-call(s32[1]{0:T(128)} %bitcast.7.position_ref, s32[8,200]{1,0:T(8,128)S(1)} %reshape.148.rest_3_.wanted_ref, bf16[64,64,256]{2,1,0:T(8,128)(2,1)} %bitcast.8.rest_0_.refs_0_, bf16[25,64,256]{2,1,0:T(8,128)(2,1)S(1)} %collective-permute-done.7.rest_1_.rest_4_), custom_call_target="tpu_custom_call" | custom-call | flops 1724999936 | tf_op jit(solution)/shard_map/pick_blocks/pallas_call | solution.py:106
  116.4 4.0 %collective-permute-start.8 = (bf16[25,64,256]{2,1,0:T(8,128)(2,1)S(1)}, bf16[25,64,256]{2,1,0:T(8,128)(2,1)S(1)}, u32[]{:S(2)}, u32[]{:S(2)}) collective-permute-start(bf16[25,64,256]{2,1,0:T(8,128)(2,1)S(1)} %pick_blocks.10), channel_id=1, source_target_pairs={{4,8},{5,9},{6,10},{7,11},{8,4},{9,5},{10,6},{11,7},{20,24},{21,25... | collective-permute-start | bytes 2457608 | tf_op jit(solution)/shard_map/ppermute | solution.py:535
  120.5 1.6 collective-permute-start.4
  122.1 5.5 %collect_blocks.1.rest_6_ = bf16[367,64,256]{2,1,0:T(8,128)(2,1)} custom-call(bf16[64,64,256]{2,1,0:T(8,128)(2,1)} %bitcast.8.rest_0_.refs_0_, bf16[64,64,256]{2,1,0:T(8,128)(2,1)} %collective-permute-done.3.rest_0_.refs_1_, bf16[64,64,256]{2,1,0:T(8,128)(2,1)} %copy-done), custom_call_target="tpu_custom_call" | custom-call | flops 4600000000 | tf_op jit(solution)/shard_map/collect_blocks/pallas_call | solution.py:227
  127.6 0.9 pick_blocks.7
  128.6 1.9 %collective-permute-start.2 = (bf16[25,64,256]{2,1,0:T(8,128)(2,1)S(1)}, bf16[25,64,256]{2,1,0:T(8,128)(2,1)S(1)}, u32[]{:S(2)}, u32[]{:S(2)}) collective-permute-start(bf16[25,64,256]{2,1,0:T(8,128)(2,1)S(1)} %pick_blocks.7), channel_id=1, source_target_pairs={{4,8},{5,9},{6,10},{7,11},{8,4},{9,5},{10,6},{11,7},{20,24},{21,25... | collective-permute-start | bytes 2457608 | tf_op jit(solution)/shard_map/ppermute | solution.py:535
  130.5 1.3 collective-permute-start.6
  131.9 1.0 copy-done.13
  132.9 17.8 %attend_blocks.3 = (bf16[64,64,256]{2,1,0:T(8,128)(2,1)}, bf16[367,64,256]{2,1,0:T(8,128)(2,1)}) custom-call(s32[2]{0:T(128)S(1)} %pad_add_fusion.2.range_ref, s32[64]{0:T(128)S(1)} %select_reduce_fusion.2.order_ref, s32[192]{0:T(256)S(1)} %get-tuple-element.38.table_ref, ...), custom_call_target="tpu_custom_call", output_to_operand_aliasing={{1}: (13, {})} | custom-call | flops 20700000256 | tf_op jit(solution)/shard_map/attend_blocks/pallas_call | solution.py:435
  150.8 2.7 %collective-permute-done.6.rest_4_ = bf16[25,64,256]{2,1,0:T(8,128)(2,1)S(1)} collective-permute-done((bf16[25,64,256]{2,1,0:T(8,128)(2,1)}, bf16[25,64,256]{2,1,0:T(8,128)(2,1)S(1)}, u32[]{:S(2)}, u32[]{:S(2)}) %collective-permute-start.6) | collective-permute-done | bytes 819232 | tf_op jit(solution)/shard_map/ppermute | solution.py:535
  153.5 15.7 %attend_blocks.4 = (bf16[64,64,256]{2,1,0:T(8,128)(2,1)}, bf16[367,64,256]{2,1,0:T(8,128)(2,1)}) custom-call(s32[2]{0:T(128)S(1)} %pad_add_fusion.1.range_ref, s32[64]{0:T(128)S(1)} %select_reduce_fusion.2.order_ref, s32[192]{0:T(256)S(1)} %get-tuple-element.38.table_ref, ...), custom_call_target="tpu_custom_call", output_to_operand_aliasing={{1}: (13, {}), {0}: (14, {})} | custom-call | flops 20700000256 | tf_op jit(solution)/shard_map/attend_blocks/pallas_call | solution.py:435
  169.2 15.1 %attend_blocks.5 = (bf16[64,64,256]{2,1,0:T(8,128)(2,1)}, bf16[367,64,256]{2,1,0:T(8,128)(2,1)}) custom-call(s32[2]{0:T(128)S(1)} %pad_add_fusion.range_ref, s32[64]{0:T(128)S(1)} %select_reduce_fusion.2.order_ref, s32[192]{0:T(256)S(1)} %get-tuple-element.38.table_ref, ...), custom_call_target="tpu_custom_call", output_to_operand_aliasing={{1}: (11, {}), {0}: (12, {})} | custom-call | flops 20700000256 | tf_op jit(solution)/shard_map/attend_blocks/pallas_call | solution.py:435
  (59 shorter events, 3.4 us)
Async XLA Ops:
  0.0 0.7 copy-start.7
  0.7 9.7 %copy-start.16 = (s32[64,3]{0,1:T(4,128)S(1)}, s32[64,3]{0,1:T(4,128)}, u32[]{:S(2)}) copy-start(s32[64,3]{0,1:T(4,128)} %param.10) | copy-start | bytes 2308
  0.7 10.2 %copy-start.15 = (bf16[256,256]{1,0:T(8,128)(2,1)S(1)}, bf16[256,256]{1,0:T(8,128)(2,1)}, u32[]{:S(2)}) copy-start(bf16[256,256]{1,0:T(8,128)(2,1)} %param.11) | copy-start | bytes 393220
  0.7 10.3 %copy-start.14 = (bf16[256,256]{1,0:T(8,128)(2,1)S(1)}, bf16[256,256]{1,0:T(8,128)(2,1)}, u32[]{:S(2)}) copy-start(bf16[256,256]{1,0:T(8,128)(2,1)} %param.13) | copy-start | bytes 393220
  0.7 10.6 %copy-start.2 = (bf16[256,256]{1,0:T(8,128)(2,1)S(1)}, bf16[256,256]{1,0:T(8,128)(2,1)}, u32[]{:S(2)}) copy-start(bf16[256,256]{1,0:T(8,128)(2,1)} %key_w_ref.3) | copy-start | bytes 393220
  7.1 1.3 copy-start.8
  8.4 86.4 %collective-permute-start = (bf16[64,64,256]{2,1,0:T(8,128)(2,1)}, bf16[64,64,256]{2,1,0:T(8,128)(2,1)S(1)}, u32[]{:S(2)}, u32[]{:S(2)}) collective-permute-start(bf16[64,64,256]{2,1,0:T(8,128)(2,1)} %bitcast.8.rest_0_.refs_0_), channel_id=1, source_target_pairs={{0,2},{1,3},{2,0},{3,1},{4,6},{5,7},{6,4},{7,5},{8,10},{9,11},{10,... | collective-permute-start | bytes 6291464 | tf_op jit(solution)/shard_map/ppermute | solution.py:535
  10.0 78.1 %collective-permute-start.3 = (bf16[64,64,256]{2,1,0:T(8,128)(2,1)}, bf16[64,64,256]{2,1,0:T(8,128)(2,1)}, u32[]{:S(2)}, u32[]{:S(2)}) collective-permute-start(bf16[64,64,256]{2,1,0:T(8,128)(2,1)} %bitcast.8.rest_0_.refs_0_), channel_id=1, source_target_pairs={{0,8},{1,9},{2,10},{3,11},{4,0},{5,1},{6,2},{7,3},{8,12},{9,13},{1... | collective-permute-start | bytes 6291464 | tf_op jit(solution)/shard_map/ppermute | solution.py:535
  11.3 15.6 %copy-start.17 = (u32[32]{0:T(128)S(1)}, u32[32]{0:T(128)}, u32[]{:S(2)}) copy-start(u32[32]{0:T(128)} %constant.125) | copy-start | bytes 388
  81.0 0.8 copy-start.10
  81.8 32.7 %collective-permute-start.7 = (bf16[25,64,256]{2,1,0:T(8,128)(2,1)}, bf16[25,64,256]{2,1,0:T(8,128)(2,1)S(1)}, u32[]{:S(2)}, u32[]{:S(2)}) collective-permute-start(bf16[25,64,256]{2,1,0:T(8,128)(2,1)} %pick_blocks.9), channel_id=1, source_target_pairs={{0,4},{1,5},{2,6},{3,7},{4,12},{5,13},{6,14},{7,15},{8,0},{9,1},{1... | collective-permute-start | bytes 2457608 | tf_op jit(solution)/shard_map/ppermute | solution.py:535
  88.1 1.0 copy-start.11
  92.1 0.9 copy-start.3
  93.0 18.1 %collective-permute-start.5 = (bf16[25,64,256]{2,1,0:T(8,128)(2,1)}, bf16[25,64,256]{2,1,0:T(8,128)(2,1)}, u32[]{:S(2)}, u32[]{:S(2)}) collective-permute-start(bf16[25,64,256]{2,1,0:T(8,128)(2,1)} %get-tuple-element.29), channel_id=1, source_target_pairs={{0,2},{1,3},{2,0},{3,1},{4,6},{5,7},{6,4},{7,5},{8,10},{9,11},{10,... | collective-permute-start | bytes 2457608 | tf_op jit(solution)/shard_map/ppermute | solution.py:535
  94.9 25.5 %copy-start.4 = (bf16[25,64,256]{2,1,0:T(8,128)(2,1)S(1)}, bf16[25,64,256]{2,1,0:T(8,128)(2,1)}, u32[]{:S(2)}) copy-start(bf16[25,64,256]{2,1,0:T(8,128)(2,1)} %copy-done.3) | copy-start | bytes 2457604
  94.9 1.1 copy-start.12
  96.0 20.4 %copy-start = (bf16[64,64,256]{2,1,0:T(8,128)(2,1)}, bf16[64,64,256]{2,1,0:T(8,128)(2,1)S(1)}, u32[]{:S(2)}) copy-start(bf16[64,64,256]{2,1,0:T(8,128)(2,1)S(1)} %collective-permute-done.rest_0_.refs_2_) | copy-start | bytes 6291460
  97.0 30.7 %collective-permute-start.1 = (bf16[25,64,256]{2,1,0:T(8,128)(2,1)S(1)}, bf16[25,64,256]{2,1,0:T(8,128)(2,1)S(1)}, u32[]{:S(2)}, u32[]{:S(2)}) collective-permute-start(bf16[25,64,256]{2,1,0:T(8,128)(2,1)S(1)} %pick_blocks.6), channel_id=1, source_target_pairs={{0,4},{1,5},{2,6},{3,7},{4,12},{5,13},{6,14},{7,15},{8,0},{9,1},{1... | collective-permute-start | bytes 2457608 | tf_op jit(solution)/shard_map/ppermute | solution.py:535
  113.0 18.9 %collective-permute-start.9 = (bf16[25,64,256]{2,1,0:T(8,128)(2,1)S(1)}, bf16[25,64,256]{2,1,0:T(8,128)(2,1)S(1)}, u32[]{:S(2)}, u32[]{:S(2)}) collective-permute-start(bf16[25,64,256]{2,1,0:T(8,128)(2,1)S(1)} %pick_blocks.11), channel_id=1, source_target_pairs={{0,2},{1,3},{2,0},{3,1},{4,6},{5,7},{6,4},{7,5},{8,10},{9,11},{10,... | collective-permute-start | bytes 2457608 | tf_op jit(solution)/shard_map/ppermute | solution.py:535
  116.4 34.4 %collective-permute-start.8 = (bf16[25,64,256]{2,1,0:T(8,128)(2,1)S(1)}, bf16[25,64,256]{2,1,0:T(8,128)(2,1)S(1)}, u32[]{:S(2)}, u32[]{:S(2)}) collective-permute-start(bf16[25,64,256]{2,1,0:T(8,128)(2,1)S(1)} %pick_blocks.10), channel_id=1, source_target_pairs={{4,8},{5,9},{6,10},{7,11},{8,4},{9,5},{10,6},{11,7},{20,24},{21,25... | collective-permute-start | bytes 2457608 | tf_op jit(solution)/shard_map/ppermute | solution.py:535
  120.4 7.2 %copy-start.1 = (bf16[64,64,256]{2,1,0:T(8,128)(2,1)S(1)}, bf16[64,64,256]{2,1,0:T(8,128)(2,1)}, u32[]{:S(2)}) copy-start(bf16[64,64,256]{2,1,0:T(8,128)(2,1)} %copy-done) | copy-start | bytes 6291460
  120.4 11.4 %copy-start.5 = (bf16[256,256]{1,0:T(8,128)(2,1)S(1)}, bf16[256,256]{1,0:T(8,128)(2,1)}, u32[]{:S(2)}) copy-start(bf16[256,256]{1,0:T(8,128)(2,1)} %rest_1_.5) | copy-start | bytes 393220
  120.4 11.4 %copy-start.6 = (bf16[256,256]{1,0:T(8,128)(2,1)S(1)}, bf16[256,256]{1,0:T(8,128)(2,1)}, u32[]{:S(2)}) copy-start(bf16[256,256]{1,0:T(8,128)(2,1)} %rest_2_.5) | copy-start | bytes 393220
  120.5 11.4 %copy-start.9 = (bf16[4096,256]{1,0:T(8,128)(2,1)S(1)}, bf16[4096,256]{1,0:T(8,128)(2,1)}, u32[]{:S(2)}) copy-start(bf16[4096,256]{1,0:T(8,128)(2,1)} %copy-done.8) | copy-start | bytes 6291460
  120.5 30.3 %collective-permute-start.4 = (bf16[25,64,256]{2,1,0:T(8,128)(2,1)S(1)}, bf16[25,64,256]{2,1,0:T(8,128)(2,1)S(1)}, u32[]{:S(2)}, u32[]{:S(2)}) collective-permute-start(bf16[25,64,256]{2,1,0:T(8,128)(2,1)S(1)} %copy-done.4), channel_id=1, source_target_pairs={{8,12},{9,13},{10,14},{11,15},{4,0},{5,1},{6,2},{7,3},{24,28},{25,... | collective-permute-start | bytes 2457608 | tf_op jit(solution)/shard_map/ppermute | solution.py:535
  128.6 40.6 %collective-permute-start.2 = (bf16[25,64,256]{2,1,0:T(8,128)(2,1)S(1)}, bf16[25,64,256]{2,1,0:T(8,128)(2,1)S(1)}, u32[]{:S(2)}, u32[]{:S(2)}) collective-permute-start(bf16[25,64,256]{2,1,0:T(8,128)(2,1)S(1)} %pick_blocks.7), channel_id=1, source_target_pairs={{4,8},{5,9},{6,10},{7,11},{8,4},{9,5},{10,6},{11,7},{20,24},{21,25... | collective-permute-start | bytes 2457608 | tf_op jit(solution)/shard_map/ppermute | solution.py:535
  130.5 23.0 %collective-permute-start.6 = (bf16[25,64,256]{2,1,0:T(8,128)(2,1)}, bf16[25,64,256]{2,1,0:T(8,128)(2,1)S(1)}, u32[]{:S(2)}, u32[]{:S(2)}) collective-permute-start(bf16[25,64,256]{2,1,0:T(8,128)(2,1)} %collective-permute-done.5.rest_1_), channel_id=1, source_target_pairs={{8,12},{9,13},{10,14},{11,15},{4,0},{5,1},{6,2},{7,3},{24,28},{25,... | collective-permute-start | bytes 2457608 | tf_op jit(solution)/shard_map/ppermute | solution.py:535
  131.9 1.0 copy-start.13

commit v14 on v13

--- a/solution.py
+++ b/solution.py
@@ -11,6 +11,7 @@
 HEADS = 16
 SPAN = 8
 SUB = 8
+HEAD_WALKERS = 6
 GROUP = 4
 STEP = 4
 SCORES_AHEAD, WEIGHTS_AHEAD = 2, 1
@@ -40,7 +41,8 @@
     return row_head == lane_head
 
 
-def place_kernel(features_ref, assignment_ref, placed_ref, normed_ref):
+def place_kernel(features_ref, assignment_ref, *rest):
+    placed_ref, normed_ref = rest[-2:]
     walkers, _, rows = assignment_ref.shape
     lane = 128
     columns = lax.broadcasted_iota(jnp.int32, (lane, rows), 1)
@@ -57,21 +59,32 @@
             normed_ref[here, :] = layer_norm(placed).astype(jnp.bfloat16)
 
 
-def place(features, assignment):
-    width = features.shape[1]
-    walkers, _, rows = assignment.shape
-    local = pl.BlockSpec((2 * rows, width), lambda i: (i, 0))
-    out = jax.ShapeDtypeStruct(features.shape, jnp.bfloat16)
+def place(features, assignment, first, count, so_far=None, after=()):
+    total, width = features.shape
+    _, _, rows = assignment.shape
+    per = 2
+    extra = ([] if so_far is None else [so_far]) + list(after)
     return pl.pallas_call(
         place_kernel,
-        grid=(walkers // 2,),
-        in_specs=[local, pl.BlockSpec((2, 1, rows), lambda i: (i, 0, 0))],
-        out_specs=[local] * 2,
-        out_shape=[out] * 2,
-        cost_estimate=lasting(6),
+        grid=(count // per,),
+        in_specs=[
+            pl.BlockSpec((per * rows, width), lambda i: (first // per + i, 0)),
+            pl.BlockSpec((per, 1, rows), lambda i: (first // per + i, 0, 0)),
+        ]
+        + [pl.BlockSpec(memory_space=pl.ANY)] * len(extra),
+        out_specs=[
+            pl.BlockSpec((per * rows, width), lambda i: (first // per + i, 0)),
+            pl.BlockSpec((per * rows, width), lambda i: (i, 0)),
+        ],
+        out_shape=[
+            jax.ShapeDtypeStruct((total, width), jnp.bfloat16),
+            jax.ShapeDtypeStruct((count * rows, width), jnp.bfloat16),
+        ],
+        input_output_aliases={} if so_far is None else {2: 0},
+        cost_estimate=lasting(count * 0.7),
         compiler_params=kernel_params(),
         name="place_rows",
-    )(features, assignment)
+    )(features, assignment, *extra)
 
 
 def choose(index, values):
@@ -81,39 +94,37 @@
     return result
 
 
-def pick_kernel(position_ref, wanted_ref, *rest, plan, capacity):
+def pick_kernel(position_ref, wanted_ref, head_ref, tail_ref, *rest, plan, capacity):
     position = position_ref[0]
-    for out_ref, pieces in zip(rest[len(rest) - len(plan) :], plan, strict=True):
-        for at, (blocks, reader_of, owner_of) in enumerate(pieces):
-            reader, first = reader_of(position), owner_of(position) * capacity
-
-            def one_slot(slot, carry, out_ref=out_ref, at=at, blocks=blocks, reader=reader, first=first):
-                out_ref[at * capacity + slot] = rest[blocks][wanted_ref[reader, first + slot]]
-                return carry
-
-            lax.fori_loop(0, capacity, one_slot, 0)
-
-
-def pick(position, wanted, sources, plan, after=()):
+    heads = head_ref.shape[0]
+    for out_ref, (reader_of, owner_of) in zip(rest[len(rest) - len(plan) :], plan, strict=True):
+        reader, first = reader_of(position), owner_of(position) * capacity
+
+        def one_slot(slot, carry, out_ref=out_ref, reader=reader, first=first):
+            block = wanted_ref[reader, first + slot]
+            head = head_ref[jnp.minimum(block, heads - 1)]
+            tail = tail_ref[jnp.maximum(block - heads, 0)]
+            out_ref[slot] = jnp.where(block < heads, head, tail)
+            return carry
+
+        lax.fori_loop(0, capacity, one_slot, 0)
+
+
+def pick(position, wanted, parts, plan, after=()):
     capacity = wanted.shape[1] // SPAN
-    block = sources[0].shape[1:]
-    outs = [
-        jax.ShapeDtypeStruct((len(pieces) * capacity,) + block, sources[0].dtype)
-        for pieces in plan
-    ]
+    block = parts[0].shape[1:]
+    outs = [jax.ShapeDtypeStruct((capacity,) + block, parts[0].dtype)] * len(plan)
     smem = pl.BlockSpec(memory_space=pltpu.SMEM)
     vmem = pl.BlockSpec(memory_space=pltpu.VMEM)
     return pl.pallas_call(
         functools.partial(pick_kernel, plan=plan, capacity=capacity),
-        in_specs=[smem, smem]
-        + [vmem] * len(sources)
-        + [pl.BlockSpec(memory_space=pl.ANY)] * len(after),
+        in_specs=[smem, smem, vmem, vmem] + [pl.BlockSpec(memory_space=pl.ANY)] * len(after),
         out_specs=[vmem] * len(outs),
         out_shape=outs,
         cost_estimate=lasting(1.5),
         compiler_params=kernel_params(),
         name="pick_blocks",
-    )(position, wanted, *sources, *after)
+    )(position, wanted, *parts, *after)
 
 
 def tiles_of(query, first, span):
@@ -170,21 +181,19 @@
         stats_ref[block] = jnp.concatenate(tops + totals, axis=0)
 
 
-def own_part(normed, w_query, w_key, w_value, cluster, half, so_far, after):
-    rows, width = normed.shape
-    blocks = rows // cluster
+def own_part(normed, weights, cluster, blocks, begin, at, count, so_far, after):
+    width = normed.shape[1]
     tile = GROUP * cluster
     tiles = HEADS // GROUP
-    steps = blocks // STEP // 2
-    first = half * steps
+    begin, at = begin // STEP, at // STEP
     whole = pl.BlockSpec((width, width), lambda i: (0, 0))
-    square = pl.BlockSpec((STEP, width, tile), lambda i: (first + i, 0, 0))
+    square = pl.BlockSpec((STEP, width, tile), lambda i: (at + i, 0, 0))
     extra = [*so_far, *after]
     return pl.pallas_call(
         functools.partial(own_kernel, head_width=width // HEADS),
-        grid=(steps,),
+        grid=(count // STEP,),
         in_specs=[
-            pl.BlockSpec((STEP * cluster, width), lambda i: (first + i, 0)),
+            pl.BlockSpec((STEP * cluster, width), lambda i: (begin + i, 0)),
             whole,
             whole,
             whole,
@@ -193,7 +202,7 @@
         out_specs=[
             square,
             square,
-            pl.BlockSpec((STEP, 2 * tiles, tile), lambda i: (first + i, 0, 0)),
+            pl.BlockSpec((STEP, 2 * tiles, tile), lambda i: (at + i, 0, 0)),
         ],
         out_shape=[
             jax.ShapeDtypeStruct((blocks, width, tile), jnp.bfloat16),
@@ -201,10 +210,10 @@
             jax.ShapeDtypeStruct((blocks, 2 * tiles, tile), jnp.float32),
         ],
         input_output_aliases={4 + n: n for n in range(len(so_far))},
-        cost_estimate=lasting(15),
+        cost_estimate=lasting(count / 2),
         compiler_params=kernel_params(),
         name="own_blocks",
-    )(normed, w_query.T, w_key, w_value.T, *extra)
+    )(normed, *weights, *extra)
 
 
 def collect_kernel(*refs, places):
@@ -459,13 +468,14 @@
 
 
 def slot_tables(owner, within, capacity):
-    entries = owner.shape[0]
-    alike = owner[:, None] == owner[None, :]
+    readers, entries = owner.shape
+    alike = owner[:, :, None] == owner[:, None, :]
     earlier = jnp.arange(entries)[None, :] < jnp.arange(entries)[:, None]
-    ranking = jnp.sum(jnp.where(alike & earlier, 1, 0), axis=1).astype(jnp.int32)
+    ranking = jnp.sum(jnp.where(alike & earlier, 1, 0), axis=2).astype(jnp.int32)
     slots = owner * capacity + ranking
-    matches = slots[None, :] == jnp.arange(SPAN * capacity, dtype=jnp.int32)[:, None]
-    return ranking, jnp.sum(jnp.where(matches, within[None, :], 0), axis=1).astype(jnp.int32)
+    every = jnp.arange(SPAN * capacity, dtype=jnp.int32)
+    matches = slots[:, None, :] == every[None, :, None]
+    return ranking, jnp.sum(jnp.where(matches, within[:, None, :], 0), axis=2).astype(jnp.int32)
 
 
 def by_class(classes, count):
@@ -512,12 +522,12 @@
     return lambda position: partner(route(position))
 
 
-SECOND_PLAN = (((0, source, itself),),)
-SECOND_CROSS_PLAN = (((0, source, partner),),)
-MIDDLE_PLAN = (((0, opposite, itself),),)
-MIDDLE_CROSS_PLAN = (((0, opposite, partner),),)
-ON_PLAN = (((0, crossed(onward), source),), ((0, onward, source),))
-NEAR_PLAN = (((0, partner, source),),)
+SECOND_PLAN = ((source, itself),)
+MIDDLE_PLAN = ((opposite, itself),)
+SECOND_CROSS_PLAN = ((source, partner),)
+MIDDLE_CROSS_PLAN = ((opposite, partner),)
+ON_PLAN = ((crossed(onward), source), (onward, source))
+NEAR_PLAN = ((partner, source),)
 
 
 def body(features, assignment, pairs, w_query, w_key, w_value, w_out, w_mix):
@@ -543,19 +553,36 @@
     middle_moves = across_z([(1, 2), (2, 1)])
     outward_moves = across_z([(2, 3), (1, 0)])
 
-    listed = pairs.reshape(-1)
-    owner = listed // block_count // stride
-    within = listed % block_count
-    ranking, tables = slot_tables(owner, within, capacity)
-    wanted = lax.all_gather(tables, "elec", axis_index_groups=groups)
-
-    shape = (block_count // SUB, 1, SUB * cluster)
-    block_shape = (block_count, cluster, width)
-    placed, normed = place(features, assignment.reshape(shape))
-    blocks = normed.reshape(block_shape)
-    own_operands = (normed, w_query, w_key, w_value, cluster)
-    own = own_part(*own_operands, 0, (), (tables,))
-    own = own_part(*own_operands, 1, own, (wanted,))
+    all_pairs = lax.all_to_all(
+        jnp.broadcast_to(pairs.reshape(1, -1), (SPAN, block_count * pair_count)),
+        "elec",
+        split_axis=0,
+        concat_axis=0,
+        axis_index_groups=groups,
+        tiled=True,
+    )
+    _, wanted = slot_tables(all_pairs // block_count // stride, all_pairs % block_count, capacity)
+
+    walkers = block_count // SUB
+    heads = HEAD_WALKERS * SUB
+    by_walker = assignment.reshape(walkers, 1, SUB * cluster)
+
+    def in_blocks(rows):
+        return rows.reshape(-1, cluster, width)
+
+    own_weights = (w_query.T, w_key, w_value.T)
+    own_shape = (own_weights, cluster, block_count)
+    placed, head = place(features, by_walker, 0, HEAD_WALKERS, after=(all_pairs,))
+    passed_head = moved(in_blocks(head), first_moves)
+    beside_head = moved(in_blocks(head), swap)
+    placed, tail = place(features, by_walker, HEAD_WALKERS, walkers - HEAD_WALKERS, placed)
+    passed_tail = moved(in_blocks(tail), first_moves)
+    beside_tail = moved(in_blocks(tail), swap)
+    own = own_part(head, *own_shape, 0, 0, heads, (), (tail,))
+    own = own_part(tail, *own_shape, 0, heads, block_count - heads, own, (wanted,))
+    blocks = (in_blocks(head), in_blocks(tail))
+    passed = (passed_head, passed_tail)
+    beside = (beside_head, beside_tail)
     own_at = 7 * capacity
     passed_at = own_at + block_count
     beside_at = passed_at + block_count
@@ -563,25 +590,28 @@
 
     beside = moved(blocks, swap)
     passed = moved(blocks, first_moves)
-    (second,) = pick(at_position, wanted, (blocks,), SECOND_PLAN, after=own[2:])
+    (second,) = pick(at_position, wanted, blocks, SECOND_PLAN, after=own[2:])
     second = moved(second, second_moves)
-    (second_cross,) = pick(at_position, wanted, (beside,), SECOND_CROSS_PLAN, after=own[2:])
+    (second_cross,) = pick(at_position, wanted, beside, SECOND_CROSS_PLAN, after=own[2:])
     second_cross = moved(second_cross, second_moves)
-    on, outward = pick(at_position, wanted, (passed,), ON_PLAN, after=own[2:])
+    on, outward = pick(at_position, wanted, passed, ON_PLAN, after=own[2:])
     on = moved(on, swap)
     outward = moved(outward, outward_moves)
-    (middle,) = pick(at_position, wanted, (blocks,), MIDDLE_PLAN, after=(second,))
+    (middle,) = pick(at_position, wanted, blocks, MIDDLE_PLAN, after=(second,))
     middle = moved(middle, middle_moves)
-    (near,) = pick(at_position, wanted, (passed,), NEAR_PLAN, after=(on,))
+    (near,) = pick(at_position, wanted, passed, NEAR_PLAN, after=(on,))
     near = moved(near, swap)
     on = moved(on, outward_moves)
-    (middle_cross,) = pick(
-        at_position, wanted, (beside,), MIDDLE_CROSS_PLAN, after=(second_cross,)
-    )
+    (middle_cross,) = pick(at_position, wanted, beside, MIDDLE_CROSS_PLAN, after=(second_cross,))
     middle_cross = moved(middle_cross, middle_moves)
 
-    buffer = collect((blocks, passed, beside), (own_at, passed_at, beside_at), total)
-
+    collected = (*blocks, *passed, *beside)
+    places = [at + part for at in (own_at, passed_at, beside_at) for part in (0, heads)]
+    buffer = collect(collected, places, total)
+
+    listed = pairs.reshape(-1)
+    owner, within = listed // block_count // stride, listed % block_count
+    (ranking,), _ = slot_tables(owner[None], within[None], capacity)
     z, y = position // 2, position % 2
     is_end = (z == 0) | (z == LEVELS - 1)
     z_owner, same = owner // 2, owner % 2 == y
@@ -605,7 +635,7 @@
     marks = [0, ends[0] // STEP, ends[1] // STEP, block_count // STEP]
     phases = [(marks[n], marks[n + 1] - marks[n]) for n in range(3)]
     weights = (jnp.concatenate([w_key, w_value], axis=1), w_out, w_mix)
-    shared = (order, table, own, placed.reshape(blocks.shape), weights)
+    shared = (order, table, own, in_blocks(placed), weights)
     arrivals = (
         ((near, 0), (second, 1), (second_cross, 2)),
         ((outward, 3), (on, 4), (middle, 5)),

time: 186 us -> 194 us (1.043)
  blocking collectives: 34.1 us -> 0 us
  waiting for transfers between devices: 15.3 us -> 47.8 us
  starting transfers between devices: 15.8 us -> 24.4 us
  Pallas kernels: 103 us -> 99.4 us
  local copies, waits for them, and re-layouts: 8.43 us -> 11.1 us
    unnamed x1 -> x0, blocking collectives: 34.1 us -> none
    ppermute x10 -> x12, waiting for transfers between devices: 15.3 us -> 47.8 us  [moved(): return lax.ppermute(x, 'elec', pairs_of)]
    all_to_all x0 -> x1, starting transfers between devices: none -> 6.28 us  [body(): lax.all_to_all(jnp.broadcast_to(pairs.reshape(1, -1), (SPAN, block_count...]
    ppermute x10 -> x12, starting transfers between devices: 15.8 us -> 18.2 us  [moved(): return lax.ppermute(x, 'elec', pairs_of)]
    pallas_call x1 -> x2, Pallas kernels: 6.36 us -> 5.07 us  [place(): pl.pallas_call(place_kernel, grid=(count // per,), in_specs=[pl.BlockSpec...]
    unnamed x43 -> x44, local copies, waits for them, and re-layouts: 8.21 us -> 9.4 us
  transfers between devices with their start and end apart: 10 -> 13, of which waited for: 2 -> 4; matrix products, arithmetic and copies ran while one was open for 2% -> 3% of each run, Pallas kernels for 44% -> 41%
where the time goes in v14:
time: 194 us; the launch traced here: 191 us
  Pallas kernels  99.4 us (51%)
  waiting for transfers between devices  47.8 us (25%)
  starting transfers between devices  24.4 us (13%)
  local copies, waits for them, and re-layouts  11.1 us (6%)
  between operations  5.34 us (3%)
  other arithmetic  3.46 us (2%)
    pallas_call x3, Pallas kernels, attend(): pl.pallas_call(kernel, in_specs=in_specs, out_specs=[hbm, hbm], out_shape...  49.3 us
    ppermute x12, waiting for transfers between devices, moved(): return lax.ppermute(x, 'elec', pairs_of)  47.8 us
    pallas_call x2, Pallas kernels, own_part(): pl.pallas_call(functools.partial(own_kernel, head_width=width // HEADS),...  30.3 us
    ppermute x12, starting transfers between devices, moved(): return lax.ppermute(x, 'elec', pairs_of)  18.2 us
    pallas_call x6, Pallas kernels, pick(): pl.pallas_call(functools.partial(pick_kernel, plan=plan, capacity=capacit...  10.4 us
    unnamed x44, local copies, waits for them, and re-layouts  9.4 us
    all_to_all x1, starting transfers between devices, body(): lax.all_to_all(jnp.broadcast_to(pairs.reshape(1, -1), (SPAN, block_count...  6.28 us
    pallas_call x2, Pallas kernels, place(): pl.pallas_call(place_kernel, grid=(count // per,), in_specs=[pl.BlockSpec...  5.07 us
  transfers between devices with their start and end apart: 13, of which 4 were waited for; matrix products, arithmetic and copies ran while one was open for 3% of the time, Pallas kernels for 41%

profile of v14, /device:TPU:8, one launch (start us, length us, event | category | flops | bytes accessed | tf_op | source)
XLA Modules:
  0.0 191.5 jit_solution(7781745852439057732)
XLA Ops:
  1.5 6.3 %all-to-all-start = ((s32[8,1,192]{2,1,0:T(1,128)}), s32[8,1,192]{2,1,0:T(1,128)S(1)}, u32[]{:S(2)}, u32[]{:S(2)}) async-start(s32[8,1,192]{2,1,0:T(1,128)} %broadcast_in_dim.119), calls=%async_computation | async-start | bytes 16384 | tf_op jit(solution)/shard_map/all_to_all | solution.py:556
  17.9 1.0 copy.27
  19.7 1.6 copy-done.9
  22.0 3.2 %place_rows.2 = (bf16[4096,256]{1,0:T(8,128)(2,1)S(1)}, bf16[3072,256]{1,0:T(8,128)(2,1)S(1)}) custom-call(bf16[4096,256]{1,0:T(8,128)(2,1)S(1)} %copy-done.9, s32[8,1,512]{2,1,0:T(1,128)S(1)} %bitcast.35, s32[8,192]{1,0:T(8,128)S(1)} %get-tuple-element.43.rest_0_), custom_call_target="tpu_custom_call" | custom-call | flops 4830000128 | tf_op jit(solution)/shard_map/place_rows/pallas_call | solution.py:67
  25.2 1.5 collective-permute-start
  27.3 1.9 place_rows.3
  29.2 2.4 %collective-permute-start.5 = (bf16[16,64,256]{2,1,0:T(8,128)(2,1)}, bf16[16,64,256]{2,1,0:T(8,128)(2,1)S(1)}, u32[]{:S(2)}, u32[]{:S(2)}) collective-permute-start(bf16[16,64,256]{2,1,0:T(8,128)(2,1)} %bitcast.12.tail_ref.refs_1_), channel_id=1, source_target_pairs={{0,8},{1,9},{2,10},{3,11},{4,0},{5,1},{6,2},{7,3},{8,12},{9,13},{1... | collective-permute-start | bytes 1572872 | tf_op jit(solution)/shard_map/ppermute | solution.py:545
  31.5 21.6 %own_blocks.2 = (bf16[64,256,256]{2,1,0:T(8,128)(2,1)}, bf16[64,256,256]{2,1,0:T(8,128)(2,1)}, f32[64,8,256]{2,1,0:T(8,128)S(1)}) custom-call(bf16[3072,256]{1,0:T(8,128)(2,1)S(1)} %get-tuple-element.24.normed_ref, bf16[256,256]{1,0:T(8,128)(2,1)S(1)} %bitcast.33, bf16[256,256]{1,0:T(8,128)(2,1)S(1)} %copy-done.6, bf16[256,256]{1,0:T(8,128)(2,1)S(1)} %bitcast.31, ...), custom_call_target="tpu_custom_call" | custom-call | flops 27599998976 | tf_op jit(solution)/shard_map/own_blocks/pallas_call | solution.py:192
  53.7 8.7 %own_blocks.3 = (bf16[64,256,256]{2,1,0:T(8,128)(2,1)}, bf16[64,256,256]{2,1,0:T(8,128)(2,1)}, f32[64,8,256]{2,1,0:T(8,128)S(1)}) custom-call(bf16[1024,256]{1,0:T(8,128)(2,1)} %get-tuple-element.23.rest_0_.normed_ref, bf16[256,256]{1,0:T(8,128)(2,1)S(1)} %bitcast.34, ...), custom_call_target="tpu_custom_call", output_to_operand_aliasing={{0}: (4, {}), {1}: (5, {}), {2}: (6, {})} | custom-call | flops 9200000000 | tf_op jit(solution)/shard_map/own_blocks/pallas_call | solution.py:192
  62.4 11.7 %collective-permute-done.5.tail_ref.refs_3_ = bf16[16,64,256]{2,1,0:T(8,128)(2,1)S(1)} collective-permute-done((bf16[16,64,256]{2,1,0:T(8,128)(2,1)}, bf16[16,64,256]{2,1,0:T(8,128)(2,1)S(1)}, u32[]{:S(2)}, u32[]{:S(2)}) %collective-permute-start.5) | collective-permute-done | bytes 524320 | tf_op jit(solution)/shard_map/ppermute | solution.py:545
  74.2 2.3 %pick_blocks.8 = (bf16[25,64,256]{2,1,0:T(8,128)(2,1)}, bf16[25,64,256]{2,1,0:T(8,128)(2,1)S(1)}) custom-call(s32[1]{0:T(128)} %bitcast.10.position_ref, s32[8,200]{1,0:T(8,128)S(1)} %select_reduce_fusion.rest_3_.wanted_ref, bf16[48,64,256]{2,1,0:T(8,128)(2,1)S(1)} %collective-permute-done.4.head_ref.refs_2_, ...), custom_call_target="tpu_custom_call" | custom-call | flops 1724999936 | tf_op jit(solution)/shard_map/pick_blocks/pallas_call | solution.py:119
  77.2 1.5 collective-permute-start.1
  78.6 2.4 %pick_blocks.9 = bf16[25,64,256]{2,1,0:T(8,128)(2,1)} custom-call(s32[1]{0:T(128)} %bitcast.10.position_ref, s32[8,200]{1,0:T(8,128)S(1)} %select_reduce_fusion.rest_3_.wanted_ref, bf16[48,64,256]{2,1,0:T(8,128)(2,1)S(1)} %bitcast.28, bf16[16,64,256]{2,1,0:T(8,128)(2,1)} %bitcast.12.tail_ref.refs_1_, f32[64,8,256]{2,1,0:T(8,128)S(1)} %get-tuple-element.30.rest_0_.stats_ref), custom_call_target="tpu_custom_call" | custom-call | flops 1724999936 | tf_op jit(solution)/shard_map/pick_blocks/pallas_call | solution.py:119
  81.0 1.5 collective-permute-start.9
  82.8 23.5 %collective-permute-done.1.tail_ref.refs_5_ = bf16[16,64,256]{2,1,0:T(8,128)(2,1)} collective-permute-done((bf16[16,64,256]{2,1,0:T(8,128)(2,1)}, bf16[16,64,256]{2,1,0:T(8,128)(2,1)}, u32[]{:S(2)}, u32[]{:S(2)}) %collective-permute-start.1) | collective-permute-done | bytes 524320 | tf_op jit(solution)/shard_map/ppermute | solution.py:545
  106.3 1.0 copy-done.18
  107.4 1.8 pick_blocks.6
  109.1 1.5 collective-permute-start.2
  110.7 1.0 pick_blocks.11
  112.4 1.5 pick_blocks.10
  113.9 1.9 %collective-permute-start.10 = (bf16[25,64,256]{2,1,0:T(8,128)(2,1)S(1)}, bf16[25,64,256]{2,1,0:T(8,128)(2,1)S(1)}, u32[]{:S(2)}, u32[]{:S(2)}) collective-permute-start(bf16[25,64,256]{2,1,0:T(8,128)(2,1)S(1)} %pick_blocks.10), channel_id=1, source_target_pairs={{4,8},{5,9},{6,10},{7,11},{8,4},{9,5},{10,6},{11,7},{20,24},{21,25... | collective-permute-start | bytes 2457608 | tf_op jit(solution)/shard_map/ppermute | solution.py:545
  115.9 1.5 collective-permute-start.6
  117.4 4.4 %collect_blocks.1.rest_6_ = bf16[367,64,256]{2,1,0:T(8,128)(2,1)} custom-call(bf16[48,64,256]{2,1,0:T(8,128)(2,1)S(1)} %bitcast.30, bf16[16,64,256]{2,1,0:T(8,128)(2,1)} %bitcast.12.tail_ref.refs_1_, bf16[48,64,256]{2,1,0:T(8,128)(2,1)S(1)} %copy-done.3, bf16[16,64,256]{2,1,0:T(8,128)(2,1)S(1)} %copy-done.5, bf16[48,64,256]{2,1,0:T(8,128)(2,1)} %copy-done, ...), custom_call_target="tpu_custom_call" | custom-call | flops 4600000000 | tf_op jit(solution)/shard_map/collect_blocks/pallas_call | solution.py:236
  121.8 7.6 %collective-permute-done.2.rest_0_.rest_5_ = bf16[25,64,256]{2,1,0:T(8,128)(2,1)S(1)} collective-permute-done((bf16[25,64,256]{2,1,0:T(8,128)(2,1)S(1)}, bf16[25,64,256]{2,1,0:T(8,128)(2,1)S(1)}, u32[]{:S(2)}, u32[]{:S(2)}) %collective-permute-start.2) | collective-permute-done | bytes 819232 | tf_op jit(solution)/shard_map/ppermute | solution.py:545
  129.4 1.4 pick_blocks.7
  130.8 1.9 %collective-permute-start.3 = (bf16[25,64,256]{2,1,0:T(8,128)(2,1)S(1)}, bf16[25,64,256]{2,1,0:T(8,128)(2,1)S(1)}, u32[]{:S(2)}, u32[]{:S(2)}) collective-permute-start(bf16[25,64,256]{2,1,0:T(8,128)(2,1)S(1)} %pick_blocks.7), channel_id=1, source_target_pairs={{4,8},{5,9},{6,10},{7,11},{8,4},{9,5},{10,6},{11,7},{20,24},{21,25... | collective-permute-start | bytes 2457608 | tf_op jit(solution)/shard_map/ppermute | solution.py:545
  132.8 2.7 %collective-permute-start.8 = (bf16[25,64,256]{2,1,0:T(8,128)(2,1)}, bf16[25,64,256]{2,1,0:T(8,128)(2,1)S(1)}, u32[]{:S(2)}, u32[]{:S(2)}) collective-permute-start(bf16[25,64,256]{2,1,0:T(8,128)(2,1)} %collective-permute-done.7.rest_0_), channel_id=1, source_target_pairs={{8,12},{9,13},{10,14},{11,15},{4,0},{5,1},{6,2},{7,3},{24,28},{25,... | collective-permute-start | bytes 2457608 | tf_op jit(solution)/shard_map/ppermute | solution.py:545
  135.5 1.6 copy-done.16
  137.1 18.4 %attend_blocks.3 = (bf16[64,64,256]{2,1,0:T(8,128)(2,1)}, bf16[367,64,256]{2,1,0:T(8,128)(2,1)}) custom-call(s32[2]{0:T(128)S(1)} %pad_add_fusion.2.range_ref, s32[64]{0:T(128)S(1)} %select_reduce_fusion.3.order_ref, s32[192]{0:T(256)S(1)} %or_select_fusion.table_ref, ...), custom_call_target="tpu_custom_call", output_to_operand_aliasing={{1}: (13, {})} | custom-call | flops 20700000256 | tf_op jit(solution)/shard_map/attend_blocks/pallas_call | solution.py:444
  155.6 4.9 %collective-permute-done.8.rest_4_ = bf16[25,64,256]{2,1,0:T(8,128)(2,1)S(1)} collective-permute-done((bf16[25,64,256]{2,1,0:T(8,128)(2,1)}, bf16[25,64,256]{2,1,0:T(8,128)(2,1)S(1)}, u32[]{:S(2)}, u32[]{:S(2)}) %collective-permute-start.8) | collective-permute-done | bytes 819232 | tf_op jit(solution)/shard_map/ppermute | solution.py:545
  160.4 13.6 %attend_blocks.4 = (bf16[64,64,256]{2,1,0:T(8,128)(2,1)}, bf16[367,64,256]{2,1,0:T(8,128)(2,1)}) custom-call(s32[2]{0:T(128)S(1)} %pad_add_fusion.1.range_ref, s32[64]{0:T(128)S(1)} %select_reduce_fusion.3.order_ref, s32[192]{0:T(256)S(1)} %or_select_fusion.table_ref, ...), custom_call_target="tpu_custom_call", output_to_operand_aliasing={{1}: (13, {}), {0}: (14, {})} | custom-call | flops 20700000256 | tf_op jit(solution)/shard_map/attend_blocks/pallas_call | solution.py:444
  174.0 17.3 %attend_blocks.5 = (bf16[64,64,256]{2,1,0:T(8,128)(2,1)}, bf16[367,64,256]{2,1,0:T(8,128)(2,1)}) custom-call(s32[2]{0:T(128)S(1)} %pad_add_fusion.range_ref, s32[64]{0:T(128)S(1)} %select_reduce_fusion.3.order_ref, s32[192]{0:T(256)S(1)} %or_select_fusion.table_ref, ...), custom_call_target="tpu_custom_call", output_to_operand_aliasing={{1}: (11, {}), {0}: (12, {})} | custom-call | flops 20700000256 | tf_op jit(solution)/shard_map/attend_blocks/pallas_call | solution.py:444
  (71 shorter events, 11.1 us)
Async XLA Ops:
  1.5 17.4 %all-to-all-start = ((s32[8,1,192]{2,1,0:T(1,128)}), s32[8,1,192]{2,1,0:T(1,128)S(1)}, u32[]{:S(2)}, u32[]{:S(2)}) async-start(s32[8,1,192]{2,1,0:T(1,128)} %broadcast_in_dim.119), calls=%async_computation | async-start | bytes 16384 | tf_op jit(solution)/shard_map/all_to_all | solution.py:556
  19.7 1.6 copy-start.9
  21.3 0.7 copy-start.14
  25.2 81.1 %collective-permute-start = (bf16[48,64,256]{2,1,0:T(8,128)(2,1)S(1)}, bf16[48,64,256]{2,1,0:T(8,128)(2,1)S(1)}, u32[]{:S(2)}, u32[]{:S(2)}) collective-permute-start(bf16[48,64,256]{2,1,0:T(8,128)(2,1)S(1)} %bitcast.26), channel_id=1, source_target_pairs={{0,2},{1,3},{2,0},{3,1},{4,6},{5,7},{6,4},{7,5},{8,10},{9,11},{10,... | collective-permute-start | bytes 4718600 | tf_op jit(solution)/shard_map/ppermute | solution.py:545
  26.7 47.4 %collective-permute-start.4 = (bf16[48,64,256]{2,1,0:T(8,128)(2,1)S(1)}, bf16[48,64,256]{2,1,0:T(8,128)(2,1)S(1)}, u32[]{:S(2)}, u32[]{:S(2)}) collective-permute-start(bf16[48,64,256]{2,1,0:T(8,128)(2,1)S(1)} %bitcast.27), channel_id=1, source_target_pairs={{0,8},{1,9},{2,10},{3,11},{4,0},{5,1},{6,2},{7,3},{8,12},{9,13},{1... | collective-permute-start | bytes 4718600 | tf_op jit(solution)/shard_map/ppermute | solution.py:545
  27.3 4.2 %copy-start.6 = (bf16[256,256]{1,0:T(8,128)(2,1)S(1)}, bf16[256,256]{1,0:T(8,128)(2,1)}, u32[]{:S(2)}) copy-start(bf16[256,256]{1,0:T(8,128)(2,1)} %key_w_ref.3) | copy-start | bytes 393220
  29.2 24.0 %copy-start.15 = (bf16[4096,256]{1,0:T(8,128)(2,1)}, bf16[4096,256]{1,0:T(8,128)(2,1)S(1)}, u32[]{:S(2)}) copy-start(bf16[4096,256]{1,0:T(8,128)(2,1)S(1)} %get-tuple-element.31) | copy-start | bytes 6291460
  29.2 45.0 %collective-permute-start.5 = (bf16[16,64,256]{2,1,0:T(8,128)(2,1)}, bf16[16,64,256]{2,1,0:T(8,128)(2,1)S(1)}, u32[]{:S(2)}, u32[]{:S(2)}) collective-permute-start(bf16[16,64,256]{2,1,0:T(8,128)(2,1)} %bitcast.12.tail_ref.refs_1_), channel_id=1, source_target_pairs={{0,8},{1,9},{2,10},{3,11},{4,0},{5,1},{6,2},{7,3},{8,12},{9,13},{1... | collective-permute-start | bytes 1572872 | tf_op jit(solution)/shard_map/ppermute | solution.py:545
  62.4 16.2 %copy-start.17 = (f32[64,8,256]{2,1,0:T(8,128)}, f32[64,8,256]{2,1,0:T(8,128)S(1)}, u32[]{:S(2)}) copy-start(f32[64,8,256]{2,1,0:T(8,128)S(1)} %get-tuple-element.30.rest_0_.stats_ref) | copy-start | bytes 1572868
  74.2 2.3 %copy-start.4 = (bf16[16,64,256]{2,1,0:T(8,128)(2,1)}, bf16[16,64,256]{2,1,0:T(8,128)(2,1)S(1)}, u32[]{:S(2)}) copy-start(bf16[16,64,256]{2,1,0:T(8,128)(2,1)S(1)} %collective-permute-done.5.tail_ref.refs_3_) | copy-start | bytes 1572868
  74.2 2.3 %copy-start.2 = (bf16[48,64,256]{2,1,0:T(8,128)(2,1)}, bf16[48,64,256]{2,1,0:T(8,128)(2,1)S(1)}, u32[]{:S(2)}) copy-start(bf16[48,64,256]{2,1,0:T(8,128)(2,1)S(1)} %collective-permute-done.4.head_ref.refs_2_) | copy-start | bytes 4718596
  76.5 4.5 %copy-start.10 = (bf16[25,64,256]{2,1,0:T(8,128)(2,1)}, bf16[25,64,256]{2,1,0:T(8,128)(2,1)S(1)}, u32[]{:S(2)}) copy-start(bf16[25,64,256]{2,1,0:T(8,128)(2,1)S(1)} %get-tuple-element.32) | copy-start | bytes 2457604
  76.5 34.2 %collective-permute-start.7 = (bf16[25,64,256]{2,1,0:T(8,128)(2,1)}, bf16[25,64,256]{2,1,0:T(8,128)(2,1)}, u32[]{:S(2)}, u32[]{:S(2)}) collective-permute-start(bf16[25,64,256]{2,1,0:T(8,128)(2,1)} %get-tuple-element.33), channel_id=1, source_target_pairs={{0,2},{1,3},{2,0},{3,1},{4,6},{5,7},{6,4},{7,5},{8,10},{9,11},{10,... | collective-permute-start | bytes 2457608 | tf_op jit(solution)/shard_map/ppermute | solution.py:545
  77.2 29.1 %collective-permute-start.1 = (bf16[16,64,256]{2,1,0:T(8,128)(2,1)}, bf16[16,64,256]{2,1,0:T(8,128)(2,1)}, u32[]{:S(2)}, u32[]{:S(2)}) collective-permute-start(bf16[16,64,256]{2,1,0:T(8,128)(2,1)} %bitcast.12.tail_ref.refs_1_), channel_id=1, source_target_pairs={{0,2},{1,3},{2,0},{3,1},{4,6},{5,7},{6,4},{7,5},{8,10},{9,11},{10,... | collective-permute-start | bytes 1572872 | tf_op jit(solution)/shard_map/ppermute | solution.py:545
  81.0 31.4 %collective-permute-start.9 = (bf16[25,64,256]{2,1,0:T(8,128)(2,1)}, bf16[25,64,256]{2,1,0:T(8,128)(2,1)}, u32[]{:S(2)}, u32[]{:S(2)}) collective-permute-start(bf16[25,64,256]{2,1,0:T(8,128)(2,1)} %pick_blocks.9), channel_id=1, source_target_pairs={{0,4},{1,5},{2,6},{3,7},{4,12},{5,13},{6,14},{7,15},{8,0},{9,1},{1... | collective-permute-start | bytes 2457608 | tf_op jit(solution)/shard_map/ppermute | solution.py:545
  82.8 27.9 %copy-start.3 = (bf16[48,64,256]{2,1,0:T(8,128)(2,1)S(1)}, bf16[48,64,256]{2,1,0:T(8,128)(2,1)}, u32[]{:S(2)}) copy-start(bf16[48,64,256]{2,1,0:T(8,128)(2,1)} %copy-done.2) | copy-start | bytes 4718596
  82.8 27.9 %copy-start.5 = (bf16[16,64,256]{2,1,0:T(8,128)(2,1)S(1)}, bf16[16,64,256]{2,1,0:T(8,128)(2,1)}, u32[]{:S(2)}) copy-start(bf16[16,64,256]{2,1,0:T(8,128)(2,1)} %copy-done.4) | copy-start | bytes 1572868
  106.3 1.0 copy-start.18
  107.4 1.8 copy-start
  109.1 20.3 %collective-permute-start.2 = (bf16[25,64,256]{2,1,0:T(8,128)(2,1)S(1)}, bf16[25,64,256]{2,1,0:T(8,128)(2,1)S(1)}, u32[]{:S(2)}, u32[]{:S(2)}) collective-permute-start(bf16[25,64,256]{2,1,0:T(8,128)(2,1)S(1)} %pick_blocks.6), channel_id=1, source_target_pairs={{0,4},{1,5},{2,6},{3,7},{4,12},{5,13},{6,14},{7,15},{8,0},{9,1},{1... | collective-permute-start | bytes 2457608 | tf_op jit(solution)/shard_map/ppermute | solution.py:545
  111.7 23.7 %collective-permute-start.11 = (bf16[25,64,256]{2,1,0:T(8,128)(2,1)S(1)}, bf16[25,64,256]{2,1,0:T(8,128)(2,1)S(1)}, u32[]{:S(2)}, u32[]{:S(2)}) collective-permute-start(bf16[25,64,256]{2,1,0:T(8,128)(2,1)S(1)} %pick_blocks.11), channel_id=1, source_target_pairs={{0,2},{1,3},{2,0},{3,1},{4,6},{5,7},{6,4},{7,5},{8,10},{9,11},{10,... | collective-permute-start | bytes 2457608 | tf_op jit(solution)/shard_map/ppermute | solution.py:545
  112.4 3.4 %copy-start.11 = (bf16[25,64,256]{2,1,0:T(8,128)(2,1)S(1)}, bf16[25,64,256]{2,1,0:T(8,128)(2,1)}, u32[]{:S(2)}) copy-start(bf16[25,64,256]{2,1,0:T(8,128)(2,1)} %copy-done.10) | copy-start | bytes 2457604
  113.9 41.6 %collective-permute-start.10 = (bf16[25,64,256]{2,1,0:T(8,128)(2,1)S(1)}, bf16[25,64,256]{2,1,0:T(8,128)(2,1)S(1)}, u32[]{:S(2)}, u32[]{:S(2)}) collective-permute-start(bf16[25,64,256]{2,1,0:T(8,128)(2,1)S(1)} %pick_blocks.10), channel_id=1, source_target_pairs={{4,8},{5,9},{6,10},{7,11},{8,4},{9,5},{10,6},{11,7},{20,24},{21,25... | collective-permute-start | bytes 2457608 | tf_op jit(solution)/shard_map/ppermute | solution.py:545
  115.9 13.5 %copy-start.1 = (bf16[48,64,256]{2,1,0:T(8,128)(2,1)S(1)}, bf16[48,64,256]{2,1,0:T(8,128)(2,1)}, u32[]{:S(2)}) copy-start(bf16[48,64,256]{2,1,0:T(8,128)(2,1)} %copy-done) | copy-start | bytes 4718596
  115.9 39.7 %collective-permute-start.6 = (bf16[25,64,256]{2,1,0:T(8,128)(2,1)S(1)}, bf16[25,64,256]{2,1,0:T(8,128)(2,1)S(1)}, u32[]{:S(2)}, u32[]{:S(2)}) collective-permute-start(bf16[25,64,256]{2,1,0:T(8,128)(2,1)S(1)} %copy-done.11), channel_id=1, source_target_pairs={{8,12},{9,13},{10,14},{11,15},{4,0},{5,1},{6,2},{7,3},{24,28},{25,... | collective-permute-start | bytes 2457608 | tf_op jit(solution)/shard_map/ppermute | solution.py:545
  121.7 13.7 %copy-start.8 = (bf16[256,512]{1,0:T(8,128)(2,1)S(1)}, bf16[256,512]{1,0:T(8,128)(2,1)}, u32[]{:S(2)}) copy-start(bf16[256,512]{1,0:T(8,128)(2,1)} %copy-done.7) | copy-start | bytes 786436
  121.7 13.7 %copy-start.12 = (bf16[256,256]{1,0:T(8,128)(2,1)S(1)}, bf16[256,256]{1,0:T(8,128)(2,1)}, u32[]{:S(2)}) copy-start(bf16[256,256]{1,0:T(8,128)(2,1)} %rest_1_.5) | copy-start | bytes 393220
  121.8 13.7 %copy-start.13 = (bf16[256,256]{1,0:T(8,128)(2,1)S(1)}, bf16[256,256]{1,0:T(8,128)(2,1)}, u32[]{:S(2)}) copy-start(bf16[256,256]{1,0:T(8,128)(2,1)} %rest_2_.5) | copy-start | bytes 393220
  121.8 13.7 %copy-start.19 = (f32[64,8,256]{2,1,0:T(8,128)S(1)}, f32[64,8,256]{2,1,0:T(8,128)}, u32[]{:S(2)}) copy-start(f32[64,8,256]{2,1,0:T(8,128)} %copy-done.17) | copy-start | bytes 1572868
  130.8 43.2 %collective-permute-start.3 = (bf16[25,64,256]{2,1,0:T(8,128)(2,1)S(1)}, bf16[25,64,256]{2,1,0:T(8,128)(2,1)S(1)}, u32[]{:S(2)}, u32[]{:S(2)}) collective-permute-start(bf16[25,64,256]{2,1,0:T(8,128)(2,1)S(1)} %pick_blocks.7), channel_id=1, source_target_pairs={{4,8},{5,9},{6,10},{7,11},{8,4},{9,5},{10,6},{11,7},{20,24},{21,25... | collective-permute-start | bytes 2457608 | tf_op jit(solution)/shard_map/ppermute | solution.py:545
  132.8 27.7 %collective-permute-start.8 = (bf16[25,64,256]{2,1,0:T(8,128)(2,1)}, bf16[25,64,256]{2,1,0:T(8,128)(2,1)S(1)}, u32[]{:S(2)}, u32[]{:S(2)}) collective-permute-start(bf16[25,64,256]{2,1,0:T(8,128)(2,1)} %collective-permute-done.7.rest_0_), channel_id=1, source_target_pairs={{8,12},{9,13},{10,14},{11,15},{4,0},{5,1},{6,2},{7,3},{24,28},{25,... | collective-permute-start | bytes 2457608 | tf_op jit(solution)/shard_map/ppermute | solution.py:545
  135.5 1.6 copy-start.16
  (1 other events, 0.7 us)

commit v15 on v13

--- a/solution.py
+++ b/solution.py
@@ -125,8 +125,9 @@
     )
 
 
-def own_kernel(normed_ref, query_w_ref, key_w_ref, value_w_ref, *rest, head_width):
-    query_ref, own_ref, stats_ref = rest[-3:]
+def own_kernel(
+    normed_ref, query_w_ref, key_w_ref, value_w_ref, query_ref, own_ref, stats_ref, *, head_width
+):
     blocks, width, tile = query_ref.shape
     cluster = tile // GROUP
     span = GROUP * head_width
@@ -170,41 +171,31 @@
         stats_ref[block] = jnp.concatenate(tops + totals, axis=0)
 
 
-def own_part(normed, w_query, w_key, w_value, cluster, half, so_far, after):
+def own_part(normed, w_query, w_key, w_value, cluster):
     rows, width = normed.shape
     blocks = rows // cluster
     tile = GROUP * cluster
     tiles = HEADS // GROUP
-    steps = blocks // STEP // 2
-    first = half * steps
     whole = pl.BlockSpec((width, width), lambda i: (0, 0))
-    square = pl.BlockSpec((STEP, width, tile), lambda i: (first + i, 0, 0))
-    extra = [*so_far, *after]
+    square = pl.BlockSpec((STEP, width, tile), lambda i: (i, 0, 0))
     return pl.pallas_call(
         functools.partial(own_kernel, head_width=width // HEADS),
-        grid=(steps,),
-        in_specs=[
-            pl.BlockSpec((STEP * cluster, width), lambda i: (first + i, 0)),
-            whole,
-            whole,
-            whole,
-        ]
-        + [pl.BlockSpec(memory_space=pl.ANY)] * len(extra),
+        grid=(blocks // STEP,),
+        in_specs=[pl.BlockSpec((STEP * cluster, width), lambda i: (i, 0)), whole, whole, whole],
         out_specs=[
             square,
             square,
-            pl.BlockSpec((STEP, 2 * tiles, tile), lambda i: (first + i, 0, 0)),
+            pl.BlockSpec((STEP, 2 * tiles, tile), lambda i: (i, 0, 0)),
         ],
         out_shape=[
             jax.ShapeDtypeStruct((blocks, width, tile), jnp.bfloat16),
             jax.ShapeDtypeStruct((blocks, width, tile), jnp.bfloat16),
             jax.ShapeDtypeStruct((blocks, 2 * tiles, tile), jnp.float32),
         ],
-        input_output_aliases={4 + n: n for n in range(len(so_far))},
-        cost_estimate=lasting(15),
+        cost_estimate=lasting(20),
         compiler_params=kernel_params(),
         name="own_blocks",
-    )(normed, w_query.T, w_key, w_value.T, *extra)
+    )(normed, w_query.T, w_key, w_value.T)
 
 
 def collect_kernel(*refs, places):
@@ -547,15 +538,20 @@
     owner = listed // block_count // stride
     within = listed % block_count
     ranking, tables = slot_tables(owner, within, capacity)
-    wanted = lax.all_gather(tables, "elec", axis_index_groups=groups)
+    wanted = lax.all_to_all(
+        jnp.broadcast_to(tables[None], (SPAN, SPAN * capacity)),
+        "elec",
+        split_axis=0,
+        concat_axis=0,
+        axis_index_groups=groups,
+        tiled=True,
+    )
 
     shape = (block_count // SUB, 1, SUB * cluster)
     block_shape = (block_count, cluster, width)
     placed, normed = place(features, assignment.reshape(shape))
     blocks = normed.reshape(block_shape)
-    own_operands = (normed, w_query, w_key, w_value, cluster)
-    own = own_part(*own_operands, 0, (), (tables,))
-    own = own_part(*own_operands, 1, own, (wanted,))
+    own = own_part(normed, w_query, w_key, w_value, cluster)
     own_at = 7 * capacity
     passed_at = own_at + block_count
     beside_at = passed_at + block_count
@@ -563,11 +559,11 @@
 
     beside = moved(blocks, swap)
     passed = moved(blocks, first_moves)
-    (second,) = pick(at_position, wanted, (blocks,), SECOND_PLAN, after=own[2:])
-    second = moved(second, second_moves)
-    (second_cross,) = pick(at_position, wanted, (beside,), SECOND_CROSS_PLAN, after=own[2:])
+    (second_pick,) = pick(at_position, wanted, (blocks,), SECOND_PLAN, after=own[2:])
+    second = moved(second_pick, second_moves)
+    on, outward = pick(at_position, wanted, (passed,), ON_PLAN, after=(second_pick,))
+    (second_cross,) = pick(at_position, wanted, (beside,), SECOND_CROSS_PLAN, after=(on,))
     second_cross = moved(second_cross, second_moves)
-    on, outward = pick(at_position, wanted, (passed,), ON_PLAN, after=own[2:])
     on = moved(on, swap)
     outward = moved(outward, outward_moves)
     (middle,) = pick(at_position, wanted, (blocks,), MIDDLE_PLAN, after=(second,))

time: 186 us -> 168 us (0.903)
  blocking collectives: 34.1 us -> 0 us
  waiting for transfers between devices: 15.3 us -> 32.7 us
  starting transfers between devices: 15.8 us -> 23.2 us
  local copies, waits for them, and re-layouts: 8.43 us -> 3.13 us
  Pallas kernels: 103 us -> 99.5 us
    unnamed x1 -> x0, blocking collectives: 34.1 us -> none
    ppermute x10, waiting for transfers between devices: 15.3 us -> 26.5 us  [moved(): return lax.ppermute(x, 'elec', pairs_of)]
    all_to_all x0 -> x1, waiting for transfers between devices: none -> 6.22 us  [body(): lax.all_to_all(jnp.broadcast_to(tables[None], (SPAN, SPAN * capacity)), '...]
    unnamed x43 -> x27, local copies, waits for them, and re-layouts: 8.21 us -> 2.38 us
    all_to_all x0 -> x1, starting transfers between devices: none -> 5.81 us  [body(): lax.all_to_all(jnp.broadcast_to(tables[None], (SPAN, SPAN * capacity)), '...]
    pallas_call x2 -> x1, Pallas kernels: 31.2 us -> 28.6 us  [own_part(): pl.pallas_call(functools.partial(own_kernel, head_width=width // HEADS),...]
  transfers between devices with their start and end apart: 10 -> 11, of which waited for: 2 -> 5; matrix products, arithmetic and copies ran while one was open for 2% -> 2% of each run, Pallas kernels for 44% -> 47%
where the time goes in v15:
time: 168 us; the launch traced here: 165 us
  Pallas kernels  99.5 us (59%)
  waiting for transfers between devices  32.7 us (19%)
  starting transfers between devices  23.2 us (14%)
  between operations  5.05 us (3%)
  local copies, waits for them, and re-layouts  3.13 us (2%)
    pallas_call x3, Pallas kernels, attend(): pl.pallas_call(kernel, in_specs=in_specs, out_specs=[hbm, hbm], out_shape...  49.3 us
    pallas_call x1, Pallas kernels, own_part(): pl.pallas_call(functools.partial(own_kernel, head_width=width // HEADS),...  28.6 us
    ppermute x10, waiting for transfers between devices, moved(): return lax.ppermute(x, 'elec', pairs_of)  26.5 us
    ppermute x10, starting transfers between devices, moved(): return lax.ppermute(x, 'elec', pairs_of)  17.4 us
    pallas_call x6, Pallas kernels, pick(): pl.pallas_call(functools.partial(pick_kernel, plan=plan, capacity=capacit...  11.4 us
    all_to_all x1, waiting for transfers between devices, body(): lax.all_to_all(jnp.broadcast_to(tables[None], (SPAN, SPAN * capacity)), '...  6.22 us
    all_to_all x1, starting transfers between devices, body(): lax.all_to_all(jnp.broadcast_to(tables[None], (SPAN, SPAN * capacity)), '...  5.81 us
    pallas_call x1, Pallas kernels, place(): pl.pallas_call(place_kernel, grid=(walkers // 2,), in_specs=[local, pl.Bl...  5.39 us
  transfers between devices with their start and end apart: 11, of which 5 were waited for; matrix products, arithmetic and copies ran while one was open for 2% of the time, Pallas kernels for 47%

profile of v15, /device:TPU:8, one launch (start us, length us, event | category | flops | bytes accessed | tf_op | source)
XLA Modules:
  0.0 165.2 jit_solution(4082836284731522442)
XLA Ops:
  0.0 0.7 copy-done.3
  0.7 5.4 %place_rows.1 = (bf16[4096,256]{1,0:T(8,128)(2,1)S(1)}, bf16[4096,256]{1,0:T(8,128)(2,1)S(1)}) custom-call(bf16[4096,256]{1,0:T(8,128)(2,1)} %features_ref.1, s32[8,1,512]{2,1,0:T(1,128)S(1)} %bitcast.27), custom_call_target="tpu_custom_call" | custom-call | flops 6899999744 | tf_op jit(solution)/shard_map/place_rows/pallas_call | solution.py:65
  6.1 1.3 copy-done.4
  7.4 2.0 %collective-permute-start = (bf16[64,64,256]{2,1,0:T(8,128)(2,1)S(1)}, bf16[64,64,256]{2,1,0:T(8,128)(2,1)}, u32[]{:S(2)}, u32[]{:S(2)}) collective-permute-start(bf16[64,64,256]{2,1,0:T(8,128)(2,1)S(1)} %bitcast.15), channel_id=1, source_target_pairs={{0,2},{1,3},{2,0},{3,1},{4,6},{5,7},{6,4},{7,5},{8,10},{9,11},{10,... | collective-permute-start | bytes 6291464 | tf_op jit(solution)/shard_map/ppermute | solution.py:526
  9.7 0.2 select_reduce_fusion.1
  10.0 0.6 broadcast_in_dim.108
  10.7 5.8 %all-to-all-start = ((s32[8,1,200]{2,1,0:T(1,128)}), s32[8,1,200]{2,1,0:T(1,128)S(1)}, u32[]{:S(2)}, u32[]{:S(2)}) async-start(s32[8,1,200]{2,1,0:T(1,128)} %broadcast_in_dim.108), calls=%async_computation | async-start | bytes 16384 | tf_op jit(solution)/shard_map/all_to_all | solution.py:541
  16.7 28.6 %own_blocks.1 = (bf16[64,256,256]{2,1,0:T(8,128)(2,1)}, bf16[64,256,256]{2,1,0:T(8,128)(2,1)}, f32[64,8,256]{2,1,0:T(8,128)S(1)}) custom-call(bf16[4096,256]{1,0:T(8,128)(2,1)S(1)} %get-tuple-element.17.normed_ref, bf16[256,256]{1,0:T(8,128)(2,1)S(1)} %bitcast.19, bf16[256,256]{1,0:T(8,128)(2,1)S(1)} %copy-done, bf16[256,256]{1,0:T(8,128)(2,1)S(1)} %bitcast.20), custom_call_target="tpu_custom_call" | custom-call | flops 23000000512 | tf_op jit(solution)/shard_map/own_blocks/pallas_call | solution.py:181
  45.3 0.7 fusion.14
  50.7 6.2 %all-to-all-done = s32[8,1,200]{2,1,0:T(1,128)S(1)} async-done(((s32[8,1,200]{2,1,0:T(1,128)}), s32[8,1,200]{2,1,0:T(1,128)S(1)}, u32[]{:S(2)}, u32[]{:S(2)}) %all-to-all-start) | async-done | bytes 6432 | tf_op jit(solution)/shard_map/all_to_all | solution.py:541
  56.9 1.8 %pick_blocks.6.rest_1_ = bf16[25,64,256]{2,1,0:T(8,128)(2,1)} custom-call(s32[1]{0:T(128)} %bitcast.6.position_ref, s32[8,200]{1,0:T(8,128)S(1)} %bitcast.21, bf16[64,64,256]{2,1,0:T(8,128)(2,1)S(1)} %bitcast.16, f32[64,8,256]{2,1,0:T(8,128)S(1)} %get-tuple-element.20.rest_1_.stats_ref), custom_call_target="tpu_custom_call" | custom-call | flops 1724999936 | tf_op jit(solution)/shard_map/pick_blocks/pallas_call | solution.py:106
  58.8 3.1 %pick_blocks.7 = (bf16[25,64,256]{2,1,0:T(8,128)(2,1)}, bf16[25,64,256]{2,1,0:T(8,128)(2,1)S(1)}) custom-call(s32[1]{0:T(128)} %bitcast.6.position_ref, s32[8,200]{1,0:T(8,128)S(1)} %bitcast.22, bf16[64,64,256]{2,1,0:T(8,128)(2,1)} %collective-permute-done.1.rest_0_.refs_1_, bf16[25,64,256]{2,1,0:T(8,128)(2,1)} %pick_blocks.6.rest_1_), custom_call_target="tpu_custom_call" | custom-call | flops 1724999936 | tf_op jit(solution)/shard_map/pick_blocks/pallas_call | solution.py:106
  61.8 0.5 collective-permute-start.5
  62.6 2.4 %collective-permute-start.7 = (bf16[25,64,256]{2,1,0:T(8,128)(2,1)}, bf16[25,64,256]{2,1,0:T(8,128)(2,1)}, u32[]{:S(2)}, u32[]{:S(2)}) collective-permute-start(bf16[25,64,256]{2,1,0:T(8,128)(2,1)} %pick_blocks.6.rest_1_), channel_id=1, source_target_pairs={{0,4},{1,5},{2,6},{3,7},{4,12},{5,13},{6,14},{7,15},{8,0},{9,1},{1... | collective-permute-start | bytes 2457608 | tf_op jit(solution)/shard_map/ppermute | solution.py:526
  65.3 1.9 %pick_blocks.8 = bf16[25,64,256]{2,1,0:T(8,128)(2,1)S(1)} custom-call(s32[1]{0:T(128)} %bitcast.6.position_ref, s32[8,200]{1,0:T(8,128)S(1)} %bitcast.23, bf16[64,64,256]{2,1,0:T(8,128)(2,1)} %collective-permute-done.rest_0_.refs_2_, bf16[25,64,256]{2,1,0:T(8,128)(2,1)} %get-tuple-element.22.rest_1_), custom_call_target="tpu_custom_call" | custom-call | flops 1724999936 | tf_op jit(solution)/shard_map/pick_blocks/pallas_call | solution.py:106
  67.2 1.0 collective-permute-start.2
  68.2 13.1 %collective-permute-done.5.rest_1_ = bf16[25,64,256]{2,1,0:T(8,128)(2,1)} collective-permute-done((bf16[25,64,256]{2,1,0:T(8,128)(2,1)}, bf16[25,64,256]{2,1,0:T(8,128)(2,1)}, u32[]{:S(2)}, u32[]{:S(2)}) %collective-permute-start.5) | collective-permute-done | bytes 819232 | tf_op jit(solution)/shard_map/ppermute | solution.py:526
  81.3 1.9 %pick_blocks.11 = bf16[25,64,256]{2,1,0:T(8,128)(2,1)S(1)} custom-call(s32[1]{0:T(128)} %bitcast.6.position_ref, s32[8,200]{1,0:T(8,128)S(1)} %bitcast.24, bf16[64,64,256]{2,1,0:T(8,128)(2,1)} %collective-permute-done.1.rest_0_.refs_1_, bf16[25,64,256]{2,1,0:T(8,128)(2,1)} %collective-permute-done.5.rest_1_), custom_call_target="tpu_custom_call" | custom-call | flops 1724999936 | tf_op jit(solution)/shard_map/pick_blocks/pallas_call | solution.py:106
  83.2 0.6 collective-permute-start.9
  83.9 0.3 collective-permute-done.7.rest_1_.rest_4_
  84.2 0.9 pick_blocks.10
  85.1 3.8 %collective-permute-start.8 = (bf16[25,64,256]{2,1,0:T(8,128)(2,1)S(1)}, bf16[25,64,256]{2,1,0:T(8,128)(2,1)S(1)}, u32[]{:S(2)}, u32[]{:S(2)}) collective-permute-start(bf16[25,64,256]{2,1,0:T(8,128)(2,1)S(1)} %pick_blocks.10), channel_id=1, source_target_pairs={{4,8},{5,9},{6,10},{7,11},{8,4},{9,5},{10,6},{11,7},{20,24},{21,25... | collective-permute-start | bytes 2457608 | tf_op jit(solution)/shard_map/ppermute | solution.py:526
  88.9 1.5 collective-permute-start.4
  90.5 4.9 %collect_blocks.1.rest_6_ = bf16[367,64,256]{2,1,0:T(8,128)(2,1)} custom-call(bf16[64,64,256]{2,1,0:T(8,128)(2,1)S(1)} %bitcast.18, bf16[64,64,256]{2,1,0:T(8,128)(2,1)} %collective-permute-done.1.rest_0_.refs_1_, bf16[64,64,256]{2,1,0:T(8,128)(2,1)} %collective-permute-done.rest_0_.refs_2_), custom_call_target="tpu_custom_call" | custom-call | flops 4600000000 | tf_op jit(solution)/shard_map/collect_blocks/pallas_call | solution.py:218
  95.4 6.1 %collective-permute-done.2.rest_1_.rest_5_ = bf16[25,64,256]{2,1,0:T(8,128)(2,1)S(1)} collective-permute-done((bf16[25,64,256]{2,1,0:T(8,128)(2,1)S(1)}, bf16[25,64,256]{2,1,0:T(8,128)(2,1)S(1)}, u32[]{:S(2)}, u32[]{:S(2)}) %collective-permute-start.2) | collective-permute-done | bytes 819232 | tf_op jit(solution)/shard_map/ppermute | solution.py:526
  101.6 1.9 %pick_blocks.9 = bf16[25,64,256]{2,1,0:T(8,128)(2,1)S(1)} custom-call(s32[1]{0:T(128)} %bitcast.6.position_ref, s32[8,200]{1,0:T(8,128)S(1)} %bitcast.26, bf16[64,64,256]{2,1,0:T(8,128)(2,1)} %collective-permute-done.rest_0_.refs_2_, bf16[25,64,256]{2,1,0:T(8,128)(2,1)S(1)} %collective-permute-done.2.rest_1_.rest_5_), custom_call_target="tpu_custom_call" | custom-call | flops 1724999936 | tf_op jit(solution)/shard_map/pick_blocks/pallas_call | solution.py:106
  103.4 2.8 %collective-permute-start.3 = (bf16[25,64,256]{2,1,0:T(8,128)(2,1)S(1)}, bf16[25,64,256]{2,1,0:T(8,128)(2,1)S(1)}, u32[]{:S(2)}, u32[]{:S(2)}) collective-permute-start(bf16[25,64,256]{2,1,0:T(8,128)(2,1)S(1)} %pick_blocks.9), channel_id=1, source_target_pairs={{4,8},{5,9},{6,10},{7,11},{8,4},{9,5},{10,6},{11,7},{20,24},{21,25... | collective-permute-start | bytes 2457608 | tf_op jit(solution)/shard_map/ppermute | solution.py:526
  106.2 2.7 %collective-permute-start.6 = (bf16[25,64,256]{2,1,0:T(8,128)(2,1)}, bf16[25,64,256]{2,1,0:T(8,128)(2,1)S(1)}, u32[]{:S(2)}, u32[]{:S(2)}) collective-permute-start(bf16[25,64,256]{2,1,0:T(8,128)(2,1)} %collective-permute-done.5.rest_1_), channel_id=1, source_target_pairs={{8,12},{9,13},{10,14},{11,15},{4,0},{5,1},{6,2},{7,3},{24,28},{25,... | collective-permute-start | bytes 2457608 | tf_op jit(solution)/shard_map/ppermute | solution.py:526
  109.0 18.5 %attend_blocks.3 = (bf16[64,64,256]{2,1,0:T(8,128)(2,1)}, bf16[367,64,256]{2,1,0:T(8,128)(2,1)}) custom-call(s32[2]{0:T(128)S(1)} %pad_add_fusion.2.range_ref, s32[64]{0:T(128)S(1)} %select_reduce_fusion.2.order_ref, s32[192]{0:T(256)S(1)} %get-tuple-element.32.table_ref, ...), custom_call_target="tpu_custom_call", output_to_operand_aliasing={{1}: (13, {})} | custom-call | flops 20700000256 | tf_op jit(solution)/shard_map/attend_blocks/pallas_call | solution.py:426
  127.4 6.9 %collective-permute-done.6.rest_4_ = bf16[25,64,256]{2,1,0:T(8,128)(2,1)S(1)} collective-permute-done((bf16[25,64,256]{2,1,0:T(8,128)(2,1)}, bf16[25,64,256]{2,1,0:T(8,128)(2,1)S(1)}, u32[]{:S(2)}, u32[]{:S(2)}) %collective-permute-start.6) | collective-permute-done | bytes 819232 | tf_op jit(solution)/shard_map/ppermute | solution.py:526
  134.4 13.6 %attend_blocks.4 = (bf16[64,64,256]{2,1,0:T(8,128)(2,1)}, bf16[367,64,256]{2,1,0:T(8,128)(2,1)}) custom-call(s32[2]{0:T(128)S(1)} %pad_add_fusion.1.range_ref, s32[64]{0:T(128)S(1)} %select_reduce_fusion.2.order_ref, s32[192]{0:T(256)S(1)} %get-tuple-element.32.table_ref, ...), custom_call_target="tpu_custom_call", output_to_operand_aliasing={{1}: (13, {}), {0}: (14, {})} | custom-call | flops 20700000256 | tf_op jit(solution)/shard_map/attend_blocks/pallas_call | solution.py:426
  148.0 17.3 %attend_blocks.5 = (bf16[64,64,256]{2,1,0:T(8,128)(2,1)}, bf16[367,64,256]{2,1,0:T(8,128)(2,1)}) custom-call(s32[2]{0:T(128)S(1)} %pad_add_fusion.range_ref, s32[64]{0:T(128)S(1)} %select_reduce_fusion.2.order_ref, s32[192]{0:T(256)S(1)} %get-tuple-element.32.table_ref, ...), custom_call_target="tpu_custom_call", output_to_operand_aliasing={{1}: (11, {}), {0}: (12, {})} | custom-call | flops 20700000256 | tf_op jit(solution)/shard_map/attend_blocks/pallas_call | solution.py:426
  (43 shorter events, 1.3 us)
Async XLA Ops:
  0.0 0.7 copy-start.3
  0.7 8.7 %copy-start.10 = (s32[64,3]{0,1:T(4,128)S(1)}, s32[64,3]{0,1:T(4,128)}, u32[]{:S(2)}) copy-start(s32[64,3]{0,1:T(4,128)} %param.10) | copy-start | bytes 2308
  0.7 15.7 %copy-start.9 = (bf16[256,256]{1,0:T(8,128)(2,1)S(1)}, bf16[256,256]{1,0:T(8,128)(2,1)}, u32[]{:S(2)}) copy-start(bf16[256,256]{1,0:T(8,128)(2,1)} %param.11) | copy-start | bytes 393220
  0.7 15.8 %copy-start.8 = (bf16[256,256]{1,0:T(8,128)(2,1)S(1)}, bf16[256,256]{1,0:T(8,128)(2,1)}, u32[]{:S(2)}) copy-start(bf16[256,256]{1,0:T(8,128)(2,1)} %param.13) | copy-start | bytes 393220
  0.7 16.0 %copy-start = (bf16[256,256]{1,0:T(8,128)(2,1)S(1)}, bf16[256,256]{1,0:T(8,128)(2,1)}, u32[]{:S(2)}) copy-start(bf16[256,256]{1,0:T(8,128)(2,1)} %key_w_ref.1) | copy-start | bytes 393220
  6.1 1.3 copy-start.4
  7.4 51.3 %collective-permute-start.1 = (bf16[64,64,256]{2,1,0:T(8,128)(2,1)S(1)}, bf16[64,64,256]{2,1,0:T(8,128)(2,1)}, u32[]{:S(2)}, u32[]{:S(2)}) collective-permute-start(bf16[64,64,256]{2,1,0:T(8,128)(2,1)S(1)} %bitcast.14), channel_id=1, source_target_pairs={{0,8},{1,9},{2,10},{3,11},{4,0},{5,1},{6,2},{7,3},{8,12},{9,13},{1... | collective-permute-start | bytes 6291464 | tf_op jit(solution)/shard_map/ppermute | solution.py:526
  7.4 57.8 %collective-permute-start = (bf16[64,64,256]{2,1,0:T(8,128)(2,1)S(1)}, bf16[64,64,256]{2,1,0:T(8,128)(2,1)}, u32[]{:S(2)}, u32[]{:S(2)}) collective-permute-start(bf16[64,64,256]{2,1,0:T(8,128)(2,1)S(1)} %bitcast.15), channel_id=1, source_target_pairs={{0,2},{1,3},{2,0},{3,1},{4,6},{5,7},{6,4},{7,5},{8,10},{9,11},{10,... | collective-permute-start | bytes 6291464 | tf_op jit(solution)/shard_map/ppermute | solution.py:526
  10.7 46.3 %all-to-all-start = ((s32[8,1,200]{2,1,0:T(1,128)}), s32[8,1,200]{2,1,0:T(1,128)S(1)}, u32[]{:S(2)}, u32[]{:S(2)}) async-start(s32[8,1,200]{2,1,0:T(1,128)} %broadcast_in_dim.108), calls=%async_computation | async-start | bytes 16384 | tf_op jit(solution)/shard_map/all_to_all | solution.py:541
  45.3 13.5 %copy-start.6 = (f32[64,8,256]{2,1,0:T(8,128)}, f32[64,8,256]{2,1,0:T(8,128)S(1)}, u32[]{:S(2)}) copy-start(f32[64,8,256]{2,1,0:T(8,128)S(1)} %get-tuple-element.20.rest_1_.stats_ref) | copy-start | bytes 1572868
  61.8 19.5 %collective-permute-start.5 = (bf16[25,64,256]{2,1,0:T(8,128)(2,1)}, bf16[25,64,256]{2,1,0:T(8,128)(2,1)}, u32[]{:S(2)}, u32[]{:S(2)}) collective-permute-start(bf16[25,64,256]{2,1,0:T(8,128)(2,1)} %get-tuple-element.22.rest_1_), channel_id=1, source_target_pairs={{0,2},{1,3},{2,0},{3,1},{4,6},{5,7},{6,4},{7,5},{8,10},{9,11},{10,... | collective-permute-start | bytes 2457608 | tf_op jit(solution)/shard_map/ppermute | solution.py:526
  62.6 21.5 %collective-permute-start.7 = (bf16[25,64,256]{2,1,0:T(8,128)(2,1)}, bf16[25,64,256]{2,1,0:T(8,128)(2,1)}, u32[]{:S(2)}, u32[]{:S(2)}) collective-permute-start(bf16[25,64,256]{2,1,0:T(8,128)(2,1)} %pick_blocks.6.rest_1_), channel_id=1, source_target_pairs={{0,4},{1,5},{2,6},{3,7},{4,12},{5,13},{6,14},{7,15},{8,0},{9,1},{1... | collective-permute-start | bytes 2457608 | tf_op jit(solution)/shard_map/ppermute | solution.py:526
  67.2 34.4 %collective-permute-start.2 = (bf16[25,64,256]{2,1,0:T(8,128)(2,1)S(1)}, bf16[25,64,256]{2,1,0:T(8,128)(2,1)S(1)}, u32[]{:S(2)}, u32[]{:S(2)}) collective-permute-start(bf16[25,64,256]{2,1,0:T(8,128)(2,1)S(1)} %pick_blocks.8), channel_id=1, source_target_pairs={{0,4},{1,5},{2,6},{3,7},{4,12},{5,13},{6,14},{7,15},{8,0},{9,1},{1... | collective-permute-start | bytes 2457608 | tf_op jit(solution)/shard_map/ppermute | solution.py:526
  83.2 25.7 %collective-permute-start.9 = (bf16[25,64,256]{2,1,0:T(8,128)(2,1)S(1)}, bf16[25,64,256]{2,1,0:T(8,128)(2,1)S(1)}, u32[]{:S(2)}, u32[]{:S(2)}) collective-permute-start(bf16[25,64,256]{2,1,0:T(8,128)(2,1)S(1)} %pick_blocks.11), channel_id=1, source_target_pairs={{0,2},{1,3},{2,0},{3,1},{4,6},{5,7},{6,4},{7,5},{8,10},{9,11},{10,... | collective-permute-start | bytes 2457608 | tf_op jit(solution)/shard_map/ppermute | solution.py:526
  85.1 42.3 %collective-permute-start.8 = (bf16[25,64,256]{2,1,0:T(8,128)(2,1)S(1)}, bf16[25,64,256]{2,1,0:T(8,128)(2,1)S(1)}, u32[]{:S(2)}, u32[]{:S(2)}) collective-permute-start(bf16[25,64,256]{2,1,0:T(8,128)(2,1)S(1)} %pick_blocks.10), channel_id=1, source_target_pairs={{4,8},{5,9},{6,10},{7,11},{8,4},{9,5},{10,6},{11,7},{20,24},{21,25... | collective-permute-start | bytes 2457608 | tf_op jit(solution)/shard_map/ppermute | solution.py:526
  88.9 38.5 %collective-permute-start.4 = (bf16[25,64,256]{2,1,0:T(8,128)(2,1)S(1)}, bf16[25,64,256]{2,1,0:T(8,128)(2,1)S(1)}, u32[]{:S(2)}, u32[]{:S(2)}) collective-permute-start(bf16[25,64,256]{2,1,0:T(8,128)(2,1)S(1)} %get-tuple-element.23), channel_id=1, source_target_pairs={{8,12},{9,13},{10,14},{11,15},{4,0},{5,1},{6,2},{7,3},{24,28},{25,... | collective-permute-start | bytes 2457608 | tf_op jit(solution)/shard_map/ppermute | solution.py:526
  95.4 13.5 %copy-start.1 = (bf16[256,256]{1,0:T(8,128)(2,1)S(1)}, bf16[256,256]{1,0:T(8,128)(2,1)}, u32[]{:S(2)}) copy-start(bf16[256,256]{1,0:T(8,128)(2,1)} %rest_1_.5) | copy-start | bytes 393220
  95.4 13.5 %copy-start.2 = (bf16[256,256]{1,0:T(8,128)(2,1)S(1)}, bf16[256,256]{1,0:T(8,128)(2,1)}, u32[]{:S(2)}) copy-start(bf16[256,256]{1,0:T(8,128)(2,1)} %rest_2_.5) | copy-start | bytes 393220
  95.4 13.5 %copy-start.5 = (bf16[4096,256]{1,0:T(8,128)(2,1)S(1)}, bf16[4096,256]{1,0:T(8,128)(2,1)}, u32[]{:S(2)}) copy-start(bf16[4096,256]{1,0:T(8,128)(2,1)} %copy-done.4) | copy-start | bytes 6291460
  95.4 13.5 %copy-start.7 = (f32[64,8,256]{2,1,0:T(8,128)S(1)}, f32[64,8,256]{2,1,0:T(8,128)}, u32[]{:S(2)}) copy-start(f32[64,8,256]{2,1,0:T(8,128)} %copy-done.6) | copy-start | bytes 1572868
  103.4 44.5 %collective-permute-start.3 = (bf16[25,64,256]{2,1,0:T(8,128)(2,1)S(1)}, bf16[25,64,256]{2,1,0:T(8,128)(2,1)S(1)}, u32[]{:S(2)}, u32[]{:S(2)}) collective-permute-start(bf16[25,64,256]{2,1,0:T(8,128)(2,1)S(1)} %pick_blocks.9), channel_id=1, source_target_pairs={{4,8},{5,9},{6,10},{7,11},{8,4},{9,5},{10,6},{11,7},{20,24},{21,25... | collective-permute-start | bytes 2457608 | tf_op jit(solution)/shard_map/ppermute | solution.py:526
  106.2 28.2 %collective-permute-start.6 = (bf16[25,64,256]{2,1,0:T(8,128)(2,1)}, bf16[25,64,256]{2,1,0:T(8,128)(2,1)S(1)}, u32[]{:S(2)}, u32[]{:S(2)}) collective-permute-start(bf16[25,64,256]{2,1,0:T(8,128)(2,1)} %collective-permute-done.5.rest_1_), channel_id=1, source_target_pairs={{8,12},{9,13},{10,14},{11,15},{4,0},{5,1},{6,2},{7,3},{24,28},{25,... | collective-permute-start | bytes 2457608 | tf_op jit(solution)/shard_map/ppermute | solution.py:526

commit v16 on v15

--- a/solution.py
+++ b/solution.py
@@ -12,7 +12,8 @@
 SPAN = 8
 SUB = 8
 GROUP = 4
-STEP = 4
+STEP = 8
+OWN_STEP = 4
 SCORES_AHEAD, WEIGHTS_AHEAD = 2, 1
 VMEM_BYTES = 48 * 1024 * 1024
 
@@ -81,39 +82,41 @@
     return result
 
 
-def pick_kernel(position_ref, wanted_ref, *rest, plan, capacity):
+def pick_kernel(position_ref, wanted_ref, blocks_ref, *rest, plan, capacity):
+    sems = rest[-1]
     position = position_ref[0]
-    for out_ref, pieces in zip(rest[len(rest) - len(plan) :], plan, strict=True):
-        for at, (blocks, reader_of, owner_of) in enumerate(pieces):
+
+    def copies():
+        for n, (reader_of, owner_of) in enumerate(plan):
             reader, first = reader_of(position), owner_of(position) * capacity
-
-            def one_slot(slot, carry, out_ref=out_ref, at=at, blocks=blocks, reader=reader, first=first):
-                out_ref[at * capacity + slot] = rest[blocks][wanted_ref[reader, first + slot]]
-                return carry
-
-            lax.fori_loop(0, capacity, one_slot, 0)
-
-
-def pick(position, wanted, sources, plan, after=()):
+            for slot in range(capacity):
+                block = wanted_ref[reader, first + slot]
+                out_ref = rest[len(rest) - 1 - len(plan) + n]
+                yield pltpu.make_async_copy(
+                    blocks_ref.at[block], out_ref.at[slot], sems.at[n, slot]
+                )
+
+    for copy in copies():
+        copy.start()
+    for copy in copies():
+        copy.wait()
+
+
+def pick(position, wanted, blocks, plan, after=()):
     capacity = wanted.shape[1] // SPAN
-    block = sources[0].shape[1:]
-    outs = [
-        jax.ShapeDtypeStruct((len(pieces) * capacity,) + block, sources[0].dtype)
-        for pieces in plan
-    ]
+    outs = [jax.ShapeDtypeStruct((capacity,) + blocks.shape[1:], blocks.dtype)] * len(plan)
     smem = pl.BlockSpec(memory_space=pltpu.SMEM)
-    vmem = pl.BlockSpec(memory_space=pltpu.VMEM)
+    hbm = pl.BlockSpec(memory_space=pl.ANY)
     return pl.pallas_call(
         functools.partial(pick_kernel, plan=plan, capacity=capacity),
-        in_specs=[smem, smem]
-        + [vmem] * len(sources)
-        + [pl.BlockSpec(memory_space=pl.ANY)] * len(after),
-        out_specs=[vmem] * len(outs),
+        in_specs=[smem, smem, hbm] + [hbm] * len(after),
+        out_specs=[pl.BlockSpec(memory_space=pltpu.VMEM)] * len(outs),
         out_shape=outs,
+        scratch_shapes=[pltpu.SemaphoreType.DMA((len(plan), capacity))],
         cost_estimate=lasting(1.5),
         compiler_params=kernel_params(),
         name="pick_blocks",
-    )(position, wanted, *sources, *after)
+    )(position, wanted, blocks, *after)
 
 
 def tiles_of(query, first, span):
@@ -177,15 +180,15 @@
     tile = GROUP * cluster
     tiles = HEADS // GROUP
     whole = pl.BlockSpec((width, width), lambda i: (0, 0))
-    square = pl.BlockSpec((STEP, width, tile), lambda i: (i, 0, 0))
+    square = pl.BlockSpec((OWN_STEP, width, tile), lambda i: (i, 0, 0))
     return pl.pallas_call(
         functools.partial(own_kernel, head_width=width // HEADS),
-        grid=(blocks // STEP,),
-        in_specs=[pl.BlockSpec((STEP * cluster, width), lambda i: (i, 0)), whole, whole, whole],
+        grid=(blocks // OWN_STEP,),
+        in_specs=[pl.BlockSpec((OWN_STEP * cluster, width), lambda i: (i, 0)), whole, whole, whole],
         out_specs=[
             square,
             square,
-            pl.BlockSpec((STEP, 2 * tiles, tile), lambda i: (i, 0, 0)),
+            pl.BlockSpec((OWN_STEP, 2 * tiles, tile), lambda i: (i, 0, 0)),
         ],
         out_shape=[
             jax.ShapeDtypeStruct((blocks, width, tile), jnp.bfloat16),
@@ -200,18 +203,18 @@
 
 def collect_kernel(*refs, places):
     buffer_ref, sems = refs[-2:]
-    copy_pieces(refs[: len(places)], buffer_ref, places, sems)
-
-
-def copy_pieces(piece_refs, buffer_ref, places, sems):
-    copies = [
-        pltpu.make_async_copy(piece, buffer_ref.at[pl.ds(at, piece.shape[0])], sems.at[n])
-        for n, (piece, at) in enumerate(zip(piece_refs, places, strict=True))
-    ]
+    copies = copy_pieces(refs[: len(places)], buffer_ref, places, sems)
     for copy in copies:
         copy.start()
     for copy in copies:
         copy.wait()
+
+
+def copy_pieces(piece_refs, buffer_ref, places, sems):
+    return [
+        pltpu.make_async_copy(piece, buffer_ref.at[pl.ds(at, piece.shape[0])], sems.at[n])
+        for n, (piece, at) in enumerate(zip(piece_refs, places, strict=True))
+    ]
 
 
 def collect(pieces, places, total):
@@ -245,21 +248,26 @@
     attended_buf, before_buf, done_buf, in_sems, out_sems, piece_sems = rest[-6:]
     begin, count = range_ref[0], range_ref[1]
     pair_count = member_buf.shape[2]
-    copy_pieces(piece_refs, buffer_ref, places, piece_sems)
-
-    def fetches(step, slot):
+    copies = copy_pieces(piece_refs, buffer_ref, places, piece_sems)
+    for copy in copies:
+        copy.start()
+
+    def fetches(step, slot, known=True, listed=True):
         for j in range(STEP):
             block = order_ref[step * STEP + j]
-            sources = [(query_ref.at[block], query_buf.at[slot, j])]
-            sources.append((own_ref.at[block], own_buf.at[slot, j]))
-            sources.append((stats_ref.at[block], stats_buf.at[slot, j]))
-            sources.append((placed_ref.at[block], placed_buf.at[slot, j]))
+            sources = [
+                (query_ref.at[block], query_buf.at[slot, j]),
+                (own_ref.at[block], own_buf.at[slot, j]),
+                (stats_ref.at[block], stats_buf.at[slot, j]),
+                (placed_ref.at[block], placed_buf.at[slot, j]),
+            ]
             for n in range(pair_count):
-                listed = table_ref[block * pair_count + n]
-                sources.append((buffer_ref.at[listed], member_buf.at[slot, j, n]))
+                member = table_ref[block * pair_count + n]
+                sources.append((buffer_ref.at[member], member_buf.at[slot, j, n]))
             for n, (source_, target) in enumerate(sources):
-                sem = in_sems.at[slot, j * (pair_count + 4) + n]
-                yield pltpu.make_async_copy(source_, target, sem)
+                if listed if n >= 4 else known:
+                    sem = in_sems.at[slot, j * (pair_count + 4) + n]
+                    yield pltpu.make_async_copy(source_, target, sem)
 
     def stores(step):
         for j in range(STEP):
@@ -303,7 +311,15 @@
 
     @pl.when(count > 0)
     def _():
-        for copy in fetches(begin, 0):
+        for copy in fetches(begin, 0, listed=False):
+            copy.start()
+
+    for copy in copies:
+        copy.wait()
+
+    @pl.when(count > 0)
+    def _():
+        for copy in fetches(begin, 0, known=False):
             copy.start()
         attended_buf[...] = jnp.zeros_like(attended_buf)
         before_buf[...] = jnp.zeros_like(before_buf)
@@ -503,12 +519,12 @@
     return lambda position: partner(route(position))
 
 
-SECOND_PLAN = (((0, source, itself),),)
-SECOND_CROSS_PLAN = (((0, source, partner),),)
-MIDDLE_PLAN = (((0, opposite, itself),),)
-MIDDLE_CROSS_PLAN = (((0, opposite, partner),),)
-ON_PLAN = (((0, crossed(onward), source),), ((0, onward, source),))
-NEAR_PLAN = (((0, partner, source),),)
+SECOND_PLAN = ((source, itself),)
+MIDDLE_PLAN = ((opposite, itself),)
+SECOND_CROSS_PLAN = ((source, partner),)
+MIDDLE_CROSS_PLAN = ((opposite, partner),)
+ON_PLAN = ((crossed(onward), source), (onward, source))
+NEAR_PLAN = ((partner, source),)
 
 
 def body(features, assignment, pairs, w_query, w_key, w_value, w_out, w_mix):
@@ -559,20 +575,20 @@
 
     beside = moved(blocks, swap)
     passed = moved(blocks, first_moves)
-    (second_pick,) = pick(at_position, wanted, (blocks,), SECOND_PLAN, after=own[2:])
+    (second_pick,) = pick(at_position, wanted, blocks, SECOND_PLAN, after=own[2:])
     second = moved(second_pick, second_moves)
-    on, outward = pick(at_position, wanted, (passed,), ON_PLAN, after=(second_pick,))
-    (second_cross,) = pick(at_position, wanted, (beside,), SECOND_CROSS_PLAN, after=(on,))
+    on, outward = pick(at_position, wanted, passed, ON_PLAN, after=(second_pick,))
+    (second_cross,) = pick(at_position, wanted, beside, SECOND_CROSS_PLAN, after=(on,))
     second_cross = moved(second_cross, second_moves)
     on = moved(on, swap)
     outward = moved(outward, outward_moves)
-    (middle,) = pick(at_position, wanted, (blocks,), MIDDLE_PLAN, after=(second,))
+    (middle,) = pick(at_position, wanted, blocks, MIDDLE_PLAN, after=(second,))
     middle = moved(middle, middle_moves)
-    (near,) = pick(at_position, wanted, (passed,), NEAR_PLAN, after=(on,))
+    (near,) = pick(at_position, wanted, passed, NEAR_PLAN, after=(on,))
     near = moved(near, swap)
     on = moved(on, outward_moves)
     (middle_cross,) = pick(
-        at_position, wanted, (beside,), MIDDLE_CROSS_PLAN, after=(second_cross,)
+        at_position, wanted, beside, MIDDLE_CROSS_PLAN, after=(second_cross,)
     )
     middle_cross = moved(middle_cross, middle_moves)
 
@@ -596,15 +612,15 @@
     whole = (z_owner == z) | (from_first & same)
     table = jnp.where(whole, whole_at + within, piece_of * capacity + ranking)
 
-    arrival = jnp.where(late, jnp.where(same | is_end, 1, 2), 0)
+    arrival = jnp.where(late & ~is_end, jnp.where(same, 1, 2), 0)
     order, ends = by_class(jnp.max(arrival.reshape(block_count, pair_count), axis=1), 2)
     marks = [0, ends[0] // STEP, ends[1] // STEP, block_count // STEP]
     phases = [(marks[n], marks[n + 1] - marks[n]) for n in range(3)]
     weights = (jnp.concatenate([w_key, w_value], axis=1), w_out, w_mix)
     shared = (order, table, own, placed.reshape(blocks.shape), weights)
     arrivals = (
-        ((near, 0), (second, 1), (second_cross, 2)),
-        ((outward, 3), (on, 4), (middle, 5)),
+        ((near, 0), (second, 1), (second_cross, 2), (outward, 3), (on, 4)),
+        ((middle, 5),),
         ((middle_cross, 6),),
     )
     mixed = None

time: 168 us -> 181 us (1.077); the launches traced: 165 us -> 180 us
  waiting for transfers between devices: 32.7 us -> 47.6 us
  Pallas kernels: 99.5 us -> 96.8 us
    ppermute x10, waiting for transfers between devices: 26.5 us -> 41.9 us  [moved(): return lax.ppermute(x, 'elec', pairs_of)]
    pallas_call x3, Pallas kernels: 49.3 us -> 43.2 us  [attend(): pl.pallas_call(kernel, in_specs=in_specs, out_specs=[hbm, hbm], out_shape...]
    pallas_call x6, Pallas kernels: 11.4 us -> 14.8 us  [pick(): pl.pallas_call(functools.partial(pick_kernel, plan=plan, capacity=capacit...]
  transfers between devices with their start and end apart: 11 -> 11, of which waited for: 5 -> 5; matrix products, arithmetic and copies ran while one was open for 2% -> 1% of each run, Pallas kernels for 47% -> 42%
where the time goes in v16:
time: 181 us; the launch traced here: 180 us
  Pallas kernels  96.8 us (53%)
  waiting for transfers between devices  47.6 us (26%)
  starting transfers between devices  24.6 us (14%)
  between operations  5.73 us (3%)
  local copies, waits for them, and re-layouts  4.09 us (2%)
    pallas_call x3, Pallas kernels, attend(): pl.pallas_call(kernel, in_specs=in_specs, out_specs=[hbm, hbm], out_shape...  43.2 us
    ppermute x10, waiting for transfers between devices, moved(): return lax.ppermute(x, 'elec', pairs_of)  41.9 us
    pallas_call x1, Pallas kernels, own_part(): pl.pallas_call(functools.partial(own_kernel, head_width=width // HEADS),...  28.6 us
    ppermute x10, starting transfers between devices, moved(): return lax.ppermute(x, 'elec', pairs_of)  18.7 us
    pallas_call x6, Pallas kernels, pick(): pl.pallas_call(functools.partial(pick_kernel, plan=plan, capacity=capacit...  14.8 us
    all_to_all x1, starting transfers between devices, body(): lax.all_to_all(jnp.broadcast_to(tables[None], (SPAN, SPAN * capacity)), '...  5.83 us
    all_to_all x1, waiting for transfers between devices, body(): lax.all_to_all(jnp.broadcast_to(tables[None], (SPAN, SPAN * capacity)), '...  5.63 us
    pallas_call x1, Pallas kernels, place(): pl.pallas_call(place_kernel, grid=(walkers // 2,), in_specs=[local, pl.Bl...  5.39 us
  transfers between devices with their start and end apart: 11, of which 5 were waited for; matrix products, arithmetic and copies ran while one was open for 1% of the time, Pallas kernels for 42%

profile of v16, /device:TPU:8, one launch (start us, length us, event | category | flops | bytes accessed | tf_op | source)
XLA Modules:
  0.0 180.5 jit_solution(1626999417031655904)
XLA Ops:
  0.0 0.7 copy-done.5
  0.7 5.4 %place_rows.1 = (bf16[4096,256]{1,0:T(8,128)(2,1)S(1)}, bf16[4096,256]{1,0:T(8,128)(2,1)S(1)}) custom-call(bf16[4096,256]{1,0:T(8,128)(2,1)} %features_ref.1, s32[8,1,512]{2,1,0:T(1,128)S(1)} %bitcast.27), custom_call_target="tpu_custom_call" | custom-call | flops 6899999744 | tf_op jit(solution)/shard_map/place_rows/pallas_call | solution.py:66
  6.1 1.3 copy-done.6
  7.5 2.0 %collective-permute-start = (bf16[64,64,256]{2,1,0:T(8,128)(2,1)S(1)}, bf16[64,64,256]{2,1,0:T(8,128)(2,1)}, u32[]{:S(2)}, u32[]{:S(2)}) collective-permute-start(bf16[64,64,256]{2,1,0:T(8,128)(2,1)S(1)} %bitcast.15), channel_id=1, source_target_pairs={{0,2},{1,3},{2,0},{3,1},{4,6},{5,7},{6,4},{7,5},{8,10},{9,11},{10,... | collective-permute-start | bytes 6291464 | tf_op jit(solution)/shard_map/ppermute | solution.py:542
  10.1 0.6 broadcast_in_dim.108
  10.7 5.8 %all-to-all-start = ((s32[8,1,200]{2,1,0:T(1,128)}), s32[8,1,200]{2,1,0:T(1,128)S(1)}, u32[]{:S(2)}, u32[]{:S(2)}) async-start(s32[8,1,200]{2,1,0:T(1,128)} %broadcast_in_dim.108), calls=%async_computation | async-start | bytes 16384 | tf_op jit(solution)/shard_map/all_to_all | solution.py:557
  16.8 28.6 %own_blocks.1 = (bf16[64,256,256]{2,1,0:T(8,128)(2,1)}, bf16[64,256,256]{2,1,0:T(8,128)(2,1)}, f32[64,8,256]{2,1,0:T(8,128)S(1)}) custom-call(bf16[4096,256]{1,0:T(8,128)(2,1)S(1)} %get-tuple-element.17.normed_ref, bf16[256,256]{1,0:T(8,128)(2,1)S(1)} %bitcast.19, bf16[256,256]{1,0:T(8,128)(2,1)S(1)} %copy-done, bf16[256,256]{1,0:T(8,128)(2,1)S(1)} %bitcast.20), custom_call_target="tpu_custom_call" | custom-call | flops 23000000512 | tf_op jit(solution)/shard_map/own_blocks/pallas_call | solution.py:184
  45.4 0.7 fusion.14
  51.3 5.6 %all-to-all-done = s32[8,1,200]{2,1,0:T(1,128)S(1)} async-done(((s32[8,1,200]{2,1,0:T(1,128)}), s32[8,1,200]{2,1,0:T(1,128)S(1)}, u32[]{:S(2)}, u32[]{:S(2)}) %all-to-all-start) | async-done | bytes 6432 | tf_op jit(solution)/shard_map/all_to_all | solution.py:557
  57.0 3.0 %pick_blocks.6.rest_0_ = bf16[25,64,256]{2,1,0:T(8,128)(2,1)} custom-call(s32[1]{0:T(128)} %bitcast.6.position_ref, s32[8,200]{1,0:T(8,128)S(1)} %bitcast.21, bf16[64,64,256]{2,1,0:T(8,128)(2,1)S(1)} %bitcast.16, f32[64,8,256]{2,1,0:T(8,128)S(1)} %get-tuple-element.20.rest_0_.stats_ref), custom_call_target="tpu_custom_call" | custom-call | flops 1724999936 | tf_op jit(solution)/shard_map/pick_blocks/pallas_call | solution.py:110
  60.0 3.4 %pick_blocks.7 = (bf16[25,64,256]{2,1,0:T(8,128)(2,1)}, bf16[25,64,256]{2,1,0:T(8,128)(2,1)S(1)}) custom-call(s32[1]{0:T(128)} %bitcast.6.position_ref, s32[8,200]{1,0:T(8,128)S(1)} %bitcast.22, bf16[64,64,256]{2,1,0:T(8,128)(2,1)} %collective-permute-done.1.blocks_ref.refs_1_, bf16[25,64,256]{2,1,0:T(8,128)(2,1)} %pick_blocks.6.rest_0_), custom_call_target="tpu_custom_call" | custom-call | flops 1724999936 | tf_op jit(solution)/shard_map/pick_blocks/pallas_call | solution.py:110
  63.5 0.9 copy-done.1
  64.4 0.6 collective-permute-start.6
  65.3 2.4 %collective-permute-start.4 = (bf16[25,64,256]{2,1,0:T(8,128)(2,1)}, bf16[25,64,256]{2,1,0:T(8,128)(2,1)S(1)}, u32[]{:S(2)}, u32[]{:S(2)}) collective-permute-start(bf16[25,64,256]{2,1,0:T(8,128)(2,1)} %pick_blocks.6.rest_0_), channel_id=1, source_target_pairs={{0,4},{1,5},{2,6},{3,7},{4,12},{5,13},{6,14},{7,15},{8,0},{9,1},{1... | collective-permute-start | bytes 2457608 | tf_op jit(solution)/shard_map/ppermute | solution.py:542
  67.9 2.0 %pick_blocks.8 = bf16[25,64,256]{2,1,0:T(8,128)(2,1)S(1)} custom-call(s32[1]{0:T(128)} %bitcast.6.position_ref, s32[8,200]{1,0:T(8,128)S(1)} %bitcast.23, bf16[64,64,256]{2,1,0:T(8,128)(2,1)} %collective-permute-done.blocks_ref.refs_2_, bf16[25,64,256]{2,1,0:T(8,128)(2,1)} %get-tuple-element.22.rest_0_), custom_call_target="tpu_custom_call" | custom-call | flops 1724999936 | tf_op jit(solution)/shard_map/pick_blocks/pallas_call | solution.py:110
  69.9 1.1 collective-permute-start.2
  71.0 3.0 %collective-permute-start.8 = (bf16[25,64,256]{2,1,0:T(8,128)(2,1)S(1)}, bf16[25,64,256]{2,1,0:T(8,128)(2,1)S(1)}, u32[]{:S(2)}, u32[]{:S(2)}) collective-permute-start(bf16[25,64,256]{2,1,0:T(8,128)(2,1)S(1)} %copy-done.2), channel_id=1, source_target_pairs={{8,12},{9,13},{10,14},{11,15},{4,0},{5,1},{6,2},{7,3},{24,28},{25,... | collective-permute-start | bytes 2457608 | tf_op jit(solution)/shard_map/ppermute | solution.py:542
  74.0 9.9 %collective-permute-done.6.rest_0_ = bf16[25,64,256]{2,1,0:T(8,128)(2,1)} collective-permute-done((bf16[25,64,256]{2,1,0:T(8,128)(2,1)}, bf16[25,64,256]{2,1,0:T(8,128)(2,1)}, u32[]{:S(2)}, u32[]{:S(2)}) %collective-permute-start.6) | collective-permute-done | bytes 819232 | tf_op jit(solution)/shard_map/ppermute | solution.py:542
  83.9 2.0 %pick_blocks.11 = bf16[25,64,256]{2,1,0:T(8,128)(2,1)S(1)} custom-call(s32[1]{0:T(128)} %bitcast.6.position_ref, s32[8,200]{1,0:T(8,128)S(1)} %bitcast.24, bf16[64,64,256]{2,1,0:T(8,128)(2,1)} %collective-permute-done.1.blocks_ref.refs_1_, bf16[25,64,256]{2,1,0:T(8,128)(2,1)} %collective-permute-done.6.rest_0_), custom_call_target="tpu_custom_call" | custom-call | flops 1724999936 | tf_op jit(solution)/shard_map/pick_blocks/pallas_call | solution.py:110
  85.9 0.7 collective-permute-start.7
  86.6 3.3 %collective-permute-start.9 = (bf16[25,64,256]{2,1,0:T(8,128)(2,1)}, bf16[25,64,256]{2,1,0:T(8,128)(2,1)S(1)}, u32[]{:S(2)}, u32[]{:S(2)}) collective-permute-start(bf16[25,64,256]{2,1,0:T(8,128)(2,1)} %collective-permute-done.6.rest_0_), channel_id=1, source_target_pairs={{8,12},{9,13},{10,14},{11,15},{4,0},{5,1},{6,2},{7,3},{24,28},{25,... | collective-permute-start | bytes 2457608 | tf_op jit(solution)/shard_map/ppermute | solution.py:542
  90.1 2.1 %pick_blocks.10 = bf16[25,64,256]{2,1,0:T(8,128)(2,1)S(1)} custom-call(s32[1]{0:T(128)} %bitcast.6.position_ref, s32[8,200]{1,0:T(8,128)S(1)} %bitcast.25, bf16[64,64,256]{2,1,0:T(8,128)(2,1)S(1)} %bitcast.17, bf16[25,64,256]{2,1,0:T(8,128)(2,1)S(1)} %collective-permute-done.4.rest_0_.rest_4_), custom_call_target="tpu_custom_call" | custom-call | flops 1724999936 | tf_op jit(solution)/shard_map/pick_blocks/pallas_call | solution.py:110
  92.2 2.9 %collective-permute-start.5 = (bf16[25,64,256]{2,1,0:T(8,128)(2,1)S(1)}, bf16[25,64,256]{2,1,0:T(8,128)(2,1)S(1)}, u32[]{:S(2)}, u32[]{:S(2)}) collective-permute-start(bf16[25,64,256]{2,1,0:T(8,128)(2,1)S(1)} %pick_blocks.10), channel_id=1, source_target_pairs={{4,8},{5,9},{6,10},{7,11},{8,4},{9,5},{10,6},{11,7},{20,24},{21,25... | collective-permute-start | bytes 2457608 | tf_op jit(solution)/shard_map/ppermute | solution.py:542
  95.2 4.9 %collect_blocks.1.rest_8_ = bf16[367,64,256]{2,1,0:T(8,128)(2,1)} custom-call(bf16[64,64,256]{2,1,0:T(8,128)(2,1)S(1)} %bitcast.18, bf16[64,64,256]{2,1,0:T(8,128)(2,1)} %collective-permute-done.1.blocks_ref.refs_1_, bf16[64,64,256]{2,1,0:T(8,128)(2,1)} %collective-permute-done.blocks_ref.refs_2_), custom_call_target="tpu_custom_call" | custom-call | flops 4600000000 | tf_op jit(solution)/shard_map/collect_blocks/pallas_call | solution.py:221
  100.1 4.1 %collective-permute-done.2.rest_0_.rest_5_ = bf16[25,64,256]{2,1,0:T(8,128)(2,1)S(1)} collective-permute-done((bf16[25,64,256]{2,1,0:T(8,128)(2,1)S(1)}, bf16[25,64,256]{2,1,0:T(8,128)(2,1)S(1)}, u32[]{:S(2)}, u32[]{:S(2)}) %collective-permute-start.2) | collective-permute-done | bytes 819232 | tf_op jit(solution)/shard_map/ppermute | solution.py:542
  104.2 2.1 %pick_blocks.9 = bf16[25,64,256]{2,1,0:T(8,128)(2,1)S(1)} custom-call(s32[1]{0:T(128)} %bitcast.6.position_ref, s32[8,200]{1,0:T(8,128)S(1)} %bitcast.26, bf16[64,64,256]{2,1,0:T(8,128)(2,1)} %collective-permute-done.blocks_ref.refs_2_, bf16[25,64,256]{2,1,0:T(8,128)(2,1)S(1)} %collective-permute-done.2.rest_0_.rest_5_), custom_call_target="tpu_custom_call" | custom-call | flops 1724999936 | tf_op jit(solution)/shard_map/pick_blocks/pallas_call | solution.py:110
  106.3 2.7 %collective-permute-start.3 = (bf16[25,64,256]{2,1,0:T(8,128)(2,1)S(1)}, bf16[25,64,256]{2,1,0:T(8,128)(2,1)S(1)}, u32[]{:S(2)}, u32[]{:S(2)}) collective-permute-start(bf16[25,64,256]{2,1,0:T(8,128)(2,1)S(1)} %pick_blocks.9), channel_id=1, source_target_pairs={{4,8},{5,9},{6,10},{7,11},{8,4},{9,5},{10,6},{11,7},{20,24},{21,25... | collective-permute-start | bytes 2457608 | tf_op jit(solution)/shard_map/ppermute | solution.py:542
  109.1 10.4 %collective-permute-done.8.rest_6_ = bf16[25,64,256]{2,1,0:T(8,128)(2,1)S(1)} collective-permute-done((bf16[25,64,256]{2,1,0:T(8,128)(2,1)S(1)}, bf16[25,64,256]{2,1,0:T(8,128)(2,1)S(1)}, u32[]{:S(2)}, u32[]{:S(2)}) %collective-permute-start.8) | collective-permute-done | bytes 819232 | tf_op jit(solution)/shard_map/ppermute | solution.py:542
  119.4 17.6 %collective-permute-done.9.rest_7_ = bf16[25,64,256]{2,1,0:T(8,128)(2,1)S(1)} collective-permute-done((bf16[25,64,256]{2,1,0:T(8,128)(2,1)}, bf16[25,64,256]{2,1,0:T(8,128)(2,1)S(1)}, u32[]{:S(2)}, u32[]{:S(2)}) %collective-permute-start.9) | collective-permute-done | bytes 819232 | tf_op jit(solution)/shard_map/ppermute | solution.py:542
  137.0 12.6 %attend_blocks.3 = (bf16[64,64,256]{2,1,0:T(8,128)(2,1)}, bf16[367,64,256]{2,1,0:T(8,128)(2,1)}) custom-call(s32[2]{0:T(128)S(1)} %pad_add_fusion.2.range_ref, s32[64]{0:T(128)S(1)} %select_reduce_fusion.2.order_ref, s32[192]{0:T(256)S(1)} %get-tuple-element.32.table_ref, ...), custom_call_target="tpu_custom_call", output_to_operand_aliasing={{1}: (15, {})} | custom-call | flops 20700000256 | tf_op jit(solution)/shard_map/attend_blocks/pallas_call | solution.py:442
  149.7 15.3 %attend_blocks.4 = (bf16[64,64,256]{2,1,0:T(8,128)(2,1)}, bf16[367,64,256]{2,1,0:T(8,128)(2,1)}) custom-call(s32[2]{0:T(128)S(1)} %pad_add_fusion.1.range_ref, s32[64]{0:T(128)S(1)} %select_reduce_fusion.2.order_ref, s32[192]{0:T(256)S(1)} %get-tuple-element.32.table_ref, ...), custom_call_target="tpu_custom_call", output_to_operand_aliasing={{1}: (11, {}), {0}: (12, {})} | custom-call | flops 20700000256 | tf_op jit(solution)/shard_map/attend_blocks/pallas_call | solution.py:442
  165.0 15.3 %attend_blocks.5 = (bf16[64,64,256]{2,1,0:T(8,128)(2,1)}, bf16[367,64,256]{2,1,0:T(8,128)(2,1)}) custom-call(s32[2]{0:T(128)S(1)} %pad_add_fusion.range_ref, s32[64]{0:T(128)S(1)} %select_reduce_fusion.2.order_ref, s32[192]{0:T(256)S(1)} %get-tuple-element.32.table_ref, ...), custom_call_target="tpu_custom_call", output_to_operand_aliasing={{1}: (11, {}), {0}: (12, {})} | custom-call | flops 20700000256 | tf_op jit(solution)/shard_map/attend_blocks/pallas_call | solution.py:442
  (47 shorter events, 1.4 us)
Async XLA Ops:
  0.0 0.7 copy-start.5
  0.7 8.7 %copy-start.12 = (s32[64,3]{0,1:T(4,128)S(1)}, s32[64,3]{0,1:T(4,128)}, u32[]{:S(2)}) copy-start(s32[64,3]{0,1:T(4,128)} %param.10) | copy-start | bytes 2308
  0.7 15.8 %copy-start.11 = (bf16[256,256]{1,0:T(8,128)(2,1)S(1)}, bf16[256,256]{1,0:T(8,128)(2,1)}, u32[]{:S(2)}) copy-start(bf16[256,256]{1,0:T(8,128)(2,1)} %param.11) | copy-start | bytes 393220
  0.7 15.9 %copy-start.10 = (bf16[256,256]{1,0:T(8,128)(2,1)S(1)}, bf16[256,256]{1,0:T(8,128)(2,1)}, u32[]{:S(2)}) copy-start(bf16[256,256]{1,0:T(8,128)(2,1)} %param.13) | copy-start | bytes 393220
  0.7 16.0 %copy-start = (bf16[256,256]{1,0:T(8,128)(2,1)S(1)}, bf16[256,256]{1,0:T(8,128)(2,1)}, u32[]{:S(2)}) copy-start(bf16[256,256]{1,0:T(8,128)(2,1)} %key_w_ref.1) | copy-start | bytes 393220
  6.1 1.4 copy-start.6
  7.5 52.5 %collective-permute-start.1 = (bf16[64,64,256]{2,1,0:T(8,128)(2,1)S(1)}, bf16[64,64,256]{2,1,0:T(8,128)(2,1)}, u32[]{:S(2)}, u32[]{:S(2)}) collective-permute-start(bf16[64,64,256]{2,1,0:T(8,128)(2,1)S(1)} %bitcast.14), channel_id=1, source_target_pairs={{0,8},{1,9},{2,10},{3,11},{4,0},{5,1},{6,2},{7,3},{8,12},{9,13},{1... | collective-permute-start | bytes 6291464 | tf_op jit(solution)/shard_map/ppermute | solution.py:542
  7.5 60.4 %collective-permute-start = (bf16[64,64,256]{2,1,0:T(8,128)(2,1)S(1)}, bf16[64,64,256]{2,1,0:T(8,128)(2,1)}, u32[]{:S(2)}, u32[]{:S(2)}) collective-permute-start(bf16[64,64,256]{2,1,0:T(8,128)(2,1)S(1)} %bitcast.15), channel_id=1, source_target_pairs={{0,2},{1,3},{2,0},{3,1},{4,6},{5,7},{6,4},{7,5},{8,10},{9,11},{10,... | collective-permute-start | bytes 6291464 | tf_op jit(solution)/shard_map/ppermute | solution.py:542
  10.7 46.3 %all-to-all-start = ((s32[8,1,200]{2,1,0:T(1,128)}), s32[8,1,200]{2,1,0:T(1,128)S(1)}, u32[]{:S(2)}, u32[]{:S(2)}) async-start(s32[8,1,200]{2,1,0:T(1,128)} %broadcast_in_dim.108), calls=%async_computation | async-start | bytes 16384 | tf_op jit(solution)/shard_map/all_to_all | solution.py:557
  45.3 14.7 %copy-start.8 = (f32[64,8,256]{2,1,0:T(8,128)}, f32[64,8,256]{2,1,0:T(8,128)S(1)}, u32[]{:S(2)}) copy-start(f32[64,8,256]{2,1,0:T(8,128)S(1)} %get-tuple-element.20.rest_0_.stats_ref) | copy-start | bytes 1572868
  63.5 0.9 copy-start.1
  64.4 19.5 %collective-permute-start.6 = (bf16[25,64,256]{2,1,0:T(8,128)(2,1)}, bf16[25,64,256]{2,1,0:T(8,128)(2,1)}, u32[]{:S(2)}, u32[]{:S(2)}) collective-permute-start(bf16[25,64,256]{2,1,0:T(8,128)(2,1)} %get-tuple-element.22.rest_0_), channel_id=1, source_target_pairs={{0,2},{1,3},{2,0},{3,1},{4,6},{5,7},{6,4},{7,5},{8,10},{9,11},{10,... | collective-permute-start | bytes 2457608 | tf_op jit(solution)/shard_map/ppermute | solution.py:542
  65.3 24.8 %collective-permute-start.4 = (bf16[25,64,256]{2,1,0:T(8,128)(2,1)}, bf16[25,64,256]{2,1,0:T(8,128)(2,1)S(1)}, u32[]{:S(2)}, u32[]{:S(2)}) collective-permute-start(bf16[25,64,256]{2,1,0:T(8,128)(2,1)} %pick_blocks.6.rest_0_), channel_id=1, source_target_pairs={{0,4},{1,5},{2,6},{3,7},{4,12},{5,13},{6,14},{7,15},{8,0},{9,1},{1... | collective-permute-start | bytes 2457608 | tf_op jit(solution)/shard_map/ppermute | solution.py:542
  67.9 3.1 %copy-start.2 = (bf16[25,64,256]{2,1,0:T(8,128)(2,1)S(1)}, bf16[25,64,256]{2,1,0:T(8,128)(2,1)}, u32[]{:S(2)}) copy-start(bf16[25,64,256]{2,1,0:T(8,128)(2,1)} %copy-done.1) | copy-start | bytes 2457604
  69.9 34.2 %collective-permute-start.2 = (bf16[25,64,256]{2,1,0:T(8,128)(2,1)S(1)}, bf16[25,64,256]{2,1,0:T(8,128)(2,1)S(1)}, u32[]{:S(2)}, u32[]{:S(2)}) collective-permute-start(bf16[25,64,256]{2,1,0:T(8,128)(2,1)S(1)} %pick_blocks.8), channel_id=1, source_target_pairs={{0,4},{1,5},{2,6},{3,7},{4,12},{5,13},{6,14},{7,15},{8,0},{9,1},{1... | collective-permute-start | bytes 2457608 | tf_op jit(solution)/shard_map/ppermute | solution.py:542
  71.0 48.4 %collective-permute-start.8 = (bf16[25,64,256]{2,1,0:T(8,128)(2,1)S(1)}, bf16[25,64,256]{2,1,0:T(8,128)(2,1)S(1)}, u32[]{:S(2)}, u32[]{:S(2)}) collective-permute-start(bf16[25,64,256]{2,1,0:T(8,128)(2,1)S(1)} %copy-done.2), channel_id=1, source_target_pairs={{8,12},{9,13},{10,14},{11,15},{4,0},{5,1},{6,2},{7,3},{24,28},{25,... | collective-permute-start | bytes 2457608 | tf_op jit(solution)/shard_map/ppermute | solution.py:542
  85.9 33.5 %collective-permute-start.7 = (bf16[25,64,256]{2,1,0:T(8,128)(2,1)S(1)}, bf16[25,64,256]{2,1,0:T(8,128)(2,1)S(1)}, u32[]{:S(2)}, u32[]{:S(2)}) collective-permute-start(bf16[25,64,256]{2,1,0:T(8,128)(2,1)S(1)} %pick_blocks.11), channel_id=1, source_target_pairs={{0,2},{1,3},{2,0},{3,1},{4,6},{5,7},{6,4},{7,5},{8,10},{9,11},{10,... | collective-permute-start | bytes 2457608 | tf_op jit(solution)/shard_map/ppermute | solution.py:542
  86.6 50.3 %collective-permute-start.9 = (bf16[25,64,256]{2,1,0:T(8,128)(2,1)}, bf16[25,64,256]{2,1,0:T(8,128)(2,1)S(1)}, u32[]{:S(2)}, u32[]{:S(2)}) collective-permute-start(bf16[25,64,256]{2,1,0:T(8,128)(2,1)} %collective-permute-done.6.rest_0_), channel_id=1, source_target_pairs={{8,12},{9,13},{10,14},{11,15},{4,0},{5,1},{6,2},{7,3},{24,28},{25,... | collective-permute-start | bytes 2457608 | tf_op jit(solution)/shard_map/ppermute | solution.py:542
  92.2 57.4 %collective-permute-start.5 = (bf16[25,64,256]{2,1,0:T(8,128)(2,1)S(1)}, bf16[25,64,256]{2,1,0:T(8,128)(2,1)S(1)}, u32[]{:S(2)}, u32[]{:S(2)}) collective-permute-start(bf16[25,64,256]{2,1,0:T(8,128)(2,1)S(1)} %pick_blocks.10), channel_id=1, source_target_pairs={{4,8},{5,9},{6,10},{7,11},{8,4},{9,5},{10,6},{11,7},{20,24},{21,25... | collective-permute-start | bytes 2457608 | tf_op jit(solution)/shard_map/ppermute | solution.py:542
  100.1 36.9 %copy-start.3 = (bf16[256,256]{1,0:T(8,128)(2,1)S(1)}, bf16[256,256]{1,0:T(8,128)(2,1)}, u32[]{:S(2)}) copy-start(bf16[256,256]{1,0:T(8,128)(2,1)} %rest_1_.5) | copy-start | bytes 393220
  100.1 36.9 %copy-start.4 = (bf16[256,256]{1,0:T(8,128)(2,1)S(1)}, bf16[256,256]{1,0:T(8,128)(2,1)}, u32[]{:S(2)}) copy-start(bf16[256,256]{1,0:T(8,128)(2,1)} %rest_2_.5) | copy-start | bytes 393220
  100.1 36.9 %copy-start.9 = (f32[64,8,256]{2,1,0:T(8,128)S(1)}, f32[64,8,256]{2,1,0:T(8,128)}, u32[]{:S(2)}) copy-start(f32[64,8,256]{2,1,0:T(8,128)} %copy-done.8) | copy-start | bytes 1572868
  106.3 58.7 %collective-permute-start.3 = (bf16[25,64,256]{2,1,0:T(8,128)(2,1)S(1)}, bf16[25,64,256]{2,1,0:T(8,128)(2,1)S(1)}, u32[]{:S(2)}, u32[]{:S(2)}) collective-permute-start(bf16[25,64,256]{2,1,0:T(8,128)(2,1)S(1)} %pick_blocks.9), channel_id=1, source_target_pairs={{4,8},{5,9},{6,10},{7,11},{8,4},{9,5},{10,6},{11,7},{20,24},{21,25... | collective-permute-start | bytes 2457608 | tf_op jit(solution)/shard_map/ppermute | solution.py:542
  137.0 12.7 %copy-start.7 = (bf16[4096,256]{1,0:T(8,128)(2,1)S(1)}, bf16[4096,256]{1,0:T(8,128)(2,1)}, u32[]{:S(2)}) copy-start(bf16[4096,256]{1,0:T(8,128)(2,1)} %copy-done.6) | copy-start | bytes 6291460

commit v17 on v16

--- a/solution.py
+++ b/solution.py
@@ -82,41 +82,35 @@
     return result
 
 
-def pick_kernel(position_ref, wanted_ref, blocks_ref, *rest, plan, capacity):
-    sems = rest[-1]
+def pick_kernel(position_ref, wanted_ref, *rest, plan, capacity):
     position = position_ref[0]
-
-    def copies():
-        for n, (reader_of, owner_of) in enumerate(plan):
-            reader, first = reader_of(position), owner_of(position) * capacity
-            for slot in range(capacity):
-                block = wanted_ref[reader, first + slot]
-                out_ref = rest[len(rest) - 1 - len(plan) + n]
-                yield pltpu.make_async_copy(
-                    blocks_ref.at[block], out_ref.at[slot], sems.at[n, slot]
-                )
-
-    for copy in copies():
-        copy.start()
-    for copy in copies():
-        copy.wait()
-
-
-def pick(position, wanted, blocks, plan, after=()):
+    for out_ref, (at, reader_of, owner_of) in zip(rest[len(rest) - len(plan) :], plan, strict=True):
+        reader, first = reader_of(position), owner_of(position) * capacity
+
+        def one_slot(slot, carry, out_ref=out_ref, at=at, reader=reader, first=first):
+            out_ref[slot] = rest[at][wanted_ref[reader, first + slot]]
+            return carry
+
+        lax.fori_loop(0, capacity, one_slot, 0)
+
+
+def pick(position, wanted, sources, plan, after=()):
     capacity = wanted.shape[1] // SPAN
-    outs = [jax.ShapeDtypeStruct((capacity,) + blocks.shape[1:], blocks.dtype)] * len(plan)
+    block = sources[0].shape[1:]
+    outs = [jax.ShapeDtypeStruct((capacity,) + block, sources[0].dtype)] * len(plan)
     smem = pl.BlockSpec(memory_space=pltpu.SMEM)
-    hbm = pl.BlockSpec(memory_space=pl.ANY)
+    vmem = pl.BlockSpec(memory_space=pltpu.VMEM)
     return pl.pallas_call(
         functools.partial(pick_kernel, plan=plan, capacity=capacity),
-        in_specs=[smem, smem, hbm] + [hbm] * len(after),
-        out_specs=[pl.BlockSpec(memory_space=pltpu.VMEM)] * len(outs),
+        in_specs=[smem, smem]
+        + [vmem] * len(sources)
+        + [pl.BlockSpec(memory_space=pl.ANY)] * len(after),
+        out_specs=[vmem] * len(outs),
         out_shape=outs,
-        scratch_shapes=[pltpu.SemaphoreType.DMA((len(plan), capacity))],
         cost_estimate=lasting(1.5),
         compiler_params=kernel_params(),
         name="pick_blocks",
-    )(position, wanted, blocks, *after)
+    )(position, wanted, *sources, *after)
 
 
 def tiles_of(query, first, span):
@@ -128,9 +122,8 @@
     )
 
 
-def own_kernel(
-    normed_ref, query_w_ref, key_w_ref, value_w_ref, query_ref, own_ref, stats_ref, *, head_width
-):
+def own_kernel(normed_ref, query_w_ref, key_w_ref, value_w_ref, *rest, head_width):
+    query_ref, own_ref, stats_ref = rest[-3:]
     blocks, width, tile = query_ref.shape
     cluster = tile // GROUP
     span = GROUP * head_width
@@ -174,7 +167,7 @@
         stats_ref[block] = jnp.concatenate(tops + totals, axis=0)
 
 
-def own_part(normed, w_query, w_key, w_value, cluster):
+def own_part(normed, w_query, w_key, w_value, cluster, after):
     rows, width = normed.shape
     blocks = rows // cluster
     tile = GROUP * cluster
@@ -184,7 +177,8 @@
     return pl.pallas_call(
         functools.partial(own_kernel, head_width=width // HEADS),
         grid=(blocks // OWN_STEP,),
-        in_specs=[pl.BlockSpec((OWN_STEP * cluster, width), lambda i: (i, 0)), whole, whole, whole],
+        in_specs=[pl.BlockSpec((OWN_STEP * cluster, width), lambda i: (i, 0)), whole, whole, whole]
+        + [pl.BlockSpec(memory_space=pl.ANY)] * len(after),
         out_specs=[
             square,
             square,
@@ -198,7 +192,7 @@
         cost_estimate=lasting(20),
         compiler_params=kernel_params(),
         name="own_blocks",
-    )(normed, w_query.T, w_key, w_value.T)
+    )(normed, w_query.T, w_key, w_value.T, *after)
 
 
 def collect_kernel(*refs, places):
@@ -423,7 +417,7 @@
     return jnp.concatenate(attended, axis=0), finished
 
 
-def attend(begin, count, order, table, own, placed, weights, buffer, pieces, places, so_far):
+def attend(steps, order, table, own, placed, weights, buffer, pieces, places, so_far):
     blocks, cluster, width = placed.shape
     pair_count = table.shape[0] // blocks
     smem = pl.BlockSpec(memory_space=pltpu.SMEM)
@@ -462,7 +456,7 @@
         cost_estimate=lasting(18),
         compiler_params=kernel_params(),
         name="attend_blocks",
-    )(jnp.stack([begin, count]).astype(jnp.int32), order, table, *operands)
+    )(steps, order, table, *operands)
 
 
 def slot_tables(owner, within, capacity):
@@ -519,12 +513,11 @@
     return lambda position: partner(route(position))
 
 
-SECOND_PLAN = ((source, itself),)
-MIDDLE_PLAN = ((opposite, itself),)
-SECOND_CROSS_PLAN = ((source, partner),)
-MIDDLE_CROSS_PLAN = ((opposite, partner),)
-ON_PLAN = ((crossed(onward), source), (onward, source))
-NEAR_PLAN = ((partner, source),)
+SECOND_PLAN = ((0, source, itself), (1, source, partner))
+MIDDLE_PLAN = ((0, opposite, itself),)
+MIDDLE_CROSS_PLAN = ((0, opposite, partner),)
+ON_PLAN = ((0, crossed(onward), source),)
+NEAR_PLAN = ((0, partner, source), (0, onward, source))
 
 
 def body(features, assignment, pairs, w_query, w_key, w_value, w_out, w_mix):
@@ -567,32 +560,10 @@
     block_shape = (block_count, cluster, width)
     placed, normed = place(features, assignment.reshape(shape))
     blocks = normed.reshape(block_shape)
-    own = own_part(normed, w_query, w_key, w_value, cluster)
     own_at = 7 * capacity
     passed_at = own_at + block_count
     beside_at = passed_at + block_count
     total = beside_at + block_count
-
-    beside = moved(blocks, swap)
-    passed = moved(blocks, first_moves)
-    (second_pick,) = pick(at_position, wanted, blocks, SECOND_PLAN, after=own[2:])
-    second = moved(second_pick, second_moves)
-    on, outward = pick(at_position, wanted, passed, ON_PLAN, after=(second_pick,))
-    (second_cross,) = pick(at_position, wanted, beside, SECOND_CROSS_PLAN, after=(on,))
-    second_cross = moved(second_cross, second_moves)
-    on = moved(on, swap)
-    outward = moved(outward, outward_moves)
-    (middle,) = pick(at_position, wanted, blocks, MIDDLE_PLAN, after=(second,))
-    middle = moved(middle, middle_moves)
-    (near,) = pick(at_position, wanted, passed, NEAR_PLAN, after=(on,))
-    near = moved(near, swap)
-    on = moved(on, outward_moves)
-    (middle_cross,) = pick(
-        at_position, wanted, beside, MIDDLE_CROSS_PLAN, after=(second_cross,)
-    )
-    middle_cross = moved(middle_cross, middle_moves)
-
-    buffer = collect((blocks, passed, beside), (own_at, passed_at, beside_at), total)
 
     z, y = position // 2, position % 2
     is_end = (z == 0) | (z == LEVELS - 1)
@@ -612,22 +583,48 @@
     whole = (z_owner == z) | (from_first & same)
     table = jnp.where(whole, whole_at + within, piece_of * capacity + ranking)
 
-    arrival = jnp.where(late & ~is_end, jnp.where(same, 1, 2), 0)
+    arrival = jnp.where(late, jnp.where(same, 1, 2), 0)
     order, ends = by_class(jnp.max(arrival.reshape(block_count, pair_count), axis=1), 2)
     marks = [0, ends[0] // STEP, ends[1] // STEP, block_count // STEP]
-    phases = [(marks[n], marks[n + 1] - marks[n]) for n in range(3)]
+    phases = [
+        jnp.stack([marks[n], marks[n + 1] - marks[n]]).astype(jnp.int32) for n in range(3)
+    ]
     weights = (jnp.concatenate([w_key, w_value], axis=1), w_out, w_mix)
+
+    own = own_part(normed, w_query, w_key, w_value, cluster, (order, table, *phases, weights[0]))
+    beside = moved(blocks, swap)
+    passed = moved(blocks, first_moves)
+    second_pick, cross_pick = pick(
+        at_position, wanted, (blocks, beside), SECOND_PLAN, after=own[2:]
+    )
+    second = moved(second_pick, second_moves)
+    second_cross = moved(cross_pick, second_moves)
+    (on,) = pick(at_position, wanted, (passed,), ON_PLAN, after=(cross_pick,))
+    on = moved(on, swap)
+    (middle,) = pick(at_position, wanted, (blocks,), MIDDLE_PLAN, after=(second,))
+    middle = moved(middle, middle_moves)
+    near, outward = pick(at_position, wanted, (passed,), NEAR_PLAN, after=(on,))
+    near = moved(near, swap)
+    outward = moved(outward, outward_moves)
+    on = moved(on, outward_moves)
+    (middle_cross,) = pick(
+        at_position, wanted, (beside,), MIDDLE_CROSS_PLAN, after=(second_cross,)
+    )
+    middle_cross = moved(middle_cross, middle_moves)
+
+    buffer = collect((blocks, passed, beside), (own_at, passed_at, beside_at), total)
+
     shared = (order, table, own, placed.reshape(blocks.shape), weights)
     arrivals = (
-        ((near, 0), (second, 1), (second_cross, 2), (outward, 3), (on, 4)),
-        ((middle, 5),),
-        ((middle_cross, 6),),
+        ((near, 0), (second, 1), (second_cross, 2)),
+        ((outward, 3), (middle, 5)),
+        ((on, 4), (middle_cross, 6)),
     )
     mixed = None
     for phase, arrived in zip(phases, arrivals, strict=True):
         pieces = [piece for piece, _ in arrived]
         places = tuple(at * capacity for _, at in arrived)
-        mixed, buffer = attend(*phase, *shared, buffer, pieces, places, mixed)
+        mixed, buffer = attend(phase, *shared, buffer, pieces, places, mixed)
     return mixed.reshape(rows_dev, width)
 
 

time: 181 us -> 157 us (0.87)
  waiting for transfers between devices: 47.6 us -> 23.2 us
  Pallas kernels: 96.8 us -> 94.3 us
  local copies, waits for them, and re-layouts: 4.09 us -> 6.04 us
    ppermute x10, waiting for transfers between devices: 41.9 us -> 18 us  [moved(): return lax.ppermute(x, 'elec', pairs_of)]
    pallas_call x6 -> x5, Pallas kernels: 14.8 us -> 9.49 us  [pick(): pl.pallas_call(functools.partial(pick_kernel, plan=plan, capacity=capacit...]
    unnamed x31 -> x27, local copies, waits for them, and re-layouts: 3.34 us -> 5.29 us
  transfers between devices with their start and end apart: 11 -> 11, of which waited for: 5 -> 3; matrix products, arithmetic and copies ran while one was open for 1% -> 2% of each run, Pallas kernels for 42% -> 45%
where the time goes in v17:
time: 157 us; the launch traced here: 156 us
  Pallas kernels  94.3 us (60%)
  starting transfers between devices  25.5 us (16%)
  waiting for transfers between devices  23.2 us (15%)
  local copies, waits for them, and re-layouts  6.04 us (4%)
  between operations  5.22 us (3%)
  other arithmetic  1.59 us (1%)
    pallas_call x3, Pallas kernels, attend(): pl.pallas_call(kernel, in_specs=in_specs, out_specs=[hbm, hbm], out_shape...  43.4 us
    pallas_call x1, Pallas kernels, own_part(): pl.pallas_call(functools.partial(own_kernel, head_width=width // HEADS),...  29.5 us
    ppermute x10, starting transfers between devices, moved(): return lax.ppermute(x, 'elec', pairs_of)  19.7 us
    ppermute x10, waiting for transfers between devices, moved(): return lax.ppermute(x, 'elec', pairs_of)  18 us
    pallas_call x5, Pallas kernels, pick(): pl.pallas_call(functools.partial(pick_kernel, plan=plan, capacity=capacit...  9.49 us
    pallas_call x1, Pallas kernels, place(): pl.pallas_call(place_kernel, grid=(walkers // 2,), in_specs=[local, pl.Bl...  6.37 us
    all_to_all x1, starting transfers between devices, body(): lax.all_to_all(jnp.broadcast_to(tables[None], (SPAN, SPAN * capacity)), '...  5.81 us
    pallas_call x1, Pallas kernels, collect(): pl.pallas_call(functools.partial(collect_kernel, places=places), in_specs...  5.54 us
  transfers between devices with their start and end apart: 11, of which 3 were waited for; matrix products, arithmetic and copies ran while one was open for 2% of the time, Pallas kernels for 45%

profile of v17, /device:TPU:8, one launch (start us, length us, event | category | flops | bytes accessed | tf_op | source)
XLA Modules:
  0.0 155.8 jit_solution(5753521351919743433)
XLA Ops:
  0.0 0.7 copy-done.5
  0.7 6.4 %place_rows.1 = (bf16[4096,256]{1,0:T(8,128)(2,1)S(1)}, bf16[4096,256]{1,0:T(8,128)(2,1)}) custom-call(bf16[4096,256]{1,0:T(8,128)(2,1)} %features_ref.1, s32[8,1,512]{2,1,0:T(1,128)S(1)} %bitcast.21), custom_call_target="tpu_custom_call" | custom-call | flops 6899999744 | tf_op jit(solution)/shard_map/place_rows/pallas_call | solution.py:66
  7.1 1.4 copy-done.6
  8.5 1.5 collective-permute-start.1
  10.0 0.5 collective-permute-start
  10.7 0.2 select_reduce_fusion.1
  11.1 0.6 broadcast_in_dim.108
  11.7 5.8 %all-to-all-start = ((s32[8,1,200]{2,1,0:T(1,128)}), s32[8,1,200]{2,1,0:T(1,128)S(1)}, u32[]{:S(2)}, u32[]{:S(2)}) async-start(s32[8,1,200]{2,1,0:T(1,128)} %broadcast_in_dim.108), calls=%async_computation | async-start | bytes 16384 | tf_op jit(solution)/shard_map/all_to_all | solution.py:550
  17.7 0.7 fusion.14
  23.7 29.5 %own_blocks.1 = (bf16[64,256,256]{2,1,0:T(8,128)(2,1)}, bf16[64,256,256]{2,1,0:T(8,128)(2,1)}, f32[64,8,256]{2,1,0:T(8,128)S(1)}) custom-call(bf16[4096,256]{1,0:T(8,128)(2,1)} %get-tuple-element.19.normed_ref, bf16[256,256]{1,0:T(8,128)(2,1)S(1)} %bitcast.14, bf16[256,256]{1,0:T(8,128)(2,1)S(1)} %copy-done.2, bf16[256,256]{1,0:T(8,128)(2,1)S(1)} %bitcast.15, ...), custom_call_target="tpu_custom_call" | custom-call | flops 23000000512 | tf_op jit(solution)/shard_map/own_blocks/pallas_call | solution.py:177
  53.2 5.2 %all-to-all-done = s32[8,1,200]{2,1,0:T(1,128)S(1)} async-done(((s32[8,1,200]{2,1,0:T(1,128)}), s32[8,1,200]{2,1,0:T(1,128)S(1)}, u32[]{:S(2)}, u32[]{:S(2)}) %all-to-all-start) | async-done | bytes 6432 | tf_op jit(solution)/shard_map/all_to_all | solution.py:550
  58.4 1.3 copy-done
  59.7 2.7 %pick_blocks.5 = (bf16[25,64,256]{2,1,0:T(8,128)(2,1)S(1)}, bf16[25,64,256]{2,1,0:T(8,128)(2,1)S(1)}) custom-call(s32[1]{0:T(128)} %bitcast.8.position_ref, s32[8,200]{1,0:T(8,128)S(1)} %bitcast.16, bf16[64,64,256]{2,1,0:T(8,128)(2,1)} %bitcast.9.rest_0_.refs_0_, bf16[64,64,256]{2,1,0:T(8,128)(2,1)} %copy-done, ...), custom_call_target="tpu_custom_call" | custom-call | flops 1724999936 | tf_op jit(solution)/shard_map/pick_blocks/pallas_call | solution.py:103
  62.5 1.9 %pick_blocks.6 = bf16[25,64,256]{2,1,0:T(8,128)(2,1)S(1)} custom-call(s32[1]{0:T(128)} %bitcast.8.position_ref, s32[8,200]{1,0:T(8,128)S(1)} %bitcast.17, bf16[64,64,256]{2,1,0:T(8,128)(2,1)} %collective-permute-done.rest_0_.refs_1_, bf16[25,64,256]{2,1,0:T(8,128)(2,1)S(1)} %get-tuple-element.24.rest_1_), custom_call_target="tpu_custom_call" | custom-call | flops 1724999936 | tf_op jit(solution)/shard_map/pick_blocks/pallas_call | solution.py:103
  64.3 1.5 collective-permute-start.2
  65.9 2.4 %collective-permute-start.7 = (bf16[25,64,256]{2,1,0:T(8,128)(2,1)S(1)}, bf16[25,64,256]{2,1,0:T(8,128)(2,1)S(1)}, u32[]{:S(2)}, u32[]{:S(2)}) collective-permute-start(bf16[25,64,256]{2,1,0:T(8,128)(2,1)S(1)} %get-tuple-element.26), channel_id=1, source_target_pairs={{0,4},{1,5},{2,6},{3,7},{4,12},{5,13},{6,14},{7,15},{8,0},{9,1},{1... | collective-permute-start | bytes 2457608 | tf_op jit(solution)/shard_map/ppermute | solution.py:535
  68.2 0.6 collective-permute-start.4
  68.8 14.5 %collective-permute-done.2.rest_1_ = bf16[25,64,256]{2,1,0:T(8,128)(2,1)S(1)} collective-permute-done((bf16[25,64,256]{2,1,0:T(8,128)(2,1)S(1)}, bf16[25,64,256]{2,1,0:T(8,128)(2,1)S(1)}, u32[]{:S(2)}, u32[]{:S(2)}) %collective-permute-start.2) | collective-permute-done | bytes 819232 | tf_op jit(solution)/shard_map/ppermute | solution.py:535
  83.3 2.1 %pick_blocks.8 = (bf16[25,64,256]{2,1,0:T(8,128)(2,1)S(1)}, bf16[25,64,256]{2,1,0:T(8,128)(2,1)S(1)}) custom-call(s32[1]{0:T(128)} %bitcast.8.position_ref, s32[8,200]{1,0:T(8,128)S(1)} %bitcast.18, bf16[64,64,256]{2,1,0:T(8,128)(2,1)} %collective-permute-done.rest_0_.refs_1_, bf16[25,64,256]{2,1,0:T(8,128)(2,1)S(1)} %collective-permute-done.2.rest_1_), custom_call_target="tpu_custom_call" | custom-call | flops 1724999936 | tf_op jit(solution)/shard_map/pick_blocks/pallas_call | solution.py:103
  85.4 1.5 collective-permute-start.9
  86.9 5.5 %collect_blocks.1.rest_6_ = bf16[367,64,256]{2,1,0:T(8,128)(2,1)} custom-call(bf16[64,64,256]{2,1,0:T(8,128)(2,1)} %bitcast.9.rest_0_.refs_0_, bf16[64,64,256]{2,1,0:T(8,128)(2,1)} %collective-permute-done.rest_0_.refs_1_, bf16[64,64,256]{2,1,0:T(8,128)(2,1)} %copy-done), custom_call_target="tpu_custom_call" | custom-call | flops 4600000000 | tf_op jit(solution)/shard_map/collect_blocks/pallas_call | solution.py:215
  92.5 3.1 %collective-permute-start.6 = (bf16[25,64,256]{2,1,0:T(8,128)(2,1)S(1)}, bf16[25,64,256]{2,1,0:T(8,128)(2,1)S(1)}, u32[]{:S(2)}, u32[]{:S(2)}) collective-permute-start(bf16[25,64,256]{2,1,0:T(8,128)(2,1)S(1)} %get-tuple-element.25), channel_id=1, source_target_pairs={{8,12},{9,13},{10,14},{11,15},{4,0},{5,1},{6,2},{7,3},{24,28},{25,... | collective-permute-start | bytes 2457608 | tf_op jit(solution)/shard_map/ppermute | solution.py:535
  95.6 1.9 %pick_blocks.9 = bf16[25,64,256]{2,1,0:T(8,128)(2,1)S(1)} custom-call(s32[1]{0:T(128)} %bitcast.8.position_ref, s32[8,200]{1,0:T(8,128)S(1)} %bitcast.19, bf16[64,64,256]{2,1,0:T(8,128)(2,1)} %bitcast.9.rest_0_.refs_0_, bf16[25,64,256]{2,1,0:T(8,128)(2,1)S(1)} %collective-permute-done.7.rest_1_.rest_4_), custom_call_target="tpu_custom_call" | custom-call | flops 1724999936 | tf_op jit(solution)/shard_map/pick_blocks/pallas_call | solution.py:103
  97.5 3.6 %collective-permute-start.8 = (bf16[25,64,256]{2,1,0:T(8,128)(2,1)S(1)}, bf16[25,64,256]{2,1,0:T(8,128)(2,1)S(1)}, u32[]{:S(2)}, u32[]{:S(2)}) collective-permute-start(bf16[25,64,256]{2,1,0:T(8,128)(2,1)S(1)} %pick_blocks.9), channel_id=1, source_target_pairs={{4,8},{5,9},{6,10},{7,11},{8,4},{9,5},{10,6},{11,7},{20,24},{21,25... | collective-permute-start | bytes 2457608 | tf_op jit(solution)/shard_map/ppermute | solution.py:535
  101.1 3.5 %collective-permute-done.4.rest_1_.rest_5_ = bf16[25,64,256]{2,1,0:T(8,128)(2,1)S(1)} collective-permute-done((bf16[25,64,256]{2,1,0:T(8,128)(2,1)S(1)}, bf16[25,64,256]{2,1,0:T(8,128)(2,1)S(1)}, u32[]{:S(2)}, u32[]{:S(2)}) %collective-permute-start.4) | collective-permute-done | bytes 819232 | tf_op jit(solution)/shard_map/ppermute | solution.py:535
  104.5 0.9 pick_blocks.7
  105.5 2.4 %collective-permute-start.5 = (bf16[25,64,256]{2,1,0:T(8,128)(2,1)S(1)}, bf16[25,64,256]{2,1,0:T(8,128)(2,1)S(1)}, u32[]{:S(2)}, u32[]{:S(2)}) collective-permute-start(bf16[25,64,256]{2,1,0:T(8,128)(2,1)S(1)} %pick_blocks.7), channel_id=1, source_target_pairs={{4,8},{5,9},{6,10},{7,11},{8,4},{9,5},{10,6},{11,7},{20,24},{21,25... | collective-permute-start | bytes 2457608 | tf_op jit(solution)/shard_map/ppermute | solution.py:535
  107.9 2.7 %collective-permute-start.3 = (bf16[25,64,256]{2,1,0:T(8,128)(2,1)S(1)}, bf16[25,64,256]{2,1,0:T(8,128)(2,1)S(1)}, u32[]{:S(2)}, u32[]{:S(2)}) collective-permute-start(bf16[25,64,256]{2,1,0:T(8,128)(2,1)S(1)} %collective-permute-done.2.rest_1_), channel_id=1, source_target_pairs={{8,12},{9,13},{10,14},{11,15},{4,0},{5,1},{6,2},{7,3},{24,28},{25,... | collective-permute-start | bytes 2457608 | tf_op jit(solution)/shard_map/ppermute | solution.py:535
  110.6 1.6 %copy-done.7 = bf16[4096,256]{1,0:T(8,128)(2,1)S(1)} copy-done((bf16[4096,256]{1,0:T(8,128)(2,1)S(1)}, bf16[4096,256]{1,0:T(8,128)(2,1)}, u32[]{:S(2)}) %copy-start.7) | copy-done | bytes 2097176
  112.2 15.8 %attend_blocks.3 = (bf16[64,64,256]{2,1,0:T(8,128)(2,1)}, bf16[367,64,256]{2,1,0:T(8,128)(2,1)}) custom-call(s32[2]{0:T(128)S(1)} %pad_add_fusion.1.rest_2_.range_ref, s32[64]{0:T(128)S(1)} %select_reduce_fusion.2.rest_0_.order_ref, s32[192]{0:T(256)S(1)} %get-tuple-element.36.rest_1_.table_ref, ...), custom_call_target="tpu_custom_call", output_to_operand_aliasing={{1}: (13, {})} | custom-call | flops 20700000256 | tf_op jit(solution)/shard_map/attend_blocks/pallas_call | solution.py:436
  128.0 12.0 %attend_blocks.4 = (bf16[64,64,256]{2,1,0:T(8,128)(2,1)}, bf16[367,64,256]{2,1,0:T(8,128)(2,1)}) custom-call(s32[2]{0:T(128)S(1)} %pad_add_fusion.2.rest_3_.range_ref, s32[64]{0:T(128)S(1)} %select_reduce_fusion.2.rest_0_.order_ref, s32[192]{0:T(256)S(1)} %get-tuple-element.36.rest_1_.table_ref, ...), custom_call_target="tpu_custom_call", output_to_operand_aliasing={{1}: (12, {}), {0}: (13, {})} | custom-call | flops 20700000256 | tf_op jit(solution)/shard_map/attend_blocks/pallas_call | solution.py:436
  140.0 15.6 %attend_blocks.5 = (bf16[64,64,256]{2,1,0:T(8,128)(2,1)}, bf16[367,64,256]{2,1,0:T(8,128)(2,1)}) custom-call(s32[2]{0:T(128)S(1)} %pad_add_fusion.rest_4_.range_ref, s32[64]{0:T(128)S(1)} %select_reduce_fusion.2.rest_0_.order_ref, s32[192]{0:T(256)S(1)} %get-tuple-element.36.rest_1_.table_ref, ...), custom_call_target="tpu_custom_call", output_to_operand_aliasing={{1}: (12, {}), {0}: (13, {})} | custom-call | flops 20700000256 | tf_op jit(solution)/shard_map/attend_blocks/pallas_call | solution.py:436
  (42 shorter events, 1.2 us)
Async XLA Ops:
  0.0 0.7 copy-start.5
  0.7 9.7 %copy-start.10 = (s32[64,3]{0,1:T(4,128)S(1)}, s32[64,3]{0,1:T(4,128)}, u32[]{:S(2)}) copy-start(s32[64,3]{0,1:T(4,128)} %param.10) | copy-start | bytes 2308
  0.7 22.7 %copy-start.9 = (bf16[256,256]{1,0:T(8,128)(2,1)S(1)}, bf16[256,256]{1,0:T(8,128)(2,1)}, u32[]{:S(2)}) copy-start(bf16[256,256]{1,0:T(8,128)(2,1)} %param.11) | copy-start | bytes 393220
  0.7 22.8 %copy-start.8 = (bf16[256,256]{1,0:T(8,128)(2,1)S(1)}, bf16[256,256]{1,0:T(8,128)(2,1)}, u32[]{:S(2)}) copy-start(bf16[256,256]{1,0:T(8,128)(2,1)} %param.13) | copy-start | bytes 393220
  0.7 22.9 %copy-start.2 = (bf16[256,256]{1,0:T(8,128)(2,1)S(1)}, bf16[256,256]{1,0:T(8,128)(2,1)}, u32[]{:S(2)}) copy-start(bf16[256,256]{1,0:T(8,128)(2,1)} %key_w_ref.1) | copy-start | bytes 393220
  7.1 1.4 copy-start.6
  8.5 50.0 %collective-permute-start.1 = (bf16[64,64,256]{2,1,0:T(8,128)(2,1)}, bf16[64,64,256]{2,1,0:T(8,128)(2,1)S(1)}, u32[]{:S(2)}, u32[]{:S(2)}) collective-permute-start(bf16[64,64,256]{2,1,0:T(8,128)(2,1)} %bitcast.9.rest_0_.refs_0_), channel_id=1, source_target_pairs={{0,2},{1,3},{2,0},{3,1},{4,6},{5,7},{6,4},{7,5},{8,10},{9,11},{10,... | collective-permute-start | bytes 6291464 | tf_op jit(solution)/shard_map/ppermute | solution.py:535
  10.0 52.5 %collective-permute-start = (bf16[64,64,256]{2,1,0:T(8,128)(2,1)}, bf16[64,64,256]{2,1,0:T(8,128)(2,1)}, u32[]{:S(2)}, u32[]{:S(2)}) collective-permute-start(bf16[64,64,256]{2,1,0:T(8,128)(2,1)} %bitcast.9.rest_0_.refs_0_), channel_id=1, source_target_pairs={{0,8},{1,9},{2,10},{3,11},{4,0},{5,1},{6,2},{7,3},{8,12},{9,13},{1... | collective-permute-start | bytes 6291464 | tf_op jit(solution)/shard_map/ppermute | solution.py:535
  11.7 46.8 %all-to-all-start = ((s32[8,1,200]{2,1,0:T(1,128)}), s32[8,1,200]{2,1,0:T(1,128)S(1)}, u32[]{:S(2)}, u32[]{:S(2)}) async-start(s32[8,1,200]{2,1,0:T(1,128)} %broadcast_in_dim.108), calls=%async_computation | async-start | bytes 16384 | tf_op jit(solution)/shard_map/all_to_all | solution.py:550
  58.4 1.3 copy-start
  64.3 18.9 %collective-permute-start.2 = (bf16[25,64,256]{2,1,0:T(8,128)(2,1)S(1)}, bf16[25,64,256]{2,1,0:T(8,128)(2,1)S(1)}, u32[]{:S(2)}, u32[]{:S(2)}) collective-permute-start(bf16[25,64,256]{2,1,0:T(8,128)(2,1)S(1)} %pick_blocks.6), channel_id=1, source_target_pairs={{0,2},{1,3},{2,0},{3,1},{4,6},{5,7},{6,4},{7,5},{8,10},{9,11},{10,... | collective-permute-start | bytes 2457608 | tf_op jit(solution)/shard_map/ppermute | solution.py:535
  65.9 29.7 %collective-permute-start.7 = (bf16[25,64,256]{2,1,0:T(8,128)(2,1)S(1)}, bf16[25,64,256]{2,1,0:T(8,128)(2,1)S(1)}, u32[]{:S(2)}, u32[]{:S(2)}) collective-permute-start(bf16[25,64,256]{2,1,0:T(8,128)(2,1)S(1)} %get-tuple-element.26), channel_id=1, source_target_pairs={{0,4},{1,5},{2,6},{3,7},{4,12},{5,13},{6,14},{7,15},{8,0},{9,1},{1... | collective-permute-start | bytes 2457608 | tf_op jit(solution)/shard_map/ppermute | solution.py:535
  68.2 36.3 %collective-permute-start.4 = (bf16[25,64,256]{2,1,0:T(8,128)(2,1)S(1)}, bf16[25,64,256]{2,1,0:T(8,128)(2,1)S(1)}, u32[]{:S(2)}, u32[]{:S(2)}) collective-permute-start(bf16[25,64,256]{2,1,0:T(8,128)(2,1)S(1)} %get-tuple-element.24.rest_1_), channel_id=1, source_target_pairs={{0,4},{1,5},{2,6},{3,7},{4,12},{5,13},{6,14},{7,15},{8,0},{9,1},{1... | collective-permute-start | bytes 2457608 | tf_op jit(solution)/shard_map/ppermute | solution.py:535
  85.4 25.1 %collective-permute-start.9 = (bf16[25,64,256]{2,1,0:T(8,128)(2,1)S(1)}, bf16[25,64,256]{2,1,0:T(8,128)(2,1)S(1)}, u32[]{:S(2)}, u32[]{:S(2)}) collective-permute-start(bf16[25,64,256]{2,1,0:T(8,128)(2,1)S(1)} %get-tuple-element.27), channel_id=1, source_target_pairs={{0,2},{1,3},{2,0},{3,1},{4,6},{5,7},{6,4},{7,5},{8,10},{9,11},{10,... | collective-permute-start | bytes 2457608 | tf_op jit(solution)/shard_map/ppermute | solution.py:535
  92.4 12.1 %copy-start.1 = (bf16[64,64,256]{2,1,0:T(8,128)(2,1)S(1)}, bf16[64,64,256]{2,1,0:T(8,128)(2,1)}, u32[]{:S(2)}) copy-start(bf16[64,64,256]{2,1,0:T(8,128)(2,1)} %copy-done) | copy-start | bytes 6291460
  92.5 35.5 %collective-permute-start.6 = (bf16[25,64,256]{2,1,0:T(8,128)(2,1)S(1)}, bf16[25,64,256]{2,1,0:T(8,128)(2,1)S(1)}, u32[]{:S(2)}, u32[]{:S(2)}) collective-permute-start(bf16[25,64,256]{2,1,0:T(8,128)(2,1)S(1)} %get-tuple-element.25), channel_id=1, source_target_pairs={{8,12},{9,13},{10,14},{11,15},{4,0},{5,1},{6,2},{7,3},{24,28},{25,... | collective-permute-start | bytes 2457608 | tf_op jit(solution)/shard_map/ppermute | solution.py:535
  97.4 13.1 %copy-start.3 = (bf16[256,256]{1,0:T(8,128)(2,1)S(1)}, bf16[256,256]{1,0:T(8,128)(2,1)}, u32[]{:S(2)}) copy-start(bf16[256,256]{1,0:T(8,128)(2,1)} %rest_1_.5) | copy-start | bytes 393220
  97.5 13.1 %copy-start.4 = (bf16[256,256]{1,0:T(8,128)(2,1)S(1)}, bf16[256,256]{1,0:T(8,128)(2,1)}, u32[]{:S(2)}) copy-start(bf16[256,256]{1,0:T(8,128)(2,1)} %rest_2_.5) | copy-start | bytes 393220
  97.5 30.5 %collective-permute-start.8 = (bf16[25,64,256]{2,1,0:T(8,128)(2,1)S(1)}, bf16[25,64,256]{2,1,0:T(8,128)(2,1)S(1)}, u32[]{:S(2)}, u32[]{:S(2)}) collective-permute-start(bf16[25,64,256]{2,1,0:T(8,128)(2,1)S(1)} %pick_blocks.9), channel_id=1, source_target_pairs={{4,8},{5,9},{6,10},{7,11},{8,4},{9,5},{10,6},{11,7},{20,24},{21,25... | collective-permute-start | bytes 2457608 | tf_op jit(solution)/shard_map/ppermute | solution.py:535
  105.5 34.6 %collective-permute-start.5 = (bf16[25,64,256]{2,1,0:T(8,128)(2,1)S(1)}, bf16[25,64,256]{2,1,0:T(8,128)(2,1)S(1)}, u32[]{:S(2)}, u32[]{:S(2)}) collective-permute-start(bf16[25,64,256]{2,1,0:T(8,128)(2,1)S(1)} %pick_blocks.7), channel_id=1, source_target_pairs={{4,8},{5,9},{6,10},{7,11},{8,4},{9,5},{10,6},{11,7},{20,24},{21,25... | collective-permute-start | bytes 2457608 | tf_op jit(solution)/shard_map/ppermute | solution.py:535
  107.9 32.2 %collective-permute-start.3 = (bf16[25,64,256]{2,1,0:T(8,128)(2,1)S(1)}, bf16[25,64,256]{2,1,0:T(8,128)(2,1)S(1)}, u32[]{:S(2)}, u32[]{:S(2)}) collective-permute-start(bf16[25,64,256]{2,1,0:T(8,128)(2,1)S(1)} %collective-permute-done.2.rest_1_), channel_id=1, source_target_pairs={{8,12},{9,13},{10,14},{11,15},{4,0},{5,1},{6,2},{7,3},{24,28},{25,... | collective-permute-start | bytes 2457608 | tf_op jit(solution)/shard_map/ppermute | solution.py:535
  110.6 1.6 %copy-start.7 = (bf16[4096,256]{1,0:T(8,128)(2,1)S(1)}, bf16[4096,256]{1,0:T(8,128)(2,1)}, u32[]{:S(2)}) copy-start(bf16[4096,256]{1,0:T(8,128)(2,1)} %copy-done.6) | copy-start | bytes 6291460

commit v18 on v17

--- a/solution.py
+++ b/solution.py
@@ -24,8 +24,8 @@
     return pl.CostEstimate(flops=int(us * 1.15e9), bytes_accessed=0, transcendentals=0)
 
 
-def kernel_params():
-    return pltpu.CompilerParams(vmem_limit_bytes=VMEM_BYTES)
+def kernel_params(share=1):
+    return pltpu.CompilerParams(vmem_limit_bytes=VMEM_BYTES // share)
 
 
 def layer_norm(rows):
@@ -68,7 +68,7 @@
         grid=(walkers // 2,),
         in_specs=[local, pl.BlockSpec((2, 1, rows), lambda i: (i, 0, 0))],
         out_specs=[local] * 2,
-        out_shape=[out] * 2,
+        out_shape=[pltpu.HBM(out.shape, out.dtype), out],
         cost_estimate=lasting(6),
         compiler_params=kernel_params(),
         name="place_rows",
@@ -108,7 +108,7 @@
         out_specs=[vmem] * len(outs),
         out_shape=outs,
         cost_estimate=lasting(1.5),
-        compiler_params=kernel_params(),
+        compiler_params=kernel_params(3),
         name="pick_blocks",
     )(position, wanted, *sources, *after)
 
@@ -204,11 +204,21 @@
         copy.wait()
 
 
+def parts_of(blocks):
+    return 5 if blocks % 5 == 0 else 4
+
+
 def copy_pieces(piece_refs, buffer_ref, places, sems):
-    return [
-        pltpu.make_async_copy(piece, buffer_ref.at[pl.ds(at, piece.shape[0])], sems.at[n])
-        for n, (piece, at) in enumerate(zip(piece_refs, places, strict=True))
-    ]
+    copies = []
+    for n, (piece, at) in enumerate(zip(piece_refs, places, strict=True)):
+        parts = parts_of(piece.shape[0])
+        per = piece.shape[0] // parts
+        for part in range(parts):
+            target = buffer_ref.at[pl.ds(at + part * per, per)]
+            copies.append(
+                pltpu.make_async_copy(piece.at[pl.ds(part * per, per)], target, sems.at[n, part])
+            )
+    return copies
 
 
 def collect(pieces, places, total):
@@ -216,10 +226,10 @@
         functools.partial(collect_kernel, places=places),
         in_specs=[pl.BlockSpec(memory_space=pltpu.VMEM)] * len(pieces),
         out_specs=pl.BlockSpec(memory_space=pl.ANY),
-        out_shape=jax.ShapeDtypeStruct((total,) + pieces[0].shape[1:], pieces[0].dtype),
-        scratch_shapes=[pltpu.SemaphoreType.DMA((len(pieces),))],
+        out_shape=pltpu.HBM((total,) + pieces[0].shape[1:], pieces[0].dtype),
+        scratch_shapes=[pltpu.SemaphoreType.DMA((len(pieces), 5))],
         cost_estimate=lasting(4),
-        compiler_params=kernel_params(),
+        compiler_params=kernel_params(3),
         name="collect_blocks",
     )(*pieces)
 
@@ -423,7 +433,7 @@
     smem = pl.BlockSpec(memory_space=pltpu.SMEM)
     vmem = pl.BlockSpec(memory_space=pltpu.VMEM)
     hbm = pl.BlockSpec(memory_space=pl.ANY)
-    in_specs = [smem] * 3 + [hbm] * (len(own) + 1) + [vmem] * (3 + len(pieces)) + [hbm]
+    in_specs = [smem] * 3 + [hbm] * len(own) + [pl.BlockSpec(memory_space=pltpu.HBM)] + [vmem] * (3 + len(pieces)) + [hbm]
     aliases = {len(in_specs) - 1: 1}
     operands = [*own, placed, *weights, *pieces, buffer]
     if so_far is not None:
@@ -450,7 +460,7 @@
             pltpu.VMEM((STEP, cluster, width), jnp.bfloat16),
             pltpu.SemaphoreType.DMA((2, STEP * (pair_count + 4))),
             pltpu.SemaphoreType.DMA((STEP,)),
-            pltpu.SemaphoreType.DMA((len(pieces),)),
+            pltpu.SemaphoreType.DMA((len(pieces), 5)),
         ],
         input_output_aliases=aliases,
         cost_estimate=lasting(18),
@@ -614,7 +624,8 @@
 
     buffer = collect((blocks, passed, beside), (own_at, passed_at, beside_at), total)
 
-    shared = (order, table, own, placed.reshape(blocks.shape), weights)
+    placed = pltpu.with_memory_space_constraint(placed.reshape(blocks.shape), pltpu.HBM)
+    shared = (order, table, own, placed, weights)
     arrivals = (
         ((near, 0), (second, 1), (second_cross, 2)),
         ((outward, 3), (middle, 5)),

time: 157 us -> 153 us (0.975); the launches traced: 156 us -> 150 us
  Pallas kernels: 94.3 us -> 90.6 us
  local copies, waits for them, and re-layouts: 6.04 us -> 3.39 us
    unnamed x27 -> x21, local copies, waits for them, and re-layouts: 5.29 us -> 2.64 us
  transfers between devices with their start and end apart: 11 -> 11, of which waited for: 3 -> 3; matrix products, arithmetic and copies ran while one was open for 2% -> 2% of each run, Pallas kernels for 45% -> 46%
where the time goes in v18:
time: 153 us; the launch traced here: 150 us
  Pallas kernels  90.6 us (59%)
  starting transfers between devices  25.3 us (17%)
  waiting for transfers between devices  23.5 us (15%)
  between operations  5.52 us (4%)
  local copies, waits for them, and re-layouts  3.39 us (2%)
  other arithmetic  1.62 us (1%)
    pallas_call x3, Pallas kernels, attend(): pl.pallas_call(kernel, in_specs=in_specs, out_specs=[hbm, hbm], out_shape...  42.1 us
    pallas_call x1, Pallas kernels, own_part(): pl.pallas_call(functools.partial(own_kernel, head_width=width // HEADS),...  29.5 us
    ppermute x10, starting transfers between devices, moved(): return lax.ppermute(x, 'elec', pairs_of)  19.5 us
    ppermute x10, waiting for transfers between devices, moved(): return lax.ppermute(x, 'elec', pairs_of)  18.6 us
    pallas_call x5, Pallas kernels, pick(): pl.pallas_call(functools.partial(pick_kernel, plan=plan, capacity=capacit...  8.86 us
    all_to_all x1, starting transfers between devices, body(): lax.all_to_all(jnp.broadcast_to(tables[None], (SPAN, SPAN * capacity)), '...  5.82 us
    pallas_call x1, Pallas kernels, place(): pl.pallas_call(place_kernel, grid=(walkers // 2,), in_specs=[local, pl.Bl...  5.09 us
    pallas_call x1, Pallas kernels, collect(): pl.pallas_call(functools.partial(collect_kernel, places=places), in_specs...  5.02 us
  transfers between devices with their start and end apart: 11, of which 3 were waited for; matrix products, arithmetic and copies ran while one was open for 2% of the time, Pallas kernels for 46%

profile of v18, /device:TPU:8, one launch (start us, length us, event | category | flops | bytes accessed | tf_op | source)
XLA Modules:
  0.0 149.9 jit_solution(14424999973884245717)
XLA Ops:
  0.0 1.6 %copy-done.1 = bf16[4096,256]{1,0:T(8,128)(2,1)S(1)} copy-done((bf16[4096,256]{1,0:T(8,128)(2,1)S(1)}, bf16[4096,256]{1,0:T(8,128)(2,1)}, u32[]{:S(2)}) %copy-start.1) | copy-done | bytes 2097176
  1.6 0.7 copy-done.4
  2.3 5.1 %place_rows.1 = (bf16[4096,256]{1,0:T(8,128)(2,1)}, bf16[4096,256]{1,0:T(8,128)(2,1)}) custom-call(bf16[4096,256]{1,0:T(8,128)(2,1)S(1)} %copy-done.1, s32[8,1,512]{2,1,0:T(1,128)S(1)} %bitcast.21), custom_call_target="tpu_custom_call" | custom-call | flops 6899999744 | tf_op jit(solution)/shard_map/place_rows/pallas_call | solution.py:66
  7.4 1.5 %collective-permute-start.1 = (bf16[64,64,256]{2,1,0:T(8,128)(2,1)}, bf16[64,64,256]{2,1,0:T(8,128)(2,1)S(1)}, u32[]{:S(2)}, u32[]{:S(2)}) collective-permute-start(bf16[64,64,256]{2,1,0:T(8,128)(2,1)} %bitcast.9.rest_0_.refs_0_), channel_id=1, source_target_pairs={{0,2},{1,3},{2,0},{3,1},{4,6},{5,7},{6,4},{7,5},{8,10},{9,11},{10,... | collective-permute-start | bytes 6291464 | tf_op jit(solution)/shard_map/ppermute | solution.py:545
  8.9 0.4 collective-permute-start
  9.5 0.1 reshape.148
  9.6 0.2 select_reduce_fusion.1
  10.0 0.6 broadcast_in_dim.108
  10.6 5.8 %all-to-all-start = ((s32[8,1,200]{2,1,0:T(1,128)}), s32[8,1,200]{2,1,0:T(1,128)S(1)}, u32[]{:S(2)}, u32[]{:S(2)}) async-start(s32[8,1,200]{2,1,0:T(1,128)} %broadcast_in_dim.108), calls=%async_computation | async-start | bytes 16384 | tf_op jit(solution)/shard_map/all_to_all | solution.py:560
  16.5 0.2 select_reduce_fusion.3
  16.6 0.7 fusion.14
  23.0 29.5 %own_blocks.1 = (bf16[64,256,256]{2,1,0:T(8,128)(2,1)}, bf16[64,256,256]{2,1,0:T(8,128)(2,1)}, f32[64,8,256]{2,1,0:T(8,128)S(1)}) custom-call(bf16[4096,256]{1,0:T(8,128)(2,1)} %get-tuple-element.19.normed_ref, bf16[256,256]{1,0:T(8,128)(2,1)S(1)} %bitcast.14, bf16[256,256]{1,0:T(8,128)(2,1)S(1)} %copy-done, bf16[256,256]{1,0:T(8,128)(2,1)S(1)} %bitcast.15, ...), custom_call_target="tpu_custom_call" | custom-call | flops 23000000512 | tf_op jit(solution)/shard_map/own_blocks/pallas_call | solution.py:177
  52.5 4.8 %all-to-all-done = s32[8,1,200]{2,1,0:T(1,128)S(1)} async-done(((s32[8,1,200]{2,1,0:T(1,128)}), s32[8,1,200]{2,1,0:T(1,128)S(1)}, u32[]{:S(2)}, u32[]{:S(2)}) %all-to-all-start) | async-done | bytes 6432 | tf_op jit(solution)/shard_map/all_to_all | solution.py:560
  57.4 2.1 %pick_blocks.5 = (bf16[25,64,256]{2,1,0:T(8,128)(2,1)S(1)}, bf16[25,64,256]{2,1,0:T(8,128)(2,1)S(1)}) custom-call(s32[1]{0:T(128)} %bitcast.8.position_ref, s32[8,200]{1,0:T(8,128)S(1)} %bitcast.16, bf16[64,64,256]{2,1,0:T(8,128)(2,1)} %bitcast.9.rest_0_.refs_0_, bf16[64,64,256]{2,1,0:T(8,128)(2,1)S(1)} %collective-permute-done.1.rest_1_.rest_0_.refs_2_, ...), custom_call_target="tpu_custom_call" | custom-call | flops 1724999936 | tf_op jit(solution)/shard_map/pick_blocks/pallas_call | solution.py:103
  59.5 1.9 %pick_blocks.6 = bf16[25,64,256]{2,1,0:T(8,128)(2,1)S(1)} custom-call(s32[1]{0:T(128)} %bitcast.8.position_ref, s32[8,200]{1,0:T(8,128)S(1)} %bitcast.17, bf16[64,64,256]{2,1,0:T(8,128)(2,1)} %collective-permute-done.rest_0_.refs_1_, bf16[25,64,256]{2,1,0:T(8,128)(2,1)S(1)} %get-tuple-element.24.rest_1_), custom_call_target="tpu_custom_call" | custom-call | flops 1724999936 | tf_op jit(solution)/shard_map/pick_blocks/pallas_call | solution.py:103
  61.4 1.5 %collective-permute-start.2 = (bf16[25,64,256]{2,1,0:T(8,128)(2,1)S(1)}, bf16[25,64,256]{2,1,0:T(8,128)(2,1)S(1)}, u32[]{:S(2)}, u32[]{:S(2)}) collective-permute-start(bf16[25,64,256]{2,1,0:T(8,128)(2,1)S(1)} %pick_blocks.6), channel_id=1, source_target_pairs={{0,2},{1,3},{2,0},{3,1},{4,6},{5,7},{6,4},{7,5},{8,10},{9,11},{10,... | collective-permute-start | bytes 2457608 | tf_op jit(solution)/shard_map/ppermute | solution.py:545
  62.9 2.4 %collective-permute-start.7 = (bf16[25,64,256]{2,1,0:T(8,128)(2,1)S(1)}, bf16[25,64,256]{2,1,0:T(8,128)(2,1)S(1)}, u32[]{:S(2)}, u32[]{:S(2)}) collective-permute-start(bf16[25,64,256]{2,1,0:T(8,128)(2,1)S(1)} %get-tuple-element.26), channel_id=1, source_target_pairs={{0,4},{1,5},{2,6},{3,7},{4,12},{5,13},{6,14},{7,15},{8,0},{9,1},{1... | collective-permute-start | bytes 2457608 | tf_op jit(solution)/shard_map/ppermute | solution.py:545
  65.3 0.6 collective-permute-start.4
  65.9 14.5 %collective-permute-done.2.rest_1_ = bf16[25,64,256]{2,1,0:T(8,128)(2,1)S(1)} collective-permute-done((bf16[25,64,256]{2,1,0:T(8,128)(2,1)S(1)}, bf16[25,64,256]{2,1,0:T(8,128)(2,1)S(1)}, u32[]{:S(2)}, u32[]{:S(2)}) %collective-permute-start.2) | collective-permute-done | bytes 819232 | tf_op jit(solution)/shard_map/ppermute | solution.py:545
  80.3 2.1 %pick_blocks.8 = (bf16[25,64,256]{2,1,0:T(8,128)(2,1)S(1)}, bf16[25,64,256]{2,1,0:T(8,128)(2,1)S(1)}) custom-call(s32[1]{0:T(128)} %bitcast.8.position_ref, s32[8,200]{1,0:T(8,128)S(1)} %bitcast.18, bf16[64,64,256]{2,1,0:T(8,128)(2,1)} %collective-permute-done.rest_0_.refs_1_, bf16[25,64,256]{2,1,0:T(8,128)(2,1)S(1)} %collective-permute-done.2.rest_1_), custom_call_target="tpu_custom_call" | custom-call | flops 1724999936 | tf_op jit(solution)/shard_map/pick_blocks/pallas_call | solution.py:103
  82.4 1.5 collective-permute-start.9
  83.9 5.0 %collect_blocks.1.rest_6_ = bf16[367,64,256]{2,1,0:T(8,128)(2,1)} custom-call(bf16[64,64,256]{2,1,0:T(8,128)(2,1)} %bitcast.9.rest_0_.refs_0_, bf16[64,64,256]{2,1,0:T(8,128)(2,1)} %collective-permute-done.rest_0_.refs_1_, bf16[64,64,256]{2,1,0:T(8,128)(2,1)S(1)} %collective-permute-done.1.rest_1_.rest_0_.refs_2_), custom_call_target="tpu_custom_call" | custom-call | flops 4600000000 | tf_op jit(solution)/shard_map/collect_blocks/pallas_call | solution.py:225
  89.0 3.0 %collective-permute-start.6 = (bf16[25,64,256]{2,1,0:T(8,128)(2,1)S(1)}, bf16[25,64,256]{2,1,0:T(8,128)(2,1)S(1)}, u32[]{:S(2)}, u32[]{:S(2)}) collective-permute-start(bf16[25,64,256]{2,1,0:T(8,128)(2,1)S(1)} %get-tuple-element.25), channel_id=1, source_target_pairs={{8,12},{9,13},{10,14},{11,15},{4,0},{5,1},{6,2},{7,3},{24,28},{25,... | collective-permute-start | bytes 2457608 | tf_op jit(solution)/shard_map/ppermute | solution.py:545
  92.0 1.9 %pick_blocks.9 = bf16[25,64,256]{2,1,0:T(8,128)(2,1)S(1)} custom-call(s32[1]{0:T(128)} %bitcast.8.position_ref, s32[8,200]{1,0:T(8,128)S(1)} %bitcast.19, bf16[64,64,256]{2,1,0:T(8,128)(2,1)} %bitcast.9.rest_0_.refs_0_, bf16[25,64,256]{2,1,0:T(8,128)(2,1)S(1)} %collective-permute-done.7.rest_1_.rest_4_), custom_call_target="tpu_custom_call" | custom-call | flops 1724999936 | tf_op jit(solution)/shard_map/pick_blocks/pallas_call | solution.py:103
  93.8 3.6 %collective-permute-start.8 = (bf16[25,64,256]{2,1,0:T(8,128)(2,1)S(1)}, bf16[25,64,256]{2,1,0:T(8,128)(2,1)S(1)}, u32[]{:S(2)}, u32[]{:S(2)}) collective-permute-start(bf16[25,64,256]{2,1,0:T(8,128)(2,1)S(1)} %pick_blocks.9), channel_id=1, source_target_pairs={{4,8},{5,9},{6,10},{7,11},{8,4},{9,5},{10,6},{11,7},{20,24},{21,25... | collective-permute-start | bytes 2457608 | tf_op jit(solution)/shard_map/ppermute | solution.py:545
  97.4 4.1 %collective-permute-done.4.rest_1_.rest_5_ = bf16[25,64,256]{2,1,0:T(8,128)(2,1)S(1)} collective-permute-done((bf16[25,64,256]{2,1,0:T(8,128)(2,1)S(1)}, bf16[25,64,256]{2,1,0:T(8,128)(2,1)S(1)}, u32[]{:S(2)}, u32[]{:S(2)}) %collective-permute-start.4) | collective-permute-done | bytes 819232 | tf_op jit(solution)/shard_map/ppermute | solution.py:545
  101.6 0.9 pick_blocks.7
  102.5 2.4 %collective-permute-start.5 = (bf16[25,64,256]{2,1,0:T(8,128)(2,1)S(1)}, bf16[25,64,256]{2,1,0:T(8,128)(2,1)S(1)}, u32[]{:S(2)}, u32[]{:S(2)}) collective-permute-start(bf16[25,64,256]{2,1,0:T(8,128)(2,1)S(1)} %pick_blocks.7), channel_id=1, source_target_pairs={{4,8},{5,9},{6,10},{7,11},{8,4},{9,5},{10,6},{11,7},{20,24},{21,25... | collective-permute-start | bytes 2457608 | tf_op jit(solution)/shard_map/ppermute | solution.py:545
  104.9 2.7 %collective-permute-start.3 = (bf16[25,64,256]{2,1,0:T(8,128)(2,1)S(1)}, bf16[25,64,256]{2,1,0:T(8,128)(2,1)S(1)}, u32[]{:S(2)}, u32[]{:S(2)}) collective-permute-start(bf16[25,64,256]{2,1,0:T(8,128)(2,1)S(1)} %collective-permute-done.2.rest_1_), channel_id=1, source_target_pairs={{8,12},{9,13},{10,14},{11,15},{4,0},{5,1},{6,2},{7,3},{24,28},{25,... | collective-permute-start | bytes 2457608 | tf_op jit(solution)/shard_map/ppermute | solution.py:545
  107.6 15.3 %attend_blocks.3 = (bf16[64,64,256]{2,1,0:T(8,128)(2,1)}, bf16[367,64,256]{2,1,0:T(8,128)(2,1)}) custom-call(s32[2]{0:T(128)S(1)} %pad_add_fusion.1.rest_2_.range_ref, s32[64]{0:T(128)S(1)} %select_reduce_fusion.2.rest_0_.order_ref, s32[192]{0:T(256)S(1)} %get-tuple-element.36.rest_1_.table_ref, ...), custom_call_target="tpu_custom_call", output_to_operand_aliasing={{1}: (13, {})} | custom-call | flops 20700000256 | tf_op jit(solution)/shard_map/attend_blocks/pallas_call | solution.py:446
  123.0 11.8 %attend_blocks.4 = (bf16[64,64,256]{2,1,0:T(8,128)(2,1)}, bf16[367,64,256]{2,1,0:T(8,128)(2,1)}) custom-call(s32[2]{0:T(128)S(1)} %pad_add_fusion.2.rest_3_.range_ref, s32[64]{0:T(128)S(1)} %select_reduce_fusion.2.rest_0_.order_ref, s32[192]{0:T(256)S(1)} %get-tuple-element.36.rest_1_.table_ref, ...), custom_call_target="tpu_custom_call", output_to_operand_aliasing={{1}: (12, {}), {0}: (13, {})} | custom-call | flops 20700000256 | tf_op jit(solution)/shard_map/attend_blocks/pallas_call | solution.py:446
  134.8 15.0 %attend_blocks.5 = (bf16[64,64,256]{2,1,0:T(8,128)(2,1)}, bf16[367,64,256]{2,1,0:T(8,128)(2,1)}) custom-call(s32[2]{0:T(128)S(1)} %pad_add_fusion.rest_4_.range_ref, s32[64]{0:T(128)S(1)} %select_reduce_fusion.2.rest_0_.order_ref, s32[192]{0:T(256)S(1)} %get-tuple-element.36.rest_1_.table_ref, ...), custom_call_target="tpu_custom_call", output_to_operand_aliasing={{1}: (12, {}), {0}: (13, {})} | custom-call | flops 20700000256 | tf_op jit(solution)/shard_map/attend_blocks/pallas_call | solution.py:446
  (36 shorter events, 0.9 us)
Async XLA Ops:
  0.0 1.6 %copy-start.1 = (bf16[4096,256]{1,0:T(8,128)(2,1)S(1)}, bf16[4096,256]{1,0:T(8,128)(2,1)}, u32[]{:S(2)}) copy-start(bf16[4096,256]{1,0:T(8,128)(2,1)} %features_ref.1) | copy-start | bytes 6291460
  1.6 0.7 copy-start.4
  2.3 7.1 %copy-start.7 = (s32[64,3]{0,1:T(4,128)S(1)}, s32[64,3]{0,1:T(4,128)}, u32[]{:S(2)}) copy-start(s32[64,3]{0,1:T(4,128)} %param.10) | copy-start | bytes 2308
  2.3 20.4 %copy-start.6 = (bf16[256,256]{1,0:T(8,128)(2,1)S(1)}, bf16[256,256]{1,0:T(8,128)(2,1)}, u32[]{:S(2)}) copy-start(bf16[256,256]{1,0:T(8,128)(2,1)} %param.11) | copy-start | bytes 393220
  2.3 20.5 %copy-start.5 = (bf16[256,256]{1,0:T(8,128)(2,1)S(1)}, bf16[256,256]{1,0:T(8,128)(2,1)}, u32[]{:S(2)}) copy-start(bf16[256,256]{1,0:T(8,128)(2,1)} %param.13) | copy-start | bytes 393220
  2.3 20.6 %copy-start = (bf16[256,256]{1,0:T(8,128)(2,1)S(1)}, bf16[256,256]{1,0:T(8,128)(2,1)}, u32[]{:S(2)}) copy-start(bf16[256,256]{1,0:T(8,128)(2,1)} %key_w_ref.1) | copy-start | bytes 393220
  7.4 50.0 %collective-permute-start.1 = (bf16[64,64,256]{2,1,0:T(8,128)(2,1)}, bf16[64,64,256]{2,1,0:T(8,128)(2,1)S(1)}, u32[]{:S(2)}, u32[]{:S(2)}) collective-permute-start(bf16[64,64,256]{2,1,0:T(8,128)(2,1)} %bitcast.9.rest_0_.refs_0_), channel_id=1, source_target_pairs={{0,2},{1,3},{2,0},{3,1},{4,6},{5,7},{6,4},{7,5},{8,10},{9,11},{10,... | collective-permute-start | bytes 6291464 | tf_op jit(solution)/shard_map/ppermute | solution.py:545
  8.9 50.6 %collective-permute-start = (bf16[64,64,256]{2,1,0:T(8,128)(2,1)}, bf16[64,64,256]{2,1,0:T(8,128)(2,1)}, u32[]{:S(2)}, u32[]{:S(2)}) collective-permute-start(bf16[64,64,256]{2,1,0:T(8,128)(2,1)} %bitcast.9.rest_0_.refs_0_), channel_id=1, source_target_pairs={{0,8},{1,9},{2,10},{3,11},{4,0},{5,1},{6,2},{7,3},{8,12},{9,13},{1... | collective-permute-start | bytes 6291464 | tf_op jit(solution)/shard_map/ppermute | solution.py:545
  10.6 46.8 %all-to-all-start = ((s32[8,1,200]{2,1,0:T(1,128)}), s32[8,1,200]{2,1,0:T(1,128)S(1)}, u32[]{:S(2)}, u32[]{:S(2)}) async-start(s32[8,1,200]{2,1,0:T(1,128)} %broadcast_in_dim.108), calls=%async_computation | async-start | bytes 16384 | tf_op jit(solution)/shard_map/all_to_all | solution.py:560
  61.4 18.9 %collective-permute-start.2 = (bf16[25,64,256]{2,1,0:T(8,128)(2,1)S(1)}, bf16[25,64,256]{2,1,0:T(8,128)(2,1)S(1)}, u32[]{:S(2)}, u32[]{:S(2)}) collective-permute-start(bf16[25,64,256]{2,1,0:T(8,128)(2,1)S(1)} %pick_blocks.6), channel_id=1, source_target_pairs={{0,2},{1,3},{2,0},{3,1},{4,6},{5,7},{6,4},{7,5},{8,10},{9,11},{10,... | collective-permute-start | bytes 2457608 | tf_op jit(solution)/shard_map/ppermute | solution.py:545
  62.9 29.1 %collective-permute-start.7 = (bf16[25,64,256]{2,1,0:T(8,128)(2,1)S(1)}, bf16[25,64,256]{2,1,0:T(8,128)(2,1)S(1)}, u32[]{:S(2)}, u32[]{:S(2)}) collective-permute-start(bf16[25,64,256]{2,1,0:T(8,128)(2,1)S(1)} %get-tuple-element.26), channel_id=1, source_target_pairs={{0,4},{1,5},{2,6},{3,7},{4,12},{5,13},{6,14},{7,15},{8,0},{9,1},{1... | collective-permute-start | bytes 2457608 | tf_op jit(solution)/shard_map/ppermute | solution.py:545
  65.3 36.3 %collective-permute-start.4 = (bf16[25,64,256]{2,1,0:T(8,128)(2,1)S(1)}, bf16[25,64,256]{2,1,0:T(8,128)(2,1)S(1)}, u32[]{:S(2)}, u32[]{:S(2)}) collective-permute-start(bf16[25,64,256]{2,1,0:T(8,128)(2,1)S(1)} %get-tuple-element.24.rest_1_), channel_id=1, source_target_pairs={{0,4},{1,5},{2,6},{3,7},{4,12},{5,13},{6,14},{7,15},{8,0},{9,1},{1... | collective-permute-start | bytes 2457608 | tf_op jit(solution)/shard_map/ppermute | solution.py:545
  82.4 25.1 %collective-permute-start.9 = (bf16[25,64,256]{2,1,0:T(8,128)(2,1)S(1)}, bf16[25,64,256]{2,1,0:T(8,128)(2,1)S(1)}, u32[]{:S(2)}, u32[]{:S(2)}) collective-permute-start(bf16[25,64,256]{2,1,0:T(8,128)(2,1)S(1)} %get-tuple-element.27), channel_id=1, source_target_pairs={{0,2},{1,3},{2,0},{3,1},{4,6},{5,7},{6,4},{7,5},{8,10},{9,11},{10,... | collective-permute-start | bytes 2457608 | tf_op jit(solution)/shard_map/ppermute | solution.py:545
  89.0 34.0 %collective-permute-start.6 = (bf16[25,64,256]{2,1,0:T(8,128)(2,1)S(1)}, bf16[25,64,256]{2,1,0:T(8,128)(2,1)S(1)}, u32[]{:S(2)}, u32[]{:S(2)}) collective-permute-start(bf16[25,64,256]{2,1,0:T(8,128)(2,1)S(1)} %get-tuple-element.25), channel_id=1, source_target_pairs={{8,12},{9,13},{10,14},{11,15},{4,0},{5,1},{6,2},{7,3},{24,28},{25,... | collective-permute-start | bytes 2457608 | tf_op jit(solution)/shard_map/ppermute | solution.py:545
  93.8 13.8 %copy-start.2 = (bf16[256,256]{1,0:T(8,128)(2,1)S(1)}, bf16[256,256]{1,0:T(8,128)(2,1)}, u32[]{:S(2)}) copy-start(bf16[256,256]{1,0:T(8,128)(2,1)} %rest_1_.5) | copy-start | bytes 393220
  93.8 13.8 %copy-start.3 = (bf16[256,256]{1,0:T(8,128)(2,1)S(1)}, bf16[256,256]{1,0:T(8,128)(2,1)}, u32[]{:S(2)}) copy-start(bf16[256,256]{1,0:T(8,128)(2,1)} %rest_2_.5) | copy-start | bytes 393220
  93.8 29.1 %collective-permute-start.8 = (bf16[25,64,256]{2,1,0:T(8,128)(2,1)S(1)}, bf16[25,64,256]{2,1,0:T(8,128)(2,1)S(1)}, u32[]{:S(2)}, u32[]{:S(2)}) collective-permute-start(bf16[25,64,256]{2,1,0:T(8,128)(2,1)S(1)} %pick_blocks.9), channel_id=1, source_target_pairs={{4,8},{5,9},{6,10},{7,11},{8,4},{9,5},{10,6},{11,7},{20,24},{21,25... | collective-permute-start | bytes 2457608 | tf_op jit(solution)/shard_map/ppermute | solution.py:545
  102.5 32.3 %collective-permute-start.5 = (bf16[25,64,256]{2,1,0:T(8,128)(2,1)S(1)}, bf16[25,64,256]{2,1,0:T(8,128)(2,1)S(1)}, u32[]{:S(2)}, u32[]{:S(2)}) collective-permute-start(bf16[25,64,256]{2,1,0:T(8,128)(2,1)S(1)} %pick_blocks.7), channel_id=1, source_target_pairs={{4,8},{5,9},{6,10},{7,11},{8,4},{9,5},{10,6},{11,7},{20,24},{21,25... | collective-permute-start | bytes 2457608 | tf_op jit(solution)/shard_map/ppermute | solution.py:545
  104.9 29.9 %collective-permute-start.3 = (bf16[25,64,256]{2,1,0:T(8,128)(2,1)S(1)}, bf16[25,64,256]{2,1,0:T(8,128)(2,1)S(1)}, u32[]{:S(2)}, u32[]{:S(2)}) collective-permute-start(bf16[25,64,256]{2,1,0:T(8,128)(2,1)S(1)} %collective-permute-done.2.rest_1_), channel_id=1, source_target_pairs={{8,12},{9,13},{10,14},{11,15},{4,0},{5,1},{6,2},{7,3},{24,28},{25,... | collective-permute-start | bytes 2457608 | tf_op jit(solution)/shard_map/ppermute | solution.py:545

commit v19 on v18

--- a/solution.py
+++ b/solution.py
@@ -46,16 +46,17 @@
     lane = 128
     columns = lax.broadcasted_iota(jnp.int32, (lane, rows), 1)
     for walker in range(walkers):
-        features = features_ref[walker * rows : (walker + 1) * rows, :]
+        here = pl.ds(walker * rows, rows)
+        one_hots = []
         for part in range(rows // lane):
             chosen = assignment_ref[walker, :, part * lane : (part + 1) * lane] & (rows - 1)
             chosen = jnp.broadcast_to(chosen, (lane, lane)).T
             chosen = jnp.concatenate([chosen] * (rows // lane), axis=1)
-            one_hot = jnp.where(chosen == columns, 1.0, 0.0).astype(jnp.bfloat16)
-            placed = jnp.dot(one_hot, features, preferred_element_type=jnp.float32)
-            here = pl.ds(walker * rows + part * lane, lane)
-            placed_ref[here, :] = placed.astype(jnp.bfloat16)
-            normed_ref[here, :] = layer_norm(placed).astype(jnp.bfloat16)
+            one_hots.append(jnp.where(chosen == columns, 1.0, 0.0).astype(jnp.bfloat16))
+        one_hot = jnp.concatenate(one_hots, axis=0)
+        placed = jnp.dot(one_hot, features_ref[here, :], preferred_element_type=jnp.float32)
+        placed_ref[here, :] = placed.astype(jnp.bfloat16)
+        normed_ref[here, :] = layer_norm(placed).astype(jnp.bfloat16)
 
 
 def place(features, assignment):
@@ -371,28 +372,30 @@
     values = [both[block, :, width:].T for block in range(STEP)]
 
     def scores_of(block, pair):
-        first = pair * 2 * span
-        return jnp.dot(
-            both[block, :, first : first + 2 * span],
-            tiles_of(query_ref[block], first, span),
-            preferred_element_type=jnp.float32,
-        )
+        return [
+            jnp.dot(
+                both[block, :, t * span : (t + 1) * span],
+                query_ref[block, t * span : (t + 1) * span, :],
+                preferred_element_type=jnp.float32,
+            )
+            for t in (2 * pair, 2 * pair + 1)
+        ]
 
     def weights_of(block, pair, scores):
-        own_top = jnp.concatenate(
-            [stats_ref[block, t : t + 1, :] for t in (2 * pair, 2 * pair + 1)], axis=1
-        )
-        top = jnp.maximum(jnp.max(scores, axis=0, keepdims=True), own_top)
-        weights = jnp.exp2((scores - top).astype(jnp.bfloat16))
-        return weights, jnp.exp2(own_top - top)
+        weights, factors = [], []
+        for t, score in zip((2 * pair, 2 * pair + 1), scores, strict=True):
+            own_top = stats_ref[block, t : t + 1, :]
+            top = jnp.maximum(jnp.max(score, axis=0, keepdims=True), own_top)
+            weights.append(jnp.exp2((score - top).astype(jnp.bfloat16)))
+            factors.append(jnp.exp2(own_top - top))
+        return weights, factors
 
     def products_of(block, pair, weights, own_factor):
         for half in range(2):
             t = pair * 2 + half
-            here = slice(half * tile, (half + 1) * tile)
             lifted = jnp.concatenate([values[block][t * span : (t + 1) * span], ones], axis=0)
-            product = jnp.dot(lifted, weights[:, here], preferred_element_type=jnp.float32)
-            yield block, t, product, own_factor[:, here]
+            product = jnp.dot(lifted, weights[half], preferred_element_type=jnp.float32)
+            yield block, t, product, own_factor[half]
 
     def scaled(block, t, product, own_factor):
         own_total = stats_ref[block, tiles + t : tiles + t + 1, :] * own_factor
@@ -523,10 +526,9 @@
     return lambda position: partner(route(position))
 
 
-SECOND_PLAN = ((0, source, itself), (1, source, partner))
+FIRST_PLAN = ((0, source, itself), (1, source, partner), (2, crossed(onward), source))
 MIDDLE_PLAN = ((0, opposite, itself),)
 MIDDLE_CROSS_PLAN = ((0, opposite, partner),)
-ON_PLAN = ((0, crossed(onward), source),)
 NEAR_PLAN = ((0, partner, source), (0, onward, source))
 
 
@@ -604,21 +606,20 @@
     own = own_part(normed, w_query, w_key, w_value, cluster, (order, table, *phases, weights[0]))
     beside = moved(blocks, swap)
     passed = moved(blocks, first_moves)
-    second_pick, cross_pick = pick(
-        at_position, wanted, (blocks, beside), SECOND_PLAN, after=own[2:]
-    )
-    second = moved(second_pick, second_moves)
-    second_cross = moved(cross_pick, second_moves)
-    (on,) = pick(at_position, wanted, (passed,), ON_PLAN, after=(cross_pick,))
+    second, second_cross, on = pick(
+        at_position, wanted, (blocks, beside, passed), FIRST_PLAN, after=own[2:]
+    )
+    second = moved(second, second_moves)
+    second_cross = moved(second_cross, second_moves)
     on = moved(on, swap)
-    (middle,) = pick(at_position, wanted, (blocks,), MIDDLE_PLAN, after=(second,))
-    middle = moved(middle, middle_moves)
+    (middle_pick,) = pick(at_position, wanted, (blocks,), MIDDLE_PLAN, after=(second,))
+    middle = moved(middle_pick, middle_moves)
     near, outward = pick(at_position, wanted, (passed,), NEAR_PLAN, after=(on,))
     near = moved(near, swap)
     outward = moved(outward, outward_moves)
     on = moved(on, outward_moves)
     (middle_cross,) = pick(
-        at_position, wanted, (beside,), MIDDLE_CROSS_PLAN, after=(second_cross,)
+        at_position, wanted, (beside,), MIDDLE_CROSS_PLAN, after=(second_cross, middle_pick)
     )
     middle_cross = moved(middle_cross, middle_moves)
 

time: 153 us -> 149 us (0.974)
  Pallas kernels: 90.6 us -> 87 us
  waiting for transfers between devices: 23.5 us -> 25.1 us
    pallas_call x1, Pallas kernels: 5.09 us -> 3.53 us  [place(): pl.pallas_call(place_kernel, grid=(walkers // 2,), in_specs=[local, pl.Bl...]
    pallas_call x5 -> x4, Pallas kernels: 8.86 us -> 7.88 us  [pick(): pl.pallas_call(functools.partial(pick_kernel, plan=plan, capacity=capacit...]
  transfers between devices with their start and end apart: 11 -> 11, of which waited for: 3 -> 3; matrix products, arithmetic and copies ran while one was open for 2% -> 2% of each run, Pallas kernels for 46% -> 44%
where the time goes in v19:
time: 149 us; the launch traced here: 147 us
  Pallas kernels  87 us (58%)
  waiting for transfers between devices  25.1 us (17%)
  starting transfers between devices  24.4 us (16%)
  between operations  5.7 us (4%)
  local copies, waits for them, and re-layouts  3.39 us (2%)
  other arithmetic  1.64 us (1%)
    pallas_call x3, Pallas kernels, attend(): pl.pallas_call(kernel, in_specs=in_specs, out_specs=[hbm, hbm], out_shape...  42.1 us
    pallas_call x1, Pallas kernels, own_part(): pl.pallas_call(functools.partial(own_kernel, head_width=width // HEADS),...  28.5 us
    ppermute x10, waiting for transfers between devices, moved(): return lax.ppermute(x, 'elec', pairs_of)  20 us
    ppermute x10, starting transfers between devices, moved(): return lax.ppermute(x, 'elec', pairs_of)  18.6 us
    pallas_call x4, Pallas kernels, pick(): pl.pallas_call(functools.partial(pick_kernel, plan=plan, capacity=capacit...  7.88 us
    all_to_all x1, starting transfers between devices, body(): lax.all_to_all(jnp.broadcast_to(tables[None], (SPAN, SPAN * capacity)), '...  5.81 us
    all_to_all x1, waiting for transfers between devices, body(): lax.all_to_all(jnp.broadcast_to(tables[None], (SPAN, SPAN * capacity)), '...  5.09 us
    pallas_call x1, Pallas kernels, collect(): pl.pallas_call(functools.partial(collect_kernel, places=places), in_specs...  5.02 us
  transfers between devices with their start and end apart: 11, of which 3 were waited for; matrix products, arithmetic and copies ran while one was open for 2% of the time, Pallas kernels for 44%

profile of v19, /device:TPU:8, one launch (start us, length us, event | category | flops | bytes accessed | tf_op | source)
XLA Modules:
  0.0 147.3 jit_solution(7366655626955061353)
XLA Ops:
  0.0 1.6 %copy-done.1 = bf16[4096,256]{1,0:T(8,128)(2,1)S(1)} copy-done((bf16[4096,256]{1,0:T(8,128)(2,1)S(1)}, bf16[4096,256]{1,0:T(8,128)(2,1)}, u32[]{:S(2)}) %copy-start.1) | copy-done | bytes 2097176
  1.6 0.7 copy-done.4
  2.3 3.5 %place_rows.1 = (bf16[4096,256]{1,0:T(8,128)(2,1)}, bf16[4096,256]{1,0:T(8,128)(2,1)S(1)}) custom-call(bf16[4096,256]{1,0:T(8,128)(2,1)S(1)} %copy-done.1, s32[8,1,512]{2,1,0:T(1,128)S(1)} %bitcast.25), custom_call_target="tpu_custom_call" | custom-call | flops 6899999744 | tf_op jit(solution)/shard_map/place_rows/pallas_call | solution.py:67
  5.8 2.0 %collective-permute-start = (bf16[64,64,256]{2,1,0:T(8,128)(2,1)S(1)}, bf16[64,64,256]{2,1,0:T(8,128)(2,1)}, u32[]{:S(2)}, u32[]{:S(2)}) collective-permute-start(bf16[64,64,256]{2,1,0:T(8,128)(2,1)S(1)} %bitcast.15), channel_id=1, source_target_pairs={{0,2},{1,3},{2,0},{3,1},{4,6},{5,7},{6,4},{7,5},{8,10},{9,11},{10,... | collective-permute-start | bytes 6291464 | tf_op jit(solution)/shard_map/ppermute | solution.py:547
  7.9 0.1 reshape.148
  8.1 0.2 select_reduce_fusion.1
  8.3 0.1 select_reduce_fusion
  8.5 0.6 broadcast_in_dim.108
  9.1 5.8 %all-to-all-start = ((s32[8,1,200]{2,1,0:T(1,128)}), s32[8,1,200]{2,1,0:T(1,128)S(1)}, u32[]{:S(2)}, u32[]{:S(2)}) async-start(s32[8,1,200]{2,1,0:T(1,128)} %broadcast_in_dim.108), calls=%async_computation | async-start | bytes 16384 | tf_op jit(solution)/shard_map/all_to_all | solution.py:562
  14.9 0.2 select_reduce_fusion.3
  15.1 0.7 fusion.14
  21.1 0.1 select_reduce_fusion.2.rest_0_.order_ref
  21.7 28.5 %own_blocks.1 = (bf16[64,256,256]{2,1,0:T(8,128)(2,1)}, bf16[64,256,256]{2,1,0:T(8,128)(2,1)}, f32[64,8,256]{2,1,0:T(8,128)S(1)}) custom-call(bf16[4096,256]{1,0:T(8,128)(2,1)S(1)} %get-tuple-element.20.normed_ref, bf16[256,256]{1,0:T(8,128)(2,1)S(1)} %bitcast.19, bf16[256,256]{1,0:T(8,128)(2,1)S(1)} %copy-done, bf16[256,256]{1,0:T(8,128)(2,1)S(1)} %bitcast.20, ...), custom_call_target="tpu_custom_call" | custom-call | flops 23000000512 | tf_op jit(solution)/shard_map/own_blocks/pallas_call | solution.py:178
  50.2 5.1 %all-to-all-done = s32[8,1,200]{2,1,0:T(1,128)S(1)} async-done(((s32[8,1,200]{2,1,0:T(1,128)}), s32[8,1,200]{2,1,0:T(1,128)S(1)}, u32[]{:S(2)}, u32[]{:S(2)}) %all-to-all-start) | async-done | bytes 6432 | tf_op jit(solution)/shard_map/all_to_all | solution.py:562
  55.3 3.0 %pick_blocks.4 = (bf16[25,64,256]{2,1,0:T(8,128)(2,1)S(1)}, bf16[25,64,256]{2,1,0:T(8,128)(2,1)S(1)}, bf16[25,64,256]{2,1,0:T(8,128)(2,1)S(1)}) custom-call(s32[1]{0:T(128)} %bitcast.8.position_ref, s32[8,200]{1,0:T(8,128)S(1)} %bitcast.21, bf16[64,64,256]{2,1,0:T(8,128)(2,1)S(1)} %bitcast.16, ...), custom_call_target="tpu_custom_call" | custom-call | flops 1724999936 | tf_op jit(solution)/shard_map/pick_blocks/pallas_call | solution.py:104
  58.3 0.6 collective-permute-start.2
  59.0 2.4 %collective-permute-start.5 = (bf16[25,64,256]{2,1,0:T(8,128)(2,1)S(1)}, bf16[25,64,256]{2,1,0:T(8,128)(2,1)S(1)}, u32[]{:S(2)}, u32[]{:S(2)}) collective-permute-start(bf16[25,64,256]{2,1,0:T(8,128)(2,1)S(1)} %get-tuple-element.27), channel_id=1, source_target_pairs={{0,4},{1,5},{2,6},{3,7},{4,12},{5,13},{6,14},{7,15},{8,0},{9,1},{1... | collective-permute-start | bytes 2457608 | tf_op jit(solution)/shard_map/ppermute | solution.py:547
  61.3 1.0 collective-permute-start.4
  62.3 15.3 %collective-permute-done.2.rest_1_ = bf16[25,64,256]{2,1,0:T(8,128)(2,1)S(1)} collective-permute-done((bf16[25,64,256]{2,1,0:T(8,128)(2,1)S(1)}, bf16[25,64,256]{2,1,0:T(8,128)(2,1)S(1)}, u32[]{:S(2)}, u32[]{:S(2)}) %collective-permute-start.2) | collective-permute-done | bytes 819232 | tf_op jit(solution)/shard_map/ppermute | solution.py:547
  77.6 2.1 %pick_blocks.7 = (bf16[25,64,256]{2,1,0:T(8,128)(2,1)S(1)}, bf16[25,64,256]{2,1,0:T(8,128)(2,1)S(1)}) custom-call(s32[1]{0:T(128)} %bitcast.8.position_ref, s32[8,200]{1,0:T(8,128)S(1)} %bitcast.22, bf16[64,64,256]{2,1,0:T(8,128)(2,1)} %collective-permute-done.1.rest_2_.rest_0_.refs_1_, bf16[25,64,256]{2,1,0:T(8,128)(2,1)S(1)} %collective-permute-done.2.rest_1_), custom_call_target="tpu_custom_call" | custom-call | flops 1724999936 | tf_op jit(solution)/shard_map/pick_blocks/pallas_call | solution.py:104
  79.7 0.6 collective-permute-start.9
  80.3 5.0 %collect_blocks.1.rest_6_ = bf16[367,64,256]{2,1,0:T(8,128)(2,1)} custom-call(bf16[64,64,256]{2,1,0:T(8,128)(2,1)S(1)} %bitcast.17, bf16[64,64,256]{2,1,0:T(8,128)(2,1)} %collective-permute-done.1.rest_2_.rest_0_.refs_1_, bf16[64,64,256]{2,1,0:T(8,128)(2,1)} %collective-permute-done.rest_1_.rest_0_.refs_2_), custom_call_target="tpu_custom_call" | custom-call | flops 4600000000 | tf_op jit(solution)/shard_map/collect_blocks/pallas_call | solution.py:226
  85.3 3.4 %collective-permute-start.7 = (bf16[25,64,256]{2,1,0:T(8,128)(2,1)S(1)}, bf16[25,64,256]{2,1,0:T(8,128)(2,1)S(1)}, u32[]{:S(2)}, u32[]{:S(2)}) collective-permute-start(bf16[25,64,256]{2,1,0:T(8,128)(2,1)S(1)} %get-tuple-element.28), channel_id=1, source_target_pairs={{8,12},{9,13},{10,14},{11,15},{4,0},{5,1},{6,2},{7,3},{24,28},{25,... | collective-permute-start | bytes 2457608 | tf_op jit(solution)/shard_map/ppermute | solution.py:547
  88.7 0.9 pick_blocks.5.rest_2_
  89.7 3.2 %collective-permute-start.8 = (bf16[25,64,256]{2,1,0:T(8,128)(2,1)S(1)}, bf16[25,64,256]{2,1,0:T(8,128)(2,1)S(1)}, u32[]{:S(2)}, u32[]{:S(2)}) collective-permute-start(bf16[25,64,256]{2,1,0:T(8,128)(2,1)S(1)} %pick_blocks.5.rest_2_), channel_id=1, source_target_pairs={{4,8},{5,9},{6,10},{7,11},{8,4},{9,5},{10,6},{11,7},{20,24},{21,25... | collective-permute-start | bytes 2457608 | tf_op jit(solution)/shard_map/ppermute | solution.py:547
  92.9 4.8 %collective-permute-done.4.rest_1_.rest_5_ = bf16[25,64,256]{2,1,0:T(8,128)(2,1)S(1)} collective-permute-done((bf16[25,64,256]{2,1,0:T(8,128)(2,1)S(1)}, bf16[25,64,256]{2,1,0:T(8,128)(2,1)S(1)}, u32[]{:S(2)}, u32[]{:S(2)}) %collective-permute-start.4) | collective-permute-done | bytes 819232 | tf_op jit(solution)/shard_map/ppermute | solution.py:547
  97.6 1.9 %pick_blocks.6 = bf16[25,64,256]{2,1,0:T(8,128)(2,1)S(1)} custom-call(s32[1]{0:T(128)} %bitcast.8.position_ref, s32[8,200]{1,0:T(8,128)S(1)} %bitcast.24, bf16[64,64,256]{2,1,0:T(8,128)(2,1)} %collective-permute-done.rest_1_.rest_0_.refs_2_, bf16[25,64,256]{2,1,0:T(8,128)(2,1)S(1)} %collective-permute-done.4.rest_1_.rest_5_, ...), custom_call_target="tpu_custom_call" | custom-call | flops 1724999936 | tf_op jit(solution)/shard_map/pick_blocks/pallas_call | solution.py:104
  99.5 2.8 %collective-permute-start.6 = (bf16[25,64,256]{2,1,0:T(8,128)(2,1)S(1)}, bf16[25,64,256]{2,1,0:T(8,128)(2,1)S(1)}, u32[]{:S(2)}, u32[]{:S(2)}) collective-permute-start(bf16[25,64,256]{2,1,0:T(8,128)(2,1)S(1)} %pick_blocks.6), channel_id=1, source_target_pairs={{4,8},{5,9},{6,10},{7,11},{8,4},{9,5},{10,6},{11,7},{20,24},{21,25... | collective-permute-start | bytes 2457608 | tf_op jit(solution)/shard_map/ppermute | solution.py:547
  102.3 2.7 %collective-permute-start.3 = (bf16[25,64,256]{2,1,0:T(8,128)(2,1)S(1)}, bf16[25,64,256]{2,1,0:T(8,128)(2,1)S(1)}, u32[]{:S(2)}, u32[]{:S(2)}) collective-permute-start(bf16[25,64,256]{2,1,0:T(8,128)(2,1)S(1)} %collective-permute-done.2.rest_1_), channel_id=1, source_target_pairs={{8,12},{9,13},{10,14},{11,15},{4,0},{5,1},{6,2},{7,3},{24,28},{25,... | collective-permute-start | bytes 2457608 | tf_op jit(solution)/shard_map/ppermute | solution.py:547
  105.0 15.3 %attend_blocks.3 = (bf16[64,64,256]{2,1,0:T(8,128)(2,1)}, bf16[367,64,256]{2,1,0:T(8,128)(2,1)}) custom-call(s32[2]{0:T(128)S(1)} %pad_add_fusion.1.rest_2_.range_ref, s32[64]{0:T(128)S(1)} %select_reduce_fusion.2.rest_0_.order_ref, s32[192]{0:T(256)S(1)} %get-tuple-element.38.rest_1_.table_ref, ...), custom_call_target="tpu_custom_call", output_to_operand_aliasing={{1}: (13, {})} | custom-call | flops 20700000256 | tf_op jit(solution)/shard_map/attend_blocks/pallas_call | solution.py:449
  120.3 11.8 %attend_blocks.4 = (bf16[64,64,256]{2,1,0:T(8,128)(2,1)}, bf16[367,64,256]{2,1,0:T(8,128)(2,1)}) custom-call(s32[2]{0:T(128)S(1)} %pad_add_fusion.2.rest_3_.range_ref, s32[64]{0:T(128)S(1)} %select_reduce_fusion.2.rest_0_.order_ref, s32[192]{0:T(256)S(1)} %get-tuple-element.38.rest_1_.table_ref, ...), custom_call_target="tpu_custom_call", output_to_operand_aliasing={{1}: (12, {}), {0}: (13, {})} | custom-call | flops 20700000256 | tf_op jit(solution)/shard_map/attend_blocks/pallas_call | solution.py:449
  132.1 15.0 %attend_blocks.5 = (bf16[64,64,256]{2,1,0:T(8,128)(2,1)}, bf16[367,64,256]{2,1,0:T(8,128)(2,1)}) custom-call(s32[2]{0:T(128)S(1)} %pad_add_fusion.rest_4_.range_ref, s32[64]{0:T(128)S(1)} %select_reduce_fusion.2.rest_0_.order_ref, s32[192]{0:T(256)S(1)} %get-tuple-element.38.rest_1_.table_ref, ...), custom_call_target="tpu_custom_call", output_to_operand_aliasing={{1}: (12, {}), {0}: (13, {})} | custom-call | flops 20700000256 | tf_op jit(solution)/shard_map/attend_blocks/pallas_call | solution.py:449
  (35 shorter events, 0.7 us)
Async XLA Ops:
  0.0 1.6 %copy-start.1 = (bf16[4096,256]{1,0:T(8,128)(2,1)S(1)}, bf16[4096,256]{1,0:T(8,128)(2,1)}, u32[]{:S(2)}) copy-start(bf16[4096,256]{1,0:T(8,128)(2,1)} %features_ref.1) | copy-start | bytes 6291460
  1.6 0.7 copy-start.4
  2.3 5.5 %copy-start.7 = (s32[64,3]{0,1:T(4,128)S(1)}, s32[64,3]{0,1:T(4,128)}, u32[]{:S(2)}) copy-start(s32[64,3]{0,1:T(4,128)} %param.10) | copy-start | bytes 2308
  2.3 19.0 %copy-start.6 = (bf16[256,256]{1,0:T(8,128)(2,1)S(1)}, bf16[256,256]{1,0:T(8,128)(2,1)}, u32[]{:S(2)}) copy-start(bf16[256,256]{1,0:T(8,128)(2,1)} %param.11) | copy-start | bytes 393220
  2.3 19.2 %copy-start.5 = (bf16[256,256]{1,0:T(8,128)(2,1)S(1)}, bf16[256,256]{1,0:T(8,128)(2,1)}, u32[]{:S(2)}) copy-start(bf16[256,256]{1,0:T(8,128)(2,1)} %param.13) | copy-start | bytes 393220
  2.3 19.3 %copy-start = (bf16[256,256]{1,0:T(8,128)(2,1)S(1)}, bf16[256,256]{1,0:T(8,128)(2,1)}, u32[]{:S(2)}) copy-start(bf16[256,256]{1,0:T(8,128)(2,1)} %key_w_ref.1) | copy-start | bytes 393220
  5.8 49.5 %collective-permute-start.1 = (bf16[64,64,256]{2,1,0:T(8,128)(2,1)S(1)}, bf16[64,64,256]{2,1,0:T(8,128)(2,1)}, u32[]{:S(2)}, u32[]{:S(2)}) collective-permute-start(bf16[64,64,256]{2,1,0:T(8,128)(2,1)S(1)} %bitcast.14), channel_id=1, source_target_pairs={{0,8},{1,9},{2,10},{3,11},{4,0},{5,1},{6,2},{7,3},{8,12},{9,13},{1... | collective-permute-start | bytes 6291464 | tf_op jit(solution)/shard_map/ppermute | solution.py:547
  5.8 49.5 %collective-permute-start = (bf16[64,64,256]{2,1,0:T(8,128)(2,1)S(1)}, bf16[64,64,256]{2,1,0:T(8,128)(2,1)}, u32[]{:S(2)}, u32[]{:S(2)}) collective-permute-start(bf16[64,64,256]{2,1,0:T(8,128)(2,1)S(1)} %bitcast.15), channel_id=1, source_target_pairs={{0,2},{1,3},{2,0},{3,1},{4,6},{5,7},{6,4},{7,5},{8,10},{9,11},{10,... | collective-permute-start | bytes 6291464 | tf_op jit(solution)/shard_map/ppermute | solution.py:547
  9.1 46.2 %all-to-all-start = ((s32[8,1,200]{2,1,0:T(1,128)}), s32[8,1,200]{2,1,0:T(1,128)S(1)}, u32[]{:S(2)}, u32[]{:S(2)}) async-start(s32[8,1,200]{2,1,0:T(1,128)} %broadcast_in_dim.108), calls=%async_computation | async-start | bytes 16384 | tf_op jit(solution)/shard_map/all_to_all | solution.py:562
  58.3 19.3 %collective-permute-start.2 = (bf16[25,64,256]{2,1,0:T(8,128)(2,1)S(1)}, bf16[25,64,256]{2,1,0:T(8,128)(2,1)S(1)}, u32[]{:S(2)}, u32[]{:S(2)}) collective-permute-start(bf16[25,64,256]{2,1,0:T(8,128)(2,1)S(1)} %get-tuple-element.25), channel_id=1, source_target_pairs={{0,2},{1,3},{2,0},{3,1},{4,6},{5,7},{6,4},{7,5},{8,10},{9,11},{10,... | collective-permute-start | bytes 2457608 | tf_op jit(solution)/shard_map/ppermute | solution.py:547
  59.0 29.7 %collective-permute-start.5 = (bf16[25,64,256]{2,1,0:T(8,128)(2,1)S(1)}, bf16[25,64,256]{2,1,0:T(8,128)(2,1)S(1)}, u32[]{:S(2)}, u32[]{:S(2)}) collective-permute-start(bf16[25,64,256]{2,1,0:T(8,128)(2,1)S(1)} %get-tuple-element.27), channel_id=1, source_target_pairs={{0,4},{1,5},{2,6},{3,7},{4,12},{5,13},{6,14},{7,15},{8,0},{9,1},{1... | collective-permute-start | bytes 2457608 | tf_op jit(solution)/shard_map/ppermute | solution.py:547
  61.3 36.3 %collective-permute-start.4 = (bf16[25,64,256]{2,1,0:T(8,128)(2,1)S(1)}, bf16[25,64,256]{2,1,0:T(8,128)(2,1)S(1)}, u32[]{:S(2)}, u32[]{:S(2)}) collective-permute-start(bf16[25,64,256]{2,1,0:T(8,128)(2,1)S(1)} %get-tuple-element.26), channel_id=1, source_target_pairs={{0,4},{1,5},{2,6},{3,7},{4,12},{5,13},{6,14},{7,15},{8,0},{9,1},{1... | collective-permute-start | bytes 2457608 | tf_op jit(solution)/shard_map/ppermute | solution.py:547
  79.7 25.3 %collective-permute-start.9 = (bf16[25,64,256]{2,1,0:T(8,128)(2,1)S(1)}, bf16[25,64,256]{2,1,0:T(8,128)(2,1)S(1)}, u32[]{:S(2)}, u32[]{:S(2)}) collective-permute-start(bf16[25,64,256]{2,1,0:T(8,128)(2,1)S(1)} %get-tuple-element.29), channel_id=1, source_target_pairs={{0,2},{1,3},{2,0},{3,1},{4,6},{5,7},{6,4},{7,5},{8,10},{9,11},{10,... | collective-permute-start | bytes 2457608 | tf_op jit(solution)/shard_map/ppermute | solution.py:547
  85.3 35.0 %collective-permute-start.7 = (bf16[25,64,256]{2,1,0:T(8,128)(2,1)S(1)}, bf16[25,64,256]{2,1,0:T(8,128)(2,1)S(1)}, u32[]{:S(2)}, u32[]{:S(2)}) collective-permute-start(bf16[25,64,256]{2,1,0:T(8,128)(2,1)S(1)} %get-tuple-element.28), channel_id=1, source_target_pairs={{8,12},{9,13},{10,14},{11,15},{4,0},{5,1},{6,2},{7,3},{24,28},{25,... | collective-permute-start | bytes 2457608 | tf_op jit(solution)/shard_map/ppermute | solution.py:547
  89.6 15.3 %copy-start.2 = (bf16[256,256]{1,0:T(8,128)(2,1)S(1)}, bf16[256,256]{1,0:T(8,128)(2,1)}, u32[]{:S(2)}) copy-start(bf16[256,256]{1,0:T(8,128)(2,1)} %rest_1_.5) | copy-start | bytes 393220
  89.7 15.3 %copy-start.3 = (bf16[256,256]{1,0:T(8,128)(2,1)S(1)}, bf16[256,256]{1,0:T(8,128)(2,1)}, u32[]{:S(2)}) copy-start(bf16[256,256]{1,0:T(8,128)(2,1)} %rest_2_.5) | copy-start | bytes 393220
  89.7 30.7 %collective-permute-start.8 = (bf16[25,64,256]{2,1,0:T(8,128)(2,1)S(1)}, bf16[25,64,256]{2,1,0:T(8,128)(2,1)S(1)}, u32[]{:S(2)}, u32[]{:S(2)}) collective-permute-start(bf16[25,64,256]{2,1,0:T(8,128)(2,1)S(1)} %pick_blocks.5.rest_2_), channel_id=1, source_target_pairs={{4,8},{5,9},{6,10},{7,11},{8,4},{9,5},{10,6},{11,7},{20,24},{21,25... | collective-permute-start | bytes 2457608 | tf_op jit(solution)/shard_map/ppermute | solution.py:547
  99.5 32.6 %collective-permute-start.6 = (bf16[25,64,256]{2,1,0:T(8,128)(2,1)S(1)}, bf16[25,64,256]{2,1,0:T(8,128)(2,1)S(1)}, u32[]{:S(2)}, u32[]{:S(2)}) collective-permute-start(bf16[25,64,256]{2,1,0:T(8,128)(2,1)S(1)} %pick_blocks.6), channel_id=1, source_target_pairs={{4,8},{5,9},{6,10},{7,11},{8,4},{9,5},{10,6},{11,7},{20,24},{21,25... | collective-permute-start | bytes 2457608 | tf_op jit(solution)/shard_map/ppermute | solution.py:547
  102.3 29.8 %collective-permute-start.3 = (bf16[25,64,256]{2,1,0:T(8,128)(2,1)S(1)}, bf16[25,64,256]{2,1,0:T(8,128)(2,1)S(1)}, u32[]{:S(2)}, u32[]{:S(2)}) collective-permute-start(bf16[25,64,256]{2,1,0:T(8,128)(2,1)S(1)} %collective-permute-done.2.rest_1_), channel_id=1, source_target_pairs={{8,12},{9,13},{10,14},{11,15},{4,0},{5,1},{6,2},{7,3},{24,28},{25,... | collective-permute-start | bytes 2457608 | tf_op jit(solution)/shard_map/ppermute | solution.py:547

commit v20 on v19

--- a/solution.py
+++ b/solution.py
@@ -246,11 +246,14 @@
     *rest,
     head_width,
     places,
+    first,
+    last,
 ):
     weight_refs, rest = rest[:3], rest[3:]
     piece_refs = rest[: len(places)]
-    mixed_ref, buffer_ref, query_buf, own_buf, stats_buf, member_buf, placed_buf = rest[-13:-6]
-    attended_buf, before_buf, done_buf, in_sems, out_sems, piece_sems = rest[-6:]
+    mixed_ref, buffer_ref, *states = rest[-16:-12]
+    query_buf, own_buf, stats_buf, member_buf, placed_buf = rest[-12:-7]
+    attended_buf, before_buf, done_buf, in_sems, out_sems, piece_sems, state_sems = rest[-7:]
     begin, count = range_ref[0], range_ref[1]
     pair_count = member_buf.shape[2]
     copies = copy_pieces(piece_refs, buffer_ref, places, piece_sems)
@@ -298,7 +301,7 @@
             finish,
         )
 
-        @pl.when(i > 1)
+        @pl.when((i > 0) & (begin + i > 1))
         def _():
             for copy in stores(begin + i - 2):
                 copy.wait()
@@ -307,12 +310,24 @@
         attended_buf[...] = attended
         before_buf[...] = placed_buf[slot].reshape(before_buf.shape)
 
-        @pl.when(i > 0)
+        @pl.when(begin + i > 0)
         def _():
             for copy in stores(begin + i - 1):
                 copy.start()
 
         return carry
+
+    held = (attended_buf, before_buf)
+    if first:
+        for buf in held:
+            buf[...] = jnp.zeros_like(buf)
+    else:
+        loads = [
+            pltpu.make_async_copy(state, buf, state_sems.at[n])
+            for n, (state, buf) in enumerate(zip(states, held, strict=True))
+        ]
+        for copy in loads:
+            copy.start()
 
     @pl.when(count > 0)
     def _():
@@ -326,22 +341,36 @@
     def _():
         for copy in fetches(begin, 0, known=False):
             copy.start()
-        attended_buf[...] = jnp.zeros_like(attended_buf)
-        before_buf[...] = jnp.zeros_like(before_buf)
+
+    if not first:
+        for copy in loads:
+            copy.wait()
+
+    @pl.when(count > 0)
+    def _():
         lax.fori_loop(0, count, one_step, 0)
         for copy in fetches(begin + count - 1, count % 2):
             copy.wait()
-        mixed = finish()
-
-        @pl.when(count > 1)
-        def _():
-            for copy in stores(begin + count - 2):
-                copy.wait()
-
-        done_buf[...] = mixed.reshape(done_buf.shape)
+
+    @pl.when((count > 0) & (begin + count > 1))
+    def _():
+        for copy in stores(begin + count - 2):
+            copy.wait()
+
+    if last:
+        done_buf[...] = finish().reshape(done_buf.shape)
         for copy in stores(begin + count - 1):
             copy.start()
         for copy in stores(begin + count - 1):
+            copy.wait()
+    else:
+        saves = [
+            pltpu.make_async_copy(buf, state, state_sems.at[n])
+            for n, (state, buf) in enumerate(zip(states, held, strict=True))
+        ]
+        for copy in saves:
+            copy.start()
+        for copy in saves:
             copy.wait()
 
 
@@ -430,7 +459,7 @@
     return jnp.concatenate(attended, axis=0), finished
 
 
-def attend(steps, order, table, own, placed, weights, buffer, pieces, places, so_far):
+def attend(steps, order, table, own, placed, weights, buffer, pieces, places, so_far, last):
     blocks, cluster, width = placed.shape
     pair_count = table.shape[0] // blocks
     smem = pl.BlockSpec(memory_space=pltpu.SMEM)
@@ -439,20 +468,27 @@
     in_specs = [smem] * 3 + [hbm] * len(own) + [pl.BlockSpec(memory_space=pltpu.HBM)] + [vmem] * (3 + len(pieces)) + [hbm]
     aliases = {len(in_specs) - 1: 1}
     operands = [*own, placed, *weights, *pieces, buffer]
-    if so_far is not None:
-        aliases[len(in_specs)] = 0
+    for at, x in zip((0, 2, 3), so_far):
+        aliases[len(in_specs)] = at
         in_specs.append(hbm)
-        operands.append(so_far)
+        operands.append(x)
     kernel = functools.partial(
-        attend_kernel, head_width=width // HEADS, places=places
-    )
+        attend_kernel,
+        head_width=width // HEADS,
+        places=places,
+        first=not so_far,
+        last=last,
+    )
+    state = jax.ShapeDtypeStruct((STEP * cluster, width), jnp.bfloat16)
     return pl.pallas_call(
         kernel,
         in_specs=in_specs,
-        out_specs=[hbm, hbm],
+        out_specs=[hbm] * 4,
         out_shape=[
             jax.ShapeDtypeStruct(placed.shape, jnp.bfloat16),
             jax.ShapeDtypeStruct(buffer.shape, jnp.bfloat16),
+            state,
+            state,
         ],
         scratch_shapes=[
             *[pltpu.VMEM((2, STEP) + x.shape[1:], x.dtype) for x in own],
@@ -464,6 +500,7 @@
             pltpu.SemaphoreType.DMA((2, STEP * (pair_count + 4))),
             pltpu.SemaphoreType.DMA((STEP,)),
             pltpu.SemaphoreType.DMA((len(pieces), 5)),
+            pltpu.SemaphoreType.DMA((2,)),
         ],
         input_output_aliases=aliases,
         cost_estimate=lasting(18),
@@ -632,11 +669,13 @@
         ((outward, 3), (middle, 5)),
         ((on, 4), (middle_cross, 6)),
     )
-    mixed = None
+    so_far = ()
     for phase, arrived in zip(phases, arrivals, strict=True):
         pieces = [piece for piece, _ in arrived]
         places = tuple(at * capacity for _, at in arrived)
-        mixed, buffer = attend(phase, *shared, buffer, pieces, places, mixed)
+        last = arrived is arrivals[-1]
+        mixed, buffer, *states = attend(phase, *shared, buffer, pieces, places, so_far, last)
+        so_far = (mixed, *states)
     return mixed.reshape(rows_dev, width)
 
 

time: 149 us -> 150 us (level)
  transfers between devices with their start and end apart: 11 -> 11, of which waited for: 3 -> 4; matrix products, arithmetic and copies ran while one was open for 2% -> 2% of each run, Pallas kernels for 44% -> 44%
where the time goes in v20:
time: 150 us; the launch traced here: 147 us
  Pallas kernels  86 us (57%)
  waiting for transfers between devices  25.9 us (17%)
  starting transfers between devices  24.4 us (16%)
  between operations  5.71 us (4%)
  local copies, waits for them, and re-layouts  3.39 us (2%)
  other arithmetic  1.64 us (1%)
    pallas_call x3, Pallas kernels, attend(): pl.pallas_call(kernel, in_specs=in_specs, out_specs=[hbm] * 4, out_shape=...  41.1 us
    pallas_call x1, Pallas kernels, own_part(): pl.pallas_call(functools.partial(own_kernel, head_width=width // HEADS),...  28.5 us
    ppermute x10, waiting for transfers between devices, moved(): return lax.ppermute(x, 'elec', pairs_of)  20.8 us
    ppermute x10, starting transfers between devices, moved(): return lax.ppermute(x, 'elec', pairs_of)  18.6 us
    pallas_call x4, Pallas kernels, pick(): pl.pallas_call(functools.partial(pick_kernel, plan=plan, capacity=capacit...  7.88 us
    all_to_all x1, starting transfers between devices, body(): lax.all_to_all(jnp.broadcast_to(tables[None], (SPAN, SPAN * capacity)), '...  5.81 us
    all_to_all x1, waiting for transfers between devices, body(): lax.all_to_all(jnp.broadcast_to(tables[None], (SPAN, SPAN * capacity)), '...  5.09 us
    pallas_call x1, Pallas kernels, collect(): pl.pallas_call(functools.partial(collect_kernel, places=places), in_specs...  5.02 us
  transfers between devices with their start and end apart: 11, of which 4 were waited for; matrix products, arithmetic and copies ran while one was open for 2% of the time, Pallas kernels for 44%

profile of v20, /device:TPU:8, one launch (start us, length us, event | category | flops | bytes accessed | tf_op | source)
XLA Modules:
  0.0 147.1 jit_solution(13609190489801010305)
XLA Ops:
  0.0 1.6 %copy-done.1 = bf16[4096,256]{1,0:T(8,128)(2,1)S(1)} copy-done((bf16[4096,256]{1,0:T(8,128)(2,1)S(1)}, bf16[4096,256]{1,0:T(8,128)(2,1)}, u32[]{:S(2)}) %copy-start.1) | copy-done | bytes 2097176
  1.6 0.7 copy-done.4
  2.3 3.5 %place_rows.1 = (bf16[4096,256]{1,0:T(8,128)(2,1)}, bf16[4096,256]{1,0:T(8,128)(2,1)S(1)}) custom-call(bf16[4096,256]{1,0:T(8,128)(2,1)S(1)} %copy-done.1, s32[8,1,512]{2,1,0:T(1,128)S(1)} %bitcast.25), custom_call_target="tpu_custom_call" | custom-call | flops 6899999744 | tf_op jit(solution)/shard_map/place_rows/pallas_call | solution.py:67
  5.8 2.0 %collective-permute-start = (bf16[64,64,256]{2,1,0:T(8,128)(2,1)S(1)}, bf16[64,64,256]{2,1,0:T(8,128)(2,1)}, u32[]{:S(2)}, u32[]{:S(2)}) collective-permute-start(bf16[64,64,256]{2,1,0:T(8,128)(2,1)S(1)} %bitcast.15), channel_id=1, source_target_pairs={{0,2},{1,3},{2,0},{3,1},{4,6},{5,7},{6,4},{7,5},{8,10},{9,11},{10,... | collective-permute-start | bytes 6291464 | tf_op jit(solution)/shard_map/ppermute | solution.py:584
  7.9 0.1 reshape.148
  8.1 0.2 select_reduce_fusion.1
  8.3 0.1 select_reduce_fusion
  8.5 0.6 broadcast_in_dim.108
  9.1 5.8 %all-to-all-start = ((s32[8,1,200]{2,1,0:T(1,128)}), s32[8,1,200]{2,1,0:T(1,128)S(1)}, u32[]{:S(2)}, u32[]{:S(2)}) async-start(s32[8,1,200]{2,1,0:T(1,128)} %broadcast_in_dim.108), calls=%async_computation | async-start | bytes 16384 | tf_op jit(solution)/shard_map/all_to_all | solution.py:599
  14.9 0.2 select_reduce_fusion.3
  15.1 0.7 fusion.14
  21.7 28.5 %own_blocks.1 = (bf16[64,256,256]{2,1,0:T(8,128)(2,1)}, bf16[64,256,256]{2,1,0:T(8,128)(2,1)}, f32[64,8,256]{2,1,0:T(8,128)S(1)}) custom-call(bf16[4096,256]{1,0:T(8,128)(2,1)S(1)} %get-tuple-element.24.normed_ref, bf16[256,256]{1,0:T(8,128)(2,1)S(1)} %bitcast.19, bf16[256,256]{1,0:T(8,128)(2,1)S(1)} %copy-done, bf16[256,256]{1,0:T(8,128)(2,1)S(1)} %bitcast.20, ...), custom_call_target="tpu_custom_call" | custom-call | flops 23000000512 | tf_op jit(solution)/shard_map/own_blocks/pallas_call | solution.py:178
  50.2 5.1 %all-to-all-done = s32[8,1,200]{2,1,0:T(1,128)S(1)} async-done(((s32[8,1,200]{2,1,0:T(1,128)}), s32[8,1,200]{2,1,0:T(1,128)S(1)}, u32[]{:S(2)}, u32[]{:S(2)}) %all-to-all-start) | async-done | bytes 6432 | tf_op jit(solution)/shard_map/all_to_all | solution.py:599
  55.3 3.0 %pick_blocks.4 = (bf16[25,64,256]{2,1,0:T(8,128)(2,1)S(1)}, bf16[25,64,256]{2,1,0:T(8,128)(2,1)S(1)}, bf16[25,64,256]{2,1,0:T(8,128)(2,1)S(1)}) custom-call(s32[1]{0:T(128)} %bitcast.8.position_ref, s32[8,200]{1,0:T(8,128)S(1)} %bitcast.21, bf16[64,64,256]{2,1,0:T(8,128)(2,1)S(1)} %bitcast.16, ...), custom_call_target="tpu_custom_call" | custom-call | flops 1724999936 | tf_op jit(solution)/shard_map/pick_blocks/pallas_call | solution.py:104
  58.3 0.6 collective-permute-start.2
  59.0 2.4 %collective-permute-start.5 = (bf16[25,64,256]{2,1,0:T(8,128)(2,1)S(1)}, bf16[25,64,256]{2,1,0:T(8,128)(2,1)S(1)}, u32[]{:S(2)}, u32[]{:S(2)}) collective-permute-start(bf16[25,64,256]{2,1,0:T(8,128)(2,1)S(1)} %get-tuple-element.31), channel_id=1, source_target_pairs={{0,4},{1,5},{2,6},{3,7},{4,12},{5,13},{6,14},{7,15},{8,0},{9,1},{1... | collective-permute-start | bytes 2457608 | tf_op jit(solution)/shard_map/ppermute | solution.py:584
  61.3 1.0 collective-permute-start.4
  62.3 15.3 %collective-permute-done.2.rest_1_ = bf16[25,64,256]{2,1,0:T(8,128)(2,1)S(1)} collective-permute-done((bf16[25,64,256]{2,1,0:T(8,128)(2,1)S(1)}, bf16[25,64,256]{2,1,0:T(8,128)(2,1)S(1)}, u32[]{:S(2)}, u32[]{:S(2)}) %collective-permute-start.2) | collective-permute-done | bytes 819232 | tf_op jit(solution)/shard_map/ppermute | solution.py:584
  77.6 2.1 %pick_blocks.7 = (bf16[25,64,256]{2,1,0:T(8,128)(2,1)S(1)}, bf16[25,64,256]{2,1,0:T(8,128)(2,1)S(1)}) custom-call(s32[1]{0:T(128)} %bitcast.8.position_ref, s32[8,200]{1,0:T(8,128)S(1)} %bitcast.22, bf16[64,64,256]{2,1,0:T(8,128)(2,1)} %collective-permute-done.1.rest_2_.rest_0_.refs_1_, bf16[25,64,256]{2,1,0:T(8,128)(2,1)S(1)} %collective-permute-done.2.rest_1_), custom_call_target="tpu_custom_call" | custom-call | flops 1724999936 | tf_op jit(solution)/shard_map/pick_blocks/pallas_call | solution.py:104
  79.7 0.6 collective-permute-start.9
  80.3 5.0 %collect_blocks.1.rest_6_ = bf16[367,64,256]{2,1,0:T(8,128)(2,1)} custom-call(bf16[64,64,256]{2,1,0:T(8,128)(2,1)S(1)} %bitcast.17, bf16[64,64,256]{2,1,0:T(8,128)(2,1)} %collective-permute-done.1.rest_2_.rest_0_.refs_1_, bf16[64,64,256]{2,1,0:T(8,128)(2,1)} %collective-permute-done.rest_1_.rest_0_.refs_2_), custom_call_target="tpu_custom_call" | custom-call | flops 4600000000 | tf_op jit(solution)/shard_map/collect_blocks/pallas_call | solution.py:226
  85.3 3.4 %collective-permute-start.7 = (bf16[25,64,256]{2,1,0:T(8,128)(2,1)S(1)}, bf16[25,64,256]{2,1,0:T(8,128)(2,1)S(1)}, u32[]{:S(2)}, u32[]{:S(2)}) collective-permute-start(bf16[25,64,256]{2,1,0:T(8,128)(2,1)S(1)} %get-tuple-element.32), channel_id=1, source_target_pairs={{8,12},{9,13},{10,14},{11,15},{4,0},{5,1},{6,2},{7,3},{24,28},{25,... | collective-permute-start | bytes 2457608 | tf_op jit(solution)/shard_map/ppermute | solution.py:584
  88.7 0.9 pick_blocks.5.rest_2_
  89.7 3.2 %collective-permute-start.8 = (bf16[25,64,256]{2,1,0:T(8,128)(2,1)S(1)}, bf16[25,64,256]{2,1,0:T(8,128)(2,1)S(1)}, u32[]{:S(2)}, u32[]{:S(2)}) collective-permute-start(bf16[25,64,256]{2,1,0:T(8,128)(2,1)S(1)} %pick_blocks.5.rest_2_), channel_id=1, source_target_pairs={{4,8},{5,9},{6,10},{7,11},{8,4},{9,5},{10,6},{11,7},{20,24},{21,25... | collective-permute-start | bytes 2457608 | tf_op jit(solution)/shard_map/ppermute | solution.py:584
  92.9 4.8 %collective-permute-done.4.rest_1_.rest_5_ = bf16[25,64,256]{2,1,0:T(8,128)(2,1)S(1)} collective-permute-done((bf16[25,64,256]{2,1,0:T(8,128)(2,1)S(1)}, bf16[25,64,256]{2,1,0:T(8,128)(2,1)S(1)}, u32[]{:S(2)}, u32[]{:S(2)}) %collective-permute-start.4) | collective-permute-done | bytes 819232 | tf_op jit(solution)/shard_map/ppermute | solution.py:584
  97.6 1.9 %pick_blocks.6 = bf16[25,64,256]{2,1,0:T(8,128)(2,1)S(1)} custom-call(s32[1]{0:T(128)} %bitcast.8.position_ref, s32[8,200]{1,0:T(8,128)S(1)} %bitcast.24, bf16[64,64,256]{2,1,0:T(8,128)(2,1)} %collective-permute-done.rest_1_.rest_0_.refs_2_, bf16[25,64,256]{2,1,0:T(8,128)(2,1)S(1)} %collective-permute-done.4.rest_1_.rest_5_, ...), custom_call_target="tpu_custom_call" | custom-call | flops 1724999936 | tf_op jit(solution)/shard_map/pick_blocks/pallas_call | solution.py:104
  99.5 2.8 %collective-permute-start.6 = (bf16[25,64,256]{2,1,0:T(8,128)(2,1)S(1)}, bf16[25,64,256]{2,1,0:T(8,128)(2,1)S(1)}, u32[]{:S(2)}, u32[]{:S(2)}) collective-permute-start(bf16[25,64,256]{2,1,0:T(8,128)(2,1)S(1)} %pick_blocks.6), channel_id=1, source_target_pairs={{4,8},{5,9},{6,10},{7,11},{8,4},{9,5},{10,6},{11,7},{20,24},{21,25... | collective-permute-start | bytes 2457608 | tf_op jit(solution)/shard_map/ppermute | solution.py:584
  102.3 2.7 %collective-permute-start.3 = (bf16[25,64,256]{2,1,0:T(8,128)(2,1)S(1)}, bf16[25,64,256]{2,1,0:T(8,128)(2,1)S(1)}, u32[]{:S(2)}, u32[]{:S(2)}) collective-permute-start(bf16[25,64,256]{2,1,0:T(8,128)(2,1)S(1)} %collective-permute-done.2.rest_1_), channel_id=1, source_target_pairs={{8,12},{9,13},{10,14},{11,15},{4,0},{5,1},{6,2},{7,3},{24,28},{25,... | collective-permute-start | bytes 2457608 | tf_op jit(solution)/shard_map/ppermute | solution.py:584
  105.0 14.5 %attend_blocks.3 = (bf16[64,64,256]{2,1,0:T(8,128)(2,1)}, bf16[367,64,256]{2,1,0:T(8,128)(2,1)}, bf16[512,256]{1,0:T(8,128)(2,1)S(1)}, bf16[512,256]{1,0:T(8,128)(2,1)S(1)}) custom-call(s32[2]{0:T(128)S(1)} %pad_add_fusion.1.rest_2_.range_ref, s32[64]{0:T(128)S(1)} %select_reduce_fusion.2.rest_0_.order_ref, ...), custom_call_target="tpu_custom_call", output_to_operand_aliasing={{1}: (13, {})} | custom-call | flops 20700000256 | tf_op jit(solution)/shard_map/attend_blocks/pallas_call | solution.py:483
  119.6 11.0 %attend_blocks.4 = (bf16[64,64,256]{2,1,0:T(8,128)(2,1)}, bf16[367,64,256]{2,1,0:T(8,128)(2,1)}, bf16[512,256]{1,0:T(8,128)(2,1)S(1)}, bf16[512,256]{1,0:T(8,128)(2,1)S(1)}) custom-call(s32[2]{0:T(128)S(1)} %pad_add_fusion.2.rest_3_.range_ref, ...), custom_call_target="tpu_custom_call", output_to_operand_aliasing={{1}: (12, {}), {0}: (13, {}), {2}: (14, {}), {3}: (15, {})} | custom-call | flops 20700000256 | tf_op jit(solution)/shard_map/attend_blocks/pallas_call | solution.py:483
  130.6 0.8 collective-permute-done.6.rest_4_
  131.4 15.5 %attend_blocks.5 = (bf16[64,64,256]{2,1,0:T(8,128)(2,1)}, bf16[367,64,256]{2,1,0:T(8,128)(2,1)}, bf16[512,256]{1,0:T(8,128)(2,1)S(1)}, bf16[512,256]{1,0:T(8,128)(2,1)S(1)}) custom-call(s32[2]{0:T(128)S(1)} %pad_add_fusion.rest_4_.range_ref, ...), custom_call_target="tpu_custom_call", output_to_operand_aliasing={{1}: (12, {}), {0}: (13, {}), {2}: (14, {}), {3}: (15, {})} | custom-call | flops 20700000256 | tf_op jit(solution)/shard_map/attend_blocks/pallas_call | solution.py:483
  (35 shorter events, 0.8 us)
Async XLA Ops:
  0.0 1.6 %copy-start.1 = (bf16[4096,256]{1,0:T(8,128)(2,1)S(1)}, bf16[4096,256]{1,0:T(8,128)(2,1)}, u32[]{:S(2)}) copy-start(bf16[4096,256]{1,0:T(8,128)(2,1)} %features_ref.1) | copy-start | bytes 6291460
  1.6 0.7 copy-start.4
  2.3 5.5 %copy-start.7 = (s32[64,3]{0,1:T(4,128)S(1)}, s32[64,3]{0,1:T(4,128)}, u32[]{:S(2)}) copy-start(s32[64,3]{0,1:T(4,128)} %param.10) | copy-start | bytes 2308
  2.3 19.0 %copy-start.6 = (bf16[256,256]{1,0:T(8,128)(2,1)S(1)}, bf16[256,256]{1,0:T(8,128)(2,1)}, u32[]{:S(2)}) copy-start(bf16[256,256]{1,0:T(8,128)(2,1)} %param.11) | copy-start | bytes 393220
  2.3 19.2 %copy-start.5 = (bf16[256,256]{1,0:T(8,128)(2,1)S(1)}, bf16[256,256]{1,0:T(8,128)(2,1)}, u32[]{:S(2)}) copy-start(bf16[256,256]{1,0:T(8,128)(2,1)} %param.13) | copy-start | bytes 393220
  2.3 19.3 %copy-start = (bf16[256,256]{1,0:T(8,128)(2,1)S(1)}, bf16[256,256]{1,0:T(8,128)(2,1)}, u32[]{:S(2)}) copy-start(bf16[256,256]{1,0:T(8,128)(2,1)} %key_w_ref.1) | copy-start | bytes 393220
  5.8 49.5 %collective-permute-start.1 = (bf16[64,64,256]{2,1,0:T(8,128)(2,1)S(1)}, bf16[64,64,256]{2,1,0:T(8,128)(2,1)}, u32[]{:S(2)}, u32[]{:S(2)}) collective-permute-start(bf16[64,64,256]{2,1,0:T(8,128)(2,1)S(1)} %bitcast.14), channel_id=1, source_target_pairs={{0,8},{1,9},{2,10},{3,11},{4,0},{5,1},{6,2},{7,3},{8,12},{9,13},{1... | collective-permute-start | bytes 6291464 | tf_op jit(solution)/shard_map/ppermute | solution.py:584
  5.8 49.5 %collective-permute-start = (bf16[64,64,256]{2,1,0:T(8,128)(2,1)S(1)}, bf16[64,64,256]{2,1,0:T(8,128)(2,1)}, u32[]{:S(2)}, u32[]{:S(2)}) collective-permute-start(bf16[64,64,256]{2,1,0:T(8,128)(2,1)S(1)} %bitcast.15), channel_id=1, source_target_pairs={{0,2},{1,3},{2,0},{3,1},{4,6},{5,7},{6,4},{7,5},{8,10},{9,11},{10,... | collective-permute-start | bytes 6291464 | tf_op jit(solution)/shard_map/ppermute | solution.py:584
  9.1 46.2 %all-to-all-start = ((s32[8,1,200]{2,1,0:T(1,128)}), s32[8,1,200]{2,1,0:T(1,128)S(1)}, u32[]{:S(2)}, u32[]{:S(2)}) async-start(s32[8,1,200]{2,1,0:T(1,128)} %broadcast_in_dim.108), calls=%async_computation | async-start | bytes 16384 | tf_op jit(solution)/shard_map/all_to_all | solution.py:599
  58.3 19.3 %collective-permute-start.2 = (bf16[25,64,256]{2,1,0:T(8,128)(2,1)S(1)}, bf16[25,64,256]{2,1,0:T(8,128)(2,1)S(1)}, u32[]{:S(2)}, u32[]{:S(2)}) collective-permute-start(bf16[25,64,256]{2,1,0:T(8,128)(2,1)S(1)} %get-tuple-element.29), channel_id=1, source_target_pairs={{0,2},{1,3},{2,0},{3,1},{4,6},{5,7},{6,4},{7,5},{8,10},{9,11},{10,... | collective-permute-start | bytes 2457608 | tf_op jit(solution)/shard_map/ppermute | solution.py:584
  59.0 29.7 %collective-permute-start.5 = (bf16[25,64,256]{2,1,0:T(8,128)(2,1)S(1)}, bf16[25,64,256]{2,1,0:T(8,128)(2,1)S(1)}, u32[]{:S(2)}, u32[]{:S(2)}) collective-permute-start(bf16[25,64,256]{2,1,0:T(8,128)(2,1)S(1)} %get-tuple-element.31), channel_id=1, source_target_pairs={{0,4},{1,5},{2,6},{3,7},{4,12},{5,13},{6,14},{7,15},{8,0},{9,1},{1... | collective-permute-start | bytes 2457608 | tf_op jit(solution)/shard_map/ppermute | solution.py:584
  61.3 36.3 %collective-permute-start.4 = (bf16[25,64,256]{2,1,0:T(8,128)(2,1)S(1)}, bf16[25,64,256]{2,1,0:T(8,128)(2,1)S(1)}, u32[]{:S(2)}, u32[]{:S(2)}) collective-permute-start(bf16[25,64,256]{2,1,0:T(8,128)(2,1)S(1)} %get-tuple-element.30), channel_id=1, source_target_pairs={{0,4},{1,5},{2,6},{3,7},{4,12},{5,13},{6,14},{7,15},{8,0},{9,1},{1... | collective-permute-start | bytes 2457608 | tf_op jit(solution)/shard_map/ppermute | solution.py:584
  79.7 25.3 %collective-permute-start.9 = (bf16[25,64,256]{2,1,0:T(8,128)(2,1)S(1)}, bf16[25,64,256]{2,1,0:T(8,128)(2,1)S(1)}, u32[]{:S(2)}, u32[]{:S(2)}) collective-permute-start(bf16[25,64,256]{2,1,0:T(8,128)(2,1)S(1)} %get-tuple-element.33), channel_id=1, source_target_pairs={{0,2},{1,3},{2,0},{3,1},{4,6},{5,7},{6,4},{7,5},{8,10},{9,11},{10,... | collective-permute-start | bytes 2457608 | tf_op jit(solution)/shard_map/ppermute | solution.py:584
  85.3 34.2 %collective-permute-start.7 = (bf16[25,64,256]{2,1,0:T(8,128)(2,1)S(1)}, bf16[25,64,256]{2,1,0:T(8,128)(2,1)S(1)}, u32[]{:S(2)}, u32[]{:S(2)}) collective-permute-start(bf16[25,64,256]{2,1,0:T(8,128)(2,1)S(1)} %get-tuple-element.32), channel_id=1, source_target_pairs={{8,12},{9,13},{10,14},{11,15},{4,0},{5,1},{6,2},{7,3},{24,28},{25,... | collective-permute-start | bytes 2457608 | tf_op jit(solution)/shard_map/ppermute | solution.py:584
  89.6 15.3 %copy-start.2 = (bf16[256,256]{1,0:T(8,128)(2,1)S(1)}, bf16[256,256]{1,0:T(8,128)(2,1)}, u32[]{:S(2)}) copy-start(bf16[256,256]{1,0:T(8,128)(2,1)} %rest_1_.5) | copy-start | bytes 393220
  89.7 15.3 %copy-start.3 = (bf16[256,256]{1,0:T(8,128)(2,1)S(1)}, bf16[256,256]{1,0:T(8,128)(2,1)}, u32[]{:S(2)}) copy-start(bf16[256,256]{1,0:T(8,128)(2,1)} %rest_2_.5) | copy-start | bytes 393220
  89.7 29.9 %collective-permute-start.8 = (bf16[25,64,256]{2,1,0:T(8,128)(2,1)S(1)}, bf16[25,64,256]{2,1,0:T(8,128)(2,1)S(1)}, u32[]{:S(2)}, u32[]{:S(2)}) collective-permute-start(bf16[25,64,256]{2,1,0:T(8,128)(2,1)S(1)} %pick_blocks.5.rest_2_), channel_id=1, source_target_pairs={{4,8},{5,9},{6,10},{7,11},{8,4},{9,5},{10,6},{11,7},{20,24},{21,25... | collective-permute-start | bytes 2457608 | tf_op jit(solution)/shard_map/ppermute | solution.py:584
  99.5 31.9 %collective-permute-start.6 = (bf16[25,64,256]{2,1,0:T(8,128)(2,1)S(1)}, bf16[25,64,256]{2,1,0:T(8,128)(2,1)S(1)}, u32[]{:S(2)}, u32[]{:S(2)}) collective-permute-start(bf16[25,64,256]{2,1,0:T(8,128)(2,1)S(1)} %pick_blocks.6), channel_id=1, source_target_pairs={{4,8},{5,9},{6,10},{7,11},{8,4},{9,5},{10,6},{11,7},{20,24},{21,25... | collective-permute-start | bytes 2457608 | tf_op jit(solution)/shard_map/ppermute | solution.py:584
  102.3 28.3 %collective-permute-start.3 = (bf16[25,64,256]{2,1,0:T(8,128)(2,1)S(1)}, bf16[25,64,256]{2,1,0:T(8,128)(2,1)S(1)}, u32[]{:S(2)}, u32[]{:S(2)}) collective-permute-start(bf16[25,64,256]{2,1,0:T(8,128)(2,1)S(1)} %collective-permute-done.2.rest_1_), channel_id=1, source_target_pairs={{8,12},{9,13},{10,14},{11,15},{4,0},{5,1},{6,2},{7,3},{24,28},{25,... | collective-permute-start | bytes 2457608 | tf_op jit(solution)/shard_map/ppermute | solution.py:584

commit v21 on v20

--- a/solution.py
+++ b/solution.py
@@ -14,7 +14,7 @@
 GROUP = 4
 STEP = 8
 OWN_STEP = 4
-SCORES_AHEAD, WEIGHTS_AHEAD = 2, 1
+SCORES_AHEAD, WEIGHTS_AHEAD = 3, 1
 VMEM_BYTES = 48 * 1024 * 1024
 
 NT = (((1,), (1,)), ((), ()))
@@ -607,6 +607,7 @@
 
     shape = (block_count // SUB, 1, SUB * cluster)
     block_shape = (block_count, cluster, width)
+    features = pltpu.with_memory_space_constraint(features, pltpu.HBM)
     placed, normed = place(features, assignment.reshape(shape))
     blocks = normed.reshape(block_shape)
     own_at = 7 * capacity

time: 150 us -> 149 us (level)
  local copies, waits for them, and re-layouts: 3.39 us -> 1.8 us
    unnamed x21 -> x19, local copies, waits for them, and re-layouts: 2.64 us -> 1.05 us
  transfers between devices with their start and end apart: 11 -> 11, of which waited for: 4 -> 5; matrix products, arithmetic and copies ran while one was open for 2% -> 2% of each run, Pallas kernels for 44% -> 43%
where the time goes in v21:
time: 149 us; the launch traced here: 147 us
  Pallas kernels  86.4 us (58%)
  waiting for transfers between devices  26.8 us (18%)
  starting transfers between devices  24.4 us (16%)
  between operations  5.44 us (4%)
  local copies, waits for them, and re-layouts  1.8 us (1%)
  other arithmetic  1.64 us (1%)
    pallas_call x3, Pallas kernels, attend(): pl.pallas_call(kernel, in_specs=in_specs, out_specs=[hbm] * 4, out_shape=...  40 us
    pallas_call x1, Pallas kernels, own_part(): pl.pallas_call(functools.partial(own_kernel, head_width=width // HEADS),...  28.5 us
    ppermute x10, waiting for transfers between devices, moved(): return lax.ppermute(x, 'elec', pairs_of)  21.5 us
    ppermute x10, starting transfers between devices, moved(): return lax.ppermute(x, 'elec', pairs_of)  18.6 us
    pallas_call x4, Pallas kernels, pick(): pl.pallas_call(functools.partial(pick_kernel, plan=plan, capacity=capacit...  7.88 us
    all_to_all x1, starting transfers between devices, body(): lax.all_to_all(jnp.broadcast_to(tables[None], (SPAN, SPAN * capacity)), '...  5.82 us
    all_to_all x1, waiting for transfers between devices, body(): lax.all_to_all(jnp.broadcast_to(tables[None], (SPAN, SPAN * capacity)), '...  5.35 us
    pallas_call x1, Pallas kernels, collect(): pl.pallas_call(functools.partial(collect_kernel, places=places), in_specs...  5.03 us
  transfers between devices with their start and end apart: 11, of which 5 were waited for; matrix products, arithmetic and copies ran while one was open for 2% of the time, Pallas kernels for 43%

profile of v21, /device:TPU:8, one launch (start us, length us, event | category | flops | bytes accessed | tf_op | source)
XLA Modules:
  0.0 146.5 jit_solution(94542982455505969)
XLA Ops:
  0.0 0.7 copy-done.3
  0.7 5.0 %place_rows.1 = (bf16[4096,256]{1,0:T(8,128)(2,1)}, bf16[4096,256]{1,0:T(8,128)(2,1)S(1)}) custom-call(bf16[4096,256]{1,0:T(8,128)(2,1)} %features_ref.1, s32[8,1,512]{2,1,0:T(1,128)S(1)} %bitcast.25), custom_call_target="tpu_custom_call" | custom-call | flops 6899999744 | tf_op jit(solution)/shard_map/place_rows/pallas_call | solution.py:67
  5.7 2.0 %collective-permute-start = (bf16[64,64,256]{2,1,0:T(8,128)(2,1)S(1)}, bf16[64,64,256]{2,1,0:T(8,128)(2,1)}, u32[]{:S(2)}, u32[]{:S(2)}) collective-permute-start(bf16[64,64,256]{2,1,0:T(8,128)(2,1)S(1)} %bitcast.15), channel_id=1, source_target_pairs={{0,2},{1,3},{2,0},{3,1},{4,6},{5,7},{6,4},{7,5},{8,10},{9,11},{10,... | collective-permute-start | bytes 6291464 | tf_op jit(solution)/shard_map/ppermute | solution.py:584
  7.8 0.1 reshape.148
  7.9 0.2 select_reduce_fusion.1
  8.2 0.1 select_reduce_fusion
  8.3 0.6 broadcast_in_dim.108
  8.9 5.8 %all-to-all-start = ((s32[8,1,200]{2,1,0:T(1,128)}), s32[8,1,200]{2,1,0:T(1,128)S(1)}, u32[]{:S(2)}, u32[]{:S(2)}) async-start(s32[8,1,200]{2,1,0:T(1,128)} %broadcast_in_dim.108), calls=%async_computation | async-start | bytes 16384 | tf_op jit(solution)/shard_map/all_to_all | solution.py:599
  14.8 0.2 select_reduce_fusion.3
  14.9 0.7 fusion.14
  21.3 28.5 %own_blocks.1 = (bf16[64,256,256]{2,1,0:T(8,128)(2,1)}, bf16[64,256,256]{2,1,0:T(8,128)(2,1)}, f32[64,8,256]{2,1,0:T(8,128)S(1)}) custom-call(bf16[4096,256]{1,0:T(8,128)(2,1)S(1)} %get-tuple-element.24.normed_ref, bf16[256,256]{1,0:T(8,128)(2,1)S(1)} %bitcast.19, bf16[256,256]{1,0:T(8,128)(2,1)S(1)} %copy-done, bf16[256,256]{1,0:T(8,128)(2,1)S(1)} %bitcast.20, ...), custom_call_target="tpu_custom_call" | custom-call | flops 23000000512 | tf_op jit(solution)/shard_map/own_blocks/pallas_call | solution.py:178
  49.8 5.3 %all-to-all-done = s32[8,1,200]{2,1,0:T(1,128)S(1)} async-done(((s32[8,1,200]{2,1,0:T(1,128)}), s32[8,1,200]{2,1,0:T(1,128)S(1)}, u32[]{:S(2)}, u32[]{:S(2)}) %all-to-all-start) | async-done | bytes 6432 | tf_op jit(solution)/shard_map/all_to_all | solution.py:599
  55.2 3.0 %pick_blocks.4 = (bf16[25,64,256]{2,1,0:T(8,128)(2,1)S(1)}, bf16[25,64,256]{2,1,0:T(8,128)(2,1)S(1)}, bf16[25,64,256]{2,1,0:T(8,128)(2,1)S(1)}) custom-call(s32[1]{0:T(128)} %bitcast.8.position_ref, s32[8,200]{1,0:T(8,128)S(1)} %bitcast.21, bf16[64,64,256]{2,1,0:T(8,128)(2,1)S(1)} %bitcast.16, ...), custom_call_target="tpu_custom_call" | custom-call | flops 1724999936 | tf_op jit(solution)/shard_map/pick_blocks/pallas_call | solution.py:104
  58.2 0.6 collective-permute-start.2
  58.8 2.4 %collective-permute-start.5 = (bf16[25,64,256]{2,1,0:T(8,128)(2,1)S(1)}, bf16[25,64,256]{2,1,0:T(8,128)(2,1)S(1)}, u32[]{:S(2)}, u32[]{:S(2)}) collective-permute-start(bf16[25,64,256]{2,1,0:T(8,128)(2,1)S(1)} %get-tuple-element.31), channel_id=1, source_target_pairs={{0,4},{1,5},{2,6},{3,7},{4,12},{5,13},{6,14},{7,15},{8,0},{9,1},{1... | collective-permute-start | bytes 2457608 | tf_op jit(solution)/shard_map/ppermute | solution.py:584
  61.2 1.0 collective-permute-start.4
  62.2 15.3 %collective-permute-done.2.rest_1_ = bf16[25,64,256]{2,1,0:T(8,128)(2,1)S(1)} collective-permute-done((bf16[25,64,256]{2,1,0:T(8,128)(2,1)S(1)}, bf16[25,64,256]{2,1,0:T(8,128)(2,1)S(1)}, u32[]{:S(2)}, u32[]{:S(2)}) %collective-permute-start.2) | collective-permute-done | bytes 819232 | tf_op jit(solution)/shard_map/ppermute | solution.py:584
  77.4 2.1 %pick_blocks.7 = (bf16[25,64,256]{2,1,0:T(8,128)(2,1)S(1)}, bf16[25,64,256]{2,1,0:T(8,128)(2,1)S(1)}) custom-call(s32[1]{0:T(128)} %bitcast.8.position_ref, s32[8,200]{1,0:T(8,128)S(1)} %bitcast.22, bf16[64,64,256]{2,1,0:T(8,128)(2,1)} %collective-permute-done.1.rest_2_.rest_0_.refs_1_, bf16[25,64,256]{2,1,0:T(8,128)(2,1)S(1)} %collective-permute-done.2.rest_1_), custom_call_target="tpu_custom_call" | custom-call | flops 1724999936 | tf_op jit(solution)/shard_map/pick_blocks/pallas_call | solution.py:104
  79.6 0.6 collective-permute-start.9
  80.1 5.0 %collect_blocks.1.rest_6_ = bf16[367,64,256]{2,1,0:T(8,128)(2,1)} custom-call(bf16[64,64,256]{2,1,0:T(8,128)(2,1)S(1)} %bitcast.17, bf16[64,64,256]{2,1,0:T(8,128)(2,1)} %collective-permute-done.1.rest_2_.rest_0_.refs_1_, bf16[64,64,256]{2,1,0:T(8,128)(2,1)} %collective-permute-done.rest_1_.rest_0_.refs_2_), custom_call_target="tpu_custom_call" | custom-call | flops 4600000000 | tf_op jit(solution)/shard_map/collect_blocks/pallas_call | solution.py:226
  85.2 3.4 %collective-permute-start.7 = (bf16[25,64,256]{2,1,0:T(8,128)(2,1)S(1)}, bf16[25,64,256]{2,1,0:T(8,128)(2,1)S(1)}, u32[]{:S(2)}, u32[]{:S(2)}) collective-permute-start(bf16[25,64,256]{2,1,0:T(8,128)(2,1)S(1)} %get-tuple-element.32), channel_id=1, source_target_pairs={{8,12},{9,13},{10,14},{11,15},{4,0},{5,1},{6,2},{7,3},{24,28},{25,... | collective-permute-start | bytes 2457608 | tf_op jit(solution)/shard_map/ppermute | solution.py:584
  88.6 0.9 pick_blocks.5.rest_2_
  89.5 3.2 %collective-permute-start.8 = (bf16[25,64,256]{2,1,0:T(8,128)(2,1)S(1)}, bf16[25,64,256]{2,1,0:T(8,128)(2,1)S(1)}, u32[]{:S(2)}, u32[]{:S(2)}) collective-permute-start(bf16[25,64,256]{2,1,0:T(8,128)(2,1)S(1)} %pick_blocks.5.rest_2_), channel_id=1, source_target_pairs={{4,8},{5,9},{6,10},{7,11},{8,4},{9,5},{10,6},{11,7},{20,24},{21,25... | collective-permute-start | bytes 2457608 | tf_op jit(solution)/shard_map/ppermute | solution.py:584
  92.7 4.7 %collective-permute-done.4.rest_1_.rest_5_ = bf16[25,64,256]{2,1,0:T(8,128)(2,1)S(1)} collective-permute-done((bf16[25,64,256]{2,1,0:T(8,128)(2,1)S(1)}, bf16[25,64,256]{2,1,0:T(8,128)(2,1)S(1)}, u32[]{:S(2)}, u32[]{:S(2)}) %collective-permute-start.4) | collective-permute-done | bytes 819232 | tf_op jit(solution)/shard_map/ppermute | solution.py:584
  97.5 1.9 %pick_blocks.6 = bf16[25,64,256]{2,1,0:T(8,128)(2,1)S(1)} custom-call(s32[1]{0:T(128)} %bitcast.8.position_ref, s32[8,200]{1,0:T(8,128)S(1)} %bitcast.24, bf16[64,64,256]{2,1,0:T(8,128)(2,1)} %collective-permute-done.rest_1_.rest_0_.refs_2_, bf16[25,64,256]{2,1,0:T(8,128)(2,1)S(1)} %collective-permute-done.4.rest_1_.rest_5_, ...), custom_call_target="tpu_custom_call" | custom-call | flops 1724999936 | tf_op jit(solution)/shard_map/pick_blocks/pallas_call | solution.py:104
  99.3 2.8 %collective-permute-start.6 = (bf16[25,64,256]{2,1,0:T(8,128)(2,1)S(1)}, bf16[25,64,256]{2,1,0:T(8,128)(2,1)S(1)}, u32[]{:S(2)}, u32[]{:S(2)}) collective-permute-start(bf16[25,64,256]{2,1,0:T(8,128)(2,1)S(1)} %pick_blocks.6), channel_id=1, source_target_pairs={{4,8},{5,9},{6,10},{7,11},{8,4},{9,5},{10,6},{11,7},{20,24},{21,25... | collective-permute-start | bytes 2457608 | tf_op jit(solution)/shard_map/ppermute | solution.py:584
  102.1 2.7 %collective-permute-start.3 = (bf16[25,64,256]{2,1,0:T(8,128)(2,1)S(1)}, bf16[25,64,256]{2,1,0:T(8,128)(2,1)S(1)}, u32[]{:S(2)}, u32[]{:S(2)}) collective-permute-start(bf16[25,64,256]{2,1,0:T(8,128)(2,1)S(1)} %collective-permute-done.2.rest_1_), channel_id=1, source_target_pairs={{8,12},{9,13},{10,14},{11,15},{4,0},{5,1},{6,2},{7,3},{24,28},{25,... | collective-permute-start | bytes 2457608 | tf_op jit(solution)/shard_map/ppermute | solution.py:584
  104.8 14.1 %attend_blocks.3 = (bf16[64,64,256]{2,1,0:T(8,128)(2,1)}, bf16[367,64,256]{2,1,0:T(8,128)(2,1)}, bf16[512,256]{1,0:T(8,128)(2,1)S(1)}, bf16[512,256]{1,0:T(8,128)(2,1)S(1)}) custom-call(s32[2]{0:T(128)S(1)} %pad_add_fusion.1.rest_2_.range_ref, s32[64]{0:T(128)S(1)} %select_reduce_fusion.2.rest_0_.order_ref, ...), custom_call_target="tpu_custom_call", output_to_operand_aliasing={{1}: (13, {})} | custom-call | flops 20700000256 | tf_op jit(solution)/shard_map/attend_blocks/pallas_call | solution.py:483
  119.0 10.8 %attend_blocks.4 = (bf16[64,64,256]{2,1,0:T(8,128)(2,1)}, bf16[367,64,256]{2,1,0:T(8,128)(2,1)}, bf16[512,256]{1,0:T(8,128)(2,1)S(1)}, bf16[512,256]{1,0:T(8,128)(2,1)S(1)}) custom-call(s32[2]{0:T(128)S(1)} %pad_add_fusion.2.rest_3_.range_ref, ...), custom_call_target="tpu_custom_call", output_to_operand_aliasing={{1}: (12, {}), {0}: (13, {}), {2}: (14, {}), {3}: (15, {})} | custom-call | flops 20700000256 | tf_op jit(solution)/shard_map/attend_blocks/pallas_call | solution.py:483
  129.8 0.4 collective-permute-done.3.rest_3_
  130.2 1.1 collective-permute-done.6.rest_4_
  131.2 15.1 %attend_blocks.5 = (bf16[64,64,256]{2,1,0:T(8,128)(2,1)}, bf16[367,64,256]{2,1,0:T(8,128)(2,1)}, bf16[512,256]{1,0:T(8,128)(2,1)S(1)}, bf16[512,256]{1,0:T(8,128)(2,1)S(1)}) custom-call(s32[2]{0:T(128)S(1)} %pad_add_fusion.rest_4_.range_ref, ...), custom_call_target="tpu_custom_call", output_to_operand_aliasing={{1}: (12, {}), {0}: (13, {}), {2}: (14, {}), {3}: (15, {})} | custom-call | flops 20700000256 | tf_op jit(solution)/shard_map/attend_blocks/pallas_call | solution.py:483
  (33 shorter events, 0.8 us)
Async XLA Ops:
  0.0 0.7 copy-start.3
  0.7 7.0 %copy-start.6 = (s32[64,3]{0,1:T(4,128)S(1)}, s32[64,3]{0,1:T(4,128)}, u32[]{:S(2)}) copy-start(s32[64,3]{0,1:T(4,128)} %param.10) | copy-start | bytes 2308
  0.7 20.2 %copy-start.5 = (bf16[256,256]{1,0:T(8,128)(2,1)S(1)}, bf16[256,256]{1,0:T(8,128)(2,1)}, u32[]{:S(2)}) copy-start(bf16[256,256]{1,0:T(8,128)(2,1)} %param.11) | copy-start | bytes 393220
  0.7 20.3 %copy-start.4 = (bf16[256,256]{1,0:T(8,128)(2,1)S(1)}, bf16[256,256]{1,0:T(8,128)(2,1)}, u32[]{:S(2)}) copy-start(bf16[256,256]{1,0:T(8,128)(2,1)} %param.13) | copy-start | bytes 393220
  0.7 20.4 %copy-start = (bf16[256,256]{1,0:T(8,128)(2,1)S(1)}, bf16[256,256]{1,0:T(8,128)(2,1)}, u32[]{:S(2)}) copy-start(bf16[256,256]{1,0:T(8,128)(2,1)} %key_w_ref.1) | copy-start | bytes 393220
  5.7 49.5 %collective-permute-start.1 = (bf16[64,64,256]{2,1,0:T(8,128)(2,1)S(1)}, bf16[64,64,256]{2,1,0:T(8,128)(2,1)}, u32[]{:S(2)}, u32[]{:S(2)}) collective-permute-start(bf16[64,64,256]{2,1,0:T(8,128)(2,1)S(1)} %bitcast.14), channel_id=1, source_target_pairs={{0,8},{1,9},{2,10},{3,11},{4,0},{5,1},{6,2},{7,3},{8,12},{9,13},{1... | collective-permute-start | bytes 6291464 | tf_op jit(solution)/shard_map/ppermute | solution.py:584
  5.7 49.5 %collective-permute-start = (bf16[64,64,256]{2,1,0:T(8,128)(2,1)S(1)}, bf16[64,64,256]{2,1,0:T(8,128)(2,1)}, u32[]{:S(2)}, u32[]{:S(2)}) collective-permute-start(bf16[64,64,256]{2,1,0:T(8,128)(2,1)S(1)} %bitcast.15), channel_id=1, source_target_pairs={{0,2},{1,3},{2,0},{3,1},{4,6},{5,7},{6,4},{7,5},{8,10},{9,11},{10,... | collective-permute-start | bytes 6291464 | tf_op jit(solution)/shard_map/ppermute | solution.py:584
  8.9 46.3 %all-to-all-start = ((s32[8,1,200]{2,1,0:T(1,128)}), s32[8,1,200]{2,1,0:T(1,128)S(1)}, u32[]{:S(2)}, u32[]{:S(2)}) async-start(s32[8,1,200]{2,1,0:T(1,128)} %broadcast_in_dim.108), calls=%async_computation | async-start | bytes 16384 | tf_op jit(solution)/shard_map/all_to_all | solution.py:599
  58.2 19.3 %collective-permute-start.2 = (bf16[25,64,256]{2,1,0:T(8,128)(2,1)S(1)}, bf16[25,64,256]{2,1,0:T(8,128)(2,1)S(1)}, u32[]{:S(2)}, u32[]{:S(2)}) collective-permute-start(bf16[25,64,256]{2,1,0:T(8,128)(2,1)S(1)} %get-tuple-element.29), channel_id=1, source_target_pairs={{0,2},{1,3},{2,0},{3,1},{4,6},{5,7},{6,4},{7,5},{8,10},{9,11},{10,... | collective-permute-start | bytes 2457608 | tf_op jit(solution)/shard_map/ppermute | solution.py:584
  58.8 29.8 %collective-permute-start.5 = (bf16[25,64,256]{2,1,0:T(8,128)(2,1)S(1)}, bf16[25,64,256]{2,1,0:T(8,128)(2,1)S(1)}, u32[]{:S(2)}, u32[]{:S(2)}) collective-permute-start(bf16[25,64,256]{2,1,0:T(8,128)(2,1)S(1)} %get-tuple-element.31), channel_id=1, source_target_pairs={{0,4},{1,5},{2,6},{3,7},{4,12},{5,13},{6,14},{7,15},{8,0},{9,1},{1... | collective-permute-start | bytes 2457608 | tf_op jit(solution)/shard_map/ppermute | solution.py:584
  61.2 36.3 %collective-permute-start.4 = (bf16[25,64,256]{2,1,0:T(8,128)(2,1)S(1)}, bf16[25,64,256]{2,1,0:T(8,128)(2,1)S(1)}, u32[]{:S(2)}, u32[]{:S(2)}) collective-permute-start(bf16[25,64,256]{2,1,0:T(8,128)(2,1)S(1)} %get-tuple-element.30), channel_id=1, source_target_pairs={{0,4},{1,5},{2,6},{3,7},{4,12},{5,13},{6,14},{7,15},{8,0},{9,1},{1... | collective-permute-start | bytes 2457608 | tf_op jit(solution)/shard_map/ppermute | solution.py:584
  79.6 25.3 %collective-permute-start.9 = (bf16[25,64,256]{2,1,0:T(8,128)(2,1)S(1)}, bf16[25,64,256]{2,1,0:T(8,128)(2,1)S(1)}, u32[]{:S(2)}, u32[]{:S(2)}) collective-permute-start(bf16[25,64,256]{2,1,0:T(8,128)(2,1)S(1)} %get-tuple-element.33), channel_id=1, source_target_pairs={{0,2},{1,3},{2,0},{3,1},{4,6},{5,7},{6,4},{7,5},{8,10},{9,11},{10,... | collective-permute-start | bytes 2457608 | tf_op jit(solution)/shard_map/ppermute | solution.py:584
  85.2 33.8 %collective-permute-start.7 = (bf16[25,64,256]{2,1,0:T(8,128)(2,1)S(1)}, bf16[25,64,256]{2,1,0:T(8,128)(2,1)S(1)}, u32[]{:S(2)}, u32[]{:S(2)}) collective-permute-start(bf16[25,64,256]{2,1,0:T(8,128)(2,1)S(1)} %get-tuple-element.32), channel_id=1, source_target_pairs={{8,12},{9,13},{10,14},{11,15},{4,0},{5,1},{6,2},{7,3},{24,28},{25,... | collective-permute-start | bytes 2457608 | tf_op jit(solution)/shard_map/ppermute | solution.py:584
  89.5 15.3 %copy-start.1 = (bf16[256,256]{1,0:T(8,128)(2,1)S(1)}, bf16[256,256]{1,0:T(8,128)(2,1)}, u32[]{:S(2)}) copy-start(bf16[256,256]{1,0:T(8,128)(2,1)} %rest_1_.5) | copy-start | bytes 393220
  89.5 15.3 %copy-start.2 = (bf16[256,256]{1,0:T(8,128)(2,1)S(1)}, bf16[256,256]{1,0:T(8,128)(2,1)}, u32[]{:S(2)}) copy-start(bf16[256,256]{1,0:T(8,128)(2,1)} %rest_2_.5) | copy-start | bytes 393220
  89.5 29.5 %collective-permute-start.8 = (bf16[25,64,256]{2,1,0:T(8,128)(2,1)S(1)}, bf16[25,64,256]{2,1,0:T(8,128)(2,1)S(1)}, u32[]{:S(2)}, u32[]{:S(2)}) collective-permute-start(bf16[25,64,256]{2,1,0:T(8,128)(2,1)S(1)} %pick_blocks.5.rest_2_), channel_id=1, source_target_pairs={{4,8},{5,9},{6,10},{7,11},{8,4},{9,5},{10,6},{11,7},{20,24},{21,25... | collective-permute-start | bytes 2457608 | tf_op jit(solution)/shard_map/ppermute | solution.py:584
  99.3 31.9 %collective-permute-start.6 = (bf16[25,64,256]{2,1,0:T(8,128)(2,1)S(1)}, bf16[25,64,256]{2,1,0:T(8,128)(2,1)S(1)}, u32[]{:S(2)}, u32[]{:S(2)}) collective-permute-start(bf16[25,64,256]{2,1,0:T(8,128)(2,1)S(1)} %pick_blocks.6), channel_id=1, source_target_pairs={{4,8},{5,9},{6,10},{7,11},{8,4},{9,5},{10,6},{11,7},{20,24},{21,25... | collective-permute-start | bytes 2457608 | tf_op jit(solution)/shard_map/ppermute | solution.py:584
  102.1 28.0 %collective-permute-start.3 = (bf16[25,64,256]{2,1,0:T(8,128)(2,1)S(1)}, bf16[25,64,256]{2,1,0:T(8,128)(2,1)S(1)}, u32[]{:S(2)}, u32[]{:S(2)}) collective-permute-start(bf16[25,64,256]{2,1,0:T(8,128)(2,1)S(1)} %collective-permute-done.2.rest_1_), channel_id=1, source_target_pairs={{8,12},{9,13},{10,14},{11,15},{4,0},{5,1},{6,2},{7,3},{24,28},{25,... | collective-permute-start | bytes 2457608 | tf_op jit(solution)/shard_map/ppermute | solution.py:584

commit v22 on v21

--- a/solution.py
+++ b/solution.py
@@ -112,6 +112,23 @@
         compiler_params=kernel_params(3),
         name="pick_blocks",
     )(position, wanted, *sources, *after)
+
+
+def held_kernel(piece_ref, *rest):
+    rest[-1][...] = piece_ref[...]
+
+
+def held_until(piece, after):
+    vmem = pl.BlockSpec(memory_space=pltpu.VMEM)
+    return pl.pallas_call(
+        held_kernel,
+        in_specs=[vmem] + [pl.BlockSpec(memory_space=pl.ANY)] * len(after),
+        out_specs=vmem,
+        out_shape=jax.ShapeDtypeStruct(piece.shape, piece.dtype),
+        cost_estimate=lasting(0.5),
+        compiler_params=kernel_params(3),
+        name="held_piece",
+    )(piece, *after)
 
 
 def tiles_of(query, first, span):
@@ -565,8 +582,7 @@
 
 FIRST_PLAN = ((0, source, itself), (1, source, partner), (2, crossed(onward), source))
 MIDDLE_PLAN = ((0, opposite, itself),)
-MIDDLE_CROSS_PLAN = ((0, opposite, partner),)
-NEAR_PLAN = ((0, partner, source), (0, onward, source))
+NEAR_PLAN = ((0, partner, source), (0, onward, source), (1, opposite, partner))
 
 
 def body(features, assignment, pairs, w_query, w_key, w_value, w_out, w_mix):
@@ -607,7 +623,6 @@
 
     shape = (block_count // SUB, 1, SUB * cluster)
     block_shape = (block_count, cluster, width)
-    features = pltpu.with_memory_space_constraint(features, pltpu.HBM)
     placed, normed = place(features, assignment.reshape(shape))
     blocks = normed.reshape(block_shape)
     own_at = 7 * capacity
@@ -652,13 +667,13 @@
     on = moved(on, swap)
     (middle_pick,) = pick(at_position, wanted, (blocks,), MIDDLE_PLAN, after=(second,))
     middle = moved(middle_pick, middle_moves)
-    near, outward = pick(at_position, wanted, (passed,), NEAR_PLAN, after=(on,))
+    near, outward, middle_cross = pick(
+        at_position, wanted, (passed, beside), NEAR_PLAN, after=(on,)
+    )
     near = moved(near, swap)
     outward = moved(outward, outward_moves)
     on = moved(on, outward_moves)
-    (middle_cross,) = pick(
-        at_position, wanted, (beside,), MIDDLE_CROSS_PLAN, after=(second_cross, middle_pick)
-    )
+    middle_cross = held_until(middle_cross, (second_cross, middle_pick))
     middle_cross = moved(middle_cross, middle_moves)
 
     buffer = collect((blocks, passed, beside), (own_at, passed_at, beside_at), total)

time: 149 us -> 150 us (level)
  the two profiles are of different devices: /device:TPU:8 before, /device:TPU:0 now
where the time goes in v22:
time: 150 us; the launch traced here: 149 us
  Pallas kernels  84.1 us (56%)
  waiting for transfers between devices  36.9 us (25%)
  starting transfers between devices  17.6 us (12%)
  between operations  5.52 us (4%)
  local copies, waits for them, and re-layouts  3.39 us (2%)
  other arithmetic  1.55 us (1%)
    pallas_call x3, Pallas kernels, attend(): pl.pallas_call(kernel, in_specs=in_specs, out_specs=[hbm] * 4, out_shape=...  40 us
    ppermute x10, waiting for transfers between devices, moved(): return lax.ppermute(x, 'elec', pairs_of)  30.3 us
    pallas_call x1, Pallas kernels, own_part(): pl.pallas_call(functools.partial(own_kernel, head_width=width // HEADS),...  28.5 us
    ppermute x10, starting transfers between devices, moved(): return lax.ppermute(x, 'elec', pairs_of)  14.3 us
    pallas_call x3, Pallas kernels, pick(): pl.pallas_call(functools.partial(pick_kernel, plan=plan, capacity=capacit...  6.92 us
    all_to_all x1, waiting for transfers between devices, body(): lax.all_to_all(jnp.broadcast_to(tables[None], (SPAN, SPAN * capacity)), '...  6.64 us
    pallas_call x1, Pallas kernels, collect(): pl.pallas_call(functools.partial(collect_kernel, places=places), in_specs...  5.02 us
    pallas_call x1, Pallas kernels, place(): pl.pallas_call(place_kernel, grid=(walkers // 2,), in_specs=[local, pl.Bl...  3.55 us
  transfers between devices with their start and end apart: 11, of which 4 were waited for; matrix products, arithmetic and copies ran while one was open for 2% of the time, Pallas kernels for 42%

profile of v22, /device:TPU:0, one launch (start us, length us, event | category | flops | bytes accessed | tf_op | source)
XLA Modules:
  0.0 149.1 jit_solution(10921449065161271)
XLA Ops:
  0.0 1.6 %copy-done.1 = bf16[4096,256]{1,0:T(8,128)(2,1)S(1)} copy-done((bf16[4096,256]{1,0:T(8,128)(2,1)S(1)}, bf16[4096,256]{1,0:T(8,128)(2,1)}, u32[]{:S(2)}) %copy-start.1) | copy-done | bytes 2097176
  1.6 0.7 copy-done.4
  2.3 3.5 %place_rows.1 = (bf16[4096,256]{1,0:T(8,128)(2,1)}, bf16[4096,256]{1,0:T(8,128)(2,1)S(1)}) custom-call(bf16[4096,256]{1,0:T(8,128)(2,1)S(1)} %copy-done.1, s32[8,1,512]{2,1,0:T(1,128)S(1)} %bitcast.24), custom_call_target="tpu_custom_call" | custom-call | flops 6899999744 | tf_op jit(solution)/shard_map/place_rows/pallas_call | solution.py:67
  5.9 4.0 %collective-permute-start.1 = (bf16[64,64,256]{2,1,0:T(8,128)(2,1)S(1)}, bf16[64,64,256]{2,1,0:T(8,128)(2,1)}, u32[]{:S(2)}, u32[]{:S(2)}) collective-permute-start(bf16[64,64,256]{2,1,0:T(8,128)(2,1)S(1)} %bitcast.14), channel_id=1, source_target_pairs={{0,8},{1,9},{2,10},{3,11},{4,0},{5,1},{6,2},{7,3},{8,12},{9,13},{1... | collective-permute-start | bytes 6291464 | tf_op jit(solution)/shard_map/ppermute | solution.py:600
  9.9 1.5 %collective-permute-start = (bf16[64,64,256]{2,1,0:T(8,128)(2,1)S(1)}, bf16[64,64,256]{2,1,0:T(8,128)(2,1)}, u32[]{:S(2)}, u32[]{:S(2)}) collective-permute-start(bf16[64,64,256]{2,1,0:T(8,128)(2,1)S(1)} %bitcast.15), channel_id=1, source_target_pairs={{0,2},{1,3},{2,0},{3,1},{4,6},{5,7},{6,4},{7,5},{8,10},{9,11},{10,... | collective-permute-start | bytes 6291464 | tf_op jit(solution)/shard_map/ppermute | solution.py:600
  11.5 0.1 reshape.148
  11.7 0.2 select_reduce_fusion.1
  11.9 0.1 select_reduce_fusion
  12.0 0.6 broadcast_in_dim.108
  12.6 3.3 %all-to-all-start = ((s32[8,1,200]{2,1,0:T(1,128)}), s32[8,1,200]{2,1,0:T(1,128)S(1)}, u32[]{:S(2)}, u32[]{:S(2)}) async-start(s32[8,1,200]{2,1,0:T(1,128)} %broadcast_in_dim.108), calls=%async_computation | async-start | bytes 16384 | tf_op jit(solution)/shard_map/all_to_all | solution.py:615
  16.0 0.2 select_reduce_fusion.3
  16.2 0.7 fusion.14
  22.5 28.5 %own_blocks.1 = (bf16[64,256,256]{2,1,0:T(8,128)(2,1)}, bf16[64,256,256]{2,1,0:T(8,128)(2,1)}, f32[64,8,256]{2,1,0:T(8,128)S(1)}) custom-call(bf16[4096,256]{1,0:T(8,128)(2,1)S(1)} %get-tuple-element.25.normed_ref, bf16[256,256]{1,0:T(8,128)(2,1)S(1)} %bitcast.19, bf16[256,256]{1,0:T(8,128)(2,1)S(1)} %copy-done, bf16[256,256]{1,0:T(8,128)(2,1)S(1)} %bitcast.20, ...), custom_call_target="tpu_custom_call" | custom-call | flops 23000000512 | tf_op jit(solution)/shard_map/own_blocks/pallas_call | solution.py:195
  51.1 6.6 %all-to-all-done = s32[8,1,200]{2,1,0:T(1,128)S(1)} async-done(((s32[8,1,200]{2,1,0:T(1,128)}), s32[8,1,200]{2,1,0:T(1,128)S(1)}, u32[]{:S(2)}, u32[]{:S(2)}) %all-to-all-start) | async-done | bytes 6432 | tf_op jit(solution)/shard_map/all_to_all | solution.py:615
  57.7 3.0 %pick_blocks.3 = (bf16[25,64,256]{2,1,0:T(8,128)(2,1)S(1)}, bf16[25,64,256]{2,1,0:T(8,128)(2,1)S(1)}, bf16[25,64,256]{2,1,0:T(8,128)(2,1)S(1)}) custom-call(s32[1]{0:T(128)} %bitcast.8.position_ref, s32[8,200]{1,0:T(8,128)S(1)} %bitcast.21, bf16[64,64,256]{2,1,0:T(8,128)(2,1)S(1)} %bitcast.16, bf16[64,64,256]{2,1,0:T(8,128)(2,1)} %collective-permute-done.rest_1_.refs_2_, ...), custom_call_target="tpu_custom_call" | custom-call | flops 1724999936 | tf_op jit(solution)/shard_map/pick_blocks/pallas_call | solution.py:104
  60.7 1.0 collective-permute-start.2
  61.7 0.2 collective-permute-start.5
  62.0 2.4 %collective-permute-start.4 = (bf16[25,64,256]{2,1,0:T(8,128)(2,1)S(1)}, bf16[25,64,256]{2,1,0:T(8,128)(2,1)S(1)}, u32[]{:S(2)}, u32[]{:S(2)}) collective-permute-start(bf16[25,64,256]{2,1,0:T(8,128)(2,1)S(1)} %get-tuple-element.32), channel_id=1, source_target_pairs={{0,4},{1,5},{2,6},{3,7},{4,12},{5,13},{6,14},{7,15},{8,0},{9,1},{1... | collective-permute-start | bytes 2457608 | tf_op jit(solution)/shard_map/ppermute | solution.py:600
  64.3 15.2 %collective-permute-done.2.rest_2_ = bf16[25,64,256]{2,1,0:T(8,128)(2,1)S(1)} collective-permute-done((bf16[25,64,256]{2,1,0:T(8,128)(2,1)S(1)}, bf16[25,64,256]{2,1,0:T(8,128)(2,1)S(1)}, u32[]{:S(2)}, u32[]{:S(2)}) %collective-permute-start.2) | collective-permute-done | bytes 819232 | tf_op jit(solution)/shard_map/ppermute | solution.py:600
  79.6 3.0 %pick_blocks.4 = (bf16[25,64,256]{2,1,0:T(8,128)(2,1)S(1)}, bf16[25,64,256]{2,1,0:T(8,128)(2,1)S(1)}, bf16[25,64,256]{2,1,0:T(8,128)(2,1)S(1)}) custom-call(s32[1]{0:T(128)} %bitcast.8.position_ref, s32[8,200]{1,0:T(8,128)S(1)} %bitcast.22, bf16[64,64,256]{2,1,0:T(8,128)(2,1)} %collective-permute-done.1.rest_2_.rest_0_.refs_1_, ...), custom_call_target="tpu_custom_call" | custom-call | flops 1724999936 | tf_op jit(solution)/shard_map/pick_blocks/pallas_call | solution.py:104
  82.6 1.0 collective-permute-start.9
  83.6 5.0 %collect_blocks.1.rest_6_ = bf16[367,64,256]{2,1,0:T(8,128)(2,1)} custom-call(bf16[64,64,256]{2,1,0:T(8,128)(2,1)S(1)} %bitcast.17, bf16[64,64,256]{2,1,0:T(8,128)(2,1)} %collective-permute-done.1.rest_2_.rest_0_.refs_1_, bf16[64,64,256]{2,1,0:T(8,128)(2,1)} %collective-permute-done.rest_1_.refs_2_), custom_call_target="tpu_custom_call" | custom-call | flops 4600000000 | tf_op jit(solution)/shard_map/collect_blocks/pallas_call | solution.py:243
  88.6 1.3 collective-permute-start.7
  89.9 0.9 pick_blocks.5.rest_1_
  90.9 0.8 collective-permute-start.8
  91.7 9.7 %collective-permute-done.4.rest_0_.rest_5_ = bf16[25,64,256]{2,1,0:T(8,128)(2,1)S(1)} collective-permute-done((bf16[25,64,256]{2,1,0:T(8,128)(2,1)S(1)}, bf16[25,64,256]{2,1,0:T(8,128)(2,1)S(1)}, u32[]{:S(2)}, u32[]{:S(2)}) %collective-permute-start.4) | collective-permute-done | bytes 819232 | tf_op jit(solution)/shard_map/ppermute | solution.py:600
  101.5 0.7 collective-permute-start.6
  102.2 1.3 collective-permute-start.3
  103.5 14.1 %attend_blocks.3 = (bf16[64,64,256]{2,1,0:T(8,128)(2,1)}, bf16[367,64,256]{2,1,0:T(8,128)(2,1)}, bf16[512,256]{1,0:T(8,128)(2,1)S(1)}, bf16[512,256]{1,0:T(8,128)(2,1)S(1)}) custom-call(s32[2]{0:T(128)S(1)} %pad_add_fusion.1.rest_2_.range_ref, s32[64]{0:T(128)S(1)} %select_reduce_fusion.2.rest_0_.order_ref, ...), custom_call_target="tpu_custom_call", output_to_operand_aliasing={{1}: (13, {})} | custom-call | flops 20700000256 | tf_op jit(solution)/shard_map/attend_blocks/pallas_call | solution.py:500
  117.7 10.8 %attend_blocks.4 = (bf16[64,64,256]{2,1,0:T(8,128)(2,1)}, bf16[367,64,256]{2,1,0:T(8,128)(2,1)}, bf16[512,256]{1,0:T(8,128)(2,1)S(1)}, bf16[512,256]{1,0:T(8,128)(2,1)S(1)}) custom-call(s32[2]{0:T(128)S(1)} %get-tuple-element.51.rest_3_.range_ref, ...), custom_call_target="tpu_custom_call", output_to_operand_aliasing={{1}: (12, {}), {0}: (13, {}), {2}: (14, {}), {3}: (15, {})} | custom-call | flops 20700000256 | tf_op jit(solution)/shard_map/attend_blocks/pallas_call | solution.py:500
  128.4 5.4 %collective-permute-done.3.rest_3_ = bf16[25,64,256]{2,1,0:T(8,128)(2,1)S(1)} collective-permute-done((bf16[25,64,256]{2,1,0:T(8,128)(2,1)S(1)}, bf16[25,64,256]{2,1,0:T(8,128)(2,1)S(1)}, u32[]{:S(2)}, u32[]{:S(2)}) %collective-permute-start.3) | collective-permute-done | bytes 819232 | tf_op jit(solution)/shard_map/ppermute | solution.py:600
  133.8 15.1 %attend_blocks.5 = (bf16[64,64,256]{2,1,0:T(8,128)(2,1)}, bf16[367,64,256]{2,1,0:T(8,128)(2,1)}, bf16[512,256]{1,0:T(8,128)(2,1)S(1)}, bf16[512,256]{1,0:T(8,128)(2,1)S(1)}) custom-call(s32[2]{0:T(128)S(1)} %get-tuple-element.50.rest_4_.range_ref, ...), custom_call_target="tpu_custom_call", output_to_operand_aliasing={{1}: (12, {}), {0}: (13, {}), {2}: (14, {}), {3}: (15, {})} | custom-call | flops 20700000256 | tf_op jit(solution)/shard_map/attend_blocks/pallas_call | solution.py:500
  (34 shorter events, 0.8 us)
Async XLA Ops:
  0.0 1.6 %copy-start.1 = (bf16[4096,256]{1,0:T(8,128)(2,1)S(1)}, bf16[4096,256]{1,0:T(8,128)(2,1)}, u32[]{:S(2)}) copy-start(bf16[4096,256]{1,0:T(8,128)(2,1)} %features_ref.1) | copy-start | bytes 6291460
  1.6 0.7 copy-start.4
  2.3 9.1 %copy-start.7 = (s32[64,3]{0,1:T(4,128)S(1)}, s32[64,3]{0,1:T(4,128)}, u32[]{:S(2)}) copy-start(s32[64,3]{0,1:T(4,128)} %param.10) | copy-start | bytes 2308
  2.3 19.8 %copy-start.6 = (bf16[256,256]{1,0:T(8,128)(2,1)S(1)}, bf16[256,256]{1,0:T(8,128)(2,1)}, u32[]{:S(2)}) copy-start(bf16[256,256]{1,0:T(8,128)(2,1)} %param.11) | copy-start | bytes 393220
  2.3 19.9 %copy-start.5 = (bf16[256,256]{1,0:T(8,128)(2,1)S(1)}, bf16[256,256]{1,0:T(8,128)(2,1)}, u32[]{:S(2)}) copy-start(bf16[256,256]{1,0:T(8,128)(2,1)} %param.13) | copy-start | bytes 393220
  2.3 20.0 %copy-start = (bf16[256,256]{1,0:T(8,128)(2,1)S(1)}, bf16[256,256]{1,0:T(8,128)(2,1)}, u32[]{:S(2)}) copy-start(bf16[256,256]{1,0:T(8,128)(2,1)} %key_w_ref.1) | copy-start | bytes 393220
  5.9 51.8 %collective-permute-start.1 = (bf16[64,64,256]{2,1,0:T(8,128)(2,1)S(1)}, bf16[64,64,256]{2,1,0:T(8,128)(2,1)}, u32[]{:S(2)}, u32[]{:S(2)}) collective-permute-start(bf16[64,64,256]{2,1,0:T(8,128)(2,1)S(1)} %bitcast.14), channel_id=1, source_target_pairs={{0,8},{1,9},{2,10},{3,11},{4,0},{5,1},{6,2},{7,3},{8,12},{9,13},{1... | collective-permute-start | bytes 6291464 | tf_op jit(solution)/shard_map/ppermute | solution.py:600
  9.9 47.8 %collective-permute-start = (bf16[64,64,256]{2,1,0:T(8,128)(2,1)S(1)}, bf16[64,64,256]{2,1,0:T(8,128)(2,1)}, u32[]{:S(2)}, u32[]{:S(2)}) collective-permute-start(bf16[64,64,256]{2,1,0:T(8,128)(2,1)S(1)} %bitcast.15), channel_id=1, source_target_pairs={{0,2},{1,3},{2,0},{3,1},{4,6},{5,7},{6,4},{7,5},{8,10},{9,11},{10,... | collective-permute-start | bytes 6291464 | tf_op jit(solution)/shard_map/ppermute | solution.py:600
  12.6 45.1 %all-to-all-start = ((s32[8,1,200]{2,1,0:T(1,128)}), s32[8,1,200]{2,1,0:T(1,128)S(1)}, u32[]{:S(2)}, u32[]{:S(2)}) async-start(s32[8,1,200]{2,1,0:T(1,128)} %broadcast_in_dim.108), calls=%async_computation | async-start | bytes 16384 | tf_op jit(solution)/shard_map/all_to_all | solution.py:615
  60.7 18.9 %collective-permute-start.2 = (bf16[25,64,256]{2,1,0:T(8,128)(2,1)S(1)}, bf16[25,64,256]{2,1,0:T(8,128)(2,1)S(1)}, u32[]{:S(2)}, u32[]{:S(2)}) collective-permute-start(bf16[25,64,256]{2,1,0:T(8,128)(2,1)S(1)} %get-tuple-element.30), channel_id=1, source_target_pairs={{0,2},{1,3},{2,0},{3,1},{4,6},{5,7},{6,4},{7,5},{8,10},{9,11},{10,... | collective-permute-start | bytes 2457608 | tf_op jit(solution)/shard_map/ppermute | solution.py:600
  61.7 28.2 %collective-permute-start.5 = (bf16[25,64,256]{2,1,0:T(8,128)(2,1)S(1)}, bf16[25,64,256]{2,1,0:T(8,128)(2,1)S(1)}, u32[]{:S(2)}, u32[]{:S(2)}) collective-permute-start(bf16[25,64,256]{2,1,0:T(8,128)(2,1)S(1)} %get-tuple-element.33), channel_id=1, source_target_pairs={{0,4},{1,5},{2,6},{3,7},{4,12},{5,13},{6,14},{7,15},{8,0},{9,1},{1... | collective-permute-start | bytes 2457608 | tf_op jit(solution)/shard_map/ppermute | solution.py:600
  62.0 39.4 %collective-permute-start.4 = (bf16[25,64,256]{2,1,0:T(8,128)(2,1)S(1)}, bf16[25,64,256]{2,1,0:T(8,128)(2,1)S(1)}, u32[]{:S(2)}, u32[]{:S(2)}) collective-permute-start(bf16[25,64,256]{2,1,0:T(8,128)(2,1)S(1)} %get-tuple-element.32), channel_id=1, source_target_pairs={{0,4},{1,5},{2,6},{3,7},{4,12},{5,13},{6,14},{7,15},{8,0},{9,1},{1... | collective-permute-start | bytes 2457608 | tf_op jit(solution)/shard_map/ppermute | solution.py:600
  82.6 20.9 %collective-permute-start.9 = (bf16[25,64,256]{2,1,0:T(8,128)(2,1)S(1)}, bf16[25,64,256]{2,1,0:T(8,128)(2,1)S(1)}, u32[]{:S(2)}, u32[]{:S(2)}) collective-permute-start(bf16[25,64,256]{2,1,0:T(8,128)(2,1)S(1)} %get-tuple-element.35), channel_id=1, source_target_pairs={{0,2},{1,3},{2,0},{3,1},{4,6},{5,7},{6,4},{7,5},{8,10},{9,11},{10,... | collective-permute-start | bytes 2457608 | tf_op jit(solution)/shard_map/ppermute | solution.py:600
  88.6 29.0 %collective-permute-start.7 = (bf16[25,64,256]{2,1,0:T(8,128)(2,1)S(1)}, bf16[25,64,256]{2,1,0:T(8,128)(2,1)S(1)}, u32[]{:S(2)}, u32[]{:S(2)}) collective-permute-start(bf16[25,64,256]{2,1,0:T(8,128)(2,1)S(1)} %get-tuple-element.34), channel_id=1, source_target_pairs={{8,12},{9,13},{10,14},{11,15},{4,0},{5,1},{6,2},{7,3},{24,28},{25,... | collective-permute-start | bytes 2457608 | tf_op jit(solution)/shard_map/ppermute | solution.py:600
  90.9 12.6 %copy-start.2 = (bf16[256,256]{1,0:T(8,128)(2,1)S(1)}, bf16[256,256]{1,0:T(8,128)(2,1)}, u32[]{:S(2)}) copy-start(bf16[256,256]{1,0:T(8,128)(2,1)} %rest_1_.5) | copy-start | bytes 393220
  90.9 12.6 %copy-start.3 = (bf16[256,256]{1,0:T(8,128)(2,1)S(1)}, bf16[256,256]{1,0:T(8,128)(2,1)}, u32[]{:S(2)}) copy-start(bf16[256,256]{1,0:T(8,128)(2,1)} %rest_2_.5) | copy-start | bytes 393220
  90.9 26.8 %collective-permute-start.8 = (bf16[25,64,256]{2,1,0:T(8,128)(2,1)S(1)}, bf16[25,64,256]{2,1,0:T(8,128)(2,1)S(1)}, u32[]{:S(2)}, u32[]{:S(2)}) collective-permute-start(bf16[25,64,256]{2,1,0:T(8,128)(2,1)S(1)} %pick_blocks.5.rest_1_), channel_id=1, source_target_pairs={{4,8},{5,9},{6,10},{7,11},{8,4},{9,5},{10,6},{11,7},{20,24},{21,25... | collective-permute-start | bytes 2457608 | tf_op jit(solution)/shard_map/ppermute | solution.py:600
  101.5 32.3 %collective-permute-start.6 = (bf16[25,64,256]{2,1,0:T(8,128)(2,1)S(1)}, bf16[25,64,256]{2,1,0:T(8,128)(2,1)S(1)}, u32[]{:S(2)}, u32[]{:S(2)}) collective-permute-start(bf16[25,64,256]{2,1,0:T(8,128)(2,1)S(1)} %held_piece.1), channel_id=1, source_target_pairs={{4,8},{5,9},{6,10},{7,11},{8,4},{9,5},{10,6},{11,7},{20,24},{21,25... | collective-permute-start | bytes 2457608 | tf_op jit(solution)/shard_map/ppermute | solution.py:600
  102.2 31.6 %collective-permute-start.3 = (bf16[25,64,256]{2,1,0:T(8,128)(2,1)S(1)}, bf16[25,64,256]{2,1,0:T(8,128)(2,1)S(1)}, u32[]{:S(2)}, u32[]{:S(2)}) collective-permute-start(bf16[25,64,256]{2,1,0:T(8,128)(2,1)S(1)} %collective-permute-done.2.rest_2_), channel_id=1, source_target_pairs={{8,12},{9,13},{10,14},{11,15},{4,0},{5,1},{6,2},{7,3},{24,28},{25,... | collective-permute-start | bytes 2457608 | tf_op jit(solution)/shard_map/ppermute | solution.py:600
